TPU v7x, 32 devices: a whole 2x2x4 slice. The times are simulated.
32 devices in a mesh: groups: 2 (over y), ep: 16 (over z, x, core), tp: 1.
Axes of the slice: x: 2, y: 2, z: 4, core: 2. Of those that a mesh axis runs over, the one named last changes fastest.
Arguments:
- queries: bfloat16 [128, 32, 128], P(('groups', 'ep'), 'tp'), parts along dimension 0, may hold values from -6 to 6
- key_cache: bfloat16 [128, 128, 2, 128], P(('groups', 'ep'), None, 'tp'), parts along dimension 0, may hold values from -6 to 6
- value_cache: bfloat16 [128, 128, 2, 128], P(('groups', 'ep'), None, 'tp'), parts along dimension 0, may hold values from -6 to 6
- new_key: bfloat16 [128, 2, 128], P(('groups', 'ep'), 'tp'), parts along dimension 0, may hold values from -6 to 6
- new_value: bfloat16 [128, 2, 128], P(('groups', 'ep'), 'tp'), parts along dimension 0, may hold values from -6 to 6
- lengths: int32 [128], P(('groups', 'ep')), parts along dimension 0, may hold values from 1 to 128, as said below
- residual: bfloat16 [512, 2048], P(('groups', 'ep'), 'tp'), parts along dimension 0, may hold values from -6 to 6
- norm_gain: float32 [2048], replicated, may hold values from 0.5 to 1.5
- routes: int32 [512, 8], P(('groups', 'ep')), parts along dimension 0, may hold values from 0 to 15, all different within a row; in each aligned block of 16 rows (0 to 15, 16 to 31, ...) at most 16 rows name the same one
- route_weights: float32 [512, 8], P(('groups', 'ep')), parts along dimension 0, may hold values from 0.05 to 0.4
- expert_in: bfloat16 [16, 2, 2048, 768], P('ep', None, None, 'tp'), may hold values from -0.125 to 0.125
- expert_down: bfloat16 [16, 768, 2048], P('ep', 'tp'), may hold values from -0.21875 to 0.21875
Outputs:
- attended: bfloat16 [128, 32, 128], P(('groups', 'ep'), 'tp'), parts along dimension 0
- moe_out: bfloat16 [512, 2048], P(('groups', 'ep'), 'tp'), parts along dimension 0
There are 2 independent parts, one for each index of `groups`. A program takes and returns all parts, laid end to end along the dimension named above; an argument that names none is the same for every part. Nothing has to cross between parts.
Inputs may be any that keep to these rules, and one draw needn't show every extreme that they name: `routes`: each row names 8 different experts; among the 16 rows of one device (aligned blocks) no expert is named by more than 16 rows, a bound that some block reaches. `lengths`: the first row of every draw fills all 128 slots.
All inputs are finite; a program needn't handle non-finite values.
Results may differ from a plain program's by a relative error of at most 0.0075.
Values may be sent and summed in bfloat16 or wider, within the bound.
No kernel may reach another device: no remote copies, remote signals or barrier semaphores. Data moves between devices by JAX's collectives and lax.ppermute only.
A program may use at most 64 MiB of HBM per device.

v0:
```python
import functools

import jax
import jax.numpy as jnp
from jax import lax
from jax.experimental import pallas as pl
from jax.experimental.pallas import tpu as pltpu
from jax.sharding import PartitionSpec as P


def attention_block(queries, key_cache, value_cache, new_key, new_value, lengths):
    rows_here, heads_here, head_size = queries.shape
    kv_here = key_cache.shape[2]
    slots_here = key_cache.shape[1]
    group = heads_here // kv_here
    scale = 1.0 / head_size**0.5
    grouped = queries.reshape(rows_here, kv_here, group, head_size)
    scores = (
        jnp.einsum("akgd,ackd->akgc", grouped, key_cache, preferred_element_type=jnp.float32)
        * scale
    )
    valid = (jnp.arange(slots_here)[None, :] < lengths[:, None])[:, None, None, :]
    scores = jnp.where(valid, scores, -1e30)
    own_score = (
        jnp.einsum("akgd,akd->akg", grouped, new_key, preferred_element_type=jnp.float32) * scale
    )
    largest = jnp.maximum(jnp.max(scores, axis=-1), own_score)
    cache_exp = jnp.exp(scores - largest[..., None])
    own_exp = jnp.exp(own_score - largest)
    total = jnp.sum(cache_exp, axis=-1) + own_exp
    cache_probs = (cache_exp / total[..., None]).astype(jnp.bfloat16)
    own_probs = (own_exp / total).astype(jnp.bfloat16)
    mixed = jnp.einsum(
        "akgc,ackd->akgd", cache_probs, value_cache, preferred_element_type=jnp.float32
    )
    mixed = (
        mixed
        + own_probs.astype(jnp.float32)[..., None] * new_value.astype(jnp.float32)[:, :, None, :]
    )
    return mixed.reshape(rows_here, heads_here, head_size).astype(jnp.bfloat16)


def normalize(residual, norm_gain):
    wide = residual.astype(jnp.float32)
    return (
        wide * lax.rsqrt(jnp.mean(wide * wide, axis=1, keepdims=True) + 1e-06) * norm_gain
    ).astype(jnp.bfloat16)


def load(sources, targets, sems):
    copies = [
        pltpu.make_async_copy(source, target, sems.at[i])
        for i, (source, target) in enumerate(zip(sources, targets))
    ]
    for copy in copies:
        copy.start()
    return copies


def stay(array):
    return pltpu.with_memory_space_constraint(array, pltpu.HBM)


HERE = pl.BlockSpec(memory_space=pltpu.VMEM)
ANYWHERE = pl.BlockSpec(memory_space=pl.ANY)


def params(mebibytes=4):
    return pltpu.CompilerParams(vmem_limit_bytes=mebibytes * 1024 * 1024)


def cost(flops=0, bytes_accessed=0):
    return pl.CostEstimate(flops=flops, bytes_accessed=bytes_accessed, transcendentals=0)


def from_hbm(kernel, out_shape, name, arrays, after=(), cost_estimate=None):
    return pl.pallas_call(
        kernel,
        out_shape=out_shape,
        in_specs=[pl.BlockSpec(memory_space=pltpu.HBM)] * len(arrays) + [ANYWHERE] * len(after),
        scratch_shapes=[
            (pltpu.VMEM if array.ndim > 1 else pltpu.SMEM)(array.shape, array.dtype)
            for array in arrays
        ]
        + [pltpu.SemaphoreType.DMA((len(arrays),))],
        compiler_params=params(),
        cost_estimate=cost_estimate,
        name=name,
    )(*(stay(array) for array in arrays), *after)


def attend_kernel(*refs):
    attended_ref = refs[-8]
    lengths_ref, queries_ref, keys_ref, values_ref, new_keys_ref, new_values_ref = refs[-7:-1]
    copies = load(refs[:6], refs[-7:-1], refs[-1])
    row_count, heads, head_size = queries_ref.shape
    kv_heads = new_keys_ref.shape[0] // row_count
    group = heads // kv_heads
    scale = 1.0 / head_size**0.5
    across = (((1,), (1,)), ((), ()))

    def grids(columns):
        shape = (heads, columns)
        head = lax.broadcasted_iota(jnp.int32, shape, 0) // group
        return head, lax.broadcasted_iota(jnp.int32, shape, 1)

    head, column = grids(keys_ref.shape[1])
    own_head, own_column = grids(new_keys_ref.shape[0])
    same_head = column % kv_heads == head
    slot = column // kv_heads
    for copy in copies:
        copy.wait()
    for a in range(row_count):
        query = queries_ref[a]
        scores = lax.dot_general(query, keys_ref[a], across, preferred_element_type=jnp.float32)
        scores = jnp.where(same_head & (slot < lengths_ref[a]), scores * scale, -1e30)
        own = lax.dot_general(
            query, new_keys_ref[...], across, preferred_element_type=jnp.float32
        )
        own = jnp.where(own_column == own_head + a * kv_heads, own * scale, -1e30)
        largest = jnp.maximum(
            jnp.max(scores, axis=1, keepdims=True), jnp.max(own, axis=1, keepdims=True)
        )
        scores = jnp.exp(scores - largest)
        own = jnp.exp(own - largest)
        total = jnp.sum(scores, axis=1, keepdims=True) + jnp.sum(own, axis=1, keepdims=True)
        mixed = jnp.dot(
            (scores / total).astype(jnp.bfloat16),
            values_ref[a],
            preferred_element_type=jnp.float32,
        ) + jnp.dot(
            (own / total).astype(jnp.bfloat16),
            new_values_ref[...],
            preferred_element_type=jnp.float32,
        )
        attended_ref[a] = mixed.astype(jnp.bfloat16)


def attend(queries, key_cache, value_cache, new_key, new_value, lengths, after):
    rows_here, slots_here, kv_here, head_size = key_cache.shape
    lines = (rows_here, slots_here * kv_here, head_size)
    arrays = (
        lengths,
        queries,
        key_cache.reshape(lines),
        value_cache.reshape(lines),
        new_key.reshape(-1, head_size),
        new_value.reshape(-1, head_size),
    )
    out_shape = jax.ShapeDtypeStruct(queries.shape, jnp.bfloat16)
    work = cost(0, 16 * key_cache.size * key_cache.dtype.itemsize)
    return from_hbm(attend_kernel, out_shape, "attend", arrays, after, work)


def hold_kernel(count, pieces, *refs):
    sources, targets, sems = refs[:count], refs[-1 - count : -1], refs[-1]
    starts, ends = [], []
    for source, target in zip(sources, targets):
        lines = source.shape[0] // pieces
        for i in range(pieces):
            starts.append(source.at[pl.ds(i * lines, lines)])
            ends.append(target.at[pl.ds(i * lines, lines)])
    for copy in load(starts, ends, sems):
        copy.wait()


def hold(arrays, after, pieces=4):
    flat = [array.reshape(-1, array.shape[-1]) for array in arrays]
    size = sum(array.size for array in flat)
    return pl.pallas_call(
        functools.partial(hold_kernel, len(flat), pieces),
        out_shape=[pltpu.VMEM(array.shape, array.dtype) for array in flat],
        in_specs=[pl.BlockSpec(memory_space=pltpu.HBM)] * len(flat) + [ANYWHERE] * len(after),
        scratch_shapes=[pltpu.SemaphoreType.DMA((pieces * len(flat),))],
        cost_estimate=cost(0, 2 * size),
        compiler_params=params(),
        name="hold",
    )(*(stay(array) for array in flat), *after)


def prepare_kernel(*refs):
    packed_ref, residual_ref, gain_ref, routes_ref, weights_ref, sems = refs[4:]
    for copy in load(refs[:4], refs[5:9], sems):
        copy.wait()
    row_count, width = residual_ref.shape
    experts = lax.axis_size("ep")
    lanes = packed_ref.shape[1] - width
    wide = residual_ref[...].astype(jnp.float32)
    mean = jnp.mean(wide * wide, axis=1, keepdims=True)
    packed_ref[:, :width] = (wide * lax.rsqrt(mean + 1e-06) * gain_ref[...]).astype(jnp.bfloat16)
    line = lax.broadcasted_iota(jnp.int32, (lanes, row_count), 0)
    expert = lax.rem(line, experts)
    weight = jnp.zeros(line.shape, jnp.float32)
    for k in range(routes_ref.shape[0]):
        weight += jnp.where(routes_ref[k : k + 1, :] == expert, weights_ref[k : k + 1, :], 0.0)
    high = weight.astype(jnp.bfloat16).astype(jnp.float32)
    low = (weight - high).astype(jnp.bfloat16).astype(jnp.float32)
    lowest = weight - high - low
    terms = jnp.where(
        line < experts,
        high,
        jnp.where(line < 2 * experts, low, jnp.where(line < 3 * experts, lowest, 0.0)),
    )
    at = lax.broadcasted_iota(jnp.int32, (row_count, row_count), 0)
    same = at == lax.broadcasted_iota(jnp.int32, (row_count, row_count), 1)
    turned = lax.dot_general(
        same.astype(jnp.bfloat16),
        terms.astype(jnp.bfloat16),
        (((1,), (1,)), ((), ())),
        preferred_element_type=jnp.float32,
    )
    packed_ref[:, width:] = turned.astype(jnp.bfloat16)


def stack_kernel(*refs):
    for i in range(refs[-1].shape[0]):
        refs[-1][i] = refs[i][...]


def ffn_kernel(block_count, *refs):
    blocks = refs[:block_count]
    in_ref, down_ref = refs[block_count : block_count + 2]
    near_ref, far_ref = refs[-2:]
    width = down_ref.shape[1]
    packed = jnp.concatenate(
        [block[...].reshape(-1, block.shape[-1]) for block in blocks], axis=0
    )
    rows = packed[:, :width]
    terms = packed[:, width:].astype(jnp.float32)
    lane = lax.broadcasted_iota(jnp.int32, terms.shape, 1)
    mine = lax.rem(lane, lax.axis_size("ep")) == lax.axis_index("ep")
    weight = jnp.sum(jnp.where(mine, terms, 0.0), axis=1, keepdims=True)
    gate = jnp.dot(rows, in_ref[:width], preferred_element_type=jnp.float32)
    up = jnp.dot(rows, in_ref[width:], preferred_element_type=jnp.float32)
    hidden = (gate / (1.0 + jnp.exp(-gate)) * up).astype(jnp.bfloat16)
    out = jnp.dot(hidden, down_ref[...], preferred_element_type=jnp.float32)
    out = (out * weight).astype(jnp.bfloat16).reshape((2,) + near_ref.shape)
    near_ref[...] = out[0]
    far_ref[...] = out[1]


def pair_kernel(own_ref, other_ref, keep_ref, send_ref):
    half = keep_ref.shape[0]
    keep_ref[...] = own_ref[:half].astype(jnp.float32) + other_ref[:half].astype(jnp.float32)
    send = own_ref[half:].astype(jnp.float32) + other_ref[half:].astype(jnp.float32)
    send_ref[...] = send.astype(jnp.bfloat16)


def square_kernel(own_ref, other_ref, *out_refs):
    for i, out_ref in enumerate(out_refs):
        total = own_ref[i] + other_ref[i].astype(jnp.float32)
        out_ref[...] = total.astype(out_ref.dtype)


def total_kernel(residual_ref, *refs):
    total = residual_ref[...].astype(jnp.float32)
    for ref in refs[:-1]:
        total += ref[...].astype(jnp.float32)
    refs[-1][...] = total.astype(jnp.bfloat16)


def in_vmem(kernel, out_shape, name, arrays, after=(), mebibytes=4, cost_estimate=None):
    return pl.pallas_call(
        kernel,
        out_shape=out_shape,
        in_specs=[HERE] * len(arrays) + [ANYWHERE] * len(after),
        compiler_params=params(mebibytes),
        cost_estimate=cost_estimate,
        name=name,
    )(*arrays, *after)


def layer_gathered(attention, residual, norm_gain, routes, route_weights, expert_in, expert_down):
    row_count, width = residual.shape
    devices = lax.axis_size("ep")
    core, side, line = 1, 2, 4
    extra = -(-3 * devices // 128) * 128
    vmem = pltpu.VMEM
    one = (row_count, width)
    block = vmem((row_count, width + extra), jnp.bfloat16)

    def swap(value, bits):
        return lax.ppermute(value, "ep", [(i, i ^ bits) for i in range(devices)])

    def stack(members, after=()):
        shape = vmem((len(members), row_count, width + extra), jnp.bfloat16)
        return in_vmem(stack_kernel, shape, "stack", members, after)

    packed = from_hbm(
        prepare_kernel,
        block,
        "prepare",
        (residual, norm_gain.reshape(1, -1), routes.T, route_weights.T),
    )
    first, third, second = (swap(packed, d * line) for d in (1, 3, 2))
    across = swap(packed, side)
    held = hold((expert_in, expert_down), (packed,))

    diagonal = swap(across, line)
    early = stack((second, third), (diagonal, held[0]))
    early_side = swap(early, side)
    early_far = swap(early, core)
    late = stack((packed, across, first, diagonal), (early,))
    late_far = swap(late, core)
    early_side_far = swap(early_side, core)

    def ffn(members, after=()):
        return in_vmem(
            functools.partial(ffn_kernel, len(members)),
            [vmem((4,) + one, jnp.bfloat16)] * 2,
            "ffn",
            (*members, *held),
            after,
            mebibytes=16,
            cost_estimate=cost(8 * row_count * 2 * sum(h.size for h in held), 2 * held[0].size),
        )

    def pair_sum(near_out, far_out):
        shapes = [vmem((2,) + one, jnp.float32), vmem((2,) + one, jnp.bfloat16)]
        return in_vmem(pair_kernel, shapes, "pair_sum", (near_out, swap(far_out, core)))

    early_members = (early, early_side, early_far, early_side_far)
    early_keep, early_send = pair_sum(*ffn(early_members, (late_far,)))
    early_sums = in_vmem(
        square_kernel,
        [vmem(one, jnp.bfloat16)] * 2,
        "square_sum",
        (early_keep, swap(early_send, side)),
    )
    back = [swap(early_sums[1], 3 * line), swap(early_sums[0], 2 * line)]
    attended = attend(*attention, tuple(early_sums))
    late_keep, late_send = pair_sum(*ffn((late, late_far)))
    own, across_sum = in_vmem(
        square_kernel,
        [vmem(one, jnp.float32), vmem(one, jnp.bfloat16)],
        "line_sum",
        (late_keep, swap(late_send, line)),
    )
    moe_out = in_vmem(
        total_kernel,
        jax.ShapeDtypeStruct(one, jnp.bfloat16),
        "total",
        (residual, own, *back, swap(across_sum, side)),
    )
    return attended, moe_out


def expert_layer_routed(residual, norm_gain, routes, route_weights, expert_in, expert_down):
    row_count, top_count = routes.shape
    expert_count = expert_in.shape[0] * lax.axis_size("ep")
    capacity = min(row_count, max(2, 2 * row_count * top_count // expert_count))
    whole = lax.all_gather(residual, "tp", axis=1, tiled=True)
    width = whole.shape[1]
    half_width = residual.shape[1]
    normed = normalize(whole, norm_gain)
    flat_routes = routes.reshape(-1)
    hits = (flat_routes[:, None] == jnp.arange(expert_count)[None, :]).astype(jnp.int32)
    before = jnp.cumsum(hits, axis=0) - hits
    position = jnp.sum(before * hits, axis=1)
    slot_flat = flat_routes * capacity + position
    placed = (slot_flat[:, None] == jnp.arange(expert_count * capacity)[None, :]).astype(
        jnp.float32
    )
    placed = placed.reshape(row_count, top_count, expert_count * capacity)
    selector = jnp.sum(placed, axis=1).astype(jnp.bfloat16)
    buffer = jnp.einsum("rs,rd->sd", selector, normed, preferred_element_type=jnp.float32)
    buffer = buffer.astype(jnp.bfloat16).reshape(expert_count, capacity, width)
    arrived = lax.all_to_all(buffer, "ep", split_axis=0, concat_axis=0, tiled=True)
    sources = arrived.shape[0]
    flat_rows = arrived.reshape(sources * capacity, width)
    gate_act = jnp.dot(flat_rows, expert_in[0, 0], preferred_element_type=jnp.float32)
    up_act = jnp.dot(flat_rows, expert_in[0, 1], preferred_element_type=jnp.float32)
    hidden = (jax.nn.silu(gate_act) * up_act).astype(jnp.bfloat16)
    partial_value = jnp.dot(hidden, expert_down[0], preferred_element_type=jnp.float32)
    partial_value = partial_value.reshape(sources, capacity, width)
    summed = lax.psum_scatter(partial_value, "tp", scatter_dimension=2, tiled=True).astype(
        jnp.bfloat16
    )
    returned = lax.all_to_all(summed, "ep", split_axis=0, concat_axis=0, tiled=True)
    weighting = jnp.sum(placed * route_weights[:, :, None], axis=1)
    gathered_rows = returned.reshape(expert_count * capacity, half_width).astype(jnp.float32)
    combined = jnp.dot(weighting, gathered_rows, precision=lax.Precision.HIGHEST)
    return (residual.astype(jnp.float32) + combined).astype(jnp.bfloat16)


def per_device(
    queries,
    key_cache,
    value_cache,
    new_key,
    new_value,
    lengths,
    residual,
    norm_gain,
    routes,
    route_weights,
    expert_in,
    expert_down,
):
    devices = lax.axis_size("ep")
    dense = lax.axis_size("tp") == 1 and devices == 16
    attention = (queries, key_cache, value_cache, new_key, new_value, lengths)
    layer = (residual, norm_gain, routes, route_weights)
    if dense:
        return layer_gathered(attention, *layer, expert_in, expert_down)
    attended = attention_block(*attention)
    return (attended, expert_layer_routed(*layer, expert_in, expert_down))


def solution(mesh):
    in_specs = (
        P(("groups", "ep"), "tp", None),
        P(("groups", "ep"), None, "tp", None),
        P(("groups", "ep"), None, "tp", None),
        P(("groups", "ep"), "tp", None),
        P(("groups", "ep"), "tp", None),
        P(("groups", "ep")),
        P(("groups", "ep"), "tp"),
        P(),
        P(("groups", "ep"), None),
        P(("groups", "ep"), None),
        P("ep", None, None, "tp"),
        P("ep", "tp", None),
    )
    out_specs = (P(("groups", "ep"), "tp", None), P(("groups", "ep"), "tp"))
    return jax.shard_map(
        per_device, mesh=mesh, in_specs=in_specs, out_specs=out_specs, check_vma=False
    )
```

profile of v0, /device:TPU:0, one launch (start us, length us, event | category | flops | bytes accessed | tf_op | source)
XLA Modules:
  0.0 41.2 jit_solution(2715747957285005255)
XLA Ops:
  0.6 1.0 %prepare.1.refs_2_.refs_0_ = bf16[16,2176]{1,0:T(8,128)(2,1)S(1)} custom-call(bf16[16,2048]{1,0:T(8,128)(2,1)} %residual_ref.1, f32[1,2048]{1,0:T(1,128)} %bitcast.13, s32[8,16]{1,0:T(8,128)} %bitcast.14, f32[8,16]{1,0:T(8,128)} %bitcast.15), custom_call_target="tpu_custom_call" | custom-call | tf_op jit(solution)/shard_map/prepare/pallas_call | solution.py:77
  1.7 3.0 %collective-permute-start.2 = (bf16[16,2176]{1,0:T(8,128)(2,1)S(1)}, bf16[16,2176]{1,0:T(8,128)(2,1)S(1)}, u32[]{:S(2)}, u32[]{:S(2)}) collective-permute-start(bf16[16,2176]{1,0:T(8,128)(2,1)S(1)} %prepare.1.refs_2_.refs_0_), channel_id=1, source_target_pairs={{0,2},{1,3},{2,0},{3,1},{4,6},{5,7},{6,4},{7,5},{8,10},{9,11},{10,... | collective-permute-start | bytes 208904 | tf_op jit(solution)/shard_map/ppermute | solution.py:283
  4.7 2.6 %collective-permute-start = (bf16[16,2176]{1,0:T(8,128)(2,1)S(1)}, bf16[16,2176]{1,0:T(8,128)(2,1)S(1)}, u32[]{:S(2)}, u32[]{:S(2)}) collective-permute-start(bf16[16,2176]{1,0:T(8,128)(2,1)S(1)} %prepare.1.refs_2_.refs_0_), channel_id=1, source_target_pairs={{0,8},{1,9},{2,10},{3,11},{4,12},{5,13},{6,14},{7,15},{8,0},{9,1},... | collective-permute-start | bytes 208904 | tf_op jit(solution)/shard_map/ppermute | solution.py:283
  7.3 1.3 %collective-permute-start.1 = (bf16[16,2176]{1,0:T(8,128)(2,1)S(1)}, bf16[16,2176]{1,0:T(8,128)(2,1)S(1)}, u32[]{:S(2)}, u32[]{:S(2)}) collective-permute-start(bf16[16,2176]{1,0:T(8,128)(2,1)S(1)} %prepare.1.refs_2_.refs_0_), channel_id=1, source_target_pairs={{0,12},{1,13},{2,14},{3,15},{4,8},{5,9},{6,10},{7,11},{8,4},{9,5},... | collective-permute-start | bytes 208904 | tf_op jit(solution)/shard_map/ppermute | solution.py:283
  8.6 0.0 collective-permute-done.2.refs_1_
  8.6 0.5 %collective-permute-start.3 = (bf16[16,2176]{1,0:T(8,128)(2,1)S(1)}, bf16[16,2176]{1,0:T(8,128)(2,1)S(1)}, u32[]{:S(2)}, u32[]{:S(2)}) collective-permute-start(bf16[16,2176]{1,0:T(8,128)(2,1)S(1)} %collective-permute-done.2.refs_1_), channel_id=1, source_target_pairs={{0,4},{1,5},{2,6},{3,7},{4,0},{5,1},{6,2},{7,3},{8,12},{9,13},{10,... | collective-permute-start | bytes 208904 | tf_op jit(solution)/shard_map/ppermute | solution.py:283
  9.1 1.6 %collective-permute-start.7 = (bf16[16,2176]{1,0:T(8,128)(2,1)S(1)}, bf16[16,2176]{1,0:T(8,128)(2,1)S(1)}, u32[]{:S(2)}, u32[]{:S(2)}) collective-permute-start(bf16[16,2176]{1,0:T(8,128)(2,1)S(1)} %prepare.1.refs_2_.refs_0_), channel_id=1, source_target_pairs={{0,4},{1,5},{2,6},{3,7},{4,0},{5,1},{6,2},{7,3},{8,12},{9,13},{10,... | collective-permute-start | bytes 208904 | tf_op jit(solution)/shard_map/ppermute | solution.py:283
  10.6 3.7 %hold.1 = (bf16[4096,768]{1,0:T(8,128)(2,1)S(1)}, bf16[768,2048]{1,0:T(8,128)(2,1)S(1)}) custom-call(bf16[4096,768]{1,0:T(8,128)(2,1)} %bitcast.9, bf16[768,2048]{1,0:T(8,128)(2,1)} %bitcast.10, bf16[16,2176]{1,0:T(8,128)(2,1)S(1)} %prepare.1.refs_2_.refs_0_), custom_call_target="tpu_custom_call" | custom-call | bytes 9437184 | tf_op jit(solution)/shard_map/hold/pallas_call | solution.py:170
  14.4 0.0 collective-permute-done.refs_0_
  14.4 0.0 collective-permute-done.1.refs_1_
  14.4 0.0 collective-permute-done.3.refs_2_.refs_3_
  14.5 0.3 collective-permute-done.7.refs_2_
  14.8 0.1 collective-permute-start.8
  14.8 0.6 %collective-permute-start.4 = (bf16[2,16,2176]{2,1,0:T(8,128)(2,1)S(1)}, bf16[2,16,2176]{2,1,0:T(8,128)(2,1)S(1)}, u32[]{:S(2)}, u32[]{:S(2)}) collective-permute-start(bf16[2,16,2176]{2,1,0:T(8,128)(2,1)S(1)} %stack.2.refs_4_.refs_0_), channel_id=1, source_target_pairs={{0,2},{1,3},{2,0},{3,1},{4,6},{5,7},{6,4},{7,5},{8,10},{9,11},{10,... | collective-permute-start | bytes 417800 | tf_op jit(solution)/shard_map/ppermute | solution.py:283
  15.4 0.2 collective-permute-start.5
  15.6 5.3 %collective-permute-done.4.refs_1_ = bf16[2,16,2176]{2,1,0:T(8,128)(2,1)S(1)} collective-permute-done((bf16[2,16,2176]{2,1,0:T(8,128)(2,1)S(1)}, bf16[2,16,2176]{2,1,0:T(8,128)(2,1)S(1)}, u32[]{:S(2)}, u32[]{:S(2)}) %collective-permute-start.4) | collective-permute-done | bytes 139296 | tf_op jit(solution)/shard_map/ppermute | solution.py:283
  20.9 0.0 collective-permute-start.6
  20.9 0.0 collective-permute-done.8.refs_6_.refs_1_
  20.9 1.5 %ffn.3 = (bf16[4,16,2048]{2,1,0:T(8,128)(2,1)S(1)}, bf16[4,16,2048]{2,1,0:T(8,128)(2,1)S(1)}) custom-call(bf16[4,16,2176]{2,1,0:T(8,128)(2,1)S(1)} %stack.3.refs_0_, bf16[4,16,2176]{2,1,0:T(8,128)(2,1)S(1)} %collective-permute-done.8.refs_6_.refs_1_, bf16[4096,768]{1,0:T(8,128)(2,1)S(1)} %get-tuple-element.16.refs_3_.refs_4_.refs_2_, ...), custom_call_target="tpu_custom_call" | custom-call | flops 1207959552 | bytes 6291456 | tf_op jit(solution)/shard_map/ffn/pallas_call | solution.py:263
  22.4 0.0 copy-start
  22.5 0.6 %collective-permute-start.11 = (bf16[4,16,2048]{2,1,0:T(8,128)(2,1)S(1)}, bf16[4,16,2048]{2,1,0:T(8,128)(2,1)S(1)}, u32[]{:S(2)}, u32[]{:S(2)}) collective-permute-start(bf16[4,16,2048]{2,1,0:T(8,128)(2,1)S(1)} %get-tuple-element.25), channel_id=1, source_target_pairs={{0,1},{1,0},{2,3},{3,2},{4,5},{5,4},{6,7},{7,6},{8,9},{9,8},{10,11... | collective-permute-start | bytes 786440 | tf_op jit(solution)/shard_map/ppermute | solution.py:283
  23.0 0.0 collective-permute-done.5.refs_2_
  23.0 0.0 collective-permute-done.6.refs_3_
  23.0 1.5 %ffn.2 = (bf16[4,16,2048]{2,1,0:T(8,128)(2,1)S(1)}, bf16[4,16,2048]{2,1,0:T(8,128)(2,1)S(1)}) custom-call(bf16[2,16,2176]{2,1,0:T(8,128)(2,1)S(1)} %stack.2.refs_4_.refs_0_, bf16[2,16,2176]{2,1,0:T(8,128)(2,1)S(1)} %collective-permute-done.4.refs_1_, bf16[2,16,2176]{2,1,0:T(8,128)(2,1)S(1)} %collective-permute-done.5.refs_2_, ...), custom_call_target="tpu_custom_call" | custom-call | flops 1207959552 | bytes 6291456 | tf_op jit(solution)/shard_map/ffn/pallas_call | solution.py:263
  24.5 0.1 collective-permute-start.9
  24.6 0.0 collective-permute-done.11.other_ref
  24.6 0.1 pair_sum.3
  24.7 1.0 %collective-permute-start.12 = (bf16[2,16,2048]{2,1,0:T(8,128)(2,1)S(1)}, bf16[2,16,2048]{2,1,0:T(8,128)(2,1)S(1)}, u32[]{:S(2)}, u32[]{:S(2)}) collective-permute-start(bf16[2,16,2048]{2,1,0:T(8,128)(2,1)S(1)} %get-tuple-element.27), channel_id=1, source_target_pairs={{0,4},{1,5},{2,6},{3,7},{4,0},{5,1},{6,2},{7,3},{8,12},{9,13},{10,... | collective-permute-start | bytes 393224 | tf_op jit(solution)/shard_map/ppermute | solution.py:283
  25.8 0.4 collective-permute-done.9.other_ref
  26.1 0.1 pair_sum.2
  26.2 0.6 %collective-permute-start.10 = (bf16[2,16,2048]{2,1,0:T(8,128)(2,1)S(1)}, bf16[2,16,2048]{2,1,0:T(8,128)(2,1)S(1)}, u32[]{:S(2)}, u32[]{:S(2)}) collective-permute-start(bf16[2,16,2048]{2,1,0:T(8,128)(2,1)S(1)} %get-tuple-element.21), channel_id=1, source_target_pairs={{0,2},{1,3},{2,0},{3,1},{4,6},{5,7},{6,4},{7,5},{8,10},{9,11},{10,... | collective-permute-start | bytes 393224 | tf_op jit(solution)/shard_map/ppermute | solution.py:283
  26.8 3.9 %collective-permute-done.12.other_ref = bf16[2,16,2048]{2,1,0:T(8,128)(2,1)S(1)} collective-permute-done((bf16[2,16,2048]{2,1,0:T(8,128)(2,1)S(1)}, bf16[2,16,2048]{2,1,0:T(8,128)(2,1)S(1)}, u32[]{:S(2)}, u32[]{:S(2)}) %collective-permute-start.12) | collective-permute-done | bytes 131104 | tf_op jit(solution)/shard_map/ppermute | solution.py:283
  30.7 0.6 %collective-permute-start.15 = (bf16[16,2048]{1,0:T(8,128)(2,1)S(1)}, bf16[16,2048]{1,0:T(8,128)(2,1)S(1)}, u32[]{:S(2)}, u32[]{:S(2)}) collective-permute-start(bf16[16,2048]{1,0:T(8,128)(2,1)S(1)} %get-tuple-element.29), channel_id=1, source_target_pairs={{0,2},{1,3},{2,0},{3,1},{4,6},{5,7},{6,4},{7,5},{8,10},{9,11},{10,... | collective-permute-start | bytes 196616 | tf_op jit(solution)/shard_map/ppermute | solution.py:283
  31.3 0.5 %collective-permute-done.10.other_ref = bf16[2,16,2048]{2,1,0:T(8,128)(2,1)S(1)} collective-permute-done((bf16[2,16,2048]{2,1,0:T(8,128)(2,1)S(1)}, bf16[2,16,2048]{2,1,0:T(8,128)(2,1)S(1)}, u32[]{:S(2)}, u32[]{:S(2)}) %collective-permute-start.10) | collective-permute-done | bytes 131104 | tf_op jit(solution)/shard_map/ppermute | solution.py:283
  31.8 3.3 %collective-permute-start.13 = (bf16[16,2048]{1,0:T(8,128)(2,1)S(1)}, bf16[16,2048]{1,0:T(8,128)(2,1)S(1)}, u32[]{:S(2)}, u32[]{:S(2)}) collective-permute-start(bf16[16,2048]{1,0:T(8,128)(2,1)S(1)} %get-tuple-element.23.refs_7_), channel_id=1, source_target_pairs={{0,12},{1,13},{2,14},{3,15},{4,8},{5,9},{6,10},{7,11},{8,4},{9,5},... | collective-permute-start | bytes 196616 | tf_op jit(solution)/shard_map/ppermute | solution.py:283
  35.2 0.0 collective-permute-start.14
  35.2 3.2 %attend.1 = bf16[4,32,128]{2,1,0:T(8,128)(2,1)} custom-call(s32[4]{0:T(128)} %refs_0_.3, bf16[4,32,128]{2,1,0:T(8,128)(2,1)} %refs_1_.1, bf16[4,256,128]{2,1,0:T(8,128)(2,1)} %bitcast.11, bf16[4,256,128]{2,1,0:T(8,128)(2,1)} %bitcast.12, bf16[8,128]{1,0:T(8,128)(2,1)} %bitcast.16, bf16[8,128]{1,0:T(8,128)(2,1)} %bitcast.17, ...), custom_call_target="tpu_custom_call" | custom-call | bytes 4194304 | tf_op jit(solution)/shard_map/attend/pallas_call | solution.py:77
  38.4 0.0 collective-permute-done.15.refs_3_
  38.4 0.1 collective-permute-done.13.refs_1_
  38.5 2.0 %collective-permute-done.14.refs_2_ = bf16[16,2048]{1,0:T(8,128)(2,1)S(1)} collective-permute-done((bf16[16,2048]{1,0:T(8,128)(2,1)S(1)}, bf16[16,2048]{1,0:T(8,128)(2,1)S(1)}, u32[]{:S(2)}, u32[]{:S(2)}) %collective-permute-start.14) | collective-permute-done | bytes 65568 | tf_op jit(solution)/shard_map/ppermute | solution.py:283
  40.5 0.0 copy-done
  40.5 0.7 %total.1 = bf16[16,2048]{1,0:T(8,128)(2,1)} custom-call(bf16[16,2048]{1,0:T(8,128)(2,1)S(1)} %copy-done, f32[16,2048]{1,0:T(8,128)S(1)} %get-tuple-element.28.refs_0_, bf16[16,2048]{1,0:T(8,128)(2,1)S(1)} %collective-permute-done.13.refs_1_, bf16[16,2048]{1,0:T(8,128)(2,1)S(1)} %collective-permute-done.14.refs_2_, ...), custom_call_target="tpu_custom_call" | custom-call | tf_op jit(solution)/shard_map/total/pallas_call | solution.py:263
  (4 shorter events, 0.1 us)
Async XLA Ops:
  1.7 6.9 %collective-permute-start.2 = (bf16[16,2176]{1,0:T(8,128)(2,1)S(1)}, bf16[16,2176]{1,0:T(8,128)(2,1)S(1)}, u32[]{:S(2)}, u32[]{:S(2)}) collective-permute-start(bf16[16,2176]{1,0:T(8,128)(2,1)S(1)} %prepare.1.refs_2_.refs_0_), channel_id=1, source_target_pairs={{0,2},{1,3},{2,0},{3,1},{4,6},{5,7},{6,4},{7,5},{8,10},{9,11},{10,... | collective-permute-start | bytes 208904 | tf_op jit(solution)/shard_map/ppermute | solution.py:283
  4.7 9.7 %collective-permute-start = (bf16[16,2176]{1,0:T(8,128)(2,1)S(1)}, bf16[16,2176]{1,0:T(8,128)(2,1)S(1)}, u32[]{:S(2)}, u32[]{:S(2)}) collective-permute-start(bf16[16,2176]{1,0:T(8,128)(2,1)S(1)} %prepare.1.refs_2_.refs_0_), channel_id=1, source_target_pairs={{0,8},{1,9},{2,10},{3,11},{4,12},{5,13},{6,14},{7,15},{8,0},{9,1},... | collective-permute-start | bytes 208904 | tf_op jit(solution)/shard_map/ppermute | solution.py:283
  7.3 7.1 %collective-permute-start.1 = (bf16[16,2176]{1,0:T(8,128)(2,1)S(1)}, bf16[16,2176]{1,0:T(8,128)(2,1)S(1)}, u32[]{:S(2)}, u32[]{:S(2)}) collective-permute-start(bf16[16,2176]{1,0:T(8,128)(2,1)S(1)} %prepare.1.refs_2_.refs_0_), channel_id=1, source_target_pairs={{0,12},{1,13},{2,14},{3,15},{4,8},{5,9},{6,10},{7,11},{8,4},{9,5},... | collective-permute-start | bytes 208904 | tf_op jit(solution)/shard_map/ppermute | solution.py:283
  8.6 5.8 %collective-permute-start.3 = (bf16[16,2176]{1,0:T(8,128)(2,1)S(1)}, bf16[16,2176]{1,0:T(8,128)(2,1)S(1)}, u32[]{:S(2)}, u32[]{:S(2)}) collective-permute-start(bf16[16,2176]{1,0:T(8,128)(2,1)S(1)} %collective-permute-done.2.refs_1_), channel_id=1, source_target_pairs={{0,4},{1,5},{2,6},{3,7},{4,0},{5,1},{6,2},{7,3},{8,12},{9,13},{10,... | collective-permute-start | bytes 208904 | tf_op jit(solution)/shard_map/ppermute | solution.py:283
  9.1 5.7 %collective-permute-start.7 = (bf16[16,2176]{1,0:T(8,128)(2,1)S(1)}, bf16[16,2176]{1,0:T(8,128)(2,1)S(1)}, u32[]{:S(2)}, u32[]{:S(2)}) collective-permute-start(bf16[16,2176]{1,0:T(8,128)(2,1)S(1)} %prepare.1.refs_2_.refs_0_), channel_id=1, source_target_pairs={{0,4},{1,5},{2,6},{3,7},{4,0},{5,1},{6,2},{7,3},{8,12},{9,13},{10,... | collective-permute-start | bytes 208904 | tf_op jit(solution)/shard_map/ppermute | solution.py:283
  14.8 6.2 %collective-permute-start.8 = (bf16[4,16,2176]{2,1,0:T(8,128)(2,1)S(1)}, bf16[4,16,2176]{2,1,0:T(8,128)(2,1)S(1)}, u32[]{:S(2)}, u32[]{:S(2)}) collective-permute-start(bf16[4,16,2176]{2,1,0:T(8,128)(2,1)S(1)} %stack.3.refs_0_), channel_id=1, source_target_pairs={{0,1},{1,0},{2,3},{3,2},{4,5},{5,4},{6,7},{7,6},{8,9},{9,8},{10,11... | collective-permute-start | bytes 835592 | tf_op jit(solution)/shard_map/ppermute | solution.py:283
  14.8 6.1 %collective-permute-start.4 = (bf16[2,16,2176]{2,1,0:T(8,128)(2,1)S(1)}, bf16[2,16,2176]{2,1,0:T(8,128)(2,1)S(1)}, u32[]{:S(2)}, u32[]{:S(2)}) collective-permute-start(bf16[2,16,2176]{2,1,0:T(8,128)(2,1)S(1)} %stack.2.refs_4_.refs_0_), channel_id=1, source_target_pairs={{0,2},{1,3},{2,0},{3,1},{4,6},{5,7},{6,4},{7,5},{8,10},{9,11},{10,... | collective-permute-start | bytes 417800 | tf_op jit(solution)/shard_map/ppermute | solution.py:283
  15.4 7.6 %collective-permute-start.5 = (bf16[2,16,2176]{2,1,0:T(8,128)(2,1)S(1)}, bf16[2,16,2176]{2,1,0:T(8,128)(2,1)S(1)}, u32[]{:S(2)}, u32[]{:S(2)}) collective-permute-start(bf16[2,16,2176]{2,1,0:T(8,128)(2,1)S(1)} %stack.2.refs_4_.refs_0_), channel_id=1, source_target_pairs={{0,1},{1,0},{2,3},{3,2},{4,5},{5,4},{6,7},{7,6},{8,9},{9,8},{10,11... | collective-permute-start | bytes 417800 | tf_op jit(solution)/shard_map/ppermute | solution.py:283
  20.9 2.1 %collective-permute-start.6 = (bf16[2,16,2176]{2,1,0:T(8,128)(2,1)S(1)}, bf16[2,16,2176]{2,1,0:T(8,128)(2,1)S(1)}, u32[]{:S(2)}, u32[]{:S(2)}) collective-permute-start(bf16[2,16,2176]{2,1,0:T(8,128)(2,1)S(1)} %collective-permute-done.4.refs_1_), channel_id=1, source_target_pairs={{0,1},{1,0},{2,3},{3,2},{4,5},{5,4},{6,7},{7,6},{8,9},{9,8},{10,11... | collective-permute-start | bytes 417800 | tf_op jit(solution)/shard_map/ppermute | solution.py:283
  22.4 18.1 %copy-start = (bf16[16,2048]{1,0:T(8,128)(2,1)S(1)}, bf16[16,2048]{1,0:T(8,128)(2,1)}, u32[]{:S(2)}) copy-start(bf16[16,2048]{1,0:T(8,128)(2,1)} %residual_ref.1) | copy-start | bytes 196612
  22.5 2.2 %collective-permute-start.11 = (bf16[4,16,2048]{2,1,0:T(8,128)(2,1)S(1)}, bf16[4,16,2048]{2,1,0:T(8,128)(2,1)S(1)}, u32[]{:S(2)}, u32[]{:S(2)}) collective-permute-start(bf16[4,16,2048]{2,1,0:T(8,128)(2,1)S(1)} %get-tuple-element.25), channel_id=1, source_target_pairs={{0,1},{1,0},{2,3},{3,2},{4,5},{5,4},{6,7},{7,6},{8,9},{9,8},{10,11... | collective-permute-start | bytes 786440 | tf_op jit(solution)/shard_map/ppermute | solution.py:283
  24.5 1.6 %collective-permute-start.9 = (bf16[4,16,2048]{2,1,0:T(8,128)(2,1)S(1)}, bf16[4,16,2048]{2,1,0:T(8,128)(2,1)S(1)}, u32[]{:S(2)}, u32[]{:S(2)}) collective-permute-start(bf16[4,16,2048]{2,1,0:T(8,128)(2,1)S(1)} %get-tuple-element.19), channel_id=1, source_target_pairs={{0,1},{1,0},{2,3},{3,2},{4,5},{5,4},{6,7},{7,6},{8,9},{9,8},{10,11... | collective-permute-start | bytes 786440 | tf_op jit(solution)/shard_map/ppermute | solution.py:283
  24.7 5.9 %collective-permute-start.12 = (bf16[2,16,2048]{2,1,0:T(8,128)(2,1)S(1)}, bf16[2,16,2048]{2,1,0:T(8,128)(2,1)S(1)}, u32[]{:S(2)}, u32[]{:S(2)}) collective-permute-start(bf16[2,16,2048]{2,1,0:T(8,128)(2,1)S(1)} %get-tuple-element.27), channel_id=1, source_target_pairs={{0,4},{1,5},{2,6},{3,7},{4,0},{5,1},{6,2},{7,3},{8,12},{9,13},{10,... | collective-permute-start | bytes 393224 | tf_op jit(solution)/shard_map/ppermute | solution.py:283
  26.2 5.6 %collective-permute-start.10 = (bf16[2,16,2048]{2,1,0:T(8,128)(2,1)S(1)}, bf16[2,16,2048]{2,1,0:T(8,128)(2,1)S(1)}, u32[]{:S(2)}, u32[]{:S(2)}) collective-permute-start(bf16[2,16,2048]{2,1,0:T(8,128)(2,1)S(1)} %get-tuple-element.21), channel_id=1, source_target_pairs={{0,2},{1,3},{2,0},{3,1},{4,6},{5,7},{6,4},{7,5},{8,10},{9,11},{10,... | collective-permute-start | bytes 393224 | tf_op jit(solution)/shard_map/ppermute | solution.py:283
  30.7 7.7 %collective-permute-start.15 = (bf16[16,2048]{1,0:T(8,128)(2,1)S(1)}, bf16[16,2048]{1,0:T(8,128)(2,1)S(1)}, u32[]{:S(2)}, u32[]{:S(2)}) collective-permute-start(bf16[16,2048]{1,0:T(8,128)(2,1)S(1)} %get-tuple-element.29), channel_id=1, source_target_pairs={{0,2},{1,3},{2,0},{3,1},{4,6},{5,7},{6,4},{7,5},{8,10},{9,11},{10,... | collective-permute-start | bytes 196616 | tf_op jit(solution)/shard_map/ppermute | solution.py:283
  31.8 6.7 %collective-permute-start.13 = (bf16[16,2048]{1,0:T(8,128)(2,1)S(1)}, bf16[16,2048]{1,0:T(8,128)(2,1)S(1)}, u32[]{:S(2)}, u32[]{:S(2)}) collective-permute-start(bf16[16,2048]{1,0:T(8,128)(2,1)S(1)} %get-tuple-element.23.refs_7_), channel_id=1, source_target_pairs={{0,12},{1,13},{2,14},{3,15},{4,8},{5,9},{6,10},{7,11},{8,4},{9,5},... | collective-permute-start | bytes 196616 | tf_op jit(solution)/shard_map/ppermute | solution.py:283
  35.2 5.4 %collective-permute-start.14 = (bf16[16,2048]{1,0:T(8,128)(2,1)S(1)}, bf16[16,2048]{1,0:T(8,128)(2,1)S(1)}, u32[]{:S(2)}, u32[]{:S(2)}) collective-permute-start(bf16[16,2048]{1,0:T(8,128)(2,1)S(1)} %get-tuple-element.22.refs_6_), channel_id=1, source_target_pairs={{0,8},{1,9},{2,10},{3,11},{4,12},{5,13},{6,14},{7,15},{8,0},{9,1},... | collective-permute-start | bytes 196616 | tf_op jit(solution)/shard_map/ppermute | solution.py:283
where the time goes:
time: 41.4 us; the launch traced here: 41.2 us
  starting transfers between devices  16 us (39%)
  waiting for transfers between devices  12.6 us (30%)
  Pallas kernels  11.9 us (29%)
  between operations  0.76 us (2%)
    ppermute x16, starting transfers between devices, swap(): return lax.ppermute(value, 'ep', [(i, i ^ bits) for i in range(devices)])  16 us
    ppermute x16, waiting for transfers between devices, swap(): return lax.ppermute(value, 'ep', [(i, i ^ bits) for i in range(devices)])  12.6 us
    pallas_call x2, Pallas kernels, from_hbm(): pl.pallas_call(kernel, out_shape=out_shape, in_specs=[pl.BlockSpec(memory...  4.24 us
    pallas_call x9, Pallas kernels, in_vmem(): pl.pallas_call(kernel, out_shape=out_shape, in_specs=[HERE] * len(arrays)...  3.87 us
    pallas_call x1, Pallas kernels, hold(): pl.pallas_call(functools.partial(hold_kernel, len(flat), pieces), out_sha...  3.75 us
  transfers between devices with their start and end apart: 16, of which 7 were waited for; matrix products, arithmetic and copies ran while one was open for 0% of the time, Pallas kernels for 25%

commit v1 on v0

--- a/solution.py
+++ b/solution.py
@@ -217,6 +217,10 @@
         refs[-1][i] = refs[i][...]
 
 
+def relay_kernel(in_ref, *refs):
+    refs[-1][...] = in_ref[...]
+
+
 def ffn_kernel(block_count, *refs):
     blocks = refs[:block_count]
     in_ref, down_ref = refs[block_count : block_count + 2]
@@ -294,15 +298,16 @@
     )
     first, third, second = (swap(packed, d * line) for d in (1, 3, 2))
     across = swap(packed, side)
-    held = hold((expert_in, expert_down), (packed,))
-
     diagonal = swap(across, line)
-    early = stack((second, third), (diagonal, held[0]))
+    early = stack((second, third), (diagonal,))
+    held = hold((expert_in, expert_down), (early,))
     early_side = swap(early, side)
     early_far = swap(early, core)
     late = stack((packed, across, first, diagonal), (early,))
     late_far = swap(late, core)
-    early_side_far = swap(early_side, core)
+    shape = vmem(early.shape, early.dtype)
+    relayed = in_vmem(relay_kernel, shape, "relay", (early_side,), held[:1])
+    early_side_far = swap(relayed, core)
 
     def ffn(members, after=()):
         return in_vmem(

time: 41.4 us -> 41.5 us (level)
    pallas_call x9 -> x10, Pallas kernels: 3.87 us -> 3.89 us  [in_vmem(): pl.pallas_call(kernel, out_shape=out_shape, in_specs=[HERE] * len(arrays)...]
  transfers between devices with their start and end apart: 16 -> 16, of which waited for: 7 -> 9; matrix products, arithmetic and copies ran while one was open for 0% -> 0% of each run, Pallas kernels for 25% -> 25%
where the time goes in v1:
time: 41.5 us; the launch traced here: 41.3 us
  starting transfers between devices  16 us (39%)
  waiting for transfers between devices  12.6 us (30%)
  Pallas kernels  11.9 us (29%)
  between operations  0.75 us (2%)
    ppermute x16, starting transfers between devices, swap(): return lax.ppermute(value, 'ep', [(i, i ^ bits) for i in range(devices)])  16 us
    ppermute x16, waiting for transfers between devices, swap(): return lax.ppermute(value, 'ep', [(i, i ^ bits) for i in range(devices)])  12.6 us
    pallas_call x2, Pallas kernels, from_hbm(): pl.pallas_call(kernel, out_shape=out_shape, in_specs=[pl.BlockSpec(memory...  4.24 us
    pallas_call x10, Pallas kernels, in_vmem(): pl.pallas_call(kernel, out_shape=out_shape, in_specs=[HERE] * len(arrays)...  3.89 us
    pallas_call x1, Pallas kernels, hold(): pl.pallas_call(functools.partial(hold_kernel, len(flat), pieces), out_sha...  3.75 us
  transfers between devices with their start and end apart: 16, of which 9 were waited for; matrix products, arithmetic and copies ran while one was open for 0% of the time, Pallas kernels for 25%

profile of v1, /device:TPU:0, one launch (start us, length us, event | category | flops | bytes accessed | tf_op | source)
XLA Modules:
  0.0 41.3 jit_solution(18029244805637233516)
XLA Ops:
  0.6 1.0 %prepare.1.refs_0_ = bf16[16,2176]{1,0:T(8,128)(2,1)S(1)} custom-call(bf16[16,2048]{1,0:T(8,128)(2,1)} %residual_ref.1, f32[1,2048]{1,0:T(1,128)} %bitcast.13, s32[8,16]{1,0:T(8,128)} %bitcast.14, f32[8,16]{1,0:T(8,128)} %bitcast.15), custom_call_target="tpu_custom_call" | custom-call | tf_op jit(solution)/shard_map/prepare/pallas_call | solution.py:77
  1.7 3.0 %collective-permute-start.2 = (bf16[16,2176]{1,0:T(8,128)(2,1)S(1)}, bf16[16,2176]{1,0:T(8,128)(2,1)S(1)}, u32[]{:S(2)}, u32[]{:S(2)}) collective-permute-start(bf16[16,2176]{1,0:T(8,128)(2,1)S(1)} %prepare.1.refs_0_), channel_id=1, source_target_pairs={{0,2},{1,3},{2,0},{3,1},{4,6},{5,7},{6,4},{7,5},{8,10},{9,11},{10,... | collective-permute-start | bytes 208904 | tf_op jit(solution)/shard_map/ppermute | solution.py:287
  4.7 2.6 %collective-permute-start = (bf16[16,2176]{1,0:T(8,128)(2,1)S(1)}, bf16[16,2176]{1,0:T(8,128)(2,1)S(1)}, u32[]{:S(2)}, u32[]{:S(2)}) collective-permute-start(bf16[16,2176]{1,0:T(8,128)(2,1)S(1)} %prepare.1.refs_0_), channel_id=1, source_target_pairs={{0,8},{1,9},{2,10},{3,11},{4,12},{5,13},{6,14},{7,15},{8,0},{9,1},... | collective-permute-start | bytes 208904 | tf_op jit(solution)/shard_map/ppermute | solution.py:287
  7.3 1.3 %collective-permute-start.1 = (bf16[16,2176]{1,0:T(8,128)(2,1)S(1)}, bf16[16,2176]{1,0:T(8,128)(2,1)S(1)}, u32[]{:S(2)}, u32[]{:S(2)}) collective-permute-start(bf16[16,2176]{1,0:T(8,128)(2,1)S(1)} %prepare.1.refs_0_), channel_id=1, source_target_pairs={{0,12},{1,13},{2,14},{3,15},{4,8},{5,9},{6,10},{7,11},{8,4},{9,5},... | collective-permute-start | bytes 208904 | tf_op jit(solution)/shard_map/ppermute | solution.py:287
  8.6 0.0 collective-permute-done.2.refs_1_
  8.6 0.5 %collective-permute-start.3 = (bf16[16,2176]{1,0:T(8,128)(2,1)S(1)}, bf16[16,2176]{1,0:T(8,128)(2,1)S(1)}, u32[]{:S(2)}, u32[]{:S(2)}) collective-permute-start(bf16[16,2176]{1,0:T(8,128)(2,1)S(1)} %collective-permute-done.2.refs_1_), channel_id=1, source_target_pairs={{0,4},{1,5},{2,6},{3,7},{4,0},{5,1},{6,2},{7,3},{8,12},{9,13},{10,... | collective-permute-start | bytes 208904 | tf_op jit(solution)/shard_map/ppermute | solution.py:287
  9.1 1.6 %collective-permute-start.7 = (bf16[16,2176]{1,0:T(8,128)(2,1)S(1)}, bf16[16,2176]{1,0:T(8,128)(2,1)S(1)}, u32[]{:S(2)}, u32[]{:S(2)}) collective-permute-start(bf16[16,2176]{1,0:T(8,128)(2,1)S(1)} %prepare.1.refs_0_), channel_id=1, source_target_pairs={{0,4},{1,5},{2,6},{3,7},{4,0},{5,1},{6,2},{7,3},{8,12},{9,13},{10,... | collective-permute-start | bytes 208904 | tf_op jit(solution)/shard_map/ppermute | solution.py:287
  10.6 1.2 %collective-permute-done.refs_0_ = bf16[16,2176]{1,0:T(8,128)(2,1)S(1)} collective-permute-done((bf16[16,2176]{1,0:T(8,128)(2,1)S(1)}, bf16[16,2176]{1,0:T(8,128)(2,1)S(1)}, u32[]{:S(2)}, u32[]{:S(2)}) %collective-permute-start) | collective-permute-done | bytes 69664 | tf_op jit(solution)/shard_map/ppermute | solution.py:287
  11.9 2.2 %collective-permute-done.1.refs_1_ = bf16[16,2176]{1,0:T(8,128)(2,1)S(1)} collective-permute-done((bf16[16,2176]{1,0:T(8,128)(2,1)S(1)}, bf16[16,2176]{1,0:T(8,128)(2,1)S(1)}, u32[]{:S(2)}, u32[]{:S(2)}) %collective-permute-start.1) | collective-permute-done | bytes 69664 | tf_op jit(solution)/shard_map/ppermute | solution.py:287
  14.0 0.0 collective-permute-done.3.refs_2_.refs_3_
  14.0 0.7 %collective-permute-done.7.refs_2_ = bf16[16,2176]{1,0:T(8,128)(2,1)S(1)} collective-permute-done((bf16[16,2176]{1,0:T(8,128)(2,1)S(1)}, bf16[16,2176]{1,0:T(8,128)(2,1)S(1)}, u32[]{:S(2)}, u32[]{:S(2)}) %collective-permute-start.7) | collective-permute-done | bytes 69664 | tf_op jit(solution)/shard_map/ppermute | solution.py:287
  14.8 0.1 collective-permute-start.8
  14.8 0.6 %collective-permute-start.4 = (bf16[2,16,2176]{2,1,0:T(8,128)(2,1)S(1)}, bf16[2,16,2176]{2,1,0:T(8,128)(2,1)S(1)}, u32[]{:S(2)}, u32[]{:S(2)}) collective-permute-start(bf16[2,16,2176]{2,1,0:T(8,128)(2,1)S(1)} %stack.2.refs_2_.refs_4_.refs_0_), channel_id=1, source_target_pairs={{0,2},{1,3},{2,0},{3,1},{4,6},{5,7},{6,4},{7,5},{8,10},{9,11},{10,... | collective-permute-start | bytes 417800 | tf_op jit(solution)/shard_map/ppermute | solution.py:287
  15.4 0.2 collective-permute-start.5
  15.6 3.7 %hold.1 = (bf16[4096,768]{1,0:T(8,128)(2,1)S(1)}, bf16[768,2048]{1,0:T(8,128)(2,1)S(1)}) custom-call(bf16[4096,768]{1,0:T(8,128)(2,1)} %bitcast.9, bf16[768,2048]{1,0:T(8,128)(2,1)} %bitcast.10, bf16[2,16,2176]{2,1,0:T(8,128)(2,1)S(1)} %stack.2.refs_2_.refs_4_.refs_0_), custom_call_target="tpu_custom_call" | custom-call | bytes 9437184 | tf_op jit(solution)/shard_map/hold/pallas_call | solution.py:170
  19.4 1.6 %collective-permute-done.4.in_ref.refs_1_ = bf16[2,16,2176]{2,1,0:T(8,128)(2,1)S(1)} collective-permute-done((bf16[2,16,2176]{2,1,0:T(8,128)(2,1)S(1)}, bf16[2,16,2176]{2,1,0:T(8,128)(2,1)S(1)}, u32[]{:S(2)}, u32[]{:S(2)}) %collective-permute-start.4) | collective-permute-done | bytes 139296 | tf_op jit(solution)/shard_map/ppermute | solution.py:287
  20.9 0.1 collective-permute-start.6
  21.0 0.0 collective-permute-done.8.refs_6_.refs_1_
  21.0 1.5 %ffn.3 = (bf16[4,16,2048]{2,1,0:T(8,128)(2,1)S(1)}, bf16[4,16,2048]{2,1,0:T(8,128)(2,1)S(1)}) custom-call(bf16[4,16,2176]{2,1,0:T(8,128)(2,1)S(1)} %stack.3.refs_0_, bf16[4,16,2176]{2,1,0:T(8,128)(2,1)S(1)} %collective-permute-done.8.refs_6_.refs_1_, bf16[4096,768]{1,0:T(8,128)(2,1)S(1)} %get-tuple-element.16.refs_0_.refs_4_.refs_2_, ...), custom_call_target="tpu_custom_call" | custom-call | flops 1207959552 | bytes 6291456 | tf_op jit(solution)/shard_map/ffn/pallas_call | solution.py:267
  22.5 0.0 copy-start
  22.5 0.6 %collective-permute-start.11 = (bf16[4,16,2048]{2,1,0:T(8,128)(2,1)S(1)}, bf16[4,16,2048]{2,1,0:T(8,128)(2,1)S(1)}, u32[]{:S(2)}, u32[]{:S(2)}) collective-permute-start(bf16[4,16,2048]{2,1,0:T(8,128)(2,1)S(1)} %get-tuple-element.25), channel_id=1, source_target_pairs={{0,1},{1,0},{2,3},{3,2},{4,5},{5,4},{6,7},{7,6},{8,9},{9,8},{10,11... | collective-permute-start | bytes 786440 | tf_op jit(solution)/shard_map/ppermute | solution.py:287
  23.1 0.0 collective-permute-done.5.refs_2_
  23.1 0.0 collective-permute-done.6.refs_3_
  23.1 1.5 %ffn.2 = (bf16[4,16,2048]{2,1,0:T(8,128)(2,1)S(1)}, bf16[4,16,2048]{2,1,0:T(8,128)(2,1)S(1)}) custom-call(bf16[2,16,2176]{2,1,0:T(8,128)(2,1)S(1)} %stack.2.refs_2_.refs_4_.refs_0_, bf16[2,16,2176]{2,1,0:T(8,128)(2,1)S(1)} %collective-permute-done.4.in_ref.refs_1_, bf16[2,16,2176]{2,1,0:T(8,128)(2,1)S(1)} %collective-permute-done.5.refs_2_, ...), custom_call_target="tpu_custom_call" | custom-call | flops 1207959552 | bytes 6291456 | tf_op jit(solution)/shard_map/ffn/pallas_call | solution.py:267
  24.6 0.1 collective-permute-start.9
  24.7 0.0 collective-permute-done.11.other_ref
  24.7 0.1 pair_sum.3
  24.8 1.0 %collective-permute-start.12 = (bf16[2,16,2048]{2,1,0:T(8,128)(2,1)S(1)}, bf16[2,16,2048]{2,1,0:T(8,128)(2,1)S(1)}, u32[]{:S(2)}, u32[]{:S(2)}) collective-permute-start(bf16[2,16,2048]{2,1,0:T(8,128)(2,1)S(1)} %get-tuple-element.27), channel_id=1, source_target_pairs={{0,4},{1,5},{2,6},{3,7},{4,0},{5,1},{6,2},{7,3},{8,12},{9,13},{10,... | collective-permute-start | bytes 393224 | tf_op jit(solution)/shard_map/ppermute | solution.py:287
  25.8 0.4 collective-permute-done.9.other_ref
  26.2 0.1 pair_sum.2
  26.3 0.6 %collective-permute-start.10 = (bf16[2,16,2048]{2,1,0:T(8,128)(2,1)S(1)}, bf16[2,16,2048]{2,1,0:T(8,128)(2,1)S(1)}, u32[]{:S(2)}, u32[]{:S(2)}) collective-permute-start(bf16[2,16,2048]{2,1,0:T(8,128)(2,1)S(1)} %get-tuple-element.21), channel_id=1, source_target_pairs={{0,2},{1,3},{2,0},{3,1},{4,6},{5,7},{6,4},{7,5},{8,10},{9,11},{10,... | collective-permute-start | bytes 393224 | tf_op jit(solution)/shard_map/ppermute | solution.py:287
  26.9 3.9 %collective-permute-done.12.other_ref = bf16[2,16,2048]{2,1,0:T(8,128)(2,1)S(1)} collective-permute-done((bf16[2,16,2048]{2,1,0:T(8,128)(2,1)S(1)}, bf16[2,16,2048]{2,1,0:T(8,128)(2,1)S(1)}, u32[]{:S(2)}, u32[]{:S(2)}) %collective-permute-start.12) | collective-permute-done | bytes 131104 | tf_op jit(solution)/shard_map/ppermute | solution.py:287
  30.8 0.6 %collective-permute-start.15 = (bf16[16,2048]{1,0:T(8,128)(2,1)S(1)}, bf16[16,2048]{1,0:T(8,128)(2,1)S(1)}, u32[]{:S(2)}, u32[]{:S(2)}) collective-permute-start(bf16[16,2048]{1,0:T(8,128)(2,1)S(1)} %get-tuple-element.29), channel_id=1, source_target_pairs={{0,2},{1,3},{2,0},{3,1},{4,6},{5,7},{6,4},{7,5},{8,10},{9,11},{10,... | collective-permute-start | bytes 196616 | tf_op jit(solution)/shard_map/ppermute | solution.py:287
  31.4 0.5 %collective-permute-done.10.other_ref = bf16[2,16,2048]{2,1,0:T(8,128)(2,1)S(1)} collective-permute-done((bf16[2,16,2048]{2,1,0:T(8,128)(2,1)S(1)}, bf16[2,16,2048]{2,1,0:T(8,128)(2,1)S(1)}, u32[]{:S(2)}, u32[]{:S(2)}) %collective-permute-start.10) | collective-permute-done | bytes 131104 | tf_op jit(solution)/shard_map/ppermute | solution.py:287
  31.9 3.3 %collective-permute-start.13 = (bf16[16,2048]{1,0:T(8,128)(2,1)S(1)}, bf16[16,2048]{1,0:T(8,128)(2,1)S(1)}, u32[]{:S(2)}, u32[]{:S(2)}) collective-permute-start(bf16[16,2048]{1,0:T(8,128)(2,1)S(1)} %get-tuple-element.23.refs_7_), channel_id=1, source_target_pairs={{0,12},{1,13},{2,14},{3,15},{4,8},{5,9},{6,10},{7,11},{8,4},{9,5},... | collective-permute-start | bytes 196616 | tf_op jit(solution)/shard_map/ppermute | solution.py:287
  35.2 0.0 collective-permute-start.14
  35.2 3.2 %attend.1 = bf16[4,32,128]{2,1,0:T(8,128)(2,1)} custom-call(s32[4]{0:T(128)} %refs_0_.3, bf16[4,32,128]{2,1,0:T(8,128)(2,1)} %refs_1_.1, bf16[4,256,128]{2,1,0:T(8,128)(2,1)} %bitcast.11, bf16[4,256,128]{2,1,0:T(8,128)(2,1)} %bitcast.12, bf16[8,128]{1,0:T(8,128)(2,1)} %bitcast.16, bf16[8,128]{1,0:T(8,128)(2,1)} %bitcast.17, ...), custom_call_target="tpu_custom_call" | custom-call | bytes 4194304 | tf_op jit(solution)/shard_map/attend/pallas_call | solution.py:77
  38.4 0.0 collective-permute-done.15.refs_3_
  38.5 0.1 collective-permute-done.13.refs_1_
  38.6 2.0 %collective-permute-done.14.refs_2_ = bf16[16,2048]{1,0:T(8,128)(2,1)S(1)} collective-permute-done((bf16[16,2048]{1,0:T(8,128)(2,1)S(1)}, bf16[16,2048]{1,0:T(8,128)(2,1)S(1)}, u32[]{:S(2)}, u32[]{:S(2)}) %collective-permute-start.14) | collective-permute-done | bytes 65568 | tf_op jit(solution)/shard_map/ppermute | solution.py:287
  40.6 0.0 copy-done
  40.6 0.7 %total.1 = bf16[16,2048]{1,0:T(8,128)(2,1)} custom-call(bf16[16,2048]{1,0:T(8,128)(2,1)S(1)} %copy-done, f32[16,2048]{1,0:T(8,128)S(1)} %get-tuple-element.28.refs_0_, bf16[16,2048]{1,0:T(8,128)(2,1)S(1)} %collective-permute-done.13.refs_1_, bf16[16,2048]{1,0:T(8,128)(2,1)S(1)} %collective-permute-done.14.refs_2_, ...), custom_call_target="tpu_custom_call" | custom-call | tf_op jit(solution)/shard_map/total/pallas_call | solution.py:267
  (5 shorter events, 0.1 us)
Async XLA Ops:
  1.7 6.9 %collective-permute-start.2 = (bf16[16,2176]{1,0:T(8,128)(2,1)S(1)}, bf16[16,2176]{1,0:T(8,128)(2,1)S(1)}, u32[]{:S(2)}, u32[]{:S(2)}) collective-permute-start(bf16[16,2176]{1,0:T(8,128)(2,1)S(1)} %prepare.1.refs_0_), channel_id=1, source_target_pairs={{0,2},{1,3},{2,0},{3,1},{4,6},{5,7},{6,4},{7,5},{8,10},{9,11},{10,... | collective-permute-start | bytes 208904 | tf_op jit(solution)/shard_map/ppermute | solution.py:287
  4.7 7.2 %collective-permute-start = (bf16[16,2176]{1,0:T(8,128)(2,1)S(1)}, bf16[16,2176]{1,0:T(8,128)(2,1)S(1)}, u32[]{:S(2)}, u32[]{:S(2)}) collective-permute-start(bf16[16,2176]{1,0:T(8,128)(2,1)S(1)} %prepare.1.refs_0_), channel_id=1, source_target_pairs={{0,8},{1,9},{2,10},{3,11},{4,12},{5,13},{6,14},{7,15},{8,0},{9,1},... | collective-permute-start | bytes 208904 | tf_op jit(solution)/shard_map/ppermute | solution.py:287
  7.3 6.8 %collective-permute-start.1 = (bf16[16,2176]{1,0:T(8,128)(2,1)S(1)}, bf16[16,2176]{1,0:T(8,128)(2,1)S(1)}, u32[]{:S(2)}, u32[]{:S(2)}) collective-permute-start(bf16[16,2176]{1,0:T(8,128)(2,1)S(1)} %prepare.1.refs_0_), channel_id=1, source_target_pairs={{0,12},{1,13},{2,14},{3,15},{4,8},{5,9},{6,10},{7,11},{8,4},{9,5},... | collective-permute-start | bytes 208904 | tf_op jit(solution)/shard_map/ppermute | solution.py:287
  8.6 5.4 %collective-permute-start.3 = (bf16[16,2176]{1,0:T(8,128)(2,1)S(1)}, bf16[16,2176]{1,0:T(8,128)(2,1)S(1)}, u32[]{:S(2)}, u32[]{:S(2)}) collective-permute-start(bf16[16,2176]{1,0:T(8,128)(2,1)S(1)} %collective-permute-done.2.refs_1_), channel_id=1, source_target_pairs={{0,4},{1,5},{2,6},{3,7},{4,0},{5,1},{6,2},{7,3},{8,12},{9,13},{10,... | collective-permute-start | bytes 208904 | tf_op jit(solution)/shard_map/ppermute | solution.py:287
  9.1 5.7 %collective-permute-start.7 = (bf16[16,2176]{1,0:T(8,128)(2,1)S(1)}, bf16[16,2176]{1,0:T(8,128)(2,1)S(1)}, u32[]{:S(2)}, u32[]{:S(2)}) collective-permute-start(bf16[16,2176]{1,0:T(8,128)(2,1)S(1)} %prepare.1.refs_0_), channel_id=1, source_target_pairs={{0,4},{1,5},{2,6},{3,7},{4,0},{5,1},{6,2},{7,3},{8,12},{9,13},{10,... | collective-permute-start | bytes 208904 | tf_op jit(solution)/shard_map/ppermute | solution.py:287
  14.8 6.3 %collective-permute-start.8 = (bf16[4,16,2176]{2,1,0:T(8,128)(2,1)S(1)}, bf16[4,16,2176]{2,1,0:T(8,128)(2,1)S(1)}, u32[]{:S(2)}, u32[]{:S(2)}) collective-permute-start(bf16[4,16,2176]{2,1,0:T(8,128)(2,1)S(1)} %stack.3.refs_0_), channel_id=1, source_target_pairs={{0,1},{1,0},{2,3},{3,2},{4,5},{5,4},{6,7},{7,6},{8,9},{9,8},{10,11... | collective-permute-start | bytes 835592 | tf_op jit(solution)/shard_map/ppermute | solution.py:287
  14.8 6.1 %collective-permute-start.4 = (bf16[2,16,2176]{2,1,0:T(8,128)(2,1)S(1)}, bf16[2,16,2176]{2,1,0:T(8,128)(2,1)S(1)}, u32[]{:S(2)}, u32[]{:S(2)}) collective-permute-start(bf16[2,16,2176]{2,1,0:T(8,128)(2,1)S(1)} %stack.2.refs_2_.refs_4_.refs_0_), channel_id=1, source_target_pairs={{0,2},{1,3},{2,0},{3,1},{4,6},{5,7},{6,4},{7,5},{8,10},{9,11},{10,... | collective-permute-start | bytes 417800 | tf_op jit(solution)/shard_map/ppermute | solution.py:287
  15.4 7.7 %collective-permute-start.5 = (bf16[2,16,2176]{2,1,0:T(8,128)(2,1)S(1)}, bf16[2,16,2176]{2,1,0:T(8,128)(2,1)S(1)}, u32[]{:S(2)}, u32[]{:S(2)}) collective-permute-start(bf16[2,16,2176]{2,1,0:T(8,128)(2,1)S(1)} %stack.2.refs_2_.refs_4_.refs_0_), channel_id=1, source_target_pairs={{0,1},{1,0},{2,3},{3,2},{4,5},{5,4},{6,7},{7,6},{8,9},{9,8},{10,11... | collective-permute-start | bytes 417800 | tf_op jit(solution)/shard_map/ppermute | solution.py:287
  20.9 2.2 %collective-permute-start.6 = (bf16[2,16,2176]{2,1,0:T(8,128)(2,1)S(1)}, bf16[2,16,2176]{2,1,0:T(8,128)(2,1)S(1)}, u32[]{:S(2)}, u32[]{:S(2)}) collective-permute-start(bf16[2,16,2176]{2,1,0:T(8,128)(2,1)S(1)} %relay.1), channel_id=1, source_target_pairs={{0,1},{1,0},{2,3},{3,2},{4,5},{5,4},{6,7},{7,6},{8,9},{9,8},{10,11... | collective-permute-start | bytes 417800 | tf_op jit(solution)/shard_map/ppermute | solution.py:287
  22.5 18.1 %copy-start = (bf16[16,2048]{1,0:T(8,128)(2,1)S(1)}, bf16[16,2048]{1,0:T(8,128)(2,1)}, u32[]{:S(2)}) copy-start(bf16[16,2048]{1,0:T(8,128)(2,1)} %residual_ref.1) | copy-start | bytes 196612
  22.5 2.2 %collective-permute-start.11 = (bf16[4,16,2048]{2,1,0:T(8,128)(2,1)S(1)}, bf16[4,16,2048]{2,1,0:T(8,128)(2,1)S(1)}, u32[]{:S(2)}, u32[]{:S(2)}) collective-permute-start(bf16[4,16,2048]{2,1,0:T(8,128)(2,1)S(1)} %get-tuple-element.25), channel_id=1, source_target_pairs={{0,1},{1,0},{2,3},{3,2},{4,5},{5,4},{6,7},{7,6},{8,9},{9,8},{10,11... | collective-permute-start | bytes 786440 | tf_op jit(solution)/shard_map/ppermute | solution.py:287
  24.6 1.6 %collective-permute-start.9 = (bf16[4,16,2048]{2,1,0:T(8,128)(2,1)S(1)}, bf16[4,16,2048]{2,1,0:T(8,128)(2,1)S(1)}, u32[]{:S(2)}, u32[]{:S(2)}) collective-permute-start(bf16[4,16,2048]{2,1,0:T(8,128)(2,1)S(1)} %get-tuple-element.19), channel_id=1, source_target_pairs={{0,1},{1,0},{2,3},{3,2},{4,5},{5,4},{6,7},{7,6},{8,9},{9,8},{10,11... | collective-permute-start | bytes 786440 | tf_op jit(solution)/shard_map/ppermute | solution.py:287
  24.8 6.0 %collective-permute-start.12 = (bf16[2,16,2048]{2,1,0:T(8,128)(2,1)S(1)}, bf16[2,16,2048]{2,1,0:T(8,128)(2,1)S(1)}, u32[]{:S(2)}, u32[]{:S(2)}) collective-permute-start(bf16[2,16,2048]{2,1,0:T(8,128)(2,1)S(1)} %get-tuple-element.27), channel_id=1, source_target_pairs={{0,4},{1,5},{2,6},{3,7},{4,0},{5,1},{6,2},{7,3},{8,12},{9,13},{10,... | collective-permute-start | bytes 393224 | tf_op jit(solution)/shard_map/ppermute | solution.py:287
  26.3 5.6 %collective-permute-start.10 = (bf16[2,16,2048]{2,1,0:T(8,128)(2,1)S(1)}, bf16[2,16,2048]{2,1,0:T(8,128)(2,1)S(1)}, u32[]{:S(2)}, u32[]{:S(2)}) collective-permute-start(bf16[2,16,2048]{2,1,0:T(8,128)(2,1)S(1)} %get-tuple-element.21), channel_id=1, source_target_pairs={{0,2},{1,3},{2,0},{3,1},{4,6},{5,7},{6,4},{7,5},{8,10},{9,11},{10,... | collective-permute-start | bytes 393224 | tf_op jit(solution)/shard_map/ppermute | solution.py:287
  30.8 7.7 %collective-permute-start.15 = (bf16[16,2048]{1,0:T(8,128)(2,1)S(1)}, bf16[16,2048]{1,0:T(8,128)(2,1)S(1)}, u32[]{:S(2)}, u32[]{:S(2)}) collective-permute-start(bf16[16,2048]{1,0:T(8,128)(2,1)S(1)} %get-tuple-element.29), channel_id=1, source_target_pairs={{0,2},{1,3},{2,0},{3,1},{4,6},{5,7},{6,4},{7,5},{8,10},{9,11},{10,... | collective-permute-start | bytes 196616 | tf_op jit(solution)/shard_map/ppermute | solution.py:287
  31.9 6.7 %collective-permute-start.13 = (bf16[16,2048]{1,0:T(8,128)(2,1)S(1)}, bf16[16,2048]{1,0:T(8,128)(2,1)S(1)}, u32[]{:S(2)}, u32[]{:S(2)}) collective-permute-start(bf16[16,2048]{1,0:T(8,128)(2,1)S(1)} %get-tuple-element.23.refs_7_), channel_id=1, source_target_pairs={{0,12},{1,13},{2,14},{3,15},{4,8},{5,9},{6,10},{7,11},{8,4},{9,5},... | collective-permute-start | bytes 196616 | tf_op jit(solution)/shard_map/ppermute | solution.py:287
  35.2 5.4 %collective-permute-start.14 = (bf16[16,2048]{1,0:T(8,128)(2,1)S(1)}, bf16[16,2048]{1,0:T(8,128)(2,1)S(1)}, u32[]{:S(2)}, u32[]{:S(2)}) collective-permute-start(bf16[16,2048]{1,0:T(8,128)(2,1)S(1)} %get-tuple-element.22.refs_6_), channel_id=1, source_target_pairs={{0,8},{1,9},{2,10},{3,11},{4,12},{5,13},{6,14},{7,15},{8,0},{9,1},... | collective-permute-start | bytes 196616 | tf_op jit(solution)/shard_map/ppermute | solution.py:287

commit v2 on v1

--- a/solution.py
+++ b/solution.py
@@ -221,13 +221,12 @@
     refs[-1][...] = in_ref[...]
 
 
-def ffn_kernel(block_count, *refs):
-    blocks = refs[:block_count]
-    in_ref, down_ref = refs[block_count : block_count + 2]
+def ffn_kernel(takes, *refs):
+    in_ref, down_ref = refs[4:6]
     near_ref, far_ref = refs[-2:]
     width = down_ref.shape[1]
     packed = jnp.concatenate(
-        [block[...].reshape(-1, block.shape[-1]) for block in blocks], axis=0
+        [refs[i][b] for i, start, stop in takes for b in range(start, stop)], axis=0
     )
     rows = packed[:, :width]
     terms = packed[:, width:].astype(jnp.float32)
@@ -243,7 +242,8 @@
     far_ref[...] = out[1]
 
 
-def pair_kernel(own_ref, other_ref, keep_ref, send_ref):
+def pair_kernel(own_ref, other_ref, *refs):
+    keep_ref, send_ref = refs[-2:]
     half = keep_ref.shape[0]
     keep_ref[...] = own_ref[:half].astype(jnp.float32) + other_ref[:half].astype(jnp.float32)
     send = own_ref[half:].astype(jnp.float32) + other_ref[half:].astype(jnp.float32)
@@ -286,6 +286,9 @@
     def swap(value, bits):
         return lax.ppermute(value, "ep", [(i, i ^ bits) for i in range(devices)])
 
+    def relay(value, after):
+        return in_vmem(relay_kernel, vmem(value.shape, value.dtype), "relay", (value,), after)
+
     def stack(members, after=()):
         shape = vmem((len(members), row_count, width + extra), jnp.bfloat16)
         return in_vmem(stack_kernel, shape, "stack", members, after)
@@ -296,45 +299,45 @@
         "prepare",
         (residual, norm_gain.reshape(1, -1), routes.T, route_weights.T),
     )
-    first, third, second = (swap(packed, d * line) for d in (1, 3, 2))
+    third, second, first = (swap(packed, d * line) for d in (3, 2, 1))
     across = swap(packed, side)
-    diagonal = swap(across, line)
-    early = stack((second, third), (diagonal,))
-    held = hold((expert_in, expert_down), (early,))
-    early_side = swap(early, side)
-    early_far = swap(early, core)
-    late = stack((packed, across, first, diagonal), (early,))
-    late_far = swap(late, core)
-    shape = vmem(early.shape, early.dtype)
-    relayed = in_vmem(relay_kernel, shape, "relay", (early_side,), held[:1])
-    early_side_far = swap(relayed, core)
-
-    def ffn(members, after=()):
+    along = stack((second, third, first))
+    along_side = swap(along, side)
+    near = stack((second, third, first, packed, across))
+    near_far = swap(near, core)
+    held = hold((expert_in, expert_down), (along,))
+    along_side_far = swap(relay(along_side, held[:1]), core)
+
+    def ffn(near_takes, side_takes, after=()):
+        takes = [(i, *t) for i in (0, 2) for t in near_takes]
+        takes[len(near_takes) : len(near_takes)] = [(1, *t) for t in side_takes]
+        takes += [(3, *t) for t in side_takes]
         return in_vmem(
-            functools.partial(ffn_kernel, len(members)),
+            functools.partial(ffn_kernel, takes),
             [vmem((4,) + one, jnp.bfloat16)] * 2,
             "ffn",
-            (*members, *held),
+            (near, along_side, near_far, along_side_far, *held),
             after,
             mebibytes=16,
             cost_estimate=cost(8 * row_count * 2 * sum(h.size for h in held), 2 * held[0].size),
         )
 
-    def pair_sum(near_out, far_out):
+    def pair_sum(near_out, far_out, after=()):
         shapes = [vmem((2,) + one, jnp.float32), vmem((2,) + one, jnp.bfloat16)]
-        return in_vmem(pair_kernel, shapes, "pair_sum", (near_out, swap(far_out, core)))
-
-    early_members = (early, early_side, early_far, early_side_far)
-    early_keep, early_send = pair_sum(*ffn(early_members, (late_far,)))
+        return in_vmem(pair_kernel, shapes, "pair_sum", (near_out, swap(far_out, core)), after)
+
+    early_outs = ffn([(0, 2)], [(0, 2)])
+    early_keep, early_send = pair_sum(*early_outs)
     early_sums = in_vmem(
         square_kernel,
         [vmem(one, jnp.bfloat16)] * 2,
         "square_sum",
         (early_keep, swap(early_send, side)),
     )
+    attended = attend(*attention, tuple(early_sums))
     back = [swap(early_sums[1], 3 * line), swap(early_sums[0], 2 * line)]
-    attended = attend(*attention, tuple(early_sums))
-    late_keep, late_send = pair_sum(*ffn((late, late_far)))
+    late_outs = ffn([(3, 5), (2, 3)], [(2, 3)], early_outs[:1])
+    late_keep, late_send = pair_sum(*late_outs)
     own, across_sum = in_vmem(
         square_kernel,
         [vmem(one, jnp.float32), vmem(one, jnp.bfloat16)],

time: 41.5 us -> 39.6 us (0.954)
  waiting for transfers between devices: 12.6 us -> 7.49 us
  starting transfers between devices: 16 us -> 19.3 us
    ppermute x16 -> x14, waiting for transfers between devices: 12.6 us -> 7.49 us  [swap(): return lax.ppermute(value, 'ep', [(i, i ^ bits) for i in range(devices)])]
    ppermute x16 -> x14, starting transfers between devices: 16 us -> 19.3 us  [swap(): return lax.ppermute(value, 'ep', [(i, i ^ bits) for i in range(devices)])]
  transfers between devices with their start and end apart: 16 -> 14, of which waited for: 9 -> 7; matrix products, arithmetic and copies ran while one was open for 0% -> 0% of each run, Pallas kernels for 25% -> 22%
where the time goes in v2:
time: 39.6 us; the launch traced here: 39.4 us
  starting transfers between devices  19.3 us (49%)
  Pallas kernels  11.9 us (30%)
  waiting for transfers between devices  7.49 us (19%)
  between operations  0.73 us (2%)
    ppermute x14, starting transfers between devices, swap(): return lax.ppermute(value, 'ep', [(i, i ^ bits) for i in range(devices)])  19.3 us
    ppermute x14, waiting for transfers between devices, swap(): return lax.ppermute(value, 'ep', [(i, i ^ bits) for i in range(devices)])  7.49 us
    pallas_call x2, Pallas kernels, from_hbm(): pl.pallas_call(kernel, out_shape=out_shape, in_specs=[pl.BlockSpec(memory...  4.24 us
    pallas_call x10, Pallas kernels, in_vmem(): pl.pallas_call(kernel, out_shape=out_shape, in_specs=[HERE] * len(arrays)...  3.95 us
    pallas_call x1, Pallas kernels, hold(): pl.pallas_call(functools.partial(hold_kernel, len(flat), pieces), out_sha...  3.75 us
  transfers between devices with their start and end apart: 14, of which 7 were waited for; matrix products, arithmetic and copies ran while one was open for 0% of the time, Pallas kernels for 22%

profile of v2, /device:TPU:0, one launch (start us, length us, event | category | flops | bytes accessed | tf_op | source)
XLA Modules:
  0.0 39.4 jit_solution(2022855889978213379)
XLA Ops:
  0.6 1.0 %prepare.1.refs_3_ = bf16[16,2176]{1,0:T(8,128)(2,1)S(1)} custom-call(bf16[16,2048]{1,0:T(8,128)(2,1)} %residual_ref.1, f32[1,2048]{1,0:T(1,128)} %bitcast.13, s32[8,16]{1,0:T(8,128)} %bitcast.14, f32[8,16]{1,0:T(8,128)} %bitcast.15), custom_call_target="tpu_custom_call" | custom-call | tf_op jit(solution)/shard_map/prepare/pallas_call | solution.py:77
  1.7 4.1 %collective-permute-start = (bf16[16,2176]{1,0:T(8,128)(2,1)S(1)}, bf16[16,2176]{1,0:T(8,128)(2,1)S(1)}, u32[]{:S(2)}, u32[]{:S(2)}) collective-permute-start(bf16[16,2176]{1,0:T(8,128)(2,1)S(1)} %prepare.1.refs_3_), channel_id=1, source_target_pairs={{0,8},{1,9},{2,10},{3,11},{4,12},{5,13},{6,14},{7,15},{8,0},{9,1},... | collective-permute-start | bytes 208904 | tf_op jit(solution)/shard_map/ppermute | solution.py:287
  5.8 1.3 %collective-permute-start.1 = (bf16[16,2176]{1,0:T(8,128)(2,1)S(1)}, bf16[16,2176]{1,0:T(8,128)(2,1)S(1)}, u32[]{:S(2)}, u32[]{:S(2)}) collective-permute-start(bf16[16,2176]{1,0:T(8,128)(2,1)S(1)} %prepare.1.refs_3_), channel_id=1, source_target_pairs={{0,12},{1,13},{2,14},{3,15},{4,8},{5,9},{6,10},{7,11},{8,4},{9,5},... | collective-permute-start | bytes 208904 | tf_op jit(solution)/shard_map/ppermute | solution.py:287
  7.1 0.2 collective-permute-start.2
  7.4 1.5 %collective-permute-start.3 = (bf16[16,2176]{1,0:T(8,128)(2,1)S(1)}, bf16[16,2176]{1,0:T(8,128)(2,1)S(1)}, u32[]{:S(2)}, u32[]{:S(2)}) collective-permute-start(bf16[16,2176]{1,0:T(8,128)(2,1)S(1)} %prepare.1.refs_3_), channel_id=1, source_target_pairs={{0,2},{1,3},{2,0},{3,1},{4,6},{5,7},{6,4},{7,5},{8,10},{9,11},{10,... | collective-permute-start | bytes 208904 | tf_op jit(solution)/shard_map/ppermute | solution.py:287
  8.8 0.8 %collective-permute-done.refs_0_ = bf16[16,2176]{1,0:T(8,128)(2,1)S(1)} collective-permute-done((bf16[16,2176]{1,0:T(8,128)(2,1)S(1)}, bf16[16,2176]{1,0:T(8,128)(2,1)S(1)}, u32[]{:S(2)}, u32[]{:S(2)}) %collective-permute-start) | collective-permute-done | bytes 69664 | tf_op jit(solution)/shard_map/ppermute | solution.py:287
  9.7 2.5 %collective-permute-done.1.refs_1_ = bf16[16,2176]{1,0:T(8,128)(2,1)S(1)} collective-permute-done((bf16[16,2176]{1,0:T(8,128)(2,1)S(1)}, bf16[16,2176]{1,0:T(8,128)(2,1)S(1)}, u32[]{:S(2)}, u32[]{:S(2)}) %collective-permute-start.1) | collective-permute-done | bytes 69664 | tf_op jit(solution)/shard_map/ppermute | solution.py:287
  12.1 0.1 collective-permute-done.2.refs_2_
  12.2 1.7 %collective-permute-start.4 = (bf16[3,16,2176]{2,1,0:T(8,128)(2,1)S(1)}, bf16[3,16,2176]{2,1,0:T(8,128)(2,1)S(1)}, u32[]{:S(2)}, u32[]{:S(2)}) collective-permute-start(bf16[3,16,2176]{2,1,0:T(8,128)(2,1)S(1)} %stack.3.refs_2_), channel_id=1, source_target_pairs={{0,2},{1,3},{2,0},{3,1},{4,6},{5,7},{6,4},{7,5},{8,10},{9,11},{10,... | collective-permute-start | bytes 626696 | tf_op jit(solution)/shard_map/ppermute | solution.py:287
  13.9 0.0 collective-permute-done.3.refs_4_
  14.0 0.1 collective-permute-start.5
  14.0 3.8 %hold.1 = (bf16[4096,768]{1,0:T(8,128)(2,1)S(1)}, bf16[768,2048]{1,0:T(8,128)(2,1)S(1)}) custom-call(bf16[4096,768]{1,0:T(8,128)(2,1)} %bitcast.9, bf16[768,2048]{1,0:T(8,128)(2,1)} %bitcast.10, bf16[3,16,2176]{2,1,0:T(8,128)(2,1)S(1)} %stack.3.refs_2_), custom_call_target="tpu_custom_call" | custom-call | bytes 9437184 | tf_op jit(solution)/shard_map/hold/pallas_call | solution.py:170
  17.8 0.3 collective-permute-done.4.in_ref.refs_1_
  18.1 0.3 collective-permute-start.6
  18.4 0.0 collective-permute-done.5.refs_2_
  18.4 1.2 %collective-permute-done.6.refs_3_ = bf16[3,16,2176]{2,1,0:T(8,128)(2,1)S(1)} collective-permute-done((bf16[3,16,2176]{2,1,0:T(8,128)(2,1)S(1)}, bf16[3,16,2176]{2,1,0:T(8,128)(2,1)S(1)}, u32[]{:S(2)}, u32[]{:S(2)}) %collective-permute-start.6) | collective-permute-done | bytes 208928 | tf_op jit(solution)/shard_map/ppermute | solution.py:287
  19.6 1.5 %ffn.2 = (bf16[4,16,2048]{2,1,0:T(8,128)(2,1)S(1)}, bf16[4,16,2048]{2,1,0:T(8,128)(2,1)S(1)}) custom-call(bf16[5,16,2176]{2,1,0:T(8,128)(2,1)S(1)} %stack.2.refs_0_, bf16[3,16,2176]{2,1,0:T(8,128)(2,1)S(1)} %collective-permute-done.4.in_ref.refs_1_, bf16[5,16,2176]{2,1,0:T(8,128)(2,1)S(1)} %collective-permute-done.5.refs_2_, ...), custom_call_target="tpu_custom_call" | custom-call | flops 1207959552 | bytes 6291456 | tf_op jit(solution)/shard_map/ffn/pallas_call | solution.py:267
  21.1 0.3 collective-permute-start.7
  21.4 0.0 copy-start
  21.4 1.5 %ffn.3 = (bf16[4,16,2048]{2,1,0:T(8,128)(2,1)S(1)}, bf16[4,16,2048]{2,1,0:T(8,128)(2,1)S(1)}) custom-call(bf16[5,16,2176]{2,1,0:T(8,128)(2,1)S(1)} %stack.2.refs_0_, bf16[3,16,2176]{2,1,0:T(8,128)(2,1)S(1)} %collective-permute-done.4.in_ref.refs_1_, bf16[5,16,2176]{2,1,0:T(8,128)(2,1)S(1)} %collective-permute-done.5.refs_2_, ...), custom_call_target="tpu_custom_call" | custom-call | flops 1207959552 | bytes 6291456 | tf_op jit(solution)/shard_map/ffn/pallas_call | solution.py:267
  23.0 0.3 collective-permute-start.9
  23.3 0.0 collective-permute-done.7.other_ref
  23.3 0.1 pair_sum.2
  23.4 1.7 %collective-permute-start.8 = (bf16[2,16,2048]{2,1,0:T(8,128)(2,1)S(1)}, bf16[2,16,2048]{2,1,0:T(8,128)(2,1)S(1)}, u32[]{:S(2)}, u32[]{:S(2)}) collective-permute-start(bf16[2,16,2048]{2,1,0:T(8,128)(2,1)S(1)} %get-tuple-element.21), channel_id=1, source_target_pairs={{0,2},{1,3},{2,0},{3,1},{4,6},{5,7},{6,4},{7,5},{8,10},{9,11},{10,... | collective-permute-start | bytes 393224 | tf_op jit(solution)/shard_map/ppermute | solution.py:287
  25.1 0.0 collective-permute-done.9.other_ref
  25.1 0.1 pair_sum.3
  25.2 2.1 %collective-permute-start.10 = (bf16[2,16,2048]{2,1,0:T(8,128)(2,1)S(1)}, bf16[2,16,2048]{2,1,0:T(8,128)(2,1)S(1)}, u32[]{:S(2)}, u32[]{:S(2)}) collective-permute-start(bf16[2,16,2048]{2,1,0:T(8,128)(2,1)S(1)} %get-tuple-element.27), channel_id=1, source_target_pairs={{0,4},{1,5},{2,6},{3,7},{4,0},{5,1},{6,2},{7,3},{8,12},{9,13},{10,... | collective-permute-start | bytes 393224 | tf_op jit(solution)/shard_map/ppermute | solution.py:287
  27.3 1.8 %collective-permute-done.8.other_ref = bf16[2,16,2048]{2,1,0:T(8,128)(2,1)S(1)} collective-permute-done((bf16[2,16,2048]{2,1,0:T(8,128)(2,1)S(1)}, bf16[2,16,2048]{2,1,0:T(8,128)(2,1)S(1)}, u32[]{:S(2)}, u32[]{:S(2)}) %collective-permute-start.8) | collective-permute-done | bytes 131104 | tf_op jit(solution)/shard_map/ppermute | solution.py:287
  29.1 3.6 %collective-permute-start.11 = (bf16[16,2048]{1,0:T(8,128)(2,1)S(1)}, bf16[16,2048]{1,0:T(8,128)(2,1)S(1)}, u32[]{:S(2)}, u32[]{:S(2)}) collective-permute-start(bf16[16,2048]{1,0:T(8,128)(2,1)S(1)} %get-tuple-element.23.refs_7_), channel_id=1, source_target_pairs={{0,12},{1,13},{2,14},{3,15},{4,8},{5,9},{6,10},{7,11},{8,4},{9,5},... | collective-permute-start | bytes 196616 | tf_op jit(solution)/shard_map/ppermute | solution.py:287
  32.7 0.4 %collective-permute-start.12 = (bf16[16,2048]{1,0:T(8,128)(2,1)S(1)}, bf16[16,2048]{1,0:T(8,128)(2,1)S(1)}, u32[]{:S(2)}, u32[]{:S(2)}) collective-permute-start(bf16[16,2048]{1,0:T(8,128)(2,1)S(1)} %get-tuple-element.22.refs_6_), channel_id=1, source_target_pairs={{0,8},{1,9},{2,10},{3,11},{4,12},{5,13},{6,14},{7,15},{8,0},{9,1},... | collective-permute-start | bytes 196616 | tf_op jit(solution)/shard_map/ppermute | solution.py:287
  33.1 0.0 collective-permute-done.10.other_ref
  33.2 1.5 %collective-permute-start.13 = (bf16[16,2048]{1,0:T(8,128)(2,1)S(1)}, bf16[16,2048]{1,0:T(8,128)(2,1)S(1)}, u32[]{:S(2)}, u32[]{:S(2)}) collective-permute-start(bf16[16,2048]{1,0:T(8,128)(2,1)S(1)} %get-tuple-element.29), channel_id=1, source_target_pairs={{0,2},{1,3},{2,0},{3,1},{4,6},{5,7},{6,4},{7,5},{8,10},{9,11},{10,... | collective-permute-start | bytes 196616 | tf_op jit(solution)/shard_map/ppermute | solution.py:287
  34.7 3.2 %attend.1 = bf16[4,32,128]{2,1,0:T(8,128)(2,1)} custom-call(s32[4]{0:T(128)} %refs_0_.3, bf16[4,32,128]{2,1,0:T(8,128)(2,1)} %refs_1_.1, bf16[4,256,128]{2,1,0:T(8,128)(2,1)} %bitcast.11, bf16[4,256,128]{2,1,0:T(8,128)(2,1)} %bitcast.12, bf16[8,128]{1,0:T(8,128)(2,1)} %bitcast.16, bf16[8,128]{1,0:T(8,128)(2,1)} %bitcast.17, ...), custom_call_target="tpu_custom_call" | custom-call | bytes 4194304 | tf_op jit(solution)/shard_map/attend/pallas_call | solution.py:77
  37.9 0.0 collective-permute-done.11.refs_1_
  37.9 0.8 %collective-permute-done.12.refs_2_ = bf16[16,2048]{1,0:T(8,128)(2,1)S(1)} collective-permute-done((bf16[16,2048]{1,0:T(8,128)(2,1)S(1)}, bf16[16,2048]{1,0:T(8,128)(2,1)S(1)}, u32[]{:S(2)}, u32[]{:S(2)}) %collective-permute-start.12) | collective-permute-done | bytes 65568 | tf_op jit(solution)/shard_map/ppermute | solution.py:287
  38.8 0.0 collective-permute-done.13.refs_3_
  38.8 0.0 copy-done
  38.8 0.7 %total.1 = bf16[16,2048]{1,0:T(8,128)(2,1)} custom-call(bf16[16,2048]{1,0:T(8,128)(2,1)S(1)} %copy-done, f32[16,2048]{1,0:T(8,128)S(1)} %get-tuple-element.28.refs_0_, bf16[16,2048]{1,0:T(8,128)(2,1)S(1)} %collective-permute-done.11.refs_1_, bf16[16,2048]{1,0:T(8,128)(2,1)S(1)} %collective-permute-done.12.refs_2_, ...), custom_call_target="tpu_custom_call" | custom-call | tf_op jit(solution)/shard_map/total/pallas_call | solution.py:267
  (5 shorter events, 0.1 us)
Async XLA Ops:
  1.7 8.0 %collective-permute-start = (bf16[16,2176]{1,0:T(8,128)(2,1)S(1)}, bf16[16,2176]{1,0:T(8,128)(2,1)S(1)}, u32[]{:S(2)}, u32[]{:S(2)}) collective-permute-start(bf16[16,2176]{1,0:T(8,128)(2,1)S(1)} %prepare.1.refs_3_), channel_id=1, source_target_pairs={{0,8},{1,9},{2,10},{3,11},{4,12},{5,13},{6,14},{7,15},{8,0},{9,1},... | collective-permute-start | bytes 208904 | tf_op jit(solution)/shard_map/ppermute | solution.py:287
  5.8 6.3 %collective-permute-start.1 = (bf16[16,2176]{1,0:T(8,128)(2,1)S(1)}, bf16[16,2176]{1,0:T(8,128)(2,1)S(1)}, u32[]{:S(2)}, u32[]{:S(2)}) collective-permute-start(bf16[16,2176]{1,0:T(8,128)(2,1)S(1)} %prepare.1.refs_3_), channel_id=1, source_target_pairs={{0,12},{1,13},{2,14},{3,15},{4,8},{5,9},{6,10},{7,11},{8,4},{9,5},... | collective-permute-start | bytes 208904 | tf_op jit(solution)/shard_map/ppermute | solution.py:287
  7.1 5.1 %collective-permute-start.2 = (bf16[16,2176]{1,0:T(8,128)(2,1)S(1)}, bf16[16,2176]{1,0:T(8,128)(2,1)S(1)}, u32[]{:S(2)}, u32[]{:S(2)}) collective-permute-start(bf16[16,2176]{1,0:T(8,128)(2,1)S(1)} %prepare.1.refs_3_), channel_id=1, source_target_pairs={{0,4},{1,5},{2,6},{3,7},{4,0},{5,1},{6,2},{7,3},{8,12},{9,13},{10,... | collective-permute-start | bytes 208904 | tf_op jit(solution)/shard_map/ppermute | solution.py:287
  7.4 6.6 %collective-permute-start.3 = (bf16[16,2176]{1,0:T(8,128)(2,1)S(1)}, bf16[16,2176]{1,0:T(8,128)(2,1)S(1)}, u32[]{:S(2)}, u32[]{:S(2)}) collective-permute-start(bf16[16,2176]{1,0:T(8,128)(2,1)S(1)} %prepare.1.refs_3_), channel_id=1, source_target_pairs={{0,2},{1,3},{2,0},{3,1},{4,6},{5,7},{6,4},{7,5},{8,10},{9,11},{10,... | collective-permute-start | bytes 208904 | tf_op jit(solution)/shard_map/ppermute | solution.py:287
  12.2 5.9 %collective-permute-start.4 = (bf16[3,16,2176]{2,1,0:T(8,128)(2,1)S(1)}, bf16[3,16,2176]{2,1,0:T(8,128)(2,1)S(1)}, u32[]{:S(2)}, u32[]{:S(2)}) collective-permute-start(bf16[3,16,2176]{2,1,0:T(8,128)(2,1)S(1)} %stack.3.refs_2_), channel_id=1, source_target_pairs={{0,2},{1,3},{2,0},{3,1},{4,6},{5,7},{6,4},{7,5},{8,10},{9,11},{10,... | collective-permute-start | bytes 626696 | tf_op jit(solution)/shard_map/ppermute | solution.py:287
  14.0 4.4 %collective-permute-start.5 = (bf16[5,16,2176]{2,1,0:T(8,128)(2,1)S(1)}, bf16[5,16,2176]{2,1,0:T(8,128)(2,1)S(1)}, u32[]{:S(2)}, u32[]{:S(2)}) collective-permute-start(bf16[5,16,2176]{2,1,0:T(8,128)(2,1)S(1)} %stack.2.refs_0_), channel_id=1, source_target_pairs={{0,1},{1,0},{2,3},{3,2},{4,5},{5,4},{6,7},{7,6},{8,9},{9,8},{10,11... | collective-permute-start | bytes 1044488 | tf_op jit(solution)/shard_map/ppermute | solution.py:287
  18.1 1.5 %collective-permute-start.6 = (bf16[3,16,2176]{2,1,0:T(8,128)(2,1)S(1)}, bf16[3,16,2176]{2,1,0:T(8,128)(2,1)S(1)}, u32[]{:S(2)}, u32[]{:S(2)}) collective-permute-start(bf16[3,16,2176]{2,1,0:T(8,128)(2,1)S(1)} %relay.1), channel_id=1, source_target_pairs={{0,1},{1,0},{2,3},{3,2},{4,5},{5,4},{6,7},{7,6},{8,9},{9,8},{10,11... | collective-permute-start | bytes 626696 | tf_op jit(solution)/shard_map/ppermute | solution.py:287
  21.1 2.2 %collective-permute-start.7 = (bf16[4,16,2048]{2,1,0:T(8,128)(2,1)S(1)}, bf16[4,16,2048]{2,1,0:T(8,128)(2,1)S(1)}, u32[]{:S(2)}, u32[]{:S(2)}) collective-permute-start(bf16[4,16,2048]{2,1,0:T(8,128)(2,1)S(1)} %get-tuple-element.19), channel_id=1, source_target_pairs={{0,1},{1,0},{2,3},{3,2},{4,5},{5,4},{6,7},{7,6},{8,9},{9,8},{10,11... | collective-permute-start | bytes 786440 | tf_op jit(solution)/shard_map/ppermute | solution.py:287
  21.4 17.3 %copy-start = (bf16[16,2048]{1,0:T(8,128)(2,1)S(1)}, bf16[16,2048]{1,0:T(8,128)(2,1)}, u32[]{:S(2)}) copy-start(bf16[16,2048]{1,0:T(8,128)(2,1)} %residual_ref.1) | copy-start | bytes 196612
  23.0 2.1 %collective-permute-start.9 = (bf16[4,16,2048]{2,1,0:T(8,128)(2,1)S(1)}, bf16[4,16,2048]{2,1,0:T(8,128)(2,1)S(1)}, u32[]{:S(2)}, u32[]{:S(2)}) collective-permute-start(bf16[4,16,2048]{2,1,0:T(8,128)(2,1)S(1)} %get-tuple-element.25), channel_id=1, source_target_pairs={{0,1},{1,0},{2,3},{3,2},{4,5},{5,4},{6,7},{7,6},{8,9},{9,8},{10,11... | collective-permute-start | bytes 786440 | tf_op jit(solution)/shard_map/ppermute | solution.py:287
  23.4 5.7 %collective-permute-start.8 = (bf16[2,16,2048]{2,1,0:T(8,128)(2,1)S(1)}, bf16[2,16,2048]{2,1,0:T(8,128)(2,1)S(1)}, u32[]{:S(2)}, u32[]{:S(2)}) collective-permute-start(bf16[2,16,2048]{2,1,0:T(8,128)(2,1)S(1)} %get-tuple-element.21), channel_id=1, source_target_pairs={{0,2},{1,3},{2,0},{3,1},{4,6},{5,7},{6,4},{7,5},{8,10},{9,11},{10,... | collective-permute-start | bytes 393224 | tf_op jit(solution)/shard_map/ppermute | solution.py:287
  25.2 8.0 %collective-permute-start.10 = (bf16[2,16,2048]{2,1,0:T(8,128)(2,1)S(1)}, bf16[2,16,2048]{2,1,0:T(8,128)(2,1)S(1)}, u32[]{:S(2)}, u32[]{:S(2)}) collective-permute-start(bf16[2,16,2048]{2,1,0:T(8,128)(2,1)S(1)} %get-tuple-element.27), channel_id=1, source_target_pairs={{0,4},{1,5},{2,6},{3,7},{4,0},{5,1},{6,2},{7,3},{8,12},{9,13},{10,... | collective-permute-start | bytes 393224 | tf_op jit(solution)/shard_map/ppermute | solution.py:287
  29.1 8.8 %collective-permute-start.11 = (bf16[16,2048]{1,0:T(8,128)(2,1)S(1)}, bf16[16,2048]{1,0:T(8,128)(2,1)S(1)}, u32[]{:S(2)}, u32[]{:S(2)}) collective-permute-start(bf16[16,2048]{1,0:T(8,128)(2,1)S(1)} %get-tuple-element.23.refs_7_), channel_id=1, source_target_pairs={{0,12},{1,13},{2,14},{3,15},{4,8},{5,9},{6,10},{7,11},{8,4},{9,5},... | collective-permute-start | bytes 196616 | tf_op jit(solution)/shard_map/ppermute | solution.py:287
  32.7 6.1 %collective-permute-start.12 = (bf16[16,2048]{1,0:T(8,128)(2,1)S(1)}, bf16[16,2048]{1,0:T(8,128)(2,1)S(1)}, u32[]{:S(2)}, u32[]{:S(2)}) collective-permute-start(bf16[16,2048]{1,0:T(8,128)(2,1)S(1)} %get-tuple-element.22.refs_6_), channel_id=1, source_target_pairs={{0,8},{1,9},{2,10},{3,11},{4,12},{5,13},{6,14},{7,15},{8,0},{9,1},... | collective-permute-start | bytes 196616 | tf_op jit(solution)/shard_map/ppermute | solution.py:287
  33.2 5.6 %collective-permute-start.13 = (bf16[16,2048]{1,0:T(8,128)(2,1)S(1)}, bf16[16,2048]{1,0:T(8,128)(2,1)S(1)}, u32[]{:S(2)}, u32[]{:S(2)}) collective-permute-start(bf16[16,2048]{1,0:T(8,128)(2,1)S(1)} %get-tuple-element.29), channel_id=1, source_target_pairs={{0,2},{1,3},{2,0},{3,1},{4,6},{5,7},{6,4},{7,5},{8,10},{9,11},{10,... | collective-permute-start | bytes 196616 | tf_op jit(solution)/shard_map/ppermute | solution.py:287

commit v3 on v2

--- a/solution.py
+++ b/solution.py
@@ -299,9 +299,10 @@
         "prepare",
         (residual, norm_gain.reshape(1, -1), routes.T, route_weights.T),
     )
-    third, second, first = (swap(packed, d * line) for d in (3, 2, 1))
+    second, third, first = (swap(packed, d * line) for d in (2, 3, 1))
     across = swap(packed, side)
-    along = stack((second, third, first))
+    attended = attend(*attention, (packed,))
+    along = stack((second, third, first), (stay(attended),))
     along_side = swap(along, side)
     near = stack((second, third, first, packed, across))
     near_far = swap(near, core)
@@ -334,8 +335,7 @@
         "square_sum",
         (early_keep, swap(early_send, side)),
     )
-    attended = attend(*attention, tuple(early_sums))
-    back = [swap(early_sums[1], 3 * line), swap(early_sums[0], 2 * line)]
+    back = [swap(early_sums[0], 2 * line), swap(early_sums[1], 3 * line)]
     late_outs = ffn([(3, 5), (2, 3)], [(2, 3)], early_outs[:1])
     late_keep, late_send = pair_sum(*late_outs)
     own, across_sum = in_vmem(

time: 39.6 us -> 40 us (1.010)
  transfers between devices with their start and end apart: 14 -> 14, of which waited for: 7 -> 6; matrix products, arithmetic and copies ran while one was open for 0% -> 0% of each run, Pallas kernels for 22% -> 22%
where the time goes in v3:
time: 40 us; the launch traced here: 39.8 us
  starting transfers between devices  19.4 us (48%)
  Pallas kernels  11.9 us (30%)
  waiting for transfers between devices  7.77 us (19%)
  between operations  0.73 us (2%)
    ppermute x14, starting transfers between devices, swap(): return lax.ppermute(value, 'ep', [(i, i ^ bits) for i in range(devices)])  19.4 us
    ppermute x14, waiting for transfers between devices, swap(): return lax.ppermute(value, 'ep', [(i, i ^ bits) for i in range(devices)])  7.77 us
    pallas_call x2, Pallas kernels, from_hbm(): pl.pallas_call(kernel, out_shape=out_shape, in_specs=[pl.BlockSpec(memory...  4.24 us
    pallas_call x10, Pallas kernels, in_vmem(): pl.pallas_call(kernel, out_shape=out_shape, in_specs=[HERE] * len(arrays)...  3.95 us
    pallas_call x1, Pallas kernels, hold(): pl.pallas_call(functools.partial(hold_kernel, len(flat), pieces), out_sha...  3.75 us
  transfers between devices with their start and end apart: 14, of which 6 were waited for; matrix products, arithmetic and copies ran while one was open for 0% of the time, Pallas kernels for 22%

profile of v3, /device:TPU:0, one launch (start us, length us, event | category | flops | bytes accessed | tf_op | source)
XLA Modules:
  0.0 39.8 jit_solution(14327969545268320787)
XLA Ops:
  0.6 1.0 %prepare.1.refs_6_.refs_3_ = bf16[16,2176]{1,0:T(8,128)(2,1)S(1)} custom-call(bf16[16,2048]{1,0:T(8,128)(2,1)} %residual_ref.1, f32[1,2048]{1,0:T(1,128)} %bitcast.13, s32[8,16]{1,0:T(8,128)} %bitcast.14, f32[8,16]{1,0:T(8,128)} %bitcast.15), custom_call_target="tpu_custom_call" | custom-call | tf_op jit(solution)/shard_map/prepare/pallas_call | solution.py:77
  1.7 4.1 %collective-permute-start = (bf16[16,2176]{1,0:T(8,128)(2,1)S(1)}, bf16[16,2176]{1,0:T(8,128)(2,1)S(1)}, u32[]{:S(2)}, u32[]{:S(2)}) collective-permute-start(bf16[16,2176]{1,0:T(8,128)(2,1)S(1)} %prepare.1.refs_6_.refs_3_), channel_id=1, source_target_pairs={{0,8},{1,9},{2,10},{3,11},{4,12},{5,13},{6,14},{7,15},{8,0},{9,1},... | collective-permute-start | bytes 208904 | tf_op jit(solution)/shard_map/ppermute | solution.py:287
  5.8 1.3 %collective-permute-start.1 = (bf16[16,2176]{1,0:T(8,128)(2,1)S(1)}, bf16[16,2176]{1,0:T(8,128)(2,1)S(1)}, u32[]{:S(2)}, u32[]{:S(2)}) collective-permute-start(bf16[16,2176]{1,0:T(8,128)(2,1)S(1)} %prepare.1.refs_6_.refs_3_), channel_id=1, source_target_pairs={{0,12},{1,13},{2,14},{3,15},{4,8},{5,9},{6,10},{7,11},{8,4},{9,5},... | collective-permute-start | bytes 208904 | tf_op jit(solution)/shard_map/ppermute | solution.py:287
  7.1 0.2 collective-permute-start.2
  7.4 1.5 %collective-permute-start.3 = (bf16[16,2176]{1,0:T(8,128)(2,1)S(1)}, bf16[16,2176]{1,0:T(8,128)(2,1)S(1)}, u32[]{:S(2)}, u32[]{:S(2)}) collective-permute-start(bf16[16,2176]{1,0:T(8,128)(2,1)S(1)} %prepare.1.refs_6_.refs_3_), channel_id=1, source_target_pairs={{0,2},{1,3},{2,0},{3,1},{4,6},{5,7},{6,4},{7,5},{8,10},{9,11},{10,... | collective-permute-start | bytes 208904 | tf_op jit(solution)/shard_map/ppermute | solution.py:287
  8.8 3.2 %attend.1.refs_3_ = bf16[4,32,128]{2,1,0:T(8,128)(2,1)} custom-call(s32[4]{0:T(128)} %refs_0_.3, bf16[4,32,128]{2,1,0:T(8,128)(2,1)} %refs_1_.1, bf16[4,256,128]{2,1,0:T(8,128)(2,1)} %bitcast.11, bf16[4,256,128]{2,1,0:T(8,128)(2,1)} %bitcast.12, bf16[8,128]{1,0:T(8,128)(2,1)} %bitcast.16, bf16[8,128]{1,0:T(8,128)(2,1)} %bitcast.17, ...), custom_call_target="tpu_custom_call" | custom-call | bytes 4194304 | tf_op jit(solution)/shard_map/attend/pallas_call | solution.py:77
  12.1 0.0 collective-permute-done.refs_0_
  12.1 0.0 collective-permute-done.1.refs_1_
  12.1 0.1 collective-permute-done.2.refs_2_
  12.2 1.7 %collective-permute-start.4 = (bf16[3,16,2176]{2,1,0:T(8,128)(2,1)S(1)}, bf16[3,16,2176]{2,1,0:T(8,128)(2,1)S(1)}, u32[]{:S(2)}, u32[]{:S(2)}) collective-permute-start(bf16[3,16,2176]{2,1,0:T(8,128)(2,1)S(1)} %stack.3.refs_2_), channel_id=1, source_target_pairs={{0,2},{1,3},{2,0},{3,1},{4,6},{5,7},{6,4},{7,5},{8,10},{9,11},{10,... | collective-permute-start | bytes 626696 | tf_op jit(solution)/shard_map/ppermute | solution.py:287
  13.9 0.0 collective-permute-done.3.refs_4_
  14.0 0.1 collective-permute-start.5
  14.0 3.8 %hold.1 = (bf16[4096,768]{1,0:T(8,128)(2,1)S(1)}, bf16[768,2048]{1,0:T(8,128)(2,1)S(1)}) custom-call(bf16[4096,768]{1,0:T(8,128)(2,1)} %bitcast.9, bf16[768,2048]{1,0:T(8,128)(2,1)} %bitcast.10, bf16[3,16,2176]{2,1,0:T(8,128)(2,1)S(1)} %stack.3.refs_2_), custom_call_target="tpu_custom_call" | custom-call | bytes 9437184 | tf_op jit(solution)/shard_map/hold/pallas_call | solution.py:170
  17.8 0.4 %collective-permute-done.4.in_ref.refs_1_ = bf16[3,16,2176]{2,1,0:T(8,128)(2,1)S(1)} collective-permute-done((bf16[3,16,2176]{2,1,0:T(8,128)(2,1)S(1)}, bf16[3,16,2176]{2,1,0:T(8,128)(2,1)S(1)}, u32[]{:S(2)}, u32[]{:S(2)}) %collective-permute-start.4) | collective-permute-done | bytes 208928 | tf_op jit(solution)/shard_map/ppermute | solution.py:287
  18.3 0.1 collective-permute-start.6
  18.4 0.0 collective-permute-done.5.refs_2_
  18.4 1.4 %collective-permute-done.6.refs_3_ = bf16[3,16,2176]{2,1,0:T(8,128)(2,1)S(1)} collective-permute-done((bf16[3,16,2176]{2,1,0:T(8,128)(2,1)S(1)}, bf16[3,16,2176]{2,1,0:T(8,128)(2,1)S(1)}, u32[]{:S(2)}, u32[]{:S(2)}) %collective-permute-start.6) | collective-permute-done | bytes 208928 | tf_op jit(solution)/shard_map/ppermute | solution.py:287
  19.8 1.5 %ffn.2 = (bf16[4,16,2048]{2,1,0:T(8,128)(2,1)S(1)}, bf16[4,16,2048]{2,1,0:T(8,128)(2,1)S(1)}) custom-call(bf16[5,16,2176]{2,1,0:T(8,128)(2,1)S(1)} %stack.2.refs_0_, bf16[3,16,2176]{2,1,0:T(8,128)(2,1)S(1)} %collective-permute-done.4.in_ref.refs_1_, bf16[5,16,2176]{2,1,0:T(8,128)(2,1)S(1)} %collective-permute-done.5.refs_2_, ...), custom_call_target="tpu_custom_call" | custom-call | flops 1207959552 | bytes 6291456 | tf_op jit(solution)/shard_map/ffn/pallas_call | solution.py:267
  21.3 0.2 collective-permute-start.9
  21.5 0.0 copy-start
  21.5 1.5 %ffn.3 = (bf16[4,16,2048]{2,1,0:T(8,128)(2,1)S(1)}, bf16[4,16,2048]{2,1,0:T(8,128)(2,1)S(1)}) custom-call(bf16[5,16,2176]{2,1,0:T(8,128)(2,1)S(1)} %stack.2.refs_0_, bf16[3,16,2176]{2,1,0:T(8,128)(2,1)S(1)} %collective-permute-done.4.in_ref.refs_1_, bf16[5,16,2176]{2,1,0:T(8,128)(2,1)S(1)} %collective-permute-done.5.refs_2_, ...), custom_call_target="tpu_custom_call" | custom-call | flops 1207959552 | bytes 6291456 | tf_op jit(solution)/shard_map/ffn/pallas_call | solution.py:267
  23.1 0.4 %collective-permute-start.7 = (bf16[4,16,2048]{2,1,0:T(8,128)(2,1)S(1)}, bf16[4,16,2048]{2,1,0:T(8,128)(2,1)S(1)}, u32[]{:S(2)}, u32[]{:S(2)}) collective-permute-start(bf16[4,16,2048]{2,1,0:T(8,128)(2,1)S(1)} %get-tuple-element.20), channel_id=1, source_target_pairs={{0,1},{1,0},{2,3},{3,2},{4,5},{5,4},{6,7},{7,6},{8,9},{9,8},{10,11... | collective-permute-start | bytes 786440 | tf_op jit(solution)/shard_map/ppermute | solution.py:287
  23.5 0.0 collective-permute-done.9.other_ref
  23.5 0.1 pair_sum.3
  23.5 1.6 %collective-permute-start.10 = (bf16[2,16,2048]{2,1,0:T(8,128)(2,1)S(1)}, bf16[2,16,2048]{2,1,0:T(8,128)(2,1)S(1)}, u32[]{:S(2)}, u32[]{:S(2)}) collective-permute-start(bf16[2,16,2048]{2,1,0:T(8,128)(2,1)S(1)} %get-tuple-element.26), channel_id=1, source_target_pairs={{0,2},{1,3},{2,0},{3,1},{4,6},{5,7},{6,4},{7,5},{8,10},{9,11},{10,... | collective-permute-start | bytes 393224 | tf_op jit(solution)/shard_map/ppermute | solution.py:287
  25.1 0.0 collective-permute-done.7.other_ref
  25.1 0.1 pair_sum.2
  25.2 2.1 %collective-permute-start.8 = (bf16[2,16,2048]{2,1,0:T(8,128)(2,1)S(1)}, bf16[2,16,2048]{2,1,0:T(8,128)(2,1)S(1)}, u32[]{:S(2)}, u32[]{:S(2)}) collective-permute-start(bf16[2,16,2048]{2,1,0:T(8,128)(2,1)S(1)} %get-tuple-element.22), channel_id=1, source_target_pairs={{0,4},{1,5},{2,6},{3,7},{4,0},{5,1},{6,2},{7,3},{8,12},{9,13},{10,... | collective-permute-start | bytes 393224 | tf_op jit(solution)/shard_map/ppermute | solution.py:287
  27.3 1.9 %collective-permute-done.10.other_ref = bf16[2,16,2048]{2,1,0:T(8,128)(2,1)S(1)} collective-permute-done((bf16[2,16,2048]{2,1,0:T(8,128)(2,1)S(1)}, bf16[2,16,2048]{2,1,0:T(8,128)(2,1)S(1)}, u32[]{:S(2)}, u32[]{:S(2)}) %collective-permute-start.10) | collective-permute-done | bytes 131104 | tf_op jit(solution)/shard_map/ppermute | solution.py:287
  29.2 3.9 %collective-permute-start.11 = (bf16[16,2048]{1,0:T(8,128)(2,1)S(1)}, bf16[16,2048]{1,0:T(8,128)(2,1)S(1)}, u32[]{:S(2)}, u32[]{:S(2)}) collective-permute-start(bf16[16,2048]{1,0:T(8,128)(2,1)S(1)} %get-tuple-element.27), channel_id=1, source_target_pairs={{0,8},{1,9},{2,10},{3,11},{4,12},{5,13},{6,14},{7,15},{8,0},{9,1},... | collective-permute-start | bytes 196616 | tf_op jit(solution)/shard_map/ppermute | solution.py:287
  33.1 0.5 %collective-permute-start.12 = (bf16[16,2048]{1,0:T(8,128)(2,1)S(1)}, bf16[16,2048]{1,0:T(8,128)(2,1)S(1)}, u32[]{:S(2)}, u32[]{:S(2)}) collective-permute-start(bf16[16,2048]{1,0:T(8,128)(2,1)S(1)} %get-tuple-element.28), channel_id=1, source_target_pairs={{0,12},{1,13},{2,14},{3,15},{4,8},{5,9},{6,10},{7,11},{8,4},{9,5},... | collective-permute-start | bytes 196616 | tf_op jit(solution)/shard_map/ppermute | solution.py:287
  33.5 0.0 collective-permute-done.8.other_ref
  33.6 1.7 %collective-permute-start.13 = (bf16[16,2048]{1,0:T(8,128)(2,1)S(1)}, bf16[16,2048]{1,0:T(8,128)(2,1)S(1)}, u32[]{:S(2)}, u32[]{:S(2)}) collective-permute-start(bf16[16,2048]{1,0:T(8,128)(2,1)S(1)} %get-tuple-element.29), channel_id=1, source_target_pairs={{0,2},{1,3},{2,0},{3,1},{4,6},{5,7},{6,4},{7,5},{8,10},{9,11},{10,... | collective-permute-start | bytes 196616 | tf_op jit(solution)/shard_map/ppermute | solution.py:287
  35.2 2.2 %collective-permute-done.11.refs_1_ = bf16[16,2048]{1,0:T(8,128)(2,1)S(1)} collective-permute-done((bf16[16,2048]{1,0:T(8,128)(2,1)S(1)}, bf16[16,2048]{1,0:T(8,128)(2,1)S(1)}, u32[]{:S(2)}, u32[]{:S(2)}) %collective-permute-start.11) | collective-permute-done | bytes 65568 | tf_op jit(solution)/shard_map/ppermute | solution.py:287
  37.4 1.7 %collective-permute-done.12.refs_2_ = bf16[16,2048]{1,0:T(8,128)(2,1)S(1)} collective-permute-done((bf16[16,2048]{1,0:T(8,128)(2,1)S(1)}, bf16[16,2048]{1,0:T(8,128)(2,1)S(1)}, u32[]{:S(2)}, u32[]{:S(2)}) %collective-permute-start.12) | collective-permute-done | bytes 65568 | tf_op jit(solution)/shard_map/ppermute | solution.py:287
  39.1 0.0 collective-permute-done.13.refs_3_
  39.1 0.0 copy-done
  39.1 0.7 %total.1 = bf16[16,2048]{1,0:T(8,128)(2,1)} custom-call(bf16[16,2048]{1,0:T(8,128)(2,1)S(1)} %copy-done, f32[16,2048]{1,0:T(8,128)S(1)} %get-tuple-element.23.refs_0_, bf16[16,2048]{1,0:T(8,128)(2,1)S(1)} %collective-permute-done.11.refs_1_, bf16[16,2048]{1,0:T(8,128)(2,1)S(1)} %collective-permute-done.12.refs_2_, ...), custom_call_target="tpu_custom_call" | custom-call | tf_op jit(solution)/shard_map/total/pallas_call | solution.py:267
  (5 shorter events, 0.1 us)
Async XLA Ops:
  1.7 10.4 %collective-permute-start = (bf16[16,2176]{1,0:T(8,128)(2,1)S(1)}, bf16[16,2176]{1,0:T(8,128)(2,1)S(1)}, u32[]{:S(2)}, u32[]{:S(2)}) collective-permute-start(bf16[16,2176]{1,0:T(8,128)(2,1)S(1)} %prepare.1.refs_6_.refs_3_), channel_id=1, source_target_pairs={{0,8},{1,9},{2,10},{3,11},{4,12},{5,13},{6,14},{7,15},{8,0},{9,1},... | collective-permute-start | bytes 208904 | tf_op jit(solution)/shard_map/ppermute | solution.py:287
  5.8 6.3 %collective-permute-start.1 = (bf16[16,2176]{1,0:T(8,128)(2,1)S(1)}, bf16[16,2176]{1,0:T(8,128)(2,1)S(1)}, u32[]{:S(2)}, u32[]{:S(2)}) collective-permute-start(bf16[16,2176]{1,0:T(8,128)(2,1)S(1)} %prepare.1.refs_6_.refs_3_), channel_id=1, source_target_pairs={{0,12},{1,13},{2,14},{3,15},{4,8},{5,9},{6,10},{7,11},{8,4},{9,5},... | collective-permute-start | bytes 208904 | tf_op jit(solution)/shard_map/ppermute | solution.py:287
  7.1 5.1 %collective-permute-start.2 = (bf16[16,2176]{1,0:T(8,128)(2,1)S(1)}, bf16[16,2176]{1,0:T(8,128)(2,1)S(1)}, u32[]{:S(2)}, u32[]{:S(2)}) collective-permute-start(bf16[16,2176]{1,0:T(8,128)(2,1)S(1)} %prepare.1.refs_6_.refs_3_), channel_id=1, source_target_pairs={{0,4},{1,5},{2,6},{3,7},{4,0},{5,1},{6,2},{7,3},{8,12},{9,13},{10,... | collective-permute-start | bytes 208904 | tf_op jit(solution)/shard_map/ppermute | solution.py:287
  7.4 6.6 %collective-permute-start.3 = (bf16[16,2176]{1,0:T(8,128)(2,1)S(1)}, bf16[16,2176]{1,0:T(8,128)(2,1)S(1)}, u32[]{:S(2)}, u32[]{:S(2)}) collective-permute-start(bf16[16,2176]{1,0:T(8,128)(2,1)S(1)} %prepare.1.refs_6_.refs_3_), channel_id=1, source_target_pairs={{0,2},{1,3},{2,0},{3,1},{4,6},{5,7},{6,4},{7,5},{8,10},{9,11},{10,... | collective-permute-start | bytes 208904 | tf_op jit(solution)/shard_map/ppermute | solution.py:287
  12.2 6.0 %collective-permute-start.4 = (bf16[3,16,2176]{2,1,0:T(8,128)(2,1)S(1)}, bf16[3,16,2176]{2,1,0:T(8,128)(2,1)S(1)}, u32[]{:S(2)}, u32[]{:S(2)}) collective-permute-start(bf16[3,16,2176]{2,1,0:T(8,128)(2,1)S(1)} %stack.3.refs_2_), channel_id=1, source_target_pairs={{0,2},{1,3},{2,0},{3,1},{4,6},{5,7},{6,4},{7,5},{8,10},{9,11},{10,... | collective-permute-start | bytes 626696 | tf_op jit(solution)/shard_map/ppermute | solution.py:287
  14.0 4.4 %collective-permute-start.5 = (bf16[5,16,2176]{2,1,0:T(8,128)(2,1)S(1)}, bf16[5,16,2176]{2,1,0:T(8,128)(2,1)S(1)}, u32[]{:S(2)}, u32[]{:S(2)}) collective-permute-start(bf16[5,16,2176]{2,1,0:T(8,128)(2,1)S(1)} %stack.2.refs_0_), channel_id=1, source_target_pairs={{0,1},{1,0},{2,3},{3,2},{4,5},{5,4},{6,7},{7,6},{8,9},{9,8},{10,11... | collective-permute-start | bytes 1044488 | tf_op jit(solution)/shard_map/ppermute | solution.py:287
  18.3 1.5 %collective-permute-start.6 = (bf16[3,16,2176]{2,1,0:T(8,128)(2,1)S(1)}, bf16[3,16,2176]{2,1,0:T(8,128)(2,1)S(1)}, u32[]{:S(2)}, u32[]{:S(2)}) collective-permute-start(bf16[3,16,2176]{2,1,0:T(8,128)(2,1)S(1)} %relay.1), channel_id=1, source_target_pairs={{0,1},{1,0},{2,3},{3,2},{4,5},{5,4},{6,7},{7,6},{8,9},{9,8},{10,11... | collective-permute-start | bytes 626696 | tf_op jit(solution)/shard_map/ppermute | solution.py:287
  21.3 2.2 %collective-permute-start.9 = (bf16[4,16,2048]{2,1,0:T(8,128)(2,1)S(1)}, bf16[4,16,2048]{2,1,0:T(8,128)(2,1)S(1)}, u32[]{:S(2)}, u32[]{:S(2)}) collective-permute-start(bf16[4,16,2048]{2,1,0:T(8,128)(2,1)S(1)} %get-tuple-element.24), channel_id=1, source_target_pairs={{0,1},{1,0},{2,3},{3,2},{4,5},{5,4},{6,7},{7,6},{8,9},{9,8},{10,11... | collective-permute-start | bytes 786440 | tf_op jit(solution)/shard_map/ppermute | solution.py:287
  21.5 17.6 %copy-start = (bf16[16,2048]{1,0:T(8,128)(2,1)S(1)}, bf16[16,2048]{1,0:T(8,128)(2,1)}, u32[]{:S(2)}) copy-start(bf16[16,2048]{1,0:T(8,128)(2,1)} %residual_ref.1) | copy-start | bytes 196612
  23.1 2.0 %collective-permute-start.7 = (bf16[4,16,2048]{2,1,0:T(8,128)(2,1)S(1)}, bf16[4,16,2048]{2,1,0:T(8,128)(2,1)S(1)}, u32[]{:S(2)}, u32[]{:S(2)}) collective-permute-start(bf16[4,16,2048]{2,1,0:T(8,128)(2,1)S(1)} %get-tuple-element.20), channel_id=1, source_target_pairs={{0,1},{1,0},{2,3},{3,2},{4,5},{5,4},{6,7},{7,6},{8,9},{9,8},{10,11... | collective-permute-start | bytes 786440 | tf_op jit(solution)/shard_map/ppermute | solution.py:287
  23.5 5.6 %collective-permute-start.10 = (bf16[2,16,2048]{2,1,0:T(8,128)(2,1)S(1)}, bf16[2,16,2048]{2,1,0:T(8,128)(2,1)S(1)}, u32[]{:S(2)}, u32[]{:S(2)}) collective-permute-start(bf16[2,16,2048]{2,1,0:T(8,128)(2,1)S(1)} %get-tuple-element.26), channel_id=1, source_target_pairs={{0,2},{1,3},{2,0},{3,1},{4,6},{5,7},{6,4},{7,5},{8,10},{9,11},{10,... | collective-permute-start | bytes 393224 | tf_op jit(solution)/shard_map/ppermute | solution.py:287
  25.2 8.4 %collective-permute-start.8 = (bf16[2,16,2048]{2,1,0:T(8,128)(2,1)S(1)}, bf16[2,16,2048]{2,1,0:T(8,128)(2,1)S(1)}, u32[]{:S(2)}, u32[]{:S(2)}) collective-permute-start(bf16[2,16,2048]{2,1,0:T(8,128)(2,1)S(1)} %get-tuple-element.22), channel_id=1, source_target_pairs={{0,4},{1,5},{2,6},{3,7},{4,0},{5,1},{6,2},{7,3},{8,12},{9,13},{10,... | collective-permute-start | bytes 393224 | tf_op jit(solution)/shard_map/ppermute | solution.py:287
  29.2 8.2 %collective-permute-start.11 = (bf16[16,2048]{1,0:T(8,128)(2,1)S(1)}, bf16[16,2048]{1,0:T(8,128)(2,1)S(1)}, u32[]{:S(2)}, u32[]{:S(2)}) collective-permute-start(bf16[16,2048]{1,0:T(8,128)(2,1)S(1)} %get-tuple-element.27), channel_id=1, source_target_pairs={{0,8},{1,9},{2,10},{3,11},{4,12},{5,13},{6,14},{7,15},{8,0},{9,1},... | collective-permute-start | bytes 196616 | tf_op jit(solution)/shard_map/ppermute | solution.py:287
  33.1 6.1 %collective-permute-start.12 = (bf16[16,2048]{1,0:T(8,128)(2,1)S(1)}, bf16[16,2048]{1,0:T(8,128)(2,1)S(1)}, u32[]{:S(2)}, u32[]{:S(2)}) collective-permute-start(bf16[16,2048]{1,0:T(8,128)(2,1)S(1)} %get-tuple-element.28), channel_id=1, source_target_pairs={{0,12},{1,13},{2,14},{3,15},{4,8},{5,9},{6,10},{7,11},{8,4},{9,5},... | collective-permute-start | bytes 196616 | tf_op jit(solution)/shard_map/ppermute | solution.py:287
  33.6 5.6 %collective-permute-start.13 = (bf16[16,2048]{1,0:T(8,128)(2,1)S(1)}, bf16[16,2048]{1,0:T(8,128)(2,1)S(1)}, u32[]{:S(2)}, u32[]{:S(2)}) collective-permute-start(bf16[16,2048]{1,0:T(8,128)(2,1)S(1)} %get-tuple-element.29), channel_id=1, source_target_pairs={{0,2},{1,3},{2,0},{3,1},{4,6},{5,7},{6,4},{7,5},{8,10},{9,11},{10,... | collective-permute-start | bytes 196616 | tf_op jit(solution)/shard_map/ppermute | solution.py:287

commit v4 on v2

--- a/solution.py
+++ b/solution.py
@@ -243,17 +243,13 @@
 
 
 def pair_kernel(own_ref, other_ref, *refs):
-    keep_ref, send_ref = refs[-2:]
-    half = keep_ref.shape[0]
-    keep_ref[...] = own_ref[:half].astype(jnp.float32) + other_ref[:half].astype(jnp.float32)
-    send = own_ref[half:].astype(jnp.float32) + other_ref[half:].astype(jnp.float32)
-    send_ref[...] = send.astype(jnp.bfloat16)
-
-
-def square_kernel(own_ref, other_ref, *out_refs):
-    for i, out_ref in enumerate(out_refs):
-        total = own_ref[i] + other_ref[i].astype(jnp.float32)
+    for i, out_ref in enumerate(refs[-own_ref.shape[0] :]):
+        total = own_ref[i].astype(jnp.float32) + other_ref[i].astype(jnp.float32)
         out_ref[...] = total.astype(out_ref.dtype)
+
+
+def add_kernel(own_ref, other_ref, out_ref):
+    out_ref[...] = (own_ref[...] + other_ref[...].astype(jnp.float32)).astype(out_ref.dtype)
 
 
 def total_kernel(residual_ref, *refs):
@@ -322,33 +318,35 @@
             cost_estimate=cost(8 * row_count * 2 * sum(h.size for h in held), 2 * held[0].size),
         )
 
-    def pair_sum(near_out, far_out, after=()):
-        shapes = [vmem((2,) + one, jnp.float32), vmem((2,) + one, jnp.bfloat16)]
+    def pair_sum(shapes, near_out, far_out, after=()):
         return in_vmem(pair_kernel, shapes, "pair_sum", (near_out, swap(far_out, core)), after)
 
     early_outs = ffn([(0, 2)], [(0, 2)])
-    early_keep, early_send = pair_sum(*early_outs)
-    early_sums = in_vmem(
-        square_kernel,
-        [vmem(one, jnp.bfloat16)] * 2,
-        "square_sum",
-        (early_keep, swap(early_send, side)),
-    )
-    attended = attend(*attention, tuple(early_sums))
-    back = [swap(early_sums[1], 3 * line), swap(early_sums[0], 2 * line)]
+    send = vmem(one, jnp.bfloat16)
+    second_sum, third_keep, diagonal_sum, third_send = pair_sum(
+        [send, vmem(one, jnp.float32), send, send], *early_outs
+    )
+    third_sum = in_vmem(add_kernel, send, "side_sum", (third_keep, swap(third_send, side)))
+    back = [
+        swap(second_sum, 2 * line),
+        swap(diagonal_sum, 2 * line + side),
+        swap(third_sum, 3 * line),
+    ]
+    attended = attend(*attention, (third_sum,))
     late_outs = ffn([(3, 5), (2, 3)], [(2, 3)], early_outs[:1])
-    late_keep, late_send = pair_sum(*late_outs)
-    own, across_sum = in_vmem(
-        square_kernel,
-        [vmem(one, jnp.float32), vmem(one, jnp.bfloat16)],
-        "line_sum",
-        (late_keep, swap(late_send, line)),
-    )
+    own, across_sum, first_sum, first_diagonal_sum = pair_sum(
+        [vmem(one, jnp.float32), send, send, send], *late_outs, (second_sum,)
+    )
+    back += [
+        swap(first_diagonal_sum, line + side),
+        swap(first_sum, line),
+        swap(across_sum, side),
+    ]
     moe_out = in_vmem(
         total_kernel,
         jax.ShapeDtypeStruct(one, jnp.bfloat16),
         "total",
-        (residual, own, *back, swap(across_sum, side)),
+        (residual, own, *back),
     )
     return attended, moe_out
 

time: 39.6 us -> 41.3 us (1.043)
  starting transfers between devices: 19.3 us -> 21.2 us
    ppermute x14 -> x16, starting transfers between devices: 19.3 us -> 21.2 us  [swap(): return lax.ppermute(value, 'ep', [(i, i ^ bits) for i in range(devices)])]
    ppermute x14 -> x16, waiting for transfers between devices: 7.49 us -> 7.16 us  [swap(): return lax.ppermute(value, 'ep', [(i, i ^ bits) for i in range(devices)])]
    pallas_call x10 -> x9, Pallas kernels: 3.95 us -> 3.93 us  [in_vmem(): pl.pallas_call(kernel, out_shape=out_shape, in_specs=[HERE] * len(arrays)...]
  transfers between devices with their start and end apart: 14 -> 16, of which waited for: 7 -> 7; matrix products, arithmetic and copies ran while one was open for 0% -> 0% of each run, Pallas kernels for 22% -> 21%
where the time goes in v4:
time: 41.3 us; the launch traced here: 41.1 us
  starting transfers between devices  21.2 us (51%)
  Pallas kernels  11.9 us (29%)
  waiting for transfers between devices  7.16 us (17%)
  between operations  0.75 us (2%)
    ppermute x16, starting transfers between devices, swap(): return lax.ppermute(value, 'ep', [(i, i ^ bits) for i in range(devices)])  21.2 us
    ppermute x16, waiting for transfers between devices, swap(): return lax.ppermute(value, 'ep', [(i, i ^ bits) for i in range(devices)])  7.16 us
    pallas_call x2, Pallas kernels, from_hbm(): pl.pallas_call(kernel, out_shape=out_shape, in_specs=[pl.BlockSpec(memory...  4.24 us
    pallas_call x9, Pallas kernels, in_vmem(): pl.pallas_call(kernel, out_shape=out_shape, in_specs=[HERE] * len(arrays)...  3.93 us
    pallas_call x1, Pallas kernels, hold(): pl.pallas_call(functools.partial(hold_kernel, len(flat), pieces), out_sha...  3.75 us
  transfers between devices with their start and end apart: 16, of which 7 were waited for; matrix products, arithmetic and copies ran while one was open for 0% of the time, Pallas kernels for 21%

profile of v4, /device:TPU:0, one launch (start us, length us, event | category | flops | bytes accessed | tf_op | source)
XLA Modules:
  0.0 41.1 jit_solution(3202804312362566064)
XLA Ops:
  0.6 1.0 %prepare.1.refs_3_ = bf16[16,2176]{1,0:T(8,128)(2,1)S(1)} custom-call(bf16[16,2048]{1,0:T(8,128)(2,1)} %residual_ref.1, f32[1,2048]{1,0:T(1,128)} %bitcast.13, s32[8,16]{1,0:T(8,128)} %bitcast.14, f32[8,16]{1,0:T(8,128)} %bitcast.15), custom_call_target="tpu_custom_call" | custom-call | tf_op jit(solution)/shard_map/prepare/pallas_call | solution.py:77
  1.7 4.1 %collective-permute-start = (bf16[16,2176]{1,0:T(8,128)(2,1)S(1)}, bf16[16,2176]{1,0:T(8,128)(2,1)S(1)}, u32[]{:S(2)}, u32[]{:S(2)}) collective-permute-start(bf16[16,2176]{1,0:T(8,128)(2,1)S(1)} %prepare.1.refs_3_), channel_id=1, source_target_pairs={{0,8},{1,9},{2,10},{3,11},{4,12},{5,13},{6,14},{7,15},{8,0},{9,1},... | collective-permute-start | bytes 208904 | tf_op jit(solution)/shard_map/ppermute | solution.py:283
  5.8 1.3 %collective-permute-start.1 = (bf16[16,2176]{1,0:T(8,128)(2,1)S(1)}, bf16[16,2176]{1,0:T(8,128)(2,1)S(1)}, u32[]{:S(2)}, u32[]{:S(2)}) collective-permute-start(bf16[16,2176]{1,0:T(8,128)(2,1)S(1)} %prepare.1.refs_3_), channel_id=1, source_target_pairs={{0,12},{1,13},{2,14},{3,15},{4,8},{5,9},{6,10},{7,11},{8,4},{9,5},... | collective-permute-start | bytes 208904 | tf_op jit(solution)/shard_map/ppermute | solution.py:283
  7.1 0.2 collective-permute-start.2
  7.4 1.5 %collective-permute-start.3 = (bf16[16,2176]{1,0:T(8,128)(2,1)S(1)}, bf16[16,2176]{1,0:T(8,128)(2,1)S(1)}, u32[]{:S(2)}, u32[]{:S(2)}) collective-permute-start(bf16[16,2176]{1,0:T(8,128)(2,1)S(1)} %prepare.1.refs_3_), channel_id=1, source_target_pairs={{0,2},{1,3},{2,0},{3,1},{4,6},{5,7},{6,4},{7,5},{8,10},{9,11},{10,... | collective-permute-start | bytes 208904 | tf_op jit(solution)/shard_map/ppermute | solution.py:283
  8.8 0.8 %collective-permute-done.refs_0_ = bf16[16,2176]{1,0:T(8,128)(2,1)S(1)} collective-permute-done((bf16[16,2176]{1,0:T(8,128)(2,1)S(1)}, bf16[16,2176]{1,0:T(8,128)(2,1)S(1)}, u32[]{:S(2)}, u32[]{:S(2)}) %collective-permute-start) | collective-permute-done | bytes 69664 | tf_op jit(solution)/shard_map/ppermute | solution.py:283
  9.7 2.5 %collective-permute-done.1.refs_1_ = bf16[16,2176]{1,0:T(8,128)(2,1)S(1)} collective-permute-done((bf16[16,2176]{1,0:T(8,128)(2,1)S(1)}, bf16[16,2176]{1,0:T(8,128)(2,1)S(1)}, u32[]{:S(2)}, u32[]{:S(2)}) %collective-permute-start.1) | collective-permute-done | bytes 69664 | tf_op jit(solution)/shard_map/ppermute | solution.py:283
  12.1 0.1 collective-permute-done.2.refs_2_
  12.2 1.7 %collective-permute-start.4 = (bf16[3,16,2176]{2,1,0:T(8,128)(2,1)S(1)}, bf16[3,16,2176]{2,1,0:T(8,128)(2,1)S(1)}, u32[]{:S(2)}, u32[]{:S(2)}) collective-permute-start(bf16[3,16,2176]{2,1,0:T(8,128)(2,1)S(1)} %stack.3.refs_2_), channel_id=1, source_target_pairs={{0,2},{1,3},{2,0},{3,1},{4,6},{5,7},{6,4},{7,5},{8,10},{9,11},{10,... | collective-permute-start | bytes 626696 | tf_op jit(solution)/shard_map/ppermute | solution.py:283
  13.9 0.0 collective-permute-done.3.refs_4_
  14.0 0.1 collective-permute-start.5
  14.0 3.8 %hold.1 = (bf16[4096,768]{1,0:T(8,128)(2,1)S(1)}, bf16[768,2048]{1,0:T(8,128)(2,1)S(1)}) custom-call(bf16[4096,768]{1,0:T(8,128)(2,1)} %bitcast.9, bf16[768,2048]{1,0:T(8,128)(2,1)} %bitcast.10, bf16[3,16,2176]{2,1,0:T(8,128)(2,1)S(1)} %stack.3.refs_2_), custom_call_target="tpu_custom_call" | custom-call | bytes 9437184 | tf_op jit(solution)/shard_map/hold/pallas_call | solution.py:170
  17.8 0.3 collective-permute-done.4.in_ref.refs_1_
  18.1 0.3 collective-permute-start.6
  18.4 0.0 collective-permute-done.5.refs_2_
  18.4 1.2 %collective-permute-done.6.refs_3_ = bf16[3,16,2176]{2,1,0:T(8,128)(2,1)S(1)} collective-permute-done((bf16[3,16,2176]{2,1,0:T(8,128)(2,1)S(1)}, bf16[3,16,2176]{2,1,0:T(8,128)(2,1)S(1)}, u32[]{:S(2)}, u32[]{:S(2)}) %collective-permute-start.6) | collective-permute-done | bytes 208928 | tf_op jit(solution)/shard_map/ppermute | solution.py:283
  19.6 1.5 %ffn.2 = (bf16[4,16,2048]{2,1,0:T(8,128)(2,1)S(1)}, bf16[4,16,2048]{2,1,0:T(8,128)(2,1)S(1)}) custom-call(bf16[5,16,2176]{2,1,0:T(8,128)(2,1)S(1)} %stack.2.refs_0_, bf16[3,16,2176]{2,1,0:T(8,128)(2,1)S(1)} %collective-permute-done.4.in_ref.refs_1_, bf16[5,16,2176]{2,1,0:T(8,128)(2,1)S(1)} %collective-permute-done.5.refs_2_, ...), custom_call_target="tpu_custom_call" | custom-call | flops 1207959552 | bytes 6291456 | tf_op jit(solution)/shard_map/ffn/pallas_call | solution.py:263
  21.1 0.3 collective-permute-start.7
  21.4 0.0 copy-start
  21.4 1.5 %ffn.3 = (bf16[4,16,2048]{2,1,0:T(8,128)(2,1)S(1)}, bf16[4,16,2048]{2,1,0:T(8,128)(2,1)S(1)}) custom-call(bf16[5,16,2176]{2,1,0:T(8,128)(2,1)S(1)} %stack.2.refs_0_, bf16[3,16,2176]{2,1,0:T(8,128)(2,1)S(1)} %collective-permute-done.4.in_ref.refs_1_, bf16[5,16,2176]{2,1,0:T(8,128)(2,1)S(1)} %collective-permute-done.5.refs_2_, ...), custom_call_target="tpu_custom_call" | custom-call | flops 1207959552 | bytes 6291456 | tf_op jit(solution)/shard_map/ffn/pallas_call | solution.py:263
  23.0 0.3 collective-permute-start.9
  23.3 0.0 collective-permute-done.7.other_ref
  23.3 0.1 pair_sum.2
  23.4 1.7 %collective-permute-start.8 = (bf16[16,2048]{1,0:T(8,128)(2,1)S(1)}, bf16[16,2048]{1,0:T(8,128)(2,1)S(1)}, u32[]{:S(2)}, u32[]{:S(2)}) collective-permute-start(bf16[16,2048]{1,0:T(8,128)(2,1)S(1)} %get-tuple-element.21), channel_id=1, source_target_pairs={{0,2},{1,3},{2,0},{3,1},{4,6},{5,7},{6,4},{7,5},{8,10},{9,11},{10,... | collective-permute-start | bytes 196616 | tf_op jit(solution)/shard_map/ppermute | solution.py:283
  25.1 3.8 %collective-permute-start.10 = (bf16[16,2048]{1,0:T(8,128)(2,1)S(1)}, bf16[16,2048]{1,0:T(8,128)(2,1)S(1)}, u32[]{:S(2)}, u32[]{:S(2)}) collective-permute-start(bf16[16,2048]{1,0:T(8,128)(2,1)S(1)} %get-tuple-element.24.refs_0_), channel_id=1, source_target_pairs={{0,8},{1,9},{2,10},{3,11},{4,12},{5,13},{6,14},{7,15},{8,0},{9,1},... | collective-permute-start | bytes 196616 | tf_op jit(solution)/shard_map/ppermute | solution.py:283
  28.9 0.0 collective-permute-start.11
  28.9 0.0 collective-permute-done.9.other_ref
  28.9 0.1 pair_sum.3
  29.0 2.1 %collective-permute-start.13 = (bf16[16,2048]{1,0:T(8,128)(2,1)S(1)}, bf16[16,2048]{1,0:T(8,128)(2,1)S(1)}, u32[]{:S(2)}, u32[]{:S(2)}) collective-permute-start(bf16[16,2048]{1,0:T(8,128)(2,1)S(1)} %get-tuple-element.27), channel_id=1, source_target_pairs={{0,6},{1,7},{2,4},{3,5},{4,2},{5,3},{6,0},{7,1},{8,14},{9,15},{10,... | collective-permute-start | bytes 196616 | tf_op jit(solution)/shard_map/ppermute | solution.py:283
  31.1 0.9 %collective-permute-start.14 = (bf16[16,2048]{1,0:T(8,128)(2,1)S(1)}, bf16[16,2048]{1,0:T(8,128)(2,1)S(1)}, u32[]{:S(2)}, u32[]{:S(2)}) collective-permute-start(bf16[16,2048]{1,0:T(8,128)(2,1)S(1)} %get-tuple-element.28), channel_id=1, source_target_pairs={{0,4},{1,5},{2,6},{3,7},{4,0},{5,1},{6,2},{7,3},{8,12},{9,13},{10,... | collective-permute-start | bytes 196616 | tf_op jit(solution)/shard_map/ppermute | solution.py:283
  32.0 0.0 collective-permute-done.8.other_ref
  32.0 0.6 %collective-permute-start.15 = (bf16[16,2048]{1,0:T(8,128)(2,1)S(1)}, bf16[16,2048]{1,0:T(8,128)(2,1)S(1)}, u32[]{:S(2)}, u32[]{:S(2)}) collective-permute-start(bf16[16,2048]{1,0:T(8,128)(2,1)S(1)} %get-tuple-element.29), channel_id=1, source_target_pairs={{0,2},{1,3},{2,0},{3,1},{4,6},{5,7},{6,4},{7,5},{8,10},{9,11},{10,... | collective-permute-start | bytes 196616 | tf_op jit(solution)/shard_map/ppermute | solution.py:283
  32.6 1.7 %collective-permute-done.10.refs_1_ = bf16[16,2048]{1,0:T(8,128)(2,1)S(1)} collective-permute-done((bf16[16,2048]{1,0:T(8,128)(2,1)S(1)}, bf16[16,2048]{1,0:T(8,128)(2,1)S(1)}, u32[]{:S(2)}, u32[]{:S(2)}) %collective-permute-start.10) | collective-permute-done | bytes 65568 | tf_op jit(solution)/shard_map/ppermute | solution.py:283
  34.3 2.2 %collective-permute-start.12 = (bf16[16,2048]{1,0:T(8,128)(2,1)S(1)}, bf16[16,2048]{1,0:T(8,128)(2,1)S(1)}, u32[]{:S(2)}, u32[]{:S(2)}) collective-permute-start(bf16[16,2048]{1,0:T(8,128)(2,1)S(1)} %side_sum.1.refs_6_), channel_id=1, source_target_pairs={{0,12},{1,13},{2,14},{3,15},{4,8},{5,9},{6,10},{7,11},{8,4},{9,5},... | collective-permute-start | bytes 196616 | tf_op jit(solution)/shard_map/ppermute | solution.py:283
  36.5 3.2 %attend.1 = bf16[4,32,128]{2,1,0:T(8,128)(2,1)} custom-call(s32[4]{0:T(128)} %refs_0_.3, bf16[4,32,128]{2,1,0:T(8,128)(2,1)} %refs_1_.1, bf16[4,256,128]{2,1,0:T(8,128)(2,1)} %bitcast.11, bf16[4,256,128]{2,1,0:T(8,128)(2,1)} %bitcast.12, bf16[8,128]{1,0:T(8,128)(2,1)} %bitcast.16, bf16[8,128]{1,0:T(8,128)(2,1)} %bitcast.17, bf16[16,2048]{1,0:T(8,128)(2,1)S(1)} %side_sum.1.refs_6_), custom_call_target="tpu_custom_call" | custom-call | bytes 4194304 | tf_op jit(solution)/shard_map/attend/pallas_call | solution.py:77
  39.7 0.0 collective-permute-done.11.refs_2_
  39.8 0.0 collective-permute-done.13.refs_4_
  39.8 0.0 collective-permute-done.14.refs_5_
  39.8 0.0 collective-permute-done.15.refs_6_
  39.8 0.6 %collective-permute-done.12.refs_3_ = bf16[16,2048]{1,0:T(8,128)(2,1)S(1)} collective-permute-done((bf16[16,2048]{1,0:T(8,128)(2,1)S(1)}, bf16[16,2048]{1,0:T(8,128)(2,1)S(1)}, u32[]{:S(2)}, u32[]{:S(2)}) %collective-permute-start.12) | collective-permute-done | bytes 65568 | tf_op jit(solution)/shard_map/ppermute | solution.py:283
  40.4 0.0 copy-done
  40.4 0.7 %total.1 = bf16[16,2048]{1,0:T(8,128)(2,1)} custom-call(bf16[16,2048]{1,0:T(8,128)(2,1)S(1)} %copy-done, f32[16,2048]{1,0:T(8,128)S(1)} %get-tuple-element.25.refs_0_, bf16[16,2048]{1,0:T(8,128)(2,1)S(1)} %collective-permute-done.10.refs_1_, bf16[16,2048]{1,0:T(8,128)(2,1)S(1)} %collective-permute-done.11.refs_2_, ...), custom_call_target="tpu_custom_call" | custom-call | tf_op jit(solution)/shard_map/total/pallas_call | solution.py:263
  (4 shorter events, 0.1 us)
Async XLA Ops:
  1.7 8.0 %collective-permute-start = (bf16[16,2176]{1,0:T(8,128)(2,1)S(1)}, bf16[16,2176]{1,0:T(8,128)(2,1)S(1)}, u32[]{:S(2)}, u32[]{:S(2)}) collective-permute-start(bf16[16,2176]{1,0:T(8,128)(2,1)S(1)} %prepare.1.refs_3_), channel_id=1, source_target_pairs={{0,8},{1,9},{2,10},{3,11},{4,12},{5,13},{6,14},{7,15},{8,0},{9,1},... | collective-permute-start | bytes 208904 | tf_op jit(solution)/shard_map/ppermute | solution.py:283
  5.8 6.3 %collective-permute-start.1 = (bf16[16,2176]{1,0:T(8,128)(2,1)S(1)}, bf16[16,2176]{1,0:T(8,128)(2,1)S(1)}, u32[]{:S(2)}, u32[]{:S(2)}) collective-permute-start(bf16[16,2176]{1,0:T(8,128)(2,1)S(1)} %prepare.1.refs_3_), channel_id=1, source_target_pairs={{0,12},{1,13},{2,14},{3,15},{4,8},{5,9},{6,10},{7,11},{8,4},{9,5},... | collective-permute-start | bytes 208904 | tf_op jit(solution)/shard_map/ppermute | solution.py:283
  7.1 5.1 %collective-permute-start.2 = (bf16[16,2176]{1,0:T(8,128)(2,1)S(1)}, bf16[16,2176]{1,0:T(8,128)(2,1)S(1)}, u32[]{:S(2)}, u32[]{:S(2)}) collective-permute-start(bf16[16,2176]{1,0:T(8,128)(2,1)S(1)} %prepare.1.refs_3_), channel_id=1, source_target_pairs={{0,4},{1,5},{2,6},{3,7},{4,0},{5,1},{6,2},{7,3},{8,12},{9,13},{10,... | collective-permute-start | bytes 208904 | tf_op jit(solution)/shard_map/ppermute | solution.py:283
  7.4 6.6 %collective-permute-start.3 = (bf16[16,2176]{1,0:T(8,128)(2,1)S(1)}, bf16[16,2176]{1,0:T(8,128)(2,1)S(1)}, u32[]{:S(2)}, u32[]{:S(2)}) collective-permute-start(bf16[16,2176]{1,0:T(8,128)(2,1)S(1)} %prepare.1.refs_3_), channel_id=1, source_target_pairs={{0,2},{1,3},{2,0},{3,1},{4,6},{5,7},{6,4},{7,5},{8,10},{9,11},{10,... | collective-permute-start | bytes 208904 | tf_op jit(solution)/shard_map/ppermute | solution.py:283
  12.2 5.9 %collective-permute-start.4 = (bf16[3,16,2176]{2,1,0:T(8,128)(2,1)S(1)}, bf16[3,16,2176]{2,1,0:T(8,128)(2,1)S(1)}, u32[]{:S(2)}, u32[]{:S(2)}) collective-permute-start(bf16[3,16,2176]{2,1,0:T(8,128)(2,1)S(1)} %stack.3.refs_2_), channel_id=1, source_target_pairs={{0,2},{1,3},{2,0},{3,1},{4,6},{5,7},{6,4},{7,5},{8,10},{9,11},{10,... | collective-permute-start | bytes 626696 | tf_op jit(solution)/shard_map/ppermute | solution.py:283
  14.0 4.4 %collective-permute-start.5 = (bf16[5,16,2176]{2,1,0:T(8,128)(2,1)S(1)}, bf16[5,16,2176]{2,1,0:T(8,128)(2,1)S(1)}, u32[]{:S(2)}, u32[]{:S(2)}) collective-permute-start(bf16[5,16,2176]{2,1,0:T(8,128)(2,1)S(1)} %stack.2.refs_0_), channel_id=1, source_target_pairs={{0,1},{1,0},{2,3},{3,2},{4,5},{5,4},{6,7},{7,6},{8,9},{9,8},{10,11... | collective-permute-start | bytes 1044488 | tf_op jit(solution)/shard_map/ppermute | solution.py:283
  18.1 1.5 %collective-permute-start.6 = (bf16[3,16,2176]{2,1,0:T(8,128)(2,1)S(1)}, bf16[3,16,2176]{2,1,0:T(8,128)(2,1)S(1)}, u32[]{:S(2)}, u32[]{:S(2)}) collective-permute-start(bf16[3,16,2176]{2,1,0:T(8,128)(2,1)S(1)} %relay.1), channel_id=1, source_target_pairs={{0,1},{1,0},{2,3},{3,2},{4,5},{5,4},{6,7},{7,6},{8,9},{9,8},{10,11... | collective-permute-start | bytes 626696 | tf_op jit(solution)/shard_map/ppermute | solution.py:283
  21.1 2.2 %collective-permute-start.7 = (bf16[4,16,2048]{2,1,0:T(8,128)(2,1)S(1)}, bf16[4,16,2048]{2,1,0:T(8,128)(2,1)S(1)}, u32[]{:S(2)}, u32[]{:S(2)}) collective-permute-start(bf16[4,16,2048]{2,1,0:T(8,128)(2,1)S(1)} %get-tuple-element.19), channel_id=1, source_target_pairs={{0,1},{1,0},{2,3},{3,2},{4,5},{5,4},{6,7},{7,6},{8,9},{9,8},{10,11... | collective-permute-start | bytes 786440 | tf_op jit(solution)/shard_map/ppermute | solution.py:283
  21.4 18.9 %copy-start = (bf16[16,2048]{1,0:T(8,128)(2,1)S(1)}, bf16[16,2048]{1,0:T(8,128)(2,1)}, u32[]{:S(2)}) copy-start(bf16[16,2048]{1,0:T(8,128)(2,1)} %residual_ref.1) | copy-start | bytes 196612
  23.0 5.9 %collective-permute-start.9 = (bf16[4,16,2048]{2,1,0:T(8,128)(2,1)S(1)}, bf16[4,16,2048]{2,1,0:T(8,128)(2,1)S(1)}, u32[]{:S(2)}, u32[]{:S(2)}) collective-permute-start(bf16[4,16,2048]{2,1,0:T(8,128)(2,1)S(1)} %get-tuple-element.23), channel_id=1, source_target_pairs={{0,1},{1,0},{2,3},{3,2},{4,5},{5,4},{6,7},{7,6},{8,9},{9,8},{10,11... | collective-permute-start | bytes 786440 | tf_op jit(solution)/shard_map/ppermute | solution.py:283
  23.4 8.6 %collective-permute-start.8 = (bf16[16,2048]{1,0:T(8,128)(2,1)S(1)}, bf16[16,2048]{1,0:T(8,128)(2,1)S(1)}, u32[]{:S(2)}, u32[]{:S(2)}) collective-permute-start(bf16[16,2048]{1,0:T(8,128)(2,1)S(1)} %get-tuple-element.21), channel_id=1, source_target_pairs={{0,2},{1,3},{2,0},{3,1},{4,6},{5,7},{6,4},{7,5},{8,10},{9,11},{10,... | collective-permute-start | bytes 196616 | tf_op jit(solution)/shard_map/ppermute | solution.py:283
  25.1 9.2 %collective-permute-start.10 = (bf16[16,2048]{1,0:T(8,128)(2,1)S(1)}, bf16[16,2048]{1,0:T(8,128)(2,1)S(1)}, u32[]{:S(2)}, u32[]{:S(2)}) collective-permute-start(bf16[16,2048]{1,0:T(8,128)(2,1)S(1)} %get-tuple-element.24.refs_0_), channel_id=1, source_target_pairs={{0,8},{1,9},{2,10},{3,11},{4,12},{5,13},{6,14},{7,15},{8,0},{9,1},... | collective-permute-start | bytes 196616 | tf_op jit(solution)/shard_map/ppermute | solution.py:283
  28.9 10.8 %collective-permute-start.11 = (bf16[16,2048]{1,0:T(8,128)(2,1)S(1)}, bf16[16,2048]{1,0:T(8,128)(2,1)S(1)}, u32[]{:S(2)}, u32[]{:S(2)}) collective-permute-start(bf16[16,2048]{1,0:T(8,128)(2,1)S(1)} %get-tuple-element.26), channel_id=1, source_target_pairs={{0,10},{1,11},{2,8},{3,9},{4,14},{5,15},{6,12},{7,13},{8,2},{9,3},... | collective-permute-start | bytes 196616 | tf_op jit(solution)/shard_map/ppermute | solution.py:283
  29.0 10.8 %collective-permute-start.13 = (bf16[16,2048]{1,0:T(8,128)(2,1)S(1)}, bf16[16,2048]{1,0:T(8,128)(2,1)S(1)}, u32[]{:S(2)}, u32[]{:S(2)}) collective-permute-start(bf16[16,2048]{1,0:T(8,128)(2,1)S(1)} %get-tuple-element.27), channel_id=1, source_target_pairs={{0,6},{1,7},{2,4},{3,5},{4,2},{5,3},{6,0},{7,1},{8,14},{9,15},{10,... | collective-permute-start | bytes 196616 | tf_op jit(solution)/shard_map/ppermute | solution.py:283
  31.1 8.7 %collective-permute-start.14 = (bf16[16,2048]{1,0:T(8,128)(2,1)S(1)}, bf16[16,2048]{1,0:T(8,128)(2,1)S(1)}, u32[]{:S(2)}, u32[]{:S(2)}) collective-permute-start(bf16[16,2048]{1,0:T(8,128)(2,1)S(1)} %get-tuple-element.28), channel_id=1, source_target_pairs={{0,4},{1,5},{2,6},{3,7},{4,0},{5,1},{6,2},{7,3},{8,12},{9,13},{10,... | collective-permute-start | bytes 196616 | tf_op jit(solution)/shard_map/ppermute | solution.py:283
  32.0 7.8 %collective-permute-start.15 = (bf16[16,2048]{1,0:T(8,128)(2,1)S(1)}, bf16[16,2048]{1,0:T(8,128)(2,1)S(1)}, u32[]{:S(2)}, u32[]{:S(2)}) collective-permute-start(bf16[16,2048]{1,0:T(8,128)(2,1)S(1)} %get-tuple-element.29), channel_id=1, source_target_pairs={{0,2},{1,3},{2,0},{3,1},{4,6},{5,7},{6,4},{7,5},{8,10},{9,11},{10,... | collective-permute-start | bytes 196616 | tf_op jit(solution)/shard_map/ppermute | solution.py:283
  34.3 6.1 %collective-permute-start.12 = (bf16[16,2048]{1,0:T(8,128)(2,1)S(1)}, bf16[16,2048]{1,0:T(8,128)(2,1)S(1)}, u32[]{:S(2)}, u32[]{:S(2)}) collective-permute-start(bf16[16,2048]{1,0:T(8,128)(2,1)S(1)} %side_sum.1.refs_6_), channel_id=1, source_target_pairs={{0,12},{1,13},{2,14},{3,15},{4,8},{5,9},{6,10},{7,11},{8,4},{9,5},... | collective-permute-start | bytes 196616 | tf_op jit(solution)/shard_map/ppermute | solution.py:283

commit v5 on v4

--- a/solution.py
+++ b/solution.py
@@ -256,7 +256,7 @@
     total = residual_ref[...].astype(jnp.float32)
     for ref in refs[:-1]:
         total += ref[...].astype(jnp.float32)
-    refs[-1][...] = total.astype(jnp.bfloat16)
+    refs[-1][...] = total.astype(refs[-1].dtype)
 
 
 def in_vmem(kernel, out_shape, name, arrays, after=(), mebibytes=4, cost_estimate=None):
@@ -297,7 +297,8 @@
     )
     third, second, first = (swap(packed, d * line) for d in (3, 2, 1))
     across = swap(packed, side)
-    along = stack((second, third, first))
+    attended = attend(*attention, (packed,))
+    along = stack((second, third, first), (stay(attended),))
     along_side = swap(along, side)
     near = stack((second, third, first, packed, across))
     near_far = swap(near, core)
@@ -327,26 +328,32 @@
         [send, vmem(one, jnp.float32), send, send], *early_outs
     )
     third_sum = in_vmem(add_kernel, send, "side_sum", (third_keep, swap(third_send, side)))
-    back = [
-        swap(second_sum, 2 * line),
-        swap(diagonal_sum, 2 * line + side),
-        swap(third_sum, 3 * line),
-    ]
-    attended = attend(*attention, (third_sum,))
+    partial_sum = in_vmem(
+        total_kernel,
+        vmem(one, jnp.float32),
+        "partial_sum",
+        (
+            residual,
+            swap(third_sum, 3 * line),
+            swap(second_sum, 2 * line),
+            swap(diagonal_sum, 2 * line + side),
+        ),
+    )
     late_outs = ffn([(3, 5), (2, 3)], [(2, 3)], early_outs[:1])
     own, across_sum, first_sum, first_diagonal_sum = pair_sum(
-        [vmem(one, jnp.float32), send, send, send], *late_outs, (second_sum,)
-    )
-    back += [
-        swap(first_diagonal_sum, line + side),
-        swap(first_sum, line),
-        swap(across_sum, side),
-    ]
+        [vmem(one, jnp.float32), send, send, send], *late_outs, (third_sum,)
+    )
     moe_out = in_vmem(
         total_kernel,
         jax.ShapeDtypeStruct(one, jnp.bfloat16),
         "total",
-        (residual, own, *back),
+        (
+            partial_sum,
+            own,
+            swap(first_diagonal_sum, line + side),
+            swap(first_sum, line),
+            swap(across_sum, side),
+        ),
     )
     return attended, moe_out
 

time: 41.3 us -> 40.6 us (0.983)
  starting transfers between devices: 21.2 us -> 20.7 us
    ppermute x16, starting transfers between devices: 21.2 us -> 20.7 us  [swap(): return lax.ppermute(value, 'ep', [(i, i ^ bits) for i in range(devices)])]
    pallas_call x9 -> x10, Pallas kernels: 3.93 us -> 3.93 us  [in_vmem(): pl.pallas_call(kernel, out_shape=out_shape, in_specs=[HERE] * len(arrays)...]
  transfers between devices with their start and end apart: 16 -> 16, of which waited for: 7 -> 8; matrix products, arithmetic and copies ran while one was open for 0% -> 0% of each run, Pallas kernels for 21% -> 22%
where the time goes in v5:
time: 40.6 us; the launch traced here: 40.4 us
  starting transfers between devices  20.7 us (51%)
  Pallas kernels  11.9 us (29%)
  waiting for transfers between devices  7.02 us (17%)
  between operations  0.74 us (2%)
    ppermute x16, starting transfers between devices, swap(): return lax.ppermute(value, 'ep', [(i, i ^ bits) for i in range(devices)])  20.7 us
    ppermute x16, waiting for transfers between devices, swap(): return lax.ppermute(value, 'ep', [(i, i ^ bits) for i in range(devices)])  7.02 us
    pallas_call x2, Pallas kernels, from_hbm(): pl.pallas_call(kernel, out_shape=out_shape, in_specs=[pl.BlockSpec(memory...  4.24 us
    pallas_call x10, Pallas kernels, in_vmem(): pl.pallas_call(kernel, out_shape=out_shape, in_specs=[HERE] * len(arrays)...  3.93 us
    pallas_call x1, Pallas kernels, hold(): pl.pallas_call(functools.partial(hold_kernel, len(flat), pieces), out_sha...  3.75 us
  transfers between devices with their start and end apart: 16, of which 8 were waited for; matrix products, arithmetic and copies ran while one was open for 0% of the time, Pallas kernels for 22%

profile of v5, /device:TPU:0, one launch (start us, length us, event | category | flops | bytes accessed | tf_op | source)
XLA Modules:
  0.0 40.4 jit_solution(7802875892479375399)
XLA Ops:
  0.6 1.0 %prepare.1.refs_6_.refs_3_ = bf16[16,2176]{1,0:T(8,128)(2,1)S(1)} custom-call(bf16[16,2048]{1,0:T(8,128)(2,1)} %residual_ref.1, f32[1,2048]{1,0:T(1,128)} %bitcast.13, s32[8,16]{1,0:T(8,128)} %bitcast.14, f32[8,16]{1,0:T(8,128)} %bitcast.15), custom_call_target="tpu_custom_call" | custom-call | tf_op jit(solution)/shard_map/prepare/pallas_call | solution.py:77
  1.7 4.1 %collective-permute-start = (bf16[16,2176]{1,0:T(8,128)(2,1)S(1)}, bf16[16,2176]{1,0:T(8,128)(2,1)S(1)}, u32[]{:S(2)}, u32[]{:S(2)}) collective-permute-start(bf16[16,2176]{1,0:T(8,128)(2,1)S(1)} %prepare.1.refs_6_.refs_3_), channel_id=1, source_target_pairs={{0,8},{1,9},{2,10},{3,11},{4,12},{5,13},{6,14},{7,15},{8,0},{9,1},... | collective-permute-start | bytes 208904 | tf_op jit(solution)/shard_map/ppermute | solution.py:283
  5.8 1.3 %collective-permute-start.1 = (bf16[16,2176]{1,0:T(8,128)(2,1)S(1)}, bf16[16,2176]{1,0:T(8,128)(2,1)S(1)}, u32[]{:S(2)}, u32[]{:S(2)}) collective-permute-start(bf16[16,2176]{1,0:T(8,128)(2,1)S(1)} %prepare.1.refs_6_.refs_3_), channel_id=1, source_target_pairs={{0,12},{1,13},{2,14},{3,15},{4,8},{5,9},{6,10},{7,11},{8,4},{9,5},... | collective-permute-start | bytes 208904 | tf_op jit(solution)/shard_map/ppermute | solution.py:283
  7.1 0.2 collective-permute-start.2
  7.4 1.5 %collective-permute-start.3 = (bf16[16,2176]{1,0:T(8,128)(2,1)S(1)}, bf16[16,2176]{1,0:T(8,128)(2,1)S(1)}, u32[]{:S(2)}, u32[]{:S(2)}) collective-permute-start(bf16[16,2176]{1,0:T(8,128)(2,1)S(1)} %prepare.1.refs_6_.refs_3_), channel_id=1, source_target_pairs={{0,2},{1,3},{2,0},{3,1},{4,6},{5,7},{6,4},{7,5},{8,10},{9,11},{10,... | collective-permute-start | bytes 208904 | tf_op jit(solution)/shard_map/ppermute | solution.py:283
  8.8 3.2 %attend.1.refs_3_ = bf16[4,32,128]{2,1,0:T(8,128)(2,1)} custom-call(s32[4]{0:T(128)} %refs_0_.3, bf16[4,32,128]{2,1,0:T(8,128)(2,1)} %refs_1_.1, bf16[4,256,128]{2,1,0:T(8,128)(2,1)} %bitcast.11, bf16[4,256,128]{2,1,0:T(8,128)(2,1)} %bitcast.12, bf16[8,128]{1,0:T(8,128)(2,1)} %bitcast.16, bf16[8,128]{1,0:T(8,128)(2,1)} %bitcast.17, ...), custom_call_target="tpu_custom_call" | custom-call | bytes 4194304 | tf_op jit(solution)/shard_map/attend/pallas_call | solution.py:77
  12.1 0.0 collective-permute-done.refs_0_
  12.1 0.0 collective-permute-done.1.refs_1_
  12.1 0.1 collective-permute-done.2.refs_2_
  12.2 1.7 %collective-permute-start.4 = (bf16[3,16,2176]{2,1,0:T(8,128)(2,1)S(1)}, bf16[3,16,2176]{2,1,0:T(8,128)(2,1)S(1)}, u32[]{:S(2)}, u32[]{:S(2)}) collective-permute-start(bf16[3,16,2176]{2,1,0:T(8,128)(2,1)S(1)} %stack.3.refs_2_), channel_id=1, source_target_pairs={{0,2},{1,3},{2,0},{3,1},{4,6},{5,7},{6,4},{7,5},{8,10},{9,11},{10,... | collective-permute-start | bytes 626696 | tf_op jit(solution)/shard_map/ppermute | solution.py:283
  13.9 0.0 collective-permute-done.3.refs_4_
  14.0 0.1 collective-permute-start.5
  14.0 3.8 %hold.1 = (bf16[4096,768]{1,0:T(8,128)(2,1)S(1)}, bf16[768,2048]{1,0:T(8,128)(2,1)S(1)}) custom-call(bf16[4096,768]{1,0:T(8,128)(2,1)} %bitcast.9, bf16[768,2048]{1,0:T(8,128)(2,1)} %bitcast.10, bf16[3,16,2176]{2,1,0:T(8,128)(2,1)S(1)} %stack.3.refs_2_), custom_call_target="tpu_custom_call" | custom-call | bytes 9437184 | tf_op jit(solution)/shard_map/hold/pallas_call | solution.py:170
  17.8 0.4 %collective-permute-done.4.in_ref.refs_1_ = bf16[3,16,2176]{2,1,0:T(8,128)(2,1)S(1)} collective-permute-done((bf16[3,16,2176]{2,1,0:T(8,128)(2,1)S(1)}, bf16[3,16,2176]{2,1,0:T(8,128)(2,1)S(1)}, u32[]{:S(2)}, u32[]{:S(2)}) %collective-permute-start.4) | collective-permute-done | bytes 208928 | tf_op jit(solution)/shard_map/ppermute | solution.py:283
  18.3 0.1 collective-permute-start.6
  18.4 0.0 collective-permute-done.5.refs_2_
  18.4 1.4 %collective-permute-done.6.refs_3_ = bf16[3,16,2176]{2,1,0:T(8,128)(2,1)S(1)} collective-permute-done((bf16[3,16,2176]{2,1,0:T(8,128)(2,1)S(1)}, bf16[3,16,2176]{2,1,0:T(8,128)(2,1)S(1)}, u32[]{:S(2)}, u32[]{:S(2)}) %collective-permute-start.6) | collective-permute-done | bytes 208928 | tf_op jit(solution)/shard_map/ppermute | solution.py:283
  19.8 1.5 %ffn.2 = (bf16[4,16,2048]{2,1,0:T(8,128)(2,1)S(1)}, bf16[4,16,2048]{2,1,0:T(8,128)(2,1)S(1)}) custom-call(bf16[5,16,2176]{2,1,0:T(8,128)(2,1)S(1)} %stack.2.refs_0_, bf16[3,16,2176]{2,1,0:T(8,128)(2,1)S(1)} %collective-permute-done.4.in_ref.refs_1_, bf16[5,16,2176]{2,1,0:T(8,128)(2,1)S(1)} %collective-permute-done.5.refs_2_, ...), custom_call_target="tpu_custom_call" | custom-call | flops 1207959552 | bytes 6291456 | tf_op jit(solution)/shard_map/ffn/pallas_call | solution.py:263
  21.3 0.0 copy-start
  21.3 0.2 collective-permute-start.7
  21.5 1.5 %ffn.3 = (bf16[4,16,2048]{2,1,0:T(8,128)(2,1)S(1)}, bf16[4,16,2048]{2,1,0:T(8,128)(2,1)S(1)}) custom-call(bf16[5,16,2176]{2,1,0:T(8,128)(2,1)S(1)} %stack.2.refs_0_, bf16[3,16,2176]{2,1,0:T(8,128)(2,1)S(1)} %collective-permute-done.4.in_ref.refs_1_, bf16[5,16,2176]{2,1,0:T(8,128)(2,1)S(1)} %collective-permute-done.5.refs_2_, ...), custom_call_target="tpu_custom_call" | custom-call | flops 1207959552 | bytes 6291456 | tf_op jit(solution)/shard_map/ffn/pallas_call | solution.py:263
  23.1 0.4 %collective-permute-start.12 = (bf16[4,16,2048]{2,1,0:T(8,128)(2,1)S(1)}, bf16[4,16,2048]{2,1,0:T(8,128)(2,1)S(1)}, u32[]{:S(2)}, u32[]{:S(2)}) collective-permute-start(bf16[4,16,2048]{2,1,0:T(8,128)(2,1)S(1)} %get-tuple-element.25), channel_id=1, source_target_pairs={{0,1},{1,0},{2,3},{3,2},{4,5},{5,4},{6,7},{7,6},{8,9},{9,8},{10,11... | collective-permute-start | bytes 786440 | tf_op jit(solution)/shard_map/ppermute | solution.py:283
  23.5 0.0 collective-permute-done.7.other_ref
  23.5 0.1 pair_sum.2
  23.6 1.5 %collective-permute-start.8 = (bf16[16,2048]{1,0:T(8,128)(2,1)S(1)}, bf16[16,2048]{1,0:T(8,128)(2,1)S(1)}, u32[]{:S(2)}, u32[]{:S(2)}) collective-permute-start(bf16[16,2048]{1,0:T(8,128)(2,1)S(1)} %get-tuple-element.21), channel_id=1, source_target_pairs={{0,2},{1,3},{2,0},{3,1},{4,6},{5,7},{6,4},{7,5},{8,10},{9,11},{10,... | collective-permute-start | bytes 196616 | tf_op jit(solution)/shard_map/ppermute | solution.py:283
  25.1 3.8 %collective-permute-start.10 = (bf16[16,2048]{1,0:T(8,128)(2,1)S(1)}, bf16[16,2048]{1,0:T(8,128)(2,1)S(1)}, u32[]{:S(2)}, u32[]{:S(2)}) collective-permute-start(bf16[16,2048]{1,0:T(8,128)(2,1)S(1)} %get-tuple-element.22), channel_id=1, source_target_pairs={{0,8},{1,9},{2,10},{3,11},{4,12},{5,13},{6,14},{7,15},{8,0},{9,1},... | collective-permute-start | bytes 196616 | tf_op jit(solution)/shard_map/ppermute | solution.py:283
  28.9 0.0 collective-permute-start.11
  28.9 0.0 collective-permute-done.8.other_ref
  29.0 2.6 %collective-permute-start.9 = (bf16[16,2048]{1,0:T(8,128)(2,1)S(1)}, bf16[16,2048]{1,0:T(8,128)(2,1)S(1)}, u32[]{:S(2)}, u32[]{:S(2)}) collective-permute-start(bf16[16,2048]{1,0:T(8,128)(2,1)S(1)} %side_sum.1.refs_0_), channel_id=1, source_target_pairs={{0,12},{1,13},{2,14},{3,15},{4,8},{5,9},{6,10},{7,11},{8,4},{9,5},... | collective-permute-start | bytes 196616 | tf_op jit(solution)/shard_map/ppermute | solution.py:283
  31.5 0.0 collective-permute-done.12.other_ref
  31.5 0.1 pair_sum.3
  31.6 1.9 %collective-permute-start.13 = (bf16[16,2048]{1,0:T(8,128)(2,1)S(1)}, bf16[16,2048]{1,0:T(8,128)(2,1)S(1)}, u32[]{:S(2)}, u32[]{:S(2)}) collective-permute-start(bf16[16,2048]{1,0:T(8,128)(2,1)S(1)} %get-tuple-element.27), channel_id=1, source_target_pairs={{0,6},{1,7},{2,4},{3,5},{4,2},{5,3},{6,0},{7,1},{8,14},{9,15},{10,... | collective-permute-start | bytes 196616 | tf_op jit(solution)/shard_map/ppermute | solution.py:283
  33.5 1.1 %collective-permute-start.14 = (bf16[16,2048]{1,0:T(8,128)(2,1)S(1)}, bf16[16,2048]{1,0:T(8,128)(2,1)S(1)}, u32[]{:S(2)}, u32[]{:S(2)}) collective-permute-start(bf16[16,2048]{1,0:T(8,128)(2,1)S(1)} %get-tuple-element.28), channel_id=1, source_target_pairs={{0,4},{1,5},{2,6},{3,7},{4,0},{5,1},{6,2},{7,3},{8,12},{9,13},{10,... | collective-permute-start | bytes 196616 | tf_op jit(solution)/shard_map/ppermute | solution.py:283
  34.6 0.8 %collective-permute-done.10.refs_1_ = bf16[16,2048]{1,0:T(8,128)(2,1)S(1)} collective-permute-done((bf16[16,2048]{1,0:T(8,128)(2,1)S(1)}, bf16[16,2048]{1,0:T(8,128)(2,1)S(1)}, u32[]{:S(2)}, u32[]{:S(2)}) %collective-permute-start.10) | collective-permute-done | bytes 65568 | tf_op jit(solution)/shard_map/ppermute | solution.py:283
  35.5 0.0 collective-permute-start.15
  35.5 2.0 %collective-permute-done.11.refs_2_ = bf16[16,2048]{1,0:T(8,128)(2,1)S(1)} collective-permute-done((bf16[16,2048]{1,0:T(8,128)(2,1)S(1)}, bf16[16,2048]{1,0:T(8,128)(2,1)S(1)}, u32[]{:S(2)}, u32[]{:S(2)}) %collective-permute-start.11) | collective-permute-done | bytes 65568 | tf_op jit(solution)/shard_map/ppermute | solution.py:283
  37.4 0.0 collective-permute-done.9.refs_0_
  37.5 0.0 copy-done
  37.5 0.8 %collective-permute-done.13.refs_1_ = bf16[16,2048]{1,0:T(8,128)(2,1)S(1)} collective-permute-done((bf16[16,2048]{1,0:T(8,128)(2,1)S(1)}, bf16[16,2048]{1,0:T(8,128)(2,1)S(1)}, u32[]{:S(2)}, u32[]{:S(2)}) %collective-permute-start.13) | collective-permute-done | bytes 65568 | tf_op jit(solution)/shard_map/ppermute | solution.py:283
  38.3 1.0 %collective-permute-done.14.refs_2_ = bf16[16,2048]{1,0:T(8,128)(2,1)S(1)} collective-permute-done((bf16[16,2048]{1,0:T(8,128)(2,1)S(1)}, bf16[16,2048]{1,0:T(8,128)(2,1)S(1)}, u32[]{:S(2)}, u32[]{:S(2)}) %collective-permute-start.14) | collective-permute-done | bytes 65568 | tf_op jit(solution)/shard_map/ppermute | solution.py:283
  39.3 0.4 %collective-permute-done.15.refs_3_ = bf16[16,2048]{1,0:T(8,128)(2,1)S(1)} collective-permute-done((bf16[16,2048]{1,0:T(8,128)(2,1)S(1)}, bf16[16,2048]{1,0:T(8,128)(2,1)S(1)}, u32[]{:S(2)}, u32[]{:S(2)}) %collective-permute-start.15) | collective-permute-done | bytes 65568 | tf_op jit(solution)/shard_map/ppermute | solution.py:283
  39.7 0.7 %total.1 = bf16[16,2048]{1,0:T(8,128)(2,1)} custom-call(f32[16,2048]{1,0:T(8,128)S(1)} %partial_sum.1.residual_ref, f32[16,2048]{1,0:T(8,128)S(1)} %get-tuple-element.26.refs_0_, bf16[16,2048]{1,0:T(8,128)(2,1)S(1)} %collective-permute-done.13.refs_1_, bf16[16,2048]{1,0:T(8,128)(2,1)S(1)} %collective-permute-done.14.refs_2_, ...), custom_call_target="tpu_custom_call" | custom-call | tf_op jit(solution)/shard_map/total/pallas_call | solution.py:263
  (5 shorter events, 0.1 us)
Async XLA Ops:
  1.7 10.4 %collective-permute-start = (bf16[16,2176]{1,0:T(8,128)(2,1)S(1)}, bf16[16,2176]{1,0:T(8,128)(2,1)S(1)}, u32[]{:S(2)}, u32[]{:S(2)}) collective-permute-start(bf16[16,2176]{1,0:T(8,128)(2,1)S(1)} %prepare.1.refs_6_.refs_3_), channel_id=1, source_target_pairs={{0,8},{1,9},{2,10},{3,11},{4,12},{5,13},{6,14},{7,15},{8,0},{9,1},... | collective-permute-start | bytes 208904 | tf_op jit(solution)/shard_map/ppermute | solution.py:283
  5.8 6.3 %collective-permute-start.1 = (bf16[16,2176]{1,0:T(8,128)(2,1)S(1)}, bf16[16,2176]{1,0:T(8,128)(2,1)S(1)}, u32[]{:S(2)}, u32[]{:S(2)}) collective-permute-start(bf16[16,2176]{1,0:T(8,128)(2,1)S(1)} %prepare.1.refs_6_.refs_3_), channel_id=1, source_target_pairs={{0,12},{1,13},{2,14},{3,15},{4,8},{5,9},{6,10},{7,11},{8,4},{9,5},... | collective-permute-start | bytes 208904 | tf_op jit(solution)/shard_map/ppermute | solution.py:283
  7.1 5.1 %collective-permute-start.2 = (bf16[16,2176]{1,0:T(8,128)(2,1)S(1)}, bf16[16,2176]{1,0:T(8,128)(2,1)S(1)}, u32[]{:S(2)}, u32[]{:S(2)}) collective-permute-start(bf16[16,2176]{1,0:T(8,128)(2,1)S(1)} %prepare.1.refs_6_.refs_3_), channel_id=1, source_target_pairs={{0,4},{1,5},{2,6},{3,7},{4,0},{5,1},{6,2},{7,3},{8,12},{9,13},{10,... | collective-permute-start | bytes 208904 | tf_op jit(solution)/shard_map/ppermute | solution.py:283
  7.4 6.6 %collective-permute-start.3 = (bf16[16,2176]{1,0:T(8,128)(2,1)S(1)}, bf16[16,2176]{1,0:T(8,128)(2,1)S(1)}, u32[]{:S(2)}, u32[]{:S(2)}) collective-permute-start(bf16[16,2176]{1,0:T(8,128)(2,1)S(1)} %prepare.1.refs_6_.refs_3_), channel_id=1, source_target_pairs={{0,2},{1,3},{2,0},{3,1},{4,6},{5,7},{6,4},{7,5},{8,10},{9,11},{10,... | collective-permute-start | bytes 208904 | tf_op jit(solution)/shard_map/ppermute | solution.py:283
  12.2 6.0 %collective-permute-start.4 = (bf16[3,16,2176]{2,1,0:T(8,128)(2,1)S(1)}, bf16[3,16,2176]{2,1,0:T(8,128)(2,1)S(1)}, u32[]{:S(2)}, u32[]{:S(2)}) collective-permute-start(bf16[3,16,2176]{2,1,0:T(8,128)(2,1)S(1)} %stack.3.refs_2_), channel_id=1, source_target_pairs={{0,2},{1,3},{2,0},{3,1},{4,6},{5,7},{6,4},{7,5},{8,10},{9,11},{10,... | collective-permute-start | bytes 626696 | tf_op jit(solution)/shard_map/ppermute | solution.py:283
  14.0 4.4 %collective-permute-start.5 = (bf16[5,16,2176]{2,1,0:T(8,128)(2,1)S(1)}, bf16[5,16,2176]{2,1,0:T(8,128)(2,1)S(1)}, u32[]{:S(2)}, u32[]{:S(2)}) collective-permute-start(bf16[5,16,2176]{2,1,0:T(8,128)(2,1)S(1)} %stack.2.refs_0_), channel_id=1, source_target_pairs={{0,1},{1,0},{2,3},{3,2},{4,5},{5,4},{6,7},{7,6},{8,9},{9,8},{10,11... | collective-permute-start | bytes 1044488 | tf_op jit(solution)/shard_map/ppermute | solution.py:283
  18.3 1.5 %collective-permute-start.6 = (bf16[3,16,2176]{2,1,0:T(8,128)(2,1)S(1)}, bf16[3,16,2176]{2,1,0:T(8,128)(2,1)S(1)}, u32[]{:S(2)}, u32[]{:S(2)}) collective-permute-start(bf16[3,16,2176]{2,1,0:T(8,128)(2,1)S(1)} %relay.1), channel_id=1, source_target_pairs={{0,1},{1,0},{2,3},{3,2},{4,5},{5,4},{6,7},{7,6},{8,9},{9,8},{10,11... | collective-permute-start | bytes 626696 | tf_op jit(solution)/shard_map/ppermute | solution.py:283
  21.3 16.1 %copy-start = (bf16[16,2048]{1,0:T(8,128)(2,1)S(1)}, bf16[16,2048]{1,0:T(8,128)(2,1)}, u32[]{:S(2)}) copy-start(bf16[16,2048]{1,0:T(8,128)(2,1)} %residual_ref.1) | copy-start | bytes 196612
  21.3 2.2 %collective-permute-start.7 = (bf16[4,16,2048]{2,1,0:T(8,128)(2,1)S(1)}, bf16[4,16,2048]{2,1,0:T(8,128)(2,1)S(1)}, u32[]{:S(2)}, u32[]{:S(2)}) collective-permute-start(bf16[4,16,2048]{2,1,0:T(8,128)(2,1)S(1)} %get-tuple-element.19), channel_id=1, source_target_pairs={{0,1},{1,0},{2,3},{3,2},{4,5},{5,4},{6,7},{7,6},{8,9},{9,8},{10,11... | collective-permute-start | bytes 786440 | tf_op jit(solution)/shard_map/ppermute | solution.py:283
  23.1 8.5 %collective-permute-start.12 = (bf16[4,16,2048]{2,1,0:T(8,128)(2,1)S(1)}, bf16[4,16,2048]{2,1,0:T(8,128)(2,1)S(1)}, u32[]{:S(2)}, u32[]{:S(2)}) collective-permute-start(bf16[4,16,2048]{2,1,0:T(8,128)(2,1)S(1)} %get-tuple-element.25), channel_id=1, source_target_pairs={{0,1},{1,0},{2,3},{3,2},{4,5},{5,4},{6,7},{7,6},{8,9},{9,8},{10,11... | collective-permute-start | bytes 786440 | tf_op jit(solution)/shard_map/ppermute | solution.py:283
  23.6 5.4 %collective-permute-start.8 = (bf16[16,2048]{1,0:T(8,128)(2,1)S(1)}, bf16[16,2048]{1,0:T(8,128)(2,1)S(1)}, u32[]{:S(2)}, u32[]{:S(2)}) collective-permute-start(bf16[16,2048]{1,0:T(8,128)(2,1)S(1)} %get-tuple-element.21), channel_id=1, source_target_pairs={{0,2},{1,3},{2,0},{3,1},{4,6},{5,7},{6,4},{7,5},{8,10},{9,11},{10,... | collective-permute-start | bytes 196616 | tf_op jit(solution)/shard_map/ppermute | solution.py:283
  25.1 10.4 %collective-permute-start.10 = (bf16[16,2048]{1,0:T(8,128)(2,1)S(1)}, bf16[16,2048]{1,0:T(8,128)(2,1)S(1)}, u32[]{:S(2)}, u32[]{:S(2)}) collective-permute-start(bf16[16,2048]{1,0:T(8,128)(2,1)S(1)} %get-tuple-element.22), channel_id=1, source_target_pairs={{0,8},{1,9},{2,10},{3,11},{4,12},{5,13},{6,14},{7,15},{8,0},{9,1},... | collective-permute-start | bytes 196616 | tf_op jit(solution)/shard_map/ppermute | solution.py:283
  28.9 8.5 %collective-permute-start.11 = (bf16[16,2048]{1,0:T(8,128)(2,1)S(1)}, bf16[16,2048]{1,0:T(8,128)(2,1)S(1)}, u32[]{:S(2)}, u32[]{:S(2)}) collective-permute-start(bf16[16,2048]{1,0:T(8,128)(2,1)S(1)} %get-tuple-element.23), channel_id=1, source_target_pairs={{0,10},{1,11},{2,8},{3,9},{4,14},{5,15},{6,12},{7,13},{8,2},{9,3},... | collective-permute-start | bytes 196616 | tf_op jit(solution)/shard_map/ppermute | solution.py:283
  29.0 8.5 %collective-permute-start.9 = (bf16[16,2048]{1,0:T(8,128)(2,1)S(1)}, bf16[16,2048]{1,0:T(8,128)(2,1)S(1)}, u32[]{:S(2)}, u32[]{:S(2)}) collective-permute-start(bf16[16,2048]{1,0:T(8,128)(2,1)S(1)} %side_sum.1.refs_0_), channel_id=1, source_target_pairs={{0,12},{1,13},{2,14},{3,15},{4,8},{5,9},{6,10},{7,11},{8,4},{9,5},... | collective-permute-start | bytes 196616 | tf_op jit(solution)/shard_map/ppermute | solution.py:283
  31.6 6.7 %collective-permute-start.13 = (bf16[16,2048]{1,0:T(8,128)(2,1)S(1)}, bf16[16,2048]{1,0:T(8,128)(2,1)S(1)}, u32[]{:S(2)}, u32[]{:S(2)}) collective-permute-start(bf16[16,2048]{1,0:T(8,128)(2,1)S(1)} %get-tuple-element.27), channel_id=1, source_target_pairs={{0,6},{1,7},{2,4},{3,5},{4,2},{5,3},{6,0},{7,1},{8,14},{9,15},{10,... | collective-permute-start | bytes 196616 | tf_op jit(solution)/shard_map/ppermute | solution.py:283
  33.5 5.8 %collective-permute-start.14 = (bf16[16,2048]{1,0:T(8,128)(2,1)S(1)}, bf16[16,2048]{1,0:T(8,128)(2,1)S(1)}, u32[]{:S(2)}, u32[]{:S(2)}) collective-permute-start(bf16[16,2048]{1,0:T(8,128)(2,1)S(1)} %get-tuple-element.28), channel_id=1, source_target_pairs={{0,4},{1,5},{2,6},{3,7},{4,0},{5,1},{6,2},{7,3},{8,12},{9,13},{10,... | collective-permute-start | bytes 196616 | tf_op jit(solution)/shard_map/ppermute | solution.py:283
  35.5 4.3 %collective-permute-start.15 = (bf16[16,2048]{1,0:T(8,128)(2,1)S(1)}, bf16[16,2048]{1,0:T(8,128)(2,1)S(1)}, u32[]{:S(2)}, u32[]{:S(2)}) collective-permute-start(bf16[16,2048]{1,0:T(8,128)(2,1)S(1)} %get-tuple-element.29), channel_id=1, source_target_pairs={{0,2},{1,3},{2,0},{3,1},{4,6},{5,7},{6,4},{7,5},{8,10},{9,11},{10,... | collective-permute-start | bytes 196616 | tf_op jit(solution)/shard_map/ppermute | solution.py:283

commit v6 on v2

--- a/solution.py
+++ b/solution.py
@@ -300,10 +300,10 @@
         (residual, norm_gain.reshape(1, -1), routes.T, route_weights.T),
     )
     third, second, first = (swap(packed, d * line) for d in (3, 2, 1))
-    across = swap(packed, side)
-    along = stack((second, third, first))
+    across, diagonal = swap(packed, side), swap(packed, line + side)
+    along = stack((second, third))
     along_side = swap(along, side)
-    near = stack((second, third, first, packed, across))
+    near = stack((second, third, packed, across, first, diagonal))
     near_far = swap(near, core)
     held = hold((expert_in, expert_down), (along,))
     along_side_far = swap(relay(along_side, held[:1]), core)
@@ -336,7 +336,7 @@
     )
     attended = attend(*attention, tuple(early_sums))
     back = [swap(early_sums[1], 3 * line), swap(early_sums[0], 2 * line)]
-    late_outs = ffn([(3, 5), (2, 3)], [(2, 3)], early_outs[:1])
+    late_outs = ffn([(2, 6)], [], early_outs[:1])
     late_keep, late_send = pair_sum(*late_outs)
     own, across_sum = in_vmem(
         square_kernel,

time: 39.6 us -> 41.7 us (1.053)
  waiting for transfers between devices: 7.49 us -> 12.7 us
  starting transfers between devices: 19.3 us -> 16.1 us
    ppermute x14 -> x15, waiting for transfers between devices: 7.49 us -> 12.7 us  [swap(): return lax.ppermute(value, 'ep', [(i, i ^ bits) for i in range(devices)])]
    ppermute x14 -> x15, starting transfers between devices: 19.3 us -> 16.1 us  [swap(): return lax.ppermute(value, 'ep', [(i, i ^ bits) for i in range(devices)])]
  transfers between devices with their start and end apart: 14 -> 15, of which waited for: 7 -> 8; matrix products, arithmetic and copies ran while one was open for 0% -> 0% of each run, Pallas kernels for 22% -> 21%
where the time goes in v6:
time: 41.7 us; the launch traced here: 41.5 us
  starting transfers between devices  16.1 us (39%)
  waiting for transfers between devices  12.7 us (30%)
  Pallas kernels  11.9 us (29%)
  between operations  0.74 us (2%)
    ppermute x15, starting transfers between devices, swap(): return lax.ppermute(value, 'ep', [(i, i ^ bits) for i in range(devices)])  16.1 us
    ppermute x15, waiting for transfers between devices, swap(): return lax.ppermute(value, 'ep', [(i, i ^ bits) for i in range(devices)])  12.7 us
    pallas_call x2, Pallas kernels, from_hbm(): pl.pallas_call(kernel, out_shape=out_shape, in_specs=[pl.BlockSpec(memory...  4.24 us
    pallas_call x10, Pallas kernels, in_vmem(): pl.pallas_call(kernel, out_shape=out_shape, in_specs=[HERE] * len(arrays)...  3.93 us
    pallas_call x1, Pallas kernels, hold(): pl.pallas_call(functools.partial(hold_kernel, len(flat), pieces), out_sha...  3.75 us
  transfers between devices with their start and end apart: 15, of which 8 were waited for; matrix products, arithmetic and copies ran while one was open for 0% of the time, Pallas kernels for 21%

profile of v6, /device:TPU:0, one launch (start us, length us, event | category | flops | bytes accessed | tf_op | source)
XLA Modules:
  0.0 41.5 jit_solution(3392526132211054583)
XLA Ops:
  0.6 1.0 %prepare.1.refs_2_ = bf16[16,2176]{1,0:T(8,128)(2,1)S(1)} custom-call(bf16[16,2048]{1,0:T(8,128)(2,1)} %residual_ref.1, f32[1,2048]{1,0:T(1,128)} %bitcast.13, s32[8,16]{1,0:T(8,128)} %bitcast.14, f32[8,16]{1,0:T(8,128)} %bitcast.15), custom_call_target="tpu_custom_call" | custom-call | tf_op jit(solution)/shard_map/prepare/pallas_call | solution.py:77
  1.7 4.1 %collective-permute-start = (bf16[16,2176]{1,0:T(8,128)(2,1)S(1)}, bf16[16,2176]{1,0:T(8,128)(2,1)S(1)}, u32[]{:S(2)}, u32[]{:S(2)}) collective-permute-start(bf16[16,2176]{1,0:T(8,128)(2,1)S(1)} %prepare.1.refs_2_), channel_id=1, source_target_pairs={{0,8},{1,9},{2,10},{3,11},{4,12},{5,13},{6,14},{7,15},{8,0},{9,1},... | collective-permute-start | bytes 208904 | tf_op jit(solution)/shard_map/ppermute | solution.py:287
  5.8 1.3 %collective-permute-start.1 = (bf16[16,2176]{1,0:T(8,128)(2,1)S(1)}, bf16[16,2176]{1,0:T(8,128)(2,1)S(1)}, u32[]{:S(2)}, u32[]{:S(2)}) collective-permute-start(bf16[16,2176]{1,0:T(8,128)(2,1)S(1)} %prepare.1.refs_2_), channel_id=1, source_target_pairs={{0,12},{1,13},{2,14},{3,15},{4,8},{5,9},{6,10},{7,11},{8,4},{9,5},... | collective-permute-start | bytes 208904 | tf_op jit(solution)/shard_map/ppermute | solution.py:287
  7.1 1.5 %collective-permute-start.2 = (bf16[16,2176]{1,0:T(8,128)(2,1)S(1)}, bf16[16,2176]{1,0:T(8,128)(2,1)S(1)}, u32[]{:S(2)}, u32[]{:S(2)}) collective-permute-start(bf16[16,2176]{1,0:T(8,128)(2,1)S(1)} %prepare.1.refs_2_), channel_id=1, source_target_pairs={{0,2},{1,3},{2,0},{3,1},{4,6},{5,7},{6,4},{7,5},{8,10},{9,11},{10,... | collective-permute-start | bytes 208904 | tf_op jit(solution)/shard_map/ppermute | solution.py:287
  8.6 0.2 collective-permute-start.3
  8.8 1.8 %collective-permute-start.4 = (bf16[16,2176]{1,0:T(8,128)(2,1)S(1)}, bf16[16,2176]{1,0:T(8,128)(2,1)S(1)}, u32[]{:S(2)}, u32[]{:S(2)}) collective-permute-start(bf16[16,2176]{1,0:T(8,128)(2,1)S(1)} %prepare.1.refs_2_), channel_id=1, source_target_pairs={{0,6},{1,7},{2,4},{3,5},{4,2},{5,3},{6,0},{7,1},{8,14},{9,15},{10,... | collective-permute-start | bytes 208904 | tf_op jit(solution)/shard_map/ppermute | solution.py:287
  10.6 0.0 collective-permute-done.refs_0_
  10.6 1.8 %collective-permute-done.1.refs_1_ = bf16[16,2176]{1,0:T(8,128)(2,1)S(1)} collective-permute-done((bf16[16,2176]{1,0:T(8,128)(2,1)S(1)}, bf16[16,2176]{1,0:T(8,128)(2,1)S(1)}, u32[]{:S(2)}, u32[]{:S(2)}) %collective-permute-start.1) | collective-permute-done | bytes 69664 | tf_op jit(solution)/shard_map/ppermute | solution.py:287
  12.4 0.0 collective-permute-done.2.refs_3_
  12.4 1.1 %collective-permute-done.3.refs_4_ = bf16[16,2176]{1,0:T(8,128)(2,1)S(1)} collective-permute-done((bf16[16,2176]{1,0:T(8,128)(2,1)S(1)}, bf16[16,2176]{1,0:T(8,128)(2,1)S(1)}, u32[]{:S(2)}, u32[]{:S(2)}) %collective-permute-start.3) | collective-permute-done | bytes 69664 | tf_op jit(solution)/shard_map/ppermute | solution.py:287
  13.5 1.5 %collective-permute-done.4.refs_5_ = bf16[16,2176]{1,0:T(8,128)(2,1)S(1)} collective-permute-done((bf16[16,2176]{1,0:T(8,128)(2,1)S(1)}, bf16[16,2176]{1,0:T(8,128)(2,1)S(1)}, u32[]{:S(2)}, u32[]{:S(2)}) %collective-permute-start.4) | collective-permute-done | bytes 69664 | tf_op jit(solution)/shard_map/ppermute | solution.py:287
  15.1 0.1 collective-permute-start.6
  15.2 0.7 %collective-permute-start.5 = (bf16[2,16,2176]{2,1,0:T(8,128)(2,1)S(1)}, bf16[2,16,2176]{2,1,0:T(8,128)(2,1)S(1)}, u32[]{:S(2)}, u32[]{:S(2)}) collective-permute-start(bf16[2,16,2176]{2,1,0:T(8,128)(2,1)S(1)} %stack.3.refs_2_), channel_id=1, source_target_pairs={{0,2},{1,3},{2,0},{3,1},{4,6},{5,7},{6,4},{7,5},{8,10},{9,11},{10,... | collective-permute-start | bytes 417800 | tf_op jit(solution)/shard_map/ppermute | solution.py:287
  15.9 3.7 %hold.1 = (bf16[4096,768]{1,0:T(8,128)(2,1)S(1)}, bf16[768,2048]{1,0:T(8,128)(2,1)S(1)}) custom-call(bf16[4096,768]{1,0:T(8,128)(2,1)} %bitcast.9, bf16[768,2048]{1,0:T(8,128)(2,1)} %bitcast.10, bf16[2,16,2176]{2,1,0:T(8,128)(2,1)S(1)} %stack.3.refs_2_), custom_call_target="tpu_custom_call" | custom-call | bytes 9437184 | tf_op jit(solution)/shard_map/hold/pallas_call | solution.py:170
  19.7 1.6 %collective-permute-done.5.in_ref.refs_1_ = bf16[2,16,2176]{2,1,0:T(8,128)(2,1)S(1)} collective-permute-done((bf16[2,16,2176]{2,1,0:T(8,128)(2,1)S(1)}, bf16[2,16,2176]{2,1,0:T(8,128)(2,1)S(1)}, u32[]{:S(2)}, u32[]{:S(2)}) %collective-permute-start.5) | collective-permute-done | bytes 139296 | tf_op jit(solution)/shard_map/ppermute | solution.py:287
  21.3 0.1 collective-permute-start.7
  21.4 1.3 %collective-permute-done.7.refs_3_ = bf16[2,16,2176]{2,1,0:T(8,128)(2,1)S(1)} collective-permute-done((bf16[2,16,2176]{2,1,0:T(8,128)(2,1)S(1)}, bf16[2,16,2176]{2,1,0:T(8,128)(2,1)S(1)}, u32[]{:S(2)}, u32[]{:S(2)}) %collective-permute-start.7) | collective-permute-done | bytes 139296 | tf_op jit(solution)/shard_map/ppermute | solution.py:287
  22.7 0.0 collective-permute-done.6.refs_2_
  22.7 1.5 %ffn.2 = (bf16[4,16,2048]{2,1,0:T(8,128)(2,1)S(1)}, bf16[4,16,2048]{2,1,0:T(8,128)(2,1)S(1)}) custom-call(bf16[6,16,2176]{2,1,0:T(8,128)(2,1)S(1)} %stack.2.refs_0_, bf16[2,16,2176]{2,1,0:T(8,128)(2,1)S(1)} %collective-permute-done.5.in_ref.refs_1_, bf16[6,16,2176]{2,1,0:T(8,128)(2,1)S(1)} %collective-permute-done.6.refs_2_, ...), custom_call_target="tpu_custom_call" | custom-call | flops 1207959552 | bytes 6291456 | tf_op jit(solution)/shard_map/ffn/pallas_call | solution.py:267
  24.3 0.2 collective-permute-start.8
  24.5 0.0 copy-start
  24.5 1.5 %ffn.3 = (bf16[4,16,2048]{2,1,0:T(8,128)(2,1)S(1)}, bf16[4,16,2048]{2,1,0:T(8,128)(2,1)S(1)}) custom-call(bf16[6,16,2176]{2,1,0:T(8,128)(2,1)S(1)} %stack.2.refs_0_, bf16[2,16,2176]{2,1,0:T(8,128)(2,1)S(1)} %collective-permute-done.5.in_ref.refs_1_, bf16[6,16,2176]{2,1,0:T(8,128)(2,1)S(1)} %collective-permute-done.6.refs_2_, ...), custom_call_target="tpu_custom_call" | custom-call | flops 1207959552 | bytes 6291456 | tf_op jit(solution)/shard_map/ffn/pallas_call | solution.py:267
  26.0 0.4 %collective-permute-start.10 = (bf16[4,16,2048]{2,1,0:T(8,128)(2,1)S(1)}, bf16[4,16,2048]{2,1,0:T(8,128)(2,1)S(1)}, u32[]{:S(2)}, u32[]{:S(2)}) collective-permute-start(bf16[4,16,2048]{2,1,0:T(8,128)(2,1)S(1)} %get-tuple-element.25), channel_id=1, source_target_pairs={{0,1},{1,0},{2,3},{3,2},{4,5},{5,4},{6,7},{7,6},{8,9},{9,8},{10,11... | collective-permute-start | bytes 786440 | tf_op jit(solution)/shard_map/ppermute | solution.py:287
  26.4 0.0 collective-permute-done.8.other_ref
  26.4 0.1 pair_sum.2
  26.5 0.7 %collective-permute-start.9 = (bf16[2,16,2048]{2,1,0:T(8,128)(2,1)S(1)}, bf16[2,16,2048]{2,1,0:T(8,128)(2,1)S(1)}, u32[]{:S(2)}, u32[]{:S(2)}) collective-permute-start(bf16[2,16,2048]{2,1,0:T(8,128)(2,1)S(1)} %get-tuple-element.21), channel_id=1, source_target_pairs={{0,2},{1,3},{2,0},{3,1},{4,6},{5,7},{6,4},{7,5},{8,10},{9,11},{10,... | collective-permute-start | bytes 393224 | tf_op jit(solution)/shard_map/ppermute | solution.py:287
  27.2 0.4 collective-permute-done.10.other_ref
  27.6 0.1 pair_sum.3
  27.7 0.9 %collective-permute-start.11 = (bf16[2,16,2048]{2,1,0:T(8,128)(2,1)S(1)}, bf16[2,16,2048]{2,1,0:T(8,128)(2,1)S(1)}, u32[]{:S(2)}, u32[]{:S(2)}) collective-permute-start(bf16[2,16,2048]{2,1,0:T(8,128)(2,1)S(1)} %get-tuple-element.27), channel_id=1, source_target_pairs={{0,4},{1,5},{2,6},{3,7},{4,0},{5,1},{6,2},{7,3},{8,12},{9,13},{10,... | collective-permute-start | bytes 393224 | tf_op jit(solution)/shard_map/ppermute | solution.py:287
  28.6 3.5 %collective-permute-done.9.other_ref = bf16[2,16,2048]{2,1,0:T(8,128)(2,1)S(1)} collective-permute-done((bf16[2,16,2048]{2,1,0:T(8,128)(2,1)S(1)}, bf16[2,16,2048]{2,1,0:T(8,128)(2,1)S(1)}, u32[]{:S(2)}, u32[]{:S(2)}) %collective-permute-start.9) | collective-permute-done | bytes 131104 | tf_op jit(solution)/shard_map/ppermute | solution.py:287
  32.1 3.0 %collective-permute-start.12 = (bf16[16,2048]{1,0:T(8,128)(2,1)S(1)}, bf16[16,2048]{1,0:T(8,128)(2,1)S(1)}, u32[]{:S(2)}, u32[]{:S(2)}) collective-permute-start(bf16[16,2048]{1,0:T(8,128)(2,1)S(1)} %get-tuple-element.23.refs_7_), channel_id=1, source_target_pairs={{0,12},{1,13},{2,14},{3,15},{4,8},{5,9},{6,10},{7,11},{8,4},{9,5},... | collective-permute-start | bytes 196616 | tf_op jit(solution)/shard_map/ppermute | solution.py:287
  35.1 0.0 collective-permute-start.13
  35.1 0.0 collective-permute-done.11.other_ref
  35.1 1.1 %collective-permute-start.14 = (bf16[16,2048]{1,0:T(8,128)(2,1)S(1)}, bf16[16,2048]{1,0:T(8,128)(2,1)S(1)}, u32[]{:S(2)}, u32[]{:S(2)}) collective-permute-start(bf16[16,2048]{1,0:T(8,128)(2,1)S(1)} %get-tuple-element.29), channel_id=1, source_target_pairs={{0,2},{1,3},{2,0},{3,1},{4,6},{5,7},{6,4},{7,5},{8,10},{9,11},{10,... | collective-permute-start | bytes 196616 | tf_op jit(solution)/shard_map/ppermute | solution.py:287
  36.2 3.2 %attend.1 = bf16[4,32,128]{2,1,0:T(8,128)(2,1)} custom-call(s32[4]{0:T(128)} %refs_0_.3, bf16[4,32,128]{2,1,0:T(8,128)(2,1)} %refs_1_.1, bf16[4,256,128]{2,1,0:T(8,128)(2,1)} %bitcast.11, bf16[4,256,128]{2,1,0:T(8,128)(2,1)} %bitcast.12, bf16[8,128]{1,0:T(8,128)(2,1)} %bitcast.16, bf16[8,128]{1,0:T(8,128)(2,1)} %bitcast.17, ...), custom_call_target="tpu_custom_call" | custom-call | bytes 4194304 | tf_op jit(solution)/shard_map/attend/pallas_call | solution.py:77
  39.4 0.0 collective-permute-done.12.refs_1_
  39.4 1.4 %collective-permute-done.13.refs_2_ = bf16[16,2048]{1,0:T(8,128)(2,1)S(1)} collective-permute-done((bf16[16,2048]{1,0:T(8,128)(2,1)S(1)}, bf16[16,2048]{1,0:T(8,128)(2,1)S(1)}, u32[]{:S(2)}, u32[]{:S(2)}) %collective-permute-start.13) | collective-permute-done | bytes 65568 | tf_op jit(solution)/shard_map/ppermute | solution.py:287
  40.8 0.0 collective-permute-done.14.refs_3_
  40.8 0.0 copy-done
  40.8 0.7 %total.1 = bf16[16,2048]{1,0:T(8,128)(2,1)} custom-call(bf16[16,2048]{1,0:T(8,128)(2,1)S(1)} %copy-done, f32[16,2048]{1,0:T(8,128)S(1)} %get-tuple-element.28.refs_0_, bf16[16,2048]{1,0:T(8,128)(2,1)S(1)} %collective-permute-done.12.refs_1_, bf16[16,2048]{1,0:T(8,128)(2,1)S(1)} %collective-permute-done.13.refs_2_, ...), custom_call_target="tpu_custom_call" | custom-call | tf_op jit(solution)/shard_map/total/pallas_call | solution.py:267
  (5 shorter events, 0.1 us)
Async XLA Ops:
  1.7 8.9 %collective-permute-start = (bf16[16,2176]{1,0:T(8,128)(2,1)S(1)}, bf16[16,2176]{1,0:T(8,128)(2,1)S(1)}, u32[]{:S(2)}, u32[]{:S(2)}) collective-permute-start(bf16[16,2176]{1,0:T(8,128)(2,1)S(1)} %prepare.1.refs_2_), channel_id=1, source_target_pairs={{0,8},{1,9},{2,10},{3,11},{4,12},{5,13},{6,14},{7,15},{8,0},{9,1},... | collective-permute-start | bytes 208904 | tf_op jit(solution)/shard_map/ppermute | solution.py:287
  5.8 6.7 %collective-permute-start.1 = (bf16[16,2176]{1,0:T(8,128)(2,1)S(1)}, bf16[16,2176]{1,0:T(8,128)(2,1)S(1)}, u32[]{:S(2)}, u32[]{:S(2)}) collective-permute-start(bf16[16,2176]{1,0:T(8,128)(2,1)S(1)} %prepare.1.refs_2_), channel_id=1, source_target_pairs={{0,12},{1,13},{2,14},{3,15},{4,8},{5,9},{6,10},{7,11},{8,4},{9,5},... | collective-permute-start | bytes 208904 | tf_op jit(solution)/shard_map/ppermute | solution.py:287
  7.1 5.3 %collective-permute-start.2 = (bf16[16,2176]{1,0:T(8,128)(2,1)S(1)}, bf16[16,2176]{1,0:T(8,128)(2,1)S(1)}, u32[]{:S(2)}, u32[]{:S(2)}) collective-permute-start(bf16[16,2176]{1,0:T(8,128)(2,1)S(1)} %prepare.1.refs_2_), channel_id=1, source_target_pairs={{0,2},{1,3},{2,0},{3,1},{4,6},{5,7},{6,4},{7,5},{8,10},{9,11},{10,... | collective-permute-start | bytes 208904 | tf_op jit(solution)/shard_map/ppermute | solution.py:287
  8.6 4.9 %collective-permute-start.3 = (bf16[16,2176]{1,0:T(8,128)(2,1)S(1)}, bf16[16,2176]{1,0:T(8,128)(2,1)S(1)}, u32[]{:S(2)}, u32[]{:S(2)}) collective-permute-start(bf16[16,2176]{1,0:T(8,128)(2,1)S(1)} %prepare.1.refs_2_), channel_id=1, source_target_pairs={{0,4},{1,5},{2,6},{3,7},{4,0},{5,1},{6,2},{7,3},{8,12},{9,13},{10,... | collective-permute-start | bytes 208904 | tf_op jit(solution)/shard_map/ppermute | solution.py:287
  8.8 6.2 %collective-permute-start.4 = (bf16[16,2176]{1,0:T(8,128)(2,1)S(1)}, bf16[16,2176]{1,0:T(8,128)(2,1)S(1)}, u32[]{:S(2)}, u32[]{:S(2)}) collective-permute-start(bf16[16,2176]{1,0:T(8,128)(2,1)S(1)} %prepare.1.refs_2_), channel_id=1, source_target_pairs={{0,6},{1,7},{2,4},{3,5},{4,2},{5,3},{6,0},{7,1},{8,14},{9,15},{10,... | collective-permute-start | bytes 208904 | tf_op jit(solution)/shard_map/ppermute | solution.py:287
  15.1 7.7 %collective-permute-start.6 = (bf16[6,16,2176]{2,1,0:T(8,128)(2,1)S(1)}, bf16[6,16,2176]{2,1,0:T(8,128)(2,1)S(1)}, u32[]{:S(2)}, u32[]{:S(2)}) collective-permute-start(bf16[6,16,2176]{2,1,0:T(8,128)(2,1)S(1)} %stack.2.refs_0_), channel_id=1, source_target_pairs={{0,1},{1,0},{2,3},{3,2},{4,5},{5,4},{6,7},{7,6},{8,9},{9,8},{10,11... | collective-permute-start | bytes 1253384 | tf_op jit(solution)/shard_map/ppermute | solution.py:287
  15.2 6.1 %collective-permute-start.5 = (bf16[2,16,2176]{2,1,0:T(8,128)(2,1)S(1)}, bf16[2,16,2176]{2,1,0:T(8,128)(2,1)S(1)}, u32[]{:S(2)}, u32[]{:S(2)}) collective-permute-start(bf16[2,16,2176]{2,1,0:T(8,128)(2,1)S(1)} %stack.3.refs_2_), channel_id=1, source_target_pairs={{0,2},{1,3},{2,0},{3,1},{4,6},{5,7},{6,4},{7,5},{8,10},{9,11},{10,... | collective-permute-start | bytes 417800 | tf_op jit(solution)/shard_map/ppermute | solution.py:287
  21.3 1.4 %collective-permute-start.7 = (bf16[2,16,2176]{2,1,0:T(8,128)(2,1)S(1)}, bf16[2,16,2176]{2,1,0:T(8,128)(2,1)S(1)}, u32[]{:S(2)}, u32[]{:S(2)}) collective-permute-start(bf16[2,16,2176]{2,1,0:T(8,128)(2,1)S(1)} %relay.1), channel_id=1, source_target_pairs={{0,1},{1,0},{2,3},{3,2},{4,5},{5,4},{6,7},{7,6},{8,9},{9,8},{10,11... | collective-permute-start | bytes 417800 | tf_op jit(solution)/shard_map/ppermute | solution.py:287
  24.3 2.2 %collective-permute-start.8 = (bf16[4,16,2048]{2,1,0:T(8,128)(2,1)S(1)}, bf16[4,16,2048]{2,1,0:T(8,128)(2,1)S(1)}, u32[]{:S(2)}, u32[]{:S(2)}) collective-permute-start(bf16[4,16,2048]{2,1,0:T(8,128)(2,1)S(1)} %get-tuple-element.19), channel_id=1, source_target_pairs={{0,1},{1,0},{2,3},{3,2},{4,5},{5,4},{6,7},{7,6},{8,9},{9,8},{10,11... | collective-permute-start | bytes 786440 | tf_op jit(solution)/shard_map/ppermute | solution.py:287
  24.5 16.4 %copy-start = (bf16[16,2048]{1,0:T(8,128)(2,1)S(1)}, bf16[16,2048]{1,0:T(8,128)(2,1)}, u32[]{:S(2)}) copy-start(bf16[16,2048]{1,0:T(8,128)(2,1)} %residual_ref.1) | copy-start | bytes 196612
  26.0 1.6 %collective-permute-start.10 = (bf16[4,16,2048]{2,1,0:T(8,128)(2,1)S(1)}, bf16[4,16,2048]{2,1,0:T(8,128)(2,1)S(1)}, u32[]{:S(2)}, u32[]{:S(2)}) collective-permute-start(bf16[4,16,2048]{2,1,0:T(8,128)(2,1)S(1)} %get-tuple-element.25), channel_id=1, source_target_pairs={{0,1},{1,0},{2,3},{3,2},{4,5},{5,4},{6,7},{7,6},{8,9},{9,8},{10,11... | collective-permute-start | bytes 786440 | tf_op jit(solution)/shard_map/ppermute | solution.py:287
  26.5 5.6 %collective-permute-start.9 = (bf16[2,16,2048]{2,1,0:T(8,128)(2,1)S(1)}, bf16[2,16,2048]{2,1,0:T(8,128)(2,1)S(1)}, u32[]{:S(2)}, u32[]{:S(2)}) collective-permute-start(bf16[2,16,2048]{2,1,0:T(8,128)(2,1)S(1)} %get-tuple-element.21), channel_id=1, source_target_pairs={{0,2},{1,3},{2,0},{3,1},{4,6},{5,7},{6,4},{7,5},{8,10},{9,11},{10,... | collective-permute-start | bytes 393224 | tf_op jit(solution)/shard_map/ppermute | solution.py:287
  27.7 7.4 %collective-permute-start.11 = (bf16[2,16,2048]{2,1,0:T(8,128)(2,1)S(1)}, bf16[2,16,2048]{2,1,0:T(8,128)(2,1)S(1)}, u32[]{:S(2)}, u32[]{:S(2)}) collective-permute-start(bf16[2,16,2048]{2,1,0:T(8,128)(2,1)S(1)} %get-tuple-element.27), channel_id=1, source_target_pairs={{0,4},{1,5},{2,6},{3,7},{4,0},{5,1},{6,2},{7,3},{8,12},{9,13},{10,... | collective-permute-start | bytes 393224 | tf_op jit(solution)/shard_map/ppermute | solution.py:287
  32.1 7.3 %collective-permute-start.12 = (bf16[16,2048]{1,0:T(8,128)(2,1)S(1)}, bf16[16,2048]{1,0:T(8,128)(2,1)S(1)}, u32[]{:S(2)}, u32[]{:S(2)}) collective-permute-start(bf16[16,2048]{1,0:T(8,128)(2,1)S(1)} %get-tuple-element.23.refs_7_), channel_id=1, source_target_pairs={{0,12},{1,13},{2,14},{3,15},{4,8},{5,9},{6,10},{7,11},{8,4},{9,5},... | collective-permute-start | bytes 196616 | tf_op jit(solution)/shard_map/ppermute | solution.py:287
  35.1 5.7 %collective-permute-start.13 = (bf16[16,2048]{1,0:T(8,128)(2,1)S(1)}, bf16[16,2048]{1,0:T(8,128)(2,1)S(1)}, u32[]{:S(2)}, u32[]{:S(2)}) collective-permute-start(bf16[16,2048]{1,0:T(8,128)(2,1)S(1)} %get-tuple-element.22.refs_6_), channel_id=1, source_target_pairs={{0,8},{1,9},{2,10},{3,11},{4,12},{5,13},{6,14},{7,15},{8,0},{9,1},... | collective-permute-start | bytes 196616 | tf_op jit(solution)/shard_map/ppermute | solution.py:287
  35.1 5.7 %collective-permute-start.14 = (bf16[16,2048]{1,0:T(8,128)(2,1)S(1)}, bf16[16,2048]{1,0:T(8,128)(2,1)S(1)}, u32[]{:S(2)}, u32[]{:S(2)}) collective-permute-start(bf16[16,2048]{1,0:T(8,128)(2,1)S(1)} %get-tuple-element.29), channel_id=1, source_target_pairs={{0,2},{1,3},{2,0},{3,1},{4,6},{5,7},{6,4},{7,5},{8,10},{9,11},{10,... | collective-permute-start | bytes 196616 | tf_op jit(solution)/shard_map/ppermute | solution.py:287

commit v7 on v5

--- a/solution.py
+++ b/solution.py
@@ -248,8 +248,8 @@
         out_ref[...] = total.astype(out_ref.dtype)
 
 
-def add_kernel(own_ref, other_ref, out_ref):
-    out_ref[...] = (own_ref[...] + other_ref[...].astype(jnp.float32)).astype(out_ref.dtype)
+def add_kernel(own_ref, other_ref, *refs):
+    refs[-1][...] = (own_ref[...] + other_ref[...].astype(jnp.float32)).astype(refs[-1].dtype)
 
 
 def total_kernel(residual_ref, *refs):
@@ -297,8 +297,7 @@
     )
     third, second, first = (swap(packed, d * line) for d in (3, 2, 1))
     across = swap(packed, side)
-    attended = attend(*attention, (packed,))
-    along = stack((second, third, first), (stay(attended),))
+    along = stack((second, third, first))
     along_side = swap(along, side)
     near = stack((second, third, first, packed, across))
     near_far = swap(near, core)
@@ -319,29 +318,30 @@
             cost_estimate=cost(8 * row_count * 2 * sum(h.size for h in held), 2 * held[0].size),
         )
 
-    def pair_sum(shapes, near_out, far_out, after=()):
-        return in_vmem(pair_kernel, shapes, "pair_sum", (near_out, swap(far_out, core)), after)
-
     early_outs = ffn([(0, 2)], [(0, 2)])
     send = vmem(one, jnp.bfloat16)
-    second_sum, third_keep, diagonal_sum, third_send = pair_sum(
-        [send, vmem(one, jnp.float32), send, send], *early_outs
+    keep_and_send = [vmem(one, jnp.float32)] * 2 + [send] * 2
+    second_keep, third_keep, second_send, third_send = in_vmem(
+        pair_kernel, keep_and_send, "pair_sum", (early_outs[0], swap(early_outs[1], core))
     )
     third_sum = in_vmem(add_kernel, send, "side_sum", (third_keep, swap(third_send, side)))
+    second_sum = in_vmem(
+        add_kernel, send, "side_sum", (second_keep, swap(second_send, side)), (third_sum,)
+    )
     partial_sum = in_vmem(
         total_kernel,
         vmem(one, jnp.float32),
         "partial_sum",
-        (
-            residual,
-            swap(third_sum, 3 * line),
-            swap(second_sum, 2 * line),
-            swap(diagonal_sum, 2 * line + side),
-        ),
-    )
+        (residual, swap(third_sum, 3 * line), swap(second_sum, 2 * line)),
+    )
+    attended = attend(*attention, (second_sum,))
     late_outs = ffn([(3, 5), (2, 3)], [(2, 3)], early_outs[:1])
-    own, across_sum, first_sum, first_diagonal_sum = pair_sum(
-        [vmem(one, jnp.float32), send, send, send], *late_outs, (third_sum,)
+    own, across_sum, first_sum, diagonal_sum = in_vmem(
+        pair_kernel,
+        [vmem(one, jnp.float32), send, send, send],
+        "pair_sum",
+        (late_outs[0], swap(late_outs[1], core)),
+        (third_send,),
     )
     moe_out = in_vmem(
         total_kernel,
@@ -350,7 +350,7 @@
         (
             partial_sum,
             own,
-            swap(first_diagonal_sum, line + side),
+            swap(diagonal_sum, line + side),
             swap(first_sum, line),
             swap(across_sum, side),
         ),

time: 40.6 us -> 39.6 us (0.975)
  waiting for transfers between devices: 7.02 us -> 4.84 us
  starting transfers between devices: 20.7 us -> 21.9 us
    ppermute x16, waiting for transfers between devices: 7.02 us -> 4.84 us  [swap(): return lax.ppermute(value, 'ep', [(i, i ^ bits) for i in range(devices)])]
    ppermute x16, starting transfers between devices: 20.7 us -> 21.9 us  [swap(): return lax.ppermute(value, 'ep', [(i, i ^ bits) for i in range(devices)])]
    pallas_call x10 -> x11, Pallas kernels: 3.93 us -> 3.94 us  [in_vmem(): pl.pallas_call(kernel, out_shape=out_shape, in_specs=[HERE] * len(arrays)...]
  transfers between devices with their start and end apart: 16 -> 16, of which waited for: 8 -> 5; matrix products, arithmetic and copies ran while one was open for 0% -> 0% of each run, Pallas kernels for 22% -> 22%
where the time goes in v7:
time: 39.6 us; the launch traced here: 39.4 us
  starting transfers between devices  21.9 us (55%)
  Pallas kernels  11.9 us (30%)
  waiting for transfers between devices  4.84 us (12%)
  between operations  0.77 us (2%)
    ppermute x16, starting transfers between devices, swap(): return lax.ppermute(value, 'ep', [(i, i ^ bits) for i in range(devices)])  21.9 us
    ppermute x16, waiting for transfers between devices, swap(): return lax.ppermute(value, 'ep', [(i, i ^ bits) for i in range(devices)])  4.84 us
    pallas_call x2, Pallas kernels, from_hbm(): pl.pallas_call(kernel, out_shape=out_shape, in_specs=[pl.BlockSpec(memory...  4.24 us
    pallas_call x11, Pallas kernels, in_vmem(): pl.pallas_call(kernel, out_shape=out_shape, in_specs=[HERE] * len(arrays)...  3.94 us
    pallas_call x1, Pallas kernels, hold(): pl.pallas_call(functools.partial(hold_kernel, len(flat), pieces), out_sha...  3.75 us
  transfers between devices with their start and end apart: 16, of which 5 were waited for; matrix products, arithmetic and copies ran while one was open for 0% of the time, Pallas kernels for 22%

profile of v7, /device:TPU:0, one launch (start us, length us, event | category | flops | bytes accessed | tf_op | source)
XLA Modules:
  0.0 39.4 jit_solution(7849546985866135027)
XLA Ops:
  0.6 1.0 %prepare.1.refs_3_ = bf16[16,2176]{1,0:T(8,128)(2,1)S(1)} custom-call(bf16[16,2048]{1,0:T(8,128)(2,1)} %residual_ref.1, f32[1,2048]{1,0:T(1,128)} %bitcast.13, s32[8,16]{1,0:T(8,128)} %bitcast.14, f32[8,16]{1,0:T(8,128)} %bitcast.15), custom_call_target="tpu_custom_call" | custom-call | tf_op jit(solution)/shard_map/prepare/pallas_call | solution.py:77
  1.7 4.1 %collective-permute-start = (bf16[16,2176]{1,0:T(8,128)(2,1)S(1)}, bf16[16,2176]{1,0:T(8,128)(2,1)S(1)}, u32[]{:S(2)}, u32[]{:S(2)}) collective-permute-start(bf16[16,2176]{1,0:T(8,128)(2,1)S(1)} %prepare.1.refs_3_), channel_id=1, source_target_pairs={{0,8},{1,9},{2,10},{3,11},{4,12},{5,13},{6,14},{7,15},{8,0},{9,1},... | collective-permute-start | bytes 208904 | tf_op jit(solution)/shard_map/ppermute | solution.py:283
  5.8 1.3 %collective-permute-start.1 = (bf16[16,2176]{1,0:T(8,128)(2,1)S(1)}, bf16[16,2176]{1,0:T(8,128)(2,1)S(1)}, u32[]{:S(2)}, u32[]{:S(2)}) collective-permute-start(bf16[16,2176]{1,0:T(8,128)(2,1)S(1)} %prepare.1.refs_3_), channel_id=1, source_target_pairs={{0,12},{1,13},{2,14},{3,15},{4,8},{5,9},{6,10},{7,11},{8,4},{9,5},... | collective-permute-start | bytes 208904 | tf_op jit(solution)/shard_map/ppermute | solution.py:283
  7.1 0.2 collective-permute-start.2
  7.4 1.5 %collective-permute-start.3 = (bf16[16,2176]{1,0:T(8,128)(2,1)S(1)}, bf16[16,2176]{1,0:T(8,128)(2,1)S(1)}, u32[]{:S(2)}, u32[]{:S(2)}) collective-permute-start(bf16[16,2176]{1,0:T(8,128)(2,1)S(1)} %prepare.1.refs_3_), channel_id=1, source_target_pairs={{0,2},{1,3},{2,0},{3,1},{4,6},{5,7},{6,4},{7,5},{8,10},{9,11},{10,... | collective-permute-start | bytes 208904 | tf_op jit(solution)/shard_map/ppermute | solution.py:283
  8.8 0.8 %collective-permute-done.refs_0_ = bf16[16,2176]{1,0:T(8,128)(2,1)S(1)} collective-permute-done((bf16[16,2176]{1,0:T(8,128)(2,1)S(1)}, bf16[16,2176]{1,0:T(8,128)(2,1)S(1)}, u32[]{:S(2)}, u32[]{:S(2)}) %collective-permute-start) | collective-permute-done | bytes 69664 | tf_op jit(solution)/shard_map/ppermute | solution.py:283
  9.7 2.5 %collective-permute-done.1.refs_1_ = bf16[16,2176]{1,0:T(8,128)(2,1)S(1)} collective-permute-done((bf16[16,2176]{1,0:T(8,128)(2,1)S(1)}, bf16[16,2176]{1,0:T(8,128)(2,1)S(1)}, u32[]{:S(2)}, u32[]{:S(2)}) %collective-permute-start.1) | collective-permute-done | bytes 69664 | tf_op jit(solution)/shard_map/ppermute | solution.py:283
  12.1 0.1 collective-permute-done.2.refs_2_
  12.2 1.7 %collective-permute-start.4 = (bf16[3,16,2176]{2,1,0:T(8,128)(2,1)S(1)}, bf16[3,16,2176]{2,1,0:T(8,128)(2,1)S(1)}, u32[]{:S(2)}, u32[]{:S(2)}) collective-permute-start(bf16[3,16,2176]{2,1,0:T(8,128)(2,1)S(1)} %stack.3.refs_2_), channel_id=1, source_target_pairs={{0,2},{1,3},{2,0},{3,1},{4,6},{5,7},{6,4},{7,5},{8,10},{9,11},{10,... | collective-permute-start | bytes 626696 | tf_op jit(solution)/shard_map/ppermute | solution.py:283
  13.9 0.0 collective-permute-done.3.refs_4_
  14.0 0.1 collective-permute-start.5
  14.0 3.8 %hold.1 = (bf16[4096,768]{1,0:T(8,128)(2,1)S(1)}, bf16[768,2048]{1,0:T(8,128)(2,1)S(1)}) custom-call(bf16[4096,768]{1,0:T(8,128)(2,1)} %bitcast.9, bf16[768,2048]{1,0:T(8,128)(2,1)} %bitcast.10, bf16[3,16,2176]{2,1,0:T(8,128)(2,1)S(1)} %stack.3.refs_2_), custom_call_target="tpu_custom_call" | custom-call | bytes 9437184 | tf_op jit(solution)/shard_map/hold/pallas_call | solution.py:170
  17.8 0.3 collective-permute-done.4.in_ref.refs_1_
  18.1 0.3 collective-permute-start.6
  18.4 0.0 collective-permute-done.5.refs_2_
  18.4 1.2 %collective-permute-done.6.refs_3_ = bf16[3,16,2176]{2,1,0:T(8,128)(2,1)S(1)} collective-permute-done((bf16[3,16,2176]{2,1,0:T(8,128)(2,1)S(1)}, bf16[3,16,2176]{2,1,0:T(8,128)(2,1)S(1)}, u32[]{:S(2)}, u32[]{:S(2)}) %collective-permute-start.6) | collective-permute-done | bytes 208928 | tf_op jit(solution)/shard_map/ppermute | solution.py:283
  19.6 1.5 %ffn.2 = (bf16[4,16,2048]{2,1,0:T(8,128)(2,1)S(1)}, bf16[4,16,2048]{2,1,0:T(8,128)(2,1)S(1)}) custom-call(bf16[5,16,2176]{2,1,0:T(8,128)(2,1)S(1)} %stack.2.refs_0_, bf16[3,16,2176]{2,1,0:T(8,128)(2,1)S(1)} %collective-permute-done.4.in_ref.refs_1_, bf16[5,16,2176]{2,1,0:T(8,128)(2,1)S(1)} %collective-permute-done.5.refs_2_, ...), custom_call_target="tpu_custom_call" | custom-call | flops 1207959552 | bytes 6291456 | tf_op jit(solution)/shard_map/ffn/pallas_call | solution.py:263
  21.1 0.3 collective-permute-start.7
  21.4 0.0 copy-start
  21.4 1.5 %ffn.3 = (bf16[4,16,2048]{2,1,0:T(8,128)(2,1)S(1)}, bf16[4,16,2048]{2,1,0:T(8,128)(2,1)S(1)}) custom-call(bf16[5,16,2176]{2,1,0:T(8,128)(2,1)S(1)} %stack.2.refs_0_, bf16[3,16,2176]{2,1,0:T(8,128)(2,1)S(1)} %collective-permute-done.4.in_ref.refs_1_, bf16[5,16,2176]{2,1,0:T(8,128)(2,1)S(1)} %collective-permute-done.5.refs_2_, ...), custom_call_target="tpu_custom_call" | custom-call | flops 1207959552 | bytes 6291456 | tf_op jit(solution)/shard_map/ffn/pallas_call | solution.py:263
  23.0 0.3 collective-permute-start.12
  23.3 0.0 collective-permute-done.7.other_ref
  23.3 0.1 pair_sum.2
  23.4 1.7 %collective-permute-start.9 = (bf16[16,2048]{1,0:T(8,128)(2,1)S(1)}, bf16[16,2048]{1,0:T(8,128)(2,1)S(1)}, u32[]{:S(2)}, u32[]{:S(2)}) collective-permute-start(bf16[16,2048]{1,0:T(8,128)(2,1)S(1)} %get-tuple-element.23.refs_0_), channel_id=1, source_target_pairs={{0,2},{1,3},{2,0},{3,1},{4,6},{5,7},{6,4},{7,5},{8,10},{9,11},{10,... | collective-permute-start | bytes 196616 | tf_op jit(solution)/shard_map/ppermute | solution.py:283
  25.1 0.4 collective-permute-start.8
  25.5 0.0 collective-permute-done.12.other_ref
  25.5 0.1 pair_sum.3
  25.5 3.2 %collective-permute-start.13 = (bf16[16,2048]{1,0:T(8,128)(2,1)S(1)}, bf16[16,2048]{1,0:T(8,128)(2,1)S(1)}, u32[]{:S(2)}, u32[]{:S(2)}) collective-permute-start(bf16[16,2048]{1,0:T(8,128)(2,1)S(1)} %get-tuple-element.27), channel_id=1, source_target_pairs={{0,6},{1,7},{2,4},{3,5},{4,2},{5,3},{6,0},{7,1},{8,14},{9,15},{10,... | collective-permute-start | bytes 196616 | tf_op jit(solution)/shard_map/ppermute | solution.py:283
  28.7 0.0 collective-permute-done.9.other_ref
  28.7 3.3 %collective-permute-start.10 = (bf16[16,2048]{1,0:T(8,128)(2,1)S(1)}, bf16[16,2048]{1,0:T(8,128)(2,1)S(1)}, u32[]{:S(2)}, u32[]{:S(2)}) collective-permute-start(bf16[16,2048]{1,0:T(8,128)(2,1)S(1)} %side_sum.2.refs_0_), channel_id=1, source_target_pairs={{0,12},{1,13},{2,14},{3,15},{4,8},{5,9},{6,10},{7,11},{8,4},{9,5},... | collective-permute-start | bytes 196616 | tf_op jit(solution)/shard_map/ppermute | solution.py:283
  32.0 0.0 collective-permute-done.8.other_ref
  32.1 1.9 %collective-permute-start.11 = (bf16[16,2048]{1,0:T(8,128)(2,1)S(1)}, bf16[16,2048]{1,0:T(8,128)(2,1)S(1)}, u32[]{:S(2)}, u32[]{:S(2)}) collective-permute-start(bf16[16,2048]{1,0:T(8,128)(2,1)S(1)} %side_sum.3.refs_6_), channel_id=1, source_target_pairs={{0,8},{1,9},{2,10},{3,11},{4,12},{5,13},{6,14},{7,15},{8,0},{9,1},... | collective-permute-start | bytes 196616 | tf_op jit(solution)/shard_map/ppermute | solution.py:283
  34.0 0.2 collective-permute-start.14
  34.2 1.3 %collective-permute-start.15 = (bf16[16,2048]{1,0:T(8,128)(2,1)S(1)}, bf16[16,2048]{1,0:T(8,128)(2,1)S(1)}, u32[]{:S(2)}, u32[]{:S(2)}) collective-permute-start(bf16[16,2048]{1,0:T(8,128)(2,1)S(1)} %get-tuple-element.29), channel_id=1, source_target_pairs={{0,2},{1,3},{2,0},{3,1},{4,6},{5,7},{6,4},{7,5},{8,10},{9,11},{10,... | collective-permute-start | bytes 196616 | tf_op jit(solution)/shard_map/ppermute | solution.py:283
  35.4 3.2 %attend.1 = bf16[4,32,128]{2,1,0:T(8,128)(2,1)} custom-call(s32[4]{0:T(128)} %refs_0_.3, bf16[4,32,128]{2,1,0:T(8,128)(2,1)} %refs_1_.1, bf16[4,256,128]{2,1,0:T(8,128)(2,1)} %bitcast.11, bf16[4,256,128]{2,1,0:T(8,128)(2,1)} %bitcast.12, bf16[8,128]{1,0:T(8,128)(2,1)} %bitcast.16, bf16[8,128]{1,0:T(8,128)(2,1)} %bitcast.17, bf16[16,2048]{1,0:T(8,128)(2,1)S(1)} %side_sum.3.refs_6_), custom_call_target="tpu_custom_call" | custom-call | bytes 4194304 | tf_op jit(solution)/shard_map/attend/pallas_call | solution.py:77
  38.6 0.0 collective-permute-done.10.refs_0_
  38.7 0.0 collective-permute-done.11.refs_1_
  38.7 0.0 copy-done
  38.7 0.0 collective-permute-done.13.refs_1_
  38.7 0.0 collective-permute-done.14.refs_2_
  38.7 0.0 collective-permute-done.15.refs_3_
  38.7 0.7 %total.1 = bf16[16,2048]{1,0:T(8,128)(2,1)} custom-call(f32[16,2048]{1,0:T(8,128)S(1)} %partial_sum.1.residual_ref, f32[16,2048]{1,0:T(8,128)S(1)} %get-tuple-element.26.refs_0_, bf16[16,2048]{1,0:T(8,128)(2,1)S(1)} %collective-permute-done.13.refs_1_, bf16[16,2048]{1,0:T(8,128)(2,1)S(1)} %collective-permute-done.14.refs_2_, ...), custom_call_target="tpu_custom_call" | custom-call | tf_op jit(solution)/shard_map/total/pallas_call | solution.py:263
  (6 shorter events, 0.1 us)
Async XLA Ops:
  1.7 8.0 %collective-permute-start = (bf16[16,2176]{1,0:T(8,128)(2,1)S(1)}, bf16[16,2176]{1,0:T(8,128)(2,1)S(1)}, u32[]{:S(2)}, u32[]{:S(2)}) collective-permute-start(bf16[16,2176]{1,0:T(8,128)(2,1)S(1)} %prepare.1.refs_3_), channel_id=1, source_target_pairs={{0,8},{1,9},{2,10},{3,11},{4,12},{5,13},{6,14},{7,15},{8,0},{9,1},... | collective-permute-start | bytes 208904 | tf_op jit(solution)/shard_map/ppermute | solution.py:283
  5.8 6.3 %collective-permute-start.1 = (bf16[16,2176]{1,0:T(8,128)(2,1)S(1)}, bf16[16,2176]{1,0:T(8,128)(2,1)S(1)}, u32[]{:S(2)}, u32[]{:S(2)}) collective-permute-start(bf16[16,2176]{1,0:T(8,128)(2,1)S(1)} %prepare.1.refs_3_), channel_id=1, source_target_pairs={{0,12},{1,13},{2,14},{3,15},{4,8},{5,9},{6,10},{7,11},{8,4},{9,5},... | collective-permute-start | bytes 208904 | tf_op jit(solution)/shard_map/ppermute | solution.py:283
  7.1 5.1 %collective-permute-start.2 = (bf16[16,2176]{1,0:T(8,128)(2,1)S(1)}, bf16[16,2176]{1,0:T(8,128)(2,1)S(1)}, u32[]{:S(2)}, u32[]{:S(2)}) collective-permute-start(bf16[16,2176]{1,0:T(8,128)(2,1)S(1)} %prepare.1.refs_3_), channel_id=1, source_target_pairs={{0,4},{1,5},{2,6},{3,7},{4,0},{5,1},{6,2},{7,3},{8,12},{9,13},{10,... | collective-permute-start | bytes 208904 | tf_op jit(solution)/shard_map/ppermute | solution.py:283
  7.4 6.6 %collective-permute-start.3 = (bf16[16,2176]{1,0:T(8,128)(2,1)S(1)}, bf16[16,2176]{1,0:T(8,128)(2,1)S(1)}, u32[]{:S(2)}, u32[]{:S(2)}) collective-permute-start(bf16[16,2176]{1,0:T(8,128)(2,1)S(1)} %prepare.1.refs_3_), channel_id=1, source_target_pairs={{0,2},{1,3},{2,0},{3,1},{4,6},{5,7},{6,4},{7,5},{8,10},{9,11},{10,... | collective-permute-start | bytes 208904 | tf_op jit(solution)/shard_map/ppermute | solution.py:283
  12.2 5.9 %collective-permute-start.4 = (bf16[3,16,2176]{2,1,0:T(8,128)(2,1)S(1)}, bf16[3,16,2176]{2,1,0:T(8,128)(2,1)S(1)}, u32[]{:S(2)}, u32[]{:S(2)}) collective-permute-start(bf16[3,16,2176]{2,1,0:T(8,128)(2,1)S(1)} %stack.3.refs_2_), channel_id=1, source_target_pairs={{0,2},{1,3},{2,0},{3,1},{4,6},{5,7},{6,4},{7,5},{8,10},{9,11},{10,... | collective-permute-start | bytes 626696 | tf_op jit(solution)/shard_map/ppermute | solution.py:283
  14.0 4.4 %collective-permute-start.5 = (bf16[5,16,2176]{2,1,0:T(8,128)(2,1)S(1)}, bf16[5,16,2176]{2,1,0:T(8,128)(2,1)S(1)}, u32[]{:S(2)}, u32[]{:S(2)}) collective-permute-start(bf16[5,16,2176]{2,1,0:T(8,128)(2,1)S(1)} %stack.2.refs_0_), channel_id=1, source_target_pairs={{0,1},{1,0},{2,3},{3,2},{4,5},{5,4},{6,7},{7,6},{8,9},{9,8},{10,11... | collective-permute-start | bytes 1044488 | tf_op jit(solution)/shard_map/ppermute | solution.py:283
  18.1 1.5 %collective-permute-start.6 = (bf16[3,16,2176]{2,1,0:T(8,128)(2,1)S(1)}, bf16[3,16,2176]{2,1,0:T(8,128)(2,1)S(1)}, u32[]{:S(2)}, u32[]{:S(2)}) collective-permute-start(bf16[3,16,2176]{2,1,0:T(8,128)(2,1)S(1)} %relay.1), channel_id=1, source_target_pairs={{0,1},{1,0},{2,3},{3,2},{4,5},{5,4},{6,7},{7,6},{8,9},{9,8},{10,11... | collective-permute-start | bytes 626696 | tf_op jit(solution)/shard_map/ppermute | solution.py:283
  21.1 2.2 %collective-permute-start.7 = (bf16[4,16,2048]{2,1,0:T(8,128)(2,1)S(1)}, bf16[4,16,2048]{2,1,0:T(8,128)(2,1)S(1)}, u32[]{:S(2)}, u32[]{:S(2)}) collective-permute-start(bf16[4,16,2048]{2,1,0:T(8,128)(2,1)S(1)} %get-tuple-element.19), channel_id=1, source_target_pairs={{0,1},{1,0},{2,3},{3,2},{4,5},{5,4},{6,7},{7,6},{8,9},{9,8},{10,11... | collective-permute-start | bytes 786440 | tf_op jit(solution)/shard_map/ppermute | solution.py:283
  21.4 17.2 %copy-start = (bf16[16,2048]{1,0:T(8,128)(2,1)S(1)}, bf16[16,2048]{1,0:T(8,128)(2,1)}, u32[]{:S(2)}) copy-start(bf16[16,2048]{1,0:T(8,128)(2,1)} %residual_ref.1) | copy-start | bytes 196612
  23.0 2.5 %collective-permute-start.12 = (bf16[4,16,2048]{2,1,0:T(8,128)(2,1)S(1)}, bf16[4,16,2048]{2,1,0:T(8,128)(2,1)S(1)}, u32[]{:S(2)}, u32[]{:S(2)}) collective-permute-start(bf16[4,16,2048]{2,1,0:T(8,128)(2,1)S(1)} %get-tuple-element.25), channel_id=1, source_target_pairs={{0,1},{1,0},{2,3},{3,2},{4,5},{5,4},{6,7},{7,6},{8,9},{9,8},{10,11... | collective-permute-start | bytes 786440 | tf_op jit(solution)/shard_map/ppermute | solution.py:283
  23.4 5.4 %collective-permute-start.9 = (bf16[16,2048]{1,0:T(8,128)(2,1)S(1)}, bf16[16,2048]{1,0:T(8,128)(2,1)S(1)}, u32[]{:S(2)}, u32[]{:S(2)}) collective-permute-start(bf16[16,2048]{1,0:T(8,128)(2,1)S(1)} %get-tuple-element.23.refs_0_), channel_id=1, source_target_pairs={{0,2},{1,3},{2,0},{3,1},{4,6},{5,7},{6,4},{7,5},{8,10},{9,11},{10,... | collective-permute-start | bytes 196616 | tf_op jit(solution)/shard_map/ppermute | solution.py:283
  25.1 7.0 %collective-permute-start.8 = (bf16[16,2048]{1,0:T(8,128)(2,1)S(1)}, bf16[16,2048]{1,0:T(8,128)(2,1)S(1)}, u32[]{:S(2)}, u32[]{:S(2)}) collective-permute-start(bf16[16,2048]{1,0:T(8,128)(2,1)S(1)} %get-tuple-element.21), channel_id=1, source_target_pairs={{0,2},{1,3},{2,0},{3,1},{4,6},{5,7},{6,4},{7,5},{8,10},{9,11},{10,... | collective-permute-start | bytes 196616 | tf_op jit(solution)/shard_map/ppermute | solution.py:283
  25.5 13.2 %collective-permute-start.13 = (bf16[16,2048]{1,0:T(8,128)(2,1)S(1)}, bf16[16,2048]{1,0:T(8,128)(2,1)S(1)}, u32[]{:S(2)}, u32[]{:S(2)}) collective-permute-start(bf16[16,2048]{1,0:T(8,128)(2,1)S(1)} %get-tuple-element.27), channel_id=1, source_target_pairs={{0,6},{1,7},{2,4},{3,5},{4,2},{5,3},{6,0},{7,1},{8,14},{9,15},{10,... | collective-permute-start | bytes 196616 | tf_op jit(solution)/shard_map/ppermute | solution.py:283
  28.7 9.9 %collective-permute-start.10 = (bf16[16,2048]{1,0:T(8,128)(2,1)S(1)}, bf16[16,2048]{1,0:T(8,128)(2,1)S(1)}, u32[]{:S(2)}, u32[]{:S(2)}) collective-permute-start(bf16[16,2048]{1,0:T(8,128)(2,1)S(1)} %side_sum.2.refs_0_), channel_id=1, source_target_pairs={{0,12},{1,13},{2,14},{3,15},{4,8},{5,9},{6,10},{7,11},{8,4},{9,5},... | collective-permute-start | bytes 196616 | tf_op jit(solution)/shard_map/ppermute | solution.py:283
  32.1 6.6 %collective-permute-start.11 = (bf16[16,2048]{1,0:T(8,128)(2,1)S(1)}, bf16[16,2048]{1,0:T(8,128)(2,1)S(1)}, u32[]{:S(2)}, u32[]{:S(2)}) collective-permute-start(bf16[16,2048]{1,0:T(8,128)(2,1)S(1)} %side_sum.3.refs_6_), channel_id=1, source_target_pairs={{0,8},{1,9},{2,10},{3,11},{4,12},{5,13},{6,14},{7,15},{8,0},{9,1},... | collective-permute-start | bytes 196616 | tf_op jit(solution)/shard_map/ppermute | solution.py:283
  34.0 4.8 %collective-permute-start.14 = (bf16[16,2048]{1,0:T(8,128)(2,1)S(1)}, bf16[16,2048]{1,0:T(8,128)(2,1)S(1)}, u32[]{:S(2)}, u32[]{:S(2)}) collective-permute-start(bf16[16,2048]{1,0:T(8,128)(2,1)S(1)} %get-tuple-element.28), channel_id=1, source_target_pairs={{0,4},{1,5},{2,6},{3,7},{4,0},{5,1},{6,2},{7,3},{8,12},{9,13},{10,... | collective-permute-start | bytes 196616 | tf_op jit(solution)/shard_map/ppermute | solution.py:283
  34.2 4.6 %collective-permute-start.15 = (bf16[16,2048]{1,0:T(8,128)(2,1)S(1)}, bf16[16,2048]{1,0:T(8,128)(2,1)S(1)}, u32[]{:S(2)}, u32[]{:S(2)}) collective-permute-start(bf16[16,2048]{1,0:T(8,128)(2,1)S(1)} %get-tuple-element.29), channel_id=1, source_target_pairs={{0,2},{1,3},{2,0},{3,1},{4,6},{5,7},{6,4},{7,5},{8,10},{9,11},{10,... | collective-permute-start | bytes 196616 | tf_op jit(solution)/shard_map/ppermute | solution.py:283

commit v8 on v7

--- a/solution.py
+++ b/solution.py
@@ -297,7 +297,8 @@
     )
     third, second, first = (swap(packed, d * line) for d in (3, 2, 1))
     across = swap(packed, side)
-    along = stack((second, third, first))
+    attended = attend(*attention, (packed,))
+    along = stack((second, third, first), (stay(attended),))
     along_side = swap(along, side)
     near = stack((second, third, first, packed, across))
     near_far = swap(near, core)
@@ -334,7 +335,6 @@
         "partial_sum",
         (residual, swap(third_sum, 3 * line), swap(second_sum, 2 * line)),
     )
-    attended = attend(*attention, (second_sum,))
     late_outs = ffn([(3, 5), (2, 3)], [(2, 3)], early_outs[:1])
     own, across_sum, first_sum, diagonal_sum = in_vmem(
         pair_kernel,

time: 39.6 us -> 39.6 us (level)
  starting transfers between devices: 21.9 us -> 21.5 us
  transfers between devices with their start and end apart: 16 -> 16, of which waited for: 5 -> 6; matrix products, arithmetic and copies ran while one was open for 0% -> 0% of each run, Pallas kernels for 22% -> 22%
where the time goes in v8:
time: 39.6 us; the launch traced here: 39.4 us
  starting transfers between devices  21.5 us (54%)
  Pallas kernels  11.9 us (30%)
  waiting for transfers between devices  5.22 us (13%)
  between operations  0.75 us (2%)
    ppermute x16, starting transfers between devices, swap(): return lax.ppermute(value, 'ep', [(i, i ^ bits) for i in range(devices)])  21.5 us
    ppermute x16, waiting for transfers between devices, swap(): return lax.ppermute(value, 'ep', [(i, i ^ bits) for i in range(devices)])  5.22 us
    pallas_call x2, Pallas kernels, from_hbm(): pl.pallas_call(kernel, out_shape=out_shape, in_specs=[pl.BlockSpec(memory...  4.24 us
    pallas_call x11, Pallas kernels, in_vmem(): pl.pallas_call(kernel, out_shape=out_shape, in_specs=[HERE] * len(arrays)...  3.93 us
    pallas_call x1, Pallas kernels, hold(): pl.pallas_call(functools.partial(hold_kernel, len(flat), pieces), out_sha...  3.75 us
  transfers between devices with their start and end apart: 16, of which 6 were waited for; matrix products, arithmetic and copies ran while one was open for 0% of the time, Pallas kernels for 22%

profile of v8, /device:TPU:0, one launch (start us, length us, event | category | flops | bytes accessed | tf_op | source)
XLA Modules:
  0.0 39.4 jit_solution(6491047778864929177)
XLA Ops:
  0.6 1.0 %prepare.1.refs_6_.refs_3_ = bf16[16,2176]{1,0:T(8,128)(2,1)S(1)} custom-call(bf16[16,2048]{1,0:T(8,128)(2,1)} %residual_ref.1, f32[1,2048]{1,0:T(1,128)} %bitcast.13, s32[8,16]{1,0:T(8,128)} %bitcast.14, f32[8,16]{1,0:T(8,128)} %bitcast.15), custom_call_target="tpu_custom_call" | custom-call | tf_op jit(solution)/shard_map/prepare/pallas_call | solution.py:77
  1.7 4.1 %collective-permute-start = (bf16[16,2176]{1,0:T(8,128)(2,1)S(1)}, bf16[16,2176]{1,0:T(8,128)(2,1)S(1)}, u32[]{:S(2)}, u32[]{:S(2)}) collective-permute-start(bf16[16,2176]{1,0:T(8,128)(2,1)S(1)} %prepare.1.refs_6_.refs_3_), channel_id=1, source_target_pairs={{0,8},{1,9},{2,10},{3,11},{4,12},{5,13},{6,14},{7,15},{8,0},{9,1},... | collective-permute-start | bytes 208904 | tf_op jit(solution)/shard_map/ppermute | solution.py:283
  5.8 1.3 %collective-permute-start.1 = (bf16[16,2176]{1,0:T(8,128)(2,1)S(1)}, bf16[16,2176]{1,0:T(8,128)(2,1)S(1)}, u32[]{:S(2)}, u32[]{:S(2)}) collective-permute-start(bf16[16,2176]{1,0:T(8,128)(2,1)S(1)} %prepare.1.refs_6_.refs_3_), channel_id=1, source_target_pairs={{0,12},{1,13},{2,14},{3,15},{4,8},{5,9},{6,10},{7,11},{8,4},{9,5},... | collective-permute-start | bytes 208904 | tf_op jit(solution)/shard_map/ppermute | solution.py:283
  7.1 0.2 collective-permute-start.2
  7.4 1.5 %collective-permute-start.3 = (bf16[16,2176]{1,0:T(8,128)(2,1)S(1)}, bf16[16,2176]{1,0:T(8,128)(2,1)S(1)}, u32[]{:S(2)}, u32[]{:S(2)}) collective-permute-start(bf16[16,2176]{1,0:T(8,128)(2,1)S(1)} %prepare.1.refs_6_.refs_3_), channel_id=1, source_target_pairs={{0,2},{1,3},{2,0},{3,1},{4,6},{5,7},{6,4},{7,5},{8,10},{9,11},{10,... | collective-permute-start | bytes 208904 | tf_op jit(solution)/shard_map/ppermute | solution.py:283
  8.8 3.2 %attend.1.refs_3_ = bf16[4,32,128]{2,1,0:T(8,128)(2,1)} custom-call(s32[4]{0:T(128)} %refs_0_.3, bf16[4,32,128]{2,1,0:T(8,128)(2,1)} %refs_1_.1, bf16[4,256,128]{2,1,0:T(8,128)(2,1)} %bitcast.11, bf16[4,256,128]{2,1,0:T(8,128)(2,1)} %bitcast.12, bf16[8,128]{1,0:T(8,128)(2,1)} %bitcast.16, bf16[8,128]{1,0:T(8,128)(2,1)} %bitcast.17, ...), custom_call_target="tpu_custom_call" | custom-call | bytes 4194304 | tf_op jit(solution)/shard_map/attend/pallas_call | solution.py:77
  12.1 0.0 collective-permute-done.refs_0_
  12.1 0.0 collective-permute-done.1.refs_1_
  12.1 0.1 collective-permute-done.2.refs_2_
  12.2 1.7 %collective-permute-start.4 = (bf16[3,16,2176]{2,1,0:T(8,128)(2,1)S(1)}, bf16[3,16,2176]{2,1,0:T(8,128)(2,1)S(1)}, u32[]{:S(2)}, u32[]{:S(2)}) collective-permute-start(bf16[3,16,2176]{2,1,0:T(8,128)(2,1)S(1)} %stack.3.refs_2_), channel_id=1, source_target_pairs={{0,2},{1,3},{2,0},{3,1},{4,6},{5,7},{6,4},{7,5},{8,10},{9,11},{10,... | collective-permute-start | bytes 626696 | tf_op jit(solution)/shard_map/ppermute | solution.py:283
  13.9 0.0 collective-permute-done.3.refs_4_
  14.0 0.1 collective-permute-start.5
  14.0 3.8 %hold.1 = (bf16[4096,768]{1,0:T(8,128)(2,1)S(1)}, bf16[768,2048]{1,0:T(8,128)(2,1)S(1)}) custom-call(bf16[4096,768]{1,0:T(8,128)(2,1)} %bitcast.9, bf16[768,2048]{1,0:T(8,128)(2,1)} %bitcast.10, bf16[3,16,2176]{2,1,0:T(8,128)(2,1)S(1)} %stack.3.refs_2_), custom_call_target="tpu_custom_call" | custom-call | bytes 9437184 | tf_op jit(solution)/shard_map/hold/pallas_call | solution.py:170
  17.8 0.4 %collective-permute-done.4.in_ref.refs_1_ = bf16[3,16,2176]{2,1,0:T(8,128)(2,1)S(1)} collective-permute-done((bf16[3,16,2176]{2,1,0:T(8,128)(2,1)S(1)}, bf16[3,16,2176]{2,1,0:T(8,128)(2,1)S(1)}, u32[]{:S(2)}, u32[]{:S(2)}) %collective-permute-start.4) | collective-permute-done | bytes 208928 | tf_op jit(solution)/shard_map/ppermute | solution.py:283
  18.3 0.1 collective-permute-start.6
  18.4 0.0 collective-permute-done.5.refs_2_
  18.4 1.4 %collective-permute-done.6.refs_3_ = bf16[3,16,2176]{2,1,0:T(8,128)(2,1)S(1)} collective-permute-done((bf16[3,16,2176]{2,1,0:T(8,128)(2,1)S(1)}, bf16[3,16,2176]{2,1,0:T(8,128)(2,1)S(1)}, u32[]{:S(2)}, u32[]{:S(2)}) %collective-permute-start.6) | collective-permute-done | bytes 208928 | tf_op jit(solution)/shard_map/ppermute | solution.py:283
  19.8 1.5 %ffn.2 = (bf16[4,16,2048]{2,1,0:T(8,128)(2,1)S(1)}, bf16[4,16,2048]{2,1,0:T(8,128)(2,1)S(1)}) custom-call(bf16[5,16,2176]{2,1,0:T(8,128)(2,1)S(1)} %stack.2.refs_0_, bf16[3,16,2176]{2,1,0:T(8,128)(2,1)S(1)} %collective-permute-done.4.in_ref.refs_1_, bf16[5,16,2176]{2,1,0:T(8,128)(2,1)S(1)} %collective-permute-done.5.refs_2_, ...), custom_call_target="tpu_custom_call" | custom-call | flops 1207959552 | bytes 6291456 | tf_op jit(solution)/shard_map/ffn/pallas_call | solution.py:263
  21.3 0.0 copy-start
  21.3 0.2 collective-permute-start.7
  21.5 1.5 %ffn.3 = (bf16[4,16,2048]{2,1,0:T(8,128)(2,1)S(1)}, bf16[4,16,2048]{2,1,0:T(8,128)(2,1)S(1)}) custom-call(bf16[5,16,2176]{2,1,0:T(8,128)(2,1)S(1)} %stack.2.refs_0_, bf16[3,16,2176]{2,1,0:T(8,128)(2,1)S(1)} %collective-permute-done.4.in_ref.refs_1_, bf16[5,16,2176]{2,1,0:T(8,128)(2,1)S(1)} %collective-permute-done.5.refs_2_, ...), custom_call_target="tpu_custom_call" | custom-call | flops 1207959552 | bytes 6291456 | tf_op jit(solution)/shard_map/ffn/pallas_call | solution.py:263
  23.1 0.4 %collective-permute-start.12 = (bf16[4,16,2048]{2,1,0:T(8,128)(2,1)S(1)}, bf16[4,16,2048]{2,1,0:T(8,128)(2,1)S(1)}, u32[]{:S(2)}, u32[]{:S(2)}) collective-permute-start(bf16[4,16,2048]{2,1,0:T(8,128)(2,1)S(1)} %get-tuple-element.25), channel_id=1, source_target_pairs={{0,1},{1,0},{2,3},{3,2},{4,5},{5,4},{6,7},{7,6},{8,9},{9,8},{10,11... | collective-permute-start | bytes 786440 | tf_op jit(solution)/shard_map/ppermute | solution.py:283
  23.5 0.0 collective-permute-done.7.other_ref
  23.5 0.1 pair_sum.2
  23.6 1.5 %collective-permute-start.8 = (bf16[16,2048]{1,0:T(8,128)(2,1)S(1)}, bf16[16,2048]{1,0:T(8,128)(2,1)S(1)}, u32[]{:S(2)}, u32[]{:S(2)}) collective-permute-start(bf16[16,2048]{1,0:T(8,128)(2,1)S(1)} %get-tuple-element.21.refs_0_), channel_id=1, source_target_pairs={{0,2},{1,3},{2,0},{3,1},{4,6},{5,7},{6,4},{7,5},{8,10},{9,11},{10,... | collective-permute-start | bytes 196616 | tf_op jit(solution)/shard_map/ppermute | solution.py:283
  25.1 0.5 %collective-permute-start.10 = (bf16[16,2048]{1,0:T(8,128)(2,1)S(1)}, bf16[16,2048]{1,0:T(8,128)(2,1)S(1)}, u32[]{:S(2)}, u32[]{:S(2)}) collective-permute-start(bf16[16,2048]{1,0:T(8,128)(2,1)S(1)} %get-tuple-element.23), channel_id=1, source_target_pairs={{0,2},{1,3},{2,0},{3,1},{4,6},{5,7},{6,4},{7,5},{8,10},{9,11},{10,... | collective-permute-start | bytes 196616 | tf_op jit(solution)/shard_map/ppermute | solution.py:283
  25.7 0.0 collective-permute-done.12.other_ref
  25.7 0.1 pair_sum.3
  25.7 3.0 %collective-permute-start.13 = (bf16[16,2048]{1,0:T(8,128)(2,1)S(1)}, bf16[16,2048]{1,0:T(8,128)(2,1)S(1)}, u32[]{:S(2)}, u32[]{:S(2)}) collective-permute-start(bf16[16,2048]{1,0:T(8,128)(2,1)S(1)} %get-tuple-element.27), channel_id=1, source_target_pairs={{0,6},{1,7},{2,4},{3,5},{4,2},{5,3},{6,0},{7,1},{8,14},{9,15},{10,... | collective-permute-start | bytes 196616 | tf_op jit(solution)/shard_map/ppermute | solution.py:283
  28.7 0.0 collective-permute-done.8.other_ref
  28.7 3.3 %collective-permute-start.9 = (bf16[16,2048]{1,0:T(8,128)(2,1)S(1)}, bf16[16,2048]{1,0:T(8,128)(2,1)S(1)}, u32[]{:S(2)}, u32[]{:S(2)}) collective-permute-start(bf16[16,2048]{1,0:T(8,128)(2,1)S(1)} %side_sum.2.refs_0_), channel_id=1, source_target_pairs={{0,12},{1,13},{2,14},{3,15},{4,8},{5,9},{6,10},{7,11},{8,4},{9,5},... | collective-permute-start | bytes 196616 | tf_op jit(solution)/shard_map/ppermute | solution.py:283
  32.1 0.0 collective-permute-done.10.other_ref
  32.1 1.9 %collective-permute-start.11 = (bf16[16,2048]{1,0:T(8,128)(2,1)S(1)}, bf16[16,2048]{1,0:T(8,128)(2,1)S(1)}, u32[]{:S(2)}, u32[]{:S(2)}) collective-permute-start(bf16[16,2048]{1,0:T(8,128)(2,1)S(1)} %side_sum.3), channel_id=1, source_target_pairs={{0,8},{1,9},{2,10},{3,11},{4,12},{5,13},{6,14},{7,15},{8,0},{9,1},... | collective-permute-start | bytes 196616 | tf_op jit(solution)/shard_map/ppermute | solution.py:283
  34.0 0.2 collective-permute-start.14
  34.2 1.3 %collective-permute-start.15 = (bf16[16,2048]{1,0:T(8,128)(2,1)S(1)}, bf16[16,2048]{1,0:T(8,128)(2,1)S(1)}, u32[]{:S(2)}, u32[]{:S(2)}) collective-permute-start(bf16[16,2048]{1,0:T(8,128)(2,1)S(1)} %get-tuple-element.29), channel_id=1, source_target_pairs={{0,2},{1,3},{2,0},{3,1},{4,6},{5,7},{6,4},{7,5},{8,10},{9,11},{10,... | collective-permute-start | bytes 196616 | tf_op jit(solution)/shard_map/ppermute | solution.py:283
  35.5 0.3 collective-permute-done.9.refs_0_
  35.8 2.3 %collective-permute-done.11.refs_1_ = bf16[16,2048]{1,0:T(8,128)(2,1)S(1)} collective-permute-done((bf16[16,2048]{1,0:T(8,128)(2,1)S(1)}, bf16[16,2048]{1,0:T(8,128)(2,1)S(1)}, u32[]{:S(2)}, u32[]{:S(2)}) %collective-permute-start.11) | collective-permute-done | bytes 65568 | tf_op jit(solution)/shard_map/ppermute | solution.py:283
  38.1 0.0 copy-done
  38.1 0.0 collective-permute-done.13.refs_1_
  38.1 0.6 %collective-permute-done.14.refs_2_ = bf16[16,2048]{1,0:T(8,128)(2,1)S(1)} collective-permute-done((bf16[16,2048]{1,0:T(8,128)(2,1)S(1)}, bf16[16,2048]{1,0:T(8,128)(2,1)S(1)}, u32[]{:S(2)}, u32[]{:S(2)}) %collective-permute-start.14) | collective-permute-done | bytes 65568 | tf_op jit(solution)/shard_map/ppermute | solution.py:283
  38.7 0.0 collective-permute-done.15.refs_3_
  38.7 0.7 %total.1 = bf16[16,2048]{1,0:T(8,128)(2,1)} custom-call(f32[16,2048]{1,0:T(8,128)S(1)} %partial_sum.1.residual_ref, f32[16,2048]{1,0:T(8,128)S(1)} %get-tuple-element.26.refs_0_, bf16[16,2048]{1,0:T(8,128)(2,1)S(1)} %collective-permute-done.13.refs_1_, bf16[16,2048]{1,0:T(8,128)(2,1)S(1)} %collective-permute-done.14.refs_2_, ...), custom_call_target="tpu_custom_call" | custom-call | tf_op jit(solution)/shard_map/total/pallas_call | solution.py:263
  (6 shorter events, 0.1 us)
Async XLA Ops:
  1.7 10.4 %collective-permute-start = (bf16[16,2176]{1,0:T(8,128)(2,1)S(1)}, bf16[16,2176]{1,0:T(8,128)(2,1)S(1)}, u32[]{:S(2)}, u32[]{:S(2)}) collective-permute-start(bf16[16,2176]{1,0:T(8,128)(2,1)S(1)} %prepare.1.refs_6_.refs_3_), channel_id=1, source_target_pairs={{0,8},{1,9},{2,10},{3,11},{4,12},{5,13},{6,14},{7,15},{8,0},{9,1},... | collective-permute-start | bytes 208904 | tf_op jit(solution)/shard_map/ppermute | solution.py:283
  5.8 6.3 %collective-permute-start.1 = (bf16[16,2176]{1,0:T(8,128)(2,1)S(1)}, bf16[16,2176]{1,0:T(8,128)(2,1)S(1)}, u32[]{:S(2)}, u32[]{:S(2)}) collective-permute-start(bf16[16,2176]{1,0:T(8,128)(2,1)S(1)} %prepare.1.refs_6_.refs_3_), channel_id=1, source_target_pairs={{0,12},{1,13},{2,14},{3,15},{4,8},{5,9},{6,10},{7,11},{8,4},{9,5},... | collective-permute-start | bytes 208904 | tf_op jit(solution)/shard_map/ppermute | solution.py:283
  7.1 5.1 %collective-permute-start.2 = (bf16[16,2176]{1,0:T(8,128)(2,1)S(1)}, bf16[16,2176]{1,0:T(8,128)(2,1)S(1)}, u32[]{:S(2)}, u32[]{:S(2)}) collective-permute-start(bf16[16,2176]{1,0:T(8,128)(2,1)S(1)} %prepare.1.refs_6_.refs_3_), channel_id=1, source_target_pairs={{0,4},{1,5},{2,6},{3,7},{4,0},{5,1},{6,2},{7,3},{8,12},{9,13},{10,... | collective-permute-start | bytes 208904 | tf_op jit(solution)/shard_map/ppermute | solution.py:283
  7.4 6.6 %collective-permute-start.3 = (bf16[16,2176]{1,0:T(8,128)(2,1)S(1)}, bf16[16,2176]{1,0:T(8,128)(2,1)S(1)}, u32[]{:S(2)}, u32[]{:S(2)}) collective-permute-start(bf16[16,2176]{1,0:T(8,128)(2,1)S(1)} %prepare.1.refs_6_.refs_3_), channel_id=1, source_target_pairs={{0,2},{1,3},{2,0},{3,1},{4,6},{5,7},{6,4},{7,5},{8,10},{9,11},{10,... | collective-permute-start | bytes 208904 | tf_op jit(solution)/shard_map/ppermute | solution.py:283
  12.2 6.0 %collective-permute-start.4 = (bf16[3,16,2176]{2,1,0:T(8,128)(2,1)S(1)}, bf16[3,16,2176]{2,1,0:T(8,128)(2,1)S(1)}, u32[]{:S(2)}, u32[]{:S(2)}) collective-permute-start(bf16[3,16,2176]{2,1,0:T(8,128)(2,1)S(1)} %stack.3.refs_2_), channel_id=1, source_target_pairs={{0,2},{1,3},{2,0},{3,1},{4,6},{5,7},{6,4},{7,5},{8,10},{9,11},{10,... | collective-permute-start | bytes 626696 | tf_op jit(solution)/shard_map/ppermute | solution.py:283
  14.0 4.4 %collective-permute-start.5 = (bf16[5,16,2176]{2,1,0:T(8,128)(2,1)S(1)}, bf16[5,16,2176]{2,1,0:T(8,128)(2,1)S(1)}, u32[]{:S(2)}, u32[]{:S(2)}) collective-permute-start(bf16[5,16,2176]{2,1,0:T(8,128)(2,1)S(1)} %stack.2.refs_0_), channel_id=1, source_target_pairs={{0,1},{1,0},{2,3},{3,2},{4,5},{5,4},{6,7},{7,6},{8,9},{9,8},{10,11... | collective-permute-start | bytes 1044488 | tf_op jit(solution)/shard_map/ppermute | solution.py:283
  18.3 1.5 %collective-permute-start.6 = (bf16[3,16,2176]{2,1,0:T(8,128)(2,1)S(1)}, bf16[3,16,2176]{2,1,0:T(8,128)(2,1)S(1)}, u32[]{:S(2)}, u32[]{:S(2)}) collective-permute-start(bf16[3,16,2176]{2,1,0:T(8,128)(2,1)S(1)} %relay.1), channel_id=1, source_target_pairs={{0,1},{1,0},{2,3},{3,2},{4,5},{5,4},{6,7},{7,6},{8,9},{9,8},{10,11... | collective-permute-start | bytes 626696 | tf_op jit(solution)/shard_map/ppermute | solution.py:283
  21.3 16.8 %copy-start = (bf16[16,2048]{1,0:T(8,128)(2,1)S(1)}, bf16[16,2048]{1,0:T(8,128)(2,1)}, u32[]{:S(2)}) copy-start(bf16[16,2048]{1,0:T(8,128)(2,1)} %residual_ref.1) | copy-start | bytes 196612
  21.3 2.2 %collective-permute-start.7 = (bf16[4,16,2048]{2,1,0:T(8,128)(2,1)S(1)}, bf16[4,16,2048]{2,1,0:T(8,128)(2,1)S(1)}, u32[]{:S(2)}, u32[]{:S(2)}) collective-permute-start(bf16[4,16,2048]{2,1,0:T(8,128)(2,1)S(1)} %get-tuple-element.19), channel_id=1, source_target_pairs={{0,1},{1,0},{2,3},{3,2},{4,5},{5,4},{6,7},{7,6},{8,9},{9,8},{10,11... | collective-permute-start | bytes 786440 | tf_op jit(solution)/shard_map/ppermute | solution.py:283
  23.1 2.6 %collective-permute-start.12 = (bf16[4,16,2048]{2,1,0:T(8,128)(2,1)S(1)}, bf16[4,16,2048]{2,1,0:T(8,128)(2,1)S(1)}, u32[]{:S(2)}, u32[]{:S(2)}) collective-permute-start(bf16[4,16,2048]{2,1,0:T(8,128)(2,1)S(1)} %get-tuple-element.25), channel_id=1, source_target_pairs={{0,1},{1,0},{2,3},{3,2},{4,5},{5,4},{6,7},{7,6},{8,9},{9,8},{10,11... | collective-permute-start | bytes 786440 | tf_op jit(solution)/shard_map/ppermute | solution.py:283
  23.6 5.2 %collective-permute-start.8 = (bf16[16,2048]{1,0:T(8,128)(2,1)S(1)}, bf16[16,2048]{1,0:T(8,128)(2,1)S(1)}, u32[]{:S(2)}, u32[]{:S(2)}) collective-permute-start(bf16[16,2048]{1,0:T(8,128)(2,1)S(1)} %get-tuple-element.21.refs_0_), channel_id=1, source_target_pairs={{0,2},{1,3},{2,0},{3,1},{4,6},{5,7},{6,4},{7,5},{8,10},{9,11},{10,... | collective-permute-start | bytes 196616 | tf_op jit(solution)/shard_map/ppermute | solution.py:283
  25.1 7.0 %collective-permute-start.10 = (bf16[16,2048]{1,0:T(8,128)(2,1)S(1)}, bf16[16,2048]{1,0:T(8,128)(2,1)S(1)}, u32[]{:S(2)}, u32[]{:S(2)}) collective-permute-start(bf16[16,2048]{1,0:T(8,128)(2,1)S(1)} %get-tuple-element.23), channel_id=1, source_target_pairs={{0,2},{1,3},{2,0},{3,1},{4,6},{5,7},{6,4},{7,5},{8,10},{9,11},{10,... | collective-permute-start | bytes 196616 | tf_op jit(solution)/shard_map/ppermute | solution.py:283
  25.7 12.4 %collective-permute-start.13 = (bf16[16,2048]{1,0:T(8,128)(2,1)S(1)}, bf16[16,2048]{1,0:T(8,128)(2,1)S(1)}, u32[]{:S(2)}, u32[]{:S(2)}) collective-permute-start(bf16[16,2048]{1,0:T(8,128)(2,1)S(1)} %get-tuple-element.27), channel_id=1, source_target_pairs={{0,6},{1,7},{2,4},{3,5},{4,2},{5,3},{6,0},{7,1},{8,14},{9,15},{10,... | collective-permute-start | bytes 196616 | tf_op jit(solution)/shard_map/ppermute | solution.py:283
  28.7 7.0 %collective-permute-start.9 = (bf16[16,2048]{1,0:T(8,128)(2,1)S(1)}, bf16[16,2048]{1,0:T(8,128)(2,1)S(1)}, u32[]{:S(2)}, u32[]{:S(2)}) collective-permute-start(bf16[16,2048]{1,0:T(8,128)(2,1)S(1)} %side_sum.2.refs_0_), channel_id=1, source_target_pairs={{0,12},{1,13},{2,14},{3,15},{4,8},{5,9},{6,10},{7,11},{8,4},{9,5},... | collective-permute-start | bytes 196616 | tf_op jit(solution)/shard_map/ppermute | solution.py:283
  32.1 6.0 %collective-permute-start.11 = (bf16[16,2048]{1,0:T(8,128)(2,1)S(1)}, bf16[16,2048]{1,0:T(8,128)(2,1)S(1)}, u32[]{:S(2)}, u32[]{:S(2)}) collective-permute-start(bf16[16,2048]{1,0:T(8,128)(2,1)S(1)} %side_sum.3), channel_id=1, source_target_pairs={{0,8},{1,9},{2,10},{3,11},{4,12},{5,13},{6,14},{7,15},{8,0},{9,1},... | collective-permute-start | bytes 196616 | tf_op jit(solution)/shard_map/ppermute | solution.py:283
  34.0 4.7 %collective-permute-start.14 = (bf16[16,2048]{1,0:T(8,128)(2,1)S(1)}, bf16[16,2048]{1,0:T(8,128)(2,1)S(1)}, u32[]{:S(2)}, u32[]{:S(2)}) collective-permute-start(bf16[16,2048]{1,0:T(8,128)(2,1)S(1)} %get-tuple-element.28), channel_id=1, source_target_pairs={{0,4},{1,5},{2,6},{3,7},{4,0},{5,1},{6,2},{7,3},{8,12},{9,13},{10,... | collective-permute-start | bytes 196616 | tf_op jit(solution)/shard_map/ppermute | solution.py:283
  34.2 4.6 %collective-permute-start.15 = (bf16[16,2048]{1,0:T(8,128)(2,1)S(1)}, bf16[16,2048]{1,0:T(8,128)(2,1)S(1)}, u32[]{:S(2)}, u32[]{:S(2)}) collective-permute-start(bf16[16,2048]{1,0:T(8,128)(2,1)S(1)} %get-tuple-element.29), channel_id=1, source_target_pairs={{0,2},{1,3},{2,0},{3,1},{4,6},{5,7},{6,4},{7,5},{8,10},{9,11},{10,... | collective-permute-start | bytes 196616 | tf_op jit(solution)/shard_map/ppermute | solution.py:283

commit v9 on v8

--- a/solution.py
+++ b/solution.py
@@ -341,7 +341,7 @@
         [vmem(one, jnp.float32), send, send, send],
         "pair_sum",
         (late_outs[0], swap(late_outs[1], core)),
-        (third_send,),
+        (second_sum,),
     )
     moe_out = in_vmem(
         total_kernel,

time: 39.6 us -> 41.2 us (1.040)
  waiting for transfers between devices: 5.22 us -> 8.05 us
  starting transfers between devices: 21.5 us -> 20.3 us
    ppermute x16, waiting for transfers between devices: 5.22 us -> 8.05 us  [swap(): return lax.ppermute(value, 'ep', [(i, i ^ bits) for i in range(devices)])]
    ppermute x16, starting transfers between devices: 21.5 us -> 20.3 us  [swap(): return lax.ppermute(value, 'ep', [(i, i ^ bits) for i in range(devices)])]
  transfers between devices with their start and end apart: 16 -> 16, of which waited for: 6 -> 8; matrix products, arithmetic and copies ran while one was open for 0% -> 0% of each run, Pallas kernels for 22% -> 21%
where the time goes in v9:
time: 41.2 us; the launch traced here: 41.1 us
  starting transfers between devices  20.3 us (49%)
  Pallas kernels  11.9 us (29%)
  waiting for transfers between devices  8.05 us (20%)
  between operations  0.74 us (2%)
    ppermute x16, starting transfers between devices, swap(): return lax.ppermute(value, 'ep', [(i, i ^ bits) for i in range(devices)])  20.3 us
    ppermute x16, waiting for transfers between devices, swap(): return lax.ppermute(value, 'ep', [(i, i ^ bits) for i in range(devices)])  8.05 us
    pallas_call x2, Pallas kernels, from_hbm(): pl.pallas_call(kernel, out_shape=out_shape, in_specs=[pl.BlockSpec(memory...  4.24 us
    pallas_call x11, Pallas kernels, in_vmem(): pl.pallas_call(kernel, out_shape=out_shape, in_specs=[HERE] * len(arrays)...  3.93 us
    pallas_call x1, Pallas kernels, hold(): pl.pallas_call(functools.partial(hold_kernel, len(flat), pieces), out_sha...  3.75 us
  transfers between devices with their start and end apart: 16, of which 8 were waited for; matrix products, arithmetic and copies ran while one was open for 0% of the time, Pallas kernels for 21%

profile of v9, /device:TPU:0, one launch (start us, length us, event | category | flops | bytes accessed | tf_op | source)
XLA Modules:
  0.0 41.1 jit_solution(3877247528677377595)
XLA Ops:
  0.6 1.0 %prepare.1.refs_6_.refs_3_ = bf16[16,2176]{1,0:T(8,128)(2,1)S(1)} custom-call(bf16[16,2048]{1,0:T(8,128)(2,1)} %residual_ref.1, f32[1,2048]{1,0:T(1,128)} %bitcast.13, s32[8,16]{1,0:T(8,128)} %bitcast.14, f32[8,16]{1,0:T(8,128)} %bitcast.15), custom_call_target="tpu_custom_call" | custom-call | tf_op jit(solution)/shard_map/prepare/pallas_call | solution.py:77
  1.7 4.1 %collective-permute-start = (bf16[16,2176]{1,0:T(8,128)(2,1)S(1)}, bf16[16,2176]{1,0:T(8,128)(2,1)S(1)}, u32[]{:S(2)}, u32[]{:S(2)}) collective-permute-start(bf16[16,2176]{1,0:T(8,128)(2,1)S(1)} %prepare.1.refs_6_.refs_3_), channel_id=1, source_target_pairs={{0,8},{1,9},{2,10},{3,11},{4,12},{5,13},{6,14},{7,15},{8,0},{9,1},... | collective-permute-start | bytes 208904 | tf_op jit(solution)/shard_map/ppermute | solution.py:283
  5.8 1.3 %collective-permute-start.1 = (bf16[16,2176]{1,0:T(8,128)(2,1)S(1)}, bf16[16,2176]{1,0:T(8,128)(2,1)S(1)}, u32[]{:S(2)}, u32[]{:S(2)}) collective-permute-start(bf16[16,2176]{1,0:T(8,128)(2,1)S(1)} %prepare.1.refs_6_.refs_3_), channel_id=1, source_target_pairs={{0,12},{1,13},{2,14},{3,15},{4,8},{5,9},{6,10},{7,11},{8,4},{9,5},... | collective-permute-start | bytes 208904 | tf_op jit(solution)/shard_map/ppermute | solution.py:283
  7.1 0.2 collective-permute-start.2
  7.4 1.5 %collective-permute-start.3 = (bf16[16,2176]{1,0:T(8,128)(2,1)S(1)}, bf16[16,2176]{1,0:T(8,128)(2,1)S(1)}, u32[]{:S(2)}, u32[]{:S(2)}) collective-permute-start(bf16[16,2176]{1,0:T(8,128)(2,1)S(1)} %prepare.1.refs_6_.refs_3_), channel_id=1, source_target_pairs={{0,2},{1,3},{2,0},{3,1},{4,6},{5,7},{6,4},{7,5},{8,10},{9,11},{10,... | collective-permute-start | bytes 208904 | tf_op jit(solution)/shard_map/ppermute | solution.py:283
  8.8 3.2 %attend.1.refs_3_ = bf16[4,32,128]{2,1,0:T(8,128)(2,1)} custom-call(s32[4]{0:T(128)} %refs_0_.3, bf16[4,32,128]{2,1,0:T(8,128)(2,1)} %refs_1_.1, bf16[4,256,128]{2,1,0:T(8,128)(2,1)} %bitcast.11, bf16[4,256,128]{2,1,0:T(8,128)(2,1)} %bitcast.12, bf16[8,128]{1,0:T(8,128)(2,1)} %bitcast.16, bf16[8,128]{1,0:T(8,128)(2,1)} %bitcast.17, ...), custom_call_target="tpu_custom_call" | custom-call | bytes 4194304 | tf_op jit(solution)/shard_map/attend/pallas_call | solution.py:77
  12.1 0.0 collective-permute-done.refs_0_
  12.1 0.0 collective-permute-done.1.refs_1_
  12.1 0.1 collective-permute-done.2.refs_2_
  12.2 1.7 %collective-permute-start.4 = (bf16[3,16,2176]{2,1,0:T(8,128)(2,1)S(1)}, bf16[3,16,2176]{2,1,0:T(8,128)(2,1)S(1)}, u32[]{:S(2)}, u32[]{:S(2)}) collective-permute-start(bf16[3,16,2176]{2,1,0:T(8,128)(2,1)S(1)} %stack.3.refs_2_), channel_id=1, source_target_pairs={{0,2},{1,3},{2,0},{3,1},{4,6},{5,7},{6,4},{7,5},{8,10},{9,11},{10,... | collective-permute-start | bytes 626696 | tf_op jit(solution)/shard_map/ppermute | solution.py:283
  13.9 0.0 collective-permute-done.3.refs_4_
  14.0 0.1 collective-permute-start.5
  14.0 3.8 %hold.1 = (bf16[4096,768]{1,0:T(8,128)(2,1)S(1)}, bf16[768,2048]{1,0:T(8,128)(2,1)S(1)}) custom-call(bf16[4096,768]{1,0:T(8,128)(2,1)} %bitcast.9, bf16[768,2048]{1,0:T(8,128)(2,1)} %bitcast.10, bf16[3,16,2176]{2,1,0:T(8,128)(2,1)S(1)} %stack.3.refs_2_), custom_call_target="tpu_custom_call" | custom-call | bytes 9437184 | tf_op jit(solution)/shard_map/hold/pallas_call | solution.py:170
  17.8 0.4 %collective-permute-done.4.in_ref.refs_1_ = bf16[3,16,2176]{2,1,0:T(8,128)(2,1)S(1)} collective-permute-done((bf16[3,16,2176]{2,1,0:T(8,128)(2,1)S(1)}, bf16[3,16,2176]{2,1,0:T(8,128)(2,1)S(1)}, u32[]{:S(2)}, u32[]{:S(2)}) %collective-permute-start.4) | collective-permute-done | bytes 208928 | tf_op jit(solution)/shard_map/ppermute | solution.py:283
  18.3 0.1 collective-permute-start.6
  18.4 0.0 collective-permute-done.5.refs_2_
  18.4 1.4 %collective-permute-done.6.refs_3_ = bf16[3,16,2176]{2,1,0:T(8,128)(2,1)S(1)} collective-permute-done((bf16[3,16,2176]{2,1,0:T(8,128)(2,1)S(1)}, bf16[3,16,2176]{2,1,0:T(8,128)(2,1)S(1)}, u32[]{:S(2)}, u32[]{:S(2)}) %collective-permute-start.6) | collective-permute-done | bytes 208928 | tf_op jit(solution)/shard_map/ppermute | solution.py:283
  19.8 1.5 %ffn.2 = (bf16[4,16,2048]{2,1,0:T(8,128)(2,1)S(1)}, bf16[4,16,2048]{2,1,0:T(8,128)(2,1)S(1)}) custom-call(bf16[5,16,2176]{2,1,0:T(8,128)(2,1)S(1)} %stack.2.refs_0_, bf16[3,16,2176]{2,1,0:T(8,128)(2,1)S(1)} %collective-permute-done.4.in_ref.refs_1_, bf16[5,16,2176]{2,1,0:T(8,128)(2,1)S(1)} %collective-permute-done.5.refs_2_, ...), custom_call_target="tpu_custom_call" | custom-call | flops 1207959552 | bytes 6291456 | tf_op jit(solution)/shard_map/ffn/pallas_call | solution.py:263
  21.3 0.0 copy-start
  21.3 0.2 collective-permute-start.7
  21.5 1.5 %ffn.3 = (bf16[4,16,2048]{2,1,0:T(8,128)(2,1)S(1)}, bf16[4,16,2048]{2,1,0:T(8,128)(2,1)S(1)}) custom-call(bf16[5,16,2176]{2,1,0:T(8,128)(2,1)S(1)} %stack.2.refs_0_, bf16[3,16,2176]{2,1,0:T(8,128)(2,1)S(1)} %collective-permute-done.4.in_ref.refs_1_, bf16[5,16,2176]{2,1,0:T(8,128)(2,1)S(1)} %collective-permute-done.5.refs_2_, ...), custom_call_target="tpu_custom_call" | custom-call | flops 1207959552 | bytes 6291456 | tf_op jit(solution)/shard_map/ffn/pallas_call | solution.py:263
  23.1 0.4 %collective-permute-start.12 = (bf16[4,16,2048]{2,1,0:T(8,128)(2,1)S(1)}, bf16[4,16,2048]{2,1,0:T(8,128)(2,1)S(1)}, u32[]{:S(2)}, u32[]{:S(2)}) collective-permute-start(bf16[4,16,2048]{2,1,0:T(8,128)(2,1)S(1)} %get-tuple-element.25), channel_id=1, source_target_pairs={{0,1},{1,0},{2,3},{3,2},{4,5},{5,4},{6,7},{7,6},{8,9},{9,8},{10,11... | collective-permute-start | bytes 786440 | tf_op jit(solution)/shard_map/ppermute | solution.py:283
  23.5 0.0 collective-permute-done.7.other_ref
  23.5 0.1 pair_sum.2
  23.6 1.5 %collective-permute-start.8 = (bf16[16,2048]{1,0:T(8,128)(2,1)S(1)}, bf16[16,2048]{1,0:T(8,128)(2,1)S(1)}, u32[]{:S(2)}, u32[]{:S(2)}) collective-permute-start(bf16[16,2048]{1,0:T(8,128)(2,1)S(1)} %get-tuple-element.21), channel_id=1, source_target_pairs={{0,2},{1,3},{2,0},{3,1},{4,6},{5,7},{6,4},{7,5},{8,10},{9,11},{10,... | collective-permute-start | bytes 196616 | tf_op jit(solution)/shard_map/ppermute | solution.py:283
  25.1 0.5 %collective-permute-start.10 = (bf16[16,2048]{1,0:T(8,128)(2,1)S(1)}, bf16[16,2048]{1,0:T(8,128)(2,1)S(1)}, u32[]{:S(2)}, u32[]{:S(2)}) collective-permute-start(bf16[16,2048]{1,0:T(8,128)(2,1)S(1)} %get-tuple-element.23), channel_id=1, source_target_pairs={{0,2},{1,3},{2,0},{3,1},{4,6},{5,7},{6,4},{7,5},{8,10},{9,11},{10,... | collective-permute-start | bytes 196616 | tf_op jit(solution)/shard_map/ppermute | solution.py:283
  25.7 2.7 %collective-permute-done.8.other_ref = bf16[16,2048]{1,0:T(8,128)(2,1)S(1)} collective-permute-done((bf16[16,2048]{1,0:T(8,128)(2,1)S(1)}, bf16[16,2048]{1,0:T(8,128)(2,1)S(1)}, u32[]{:S(2)}, u32[]{:S(2)}) %collective-permute-start.8) | collective-permute-done | bytes 65568 | tf_op jit(solution)/shard_map/ppermute | solution.py:283
  28.3 3.5 %collective-permute-start.9 = (bf16[16,2048]{1,0:T(8,128)(2,1)S(1)}, bf16[16,2048]{1,0:T(8,128)(2,1)S(1)}, u32[]{:S(2)}, u32[]{:S(2)}) collective-permute-start(bf16[16,2048]{1,0:T(8,128)(2,1)S(1)} %side_sum.2.refs_0_), channel_id=1, source_target_pairs={{0,12},{1,13},{2,14},{3,15},{4,8},{5,9},{6,10},{7,11},{8,4},{9,5},... | collective-permute-start | bytes 196616 | tf_op jit(solution)/shard_map/ppermute | solution.py:283
  31.8 0.0 collective-permute-done.10.other_ref
  31.8 1.5 %collective-permute-start.11 = (bf16[16,2048]{1,0:T(8,128)(2,1)S(1)}, bf16[16,2048]{1,0:T(8,128)(2,1)S(1)}, u32[]{:S(2)}, u32[]{:S(2)}) collective-permute-start(bf16[16,2048]{1,0:T(8,128)(2,1)S(1)} %side_sum.3.refs_0_), channel_id=1, source_target_pairs={{0,8},{1,9},{2,10},{3,11},{4,12},{5,13},{6,14},{7,15},{8,0},{9,1},... | collective-permute-start | bytes 196616 | tf_op jit(solution)/shard_map/ppermute | solution.py:283
  33.3 0.0 collective-permute-done.12.other_ref
  33.3 0.1 pair_sum.3
  33.4 1.0 %collective-permute-start.13 = (bf16[16,2048]{1,0:T(8,128)(2,1)S(1)}, bf16[16,2048]{1,0:T(8,128)(2,1)S(1)}, u32[]{:S(2)}, u32[]{:S(2)}) collective-permute-start(bf16[16,2048]{1,0:T(8,128)(2,1)S(1)} %get-tuple-element.27), channel_id=1, source_target_pairs={{0,6},{1,7},{2,4},{3,5},{4,2},{5,3},{6,0},{7,1},{8,14},{9,15},{10,... | collective-permute-start | bytes 196616 | tf_op jit(solution)/shard_map/ppermute | solution.py:283
  34.3 1.8 %collective-permute-start.14 = (bf16[16,2048]{1,0:T(8,128)(2,1)S(1)}, bf16[16,2048]{1,0:T(8,128)(2,1)S(1)}, u32[]{:S(2)}, u32[]{:S(2)}) collective-permute-start(bf16[16,2048]{1,0:T(8,128)(2,1)S(1)} %get-tuple-element.28), channel_id=1, source_target_pairs={{0,4},{1,5},{2,6},{3,7},{4,0},{5,1},{6,2},{7,3},{8,12},{9,13},{10,... | collective-permute-start | bytes 196616 | tf_op jit(solution)/shard_map/ppermute | solution.py:283
  36.1 0.8 %collective-permute-start.15 = (bf16[16,2048]{1,0:T(8,128)(2,1)S(1)}, bf16[16,2048]{1,0:T(8,128)(2,1)S(1)}, u32[]{:S(2)}, u32[]{:S(2)}) collective-permute-start(bf16[16,2048]{1,0:T(8,128)(2,1)S(1)} %get-tuple-element.29), channel_id=1, source_target_pairs={{0,2},{1,3},{2,0},{3,1},{4,6},{5,7},{6,4},{7,5},{8,10},{9,11},{10,... | collective-permute-start | bytes 196616 | tf_op jit(solution)/shard_map/ppermute | solution.py:283
  36.9 0.0 collective-permute-done.9.refs_0_
  36.9 0.8 %collective-permute-done.11.refs_1_ = bf16[16,2048]{1,0:T(8,128)(2,1)S(1)} collective-permute-done((bf16[16,2048]{1,0:T(8,128)(2,1)S(1)}, bf16[16,2048]{1,0:T(8,128)(2,1)S(1)}, u32[]{:S(2)}, u32[]{:S(2)}) %collective-permute-start.11) | collective-permute-done | bytes 65568 | tf_op jit(solution)/shard_map/ppermute | solution.py:283
  37.7 0.0 copy-done
  37.8 1.4 %collective-permute-done.13.refs_1_ = bf16[16,2048]{1,0:T(8,128)(2,1)S(1)} collective-permute-done((bf16[16,2048]{1,0:T(8,128)(2,1)S(1)}, bf16[16,2048]{1,0:T(8,128)(2,1)S(1)}, u32[]{:S(2)}, u32[]{:S(2)}) %collective-permute-start.13) | collective-permute-done | bytes 65568 | tf_op jit(solution)/shard_map/ppermute | solution.py:283
  39.2 0.4 collective-permute-done.14.refs_2_
  39.6 0.8 %collective-permute-done.15.refs_3_ = bf16[16,2048]{1,0:T(8,128)(2,1)S(1)} collective-permute-done((bf16[16,2048]{1,0:T(8,128)(2,1)S(1)}, bf16[16,2048]{1,0:T(8,128)(2,1)S(1)}, u32[]{:S(2)}, u32[]{:S(2)}) %collective-permute-start.15) | collective-permute-done | bytes 65568 | tf_op jit(solution)/shard_map/ppermute | solution.py:283
  40.4 0.7 %total.1 = bf16[16,2048]{1,0:T(8,128)(2,1)} custom-call(f32[16,2048]{1,0:T(8,128)S(1)} %partial_sum.1.residual_ref, f32[16,2048]{1,0:T(8,128)S(1)} %get-tuple-element.26.refs_0_, bf16[16,2048]{1,0:T(8,128)(2,1)S(1)} %collective-permute-done.13.refs_1_, bf16[16,2048]{1,0:T(8,128)(2,1)S(1)} %collective-permute-done.14.refs_2_, ...), custom_call_target="tpu_custom_call" | custom-call | tf_op jit(solution)/shard_map/total/pallas_call | solution.py:263
  (6 shorter events, 0.1 us)
Async XLA Ops:
  1.7 10.4 %collective-permute-start = (bf16[16,2176]{1,0:T(8,128)(2,1)S(1)}, bf16[16,2176]{1,0:T(8,128)(2,1)S(1)}, u32[]{:S(2)}, u32[]{:S(2)}) collective-permute-start(bf16[16,2176]{1,0:T(8,128)(2,1)S(1)} %prepare.1.refs_6_.refs_3_), channel_id=1, source_target_pairs={{0,8},{1,9},{2,10},{3,11},{4,12},{5,13},{6,14},{7,15},{8,0},{9,1},... | collective-permute-start | bytes 208904 | tf_op jit(solution)/shard_map/ppermute | solution.py:283
  5.8 6.3 %collective-permute-start.1 = (bf16[16,2176]{1,0:T(8,128)(2,1)S(1)}, bf16[16,2176]{1,0:T(8,128)(2,1)S(1)}, u32[]{:S(2)}, u32[]{:S(2)}) collective-permute-start(bf16[16,2176]{1,0:T(8,128)(2,1)S(1)} %prepare.1.refs_6_.refs_3_), channel_id=1, source_target_pairs={{0,12},{1,13},{2,14},{3,15},{4,8},{5,9},{6,10},{7,11},{8,4},{9,5},... | collective-permute-start | bytes 208904 | tf_op jit(solution)/shard_map/ppermute | solution.py:283
  7.1 5.1 %collective-permute-start.2 = (bf16[16,2176]{1,0:T(8,128)(2,1)S(1)}, bf16[16,2176]{1,0:T(8,128)(2,1)S(1)}, u32[]{:S(2)}, u32[]{:S(2)}) collective-permute-start(bf16[16,2176]{1,0:T(8,128)(2,1)S(1)} %prepare.1.refs_6_.refs_3_), channel_id=1, source_target_pairs={{0,4},{1,5},{2,6},{3,7},{4,0},{5,1},{6,2},{7,3},{8,12},{9,13},{10,... | collective-permute-start | bytes 208904 | tf_op jit(solution)/shard_map/ppermute | solution.py:283
  7.4 6.6 %collective-permute-start.3 = (bf16[16,2176]{1,0:T(8,128)(2,1)S(1)}, bf16[16,2176]{1,0:T(8,128)(2,1)S(1)}, u32[]{:S(2)}, u32[]{:S(2)}) collective-permute-start(bf16[16,2176]{1,0:T(8,128)(2,1)S(1)} %prepare.1.refs_6_.refs_3_), channel_id=1, source_target_pairs={{0,2},{1,3},{2,0},{3,1},{4,6},{5,7},{6,4},{7,5},{8,10},{9,11},{10,... | collective-permute-start | bytes 208904 | tf_op jit(solution)/shard_map/ppermute | solution.py:283
  12.2 6.0 %collective-permute-start.4 = (bf16[3,16,2176]{2,1,0:T(8,128)(2,1)S(1)}, bf16[3,16,2176]{2,1,0:T(8,128)(2,1)S(1)}, u32[]{:S(2)}, u32[]{:S(2)}) collective-permute-start(bf16[3,16,2176]{2,1,0:T(8,128)(2,1)S(1)} %stack.3.refs_2_), channel_id=1, source_target_pairs={{0,2},{1,3},{2,0},{3,1},{4,6},{5,7},{6,4},{7,5},{8,10},{9,11},{10,... | collective-permute-start | bytes 626696 | tf_op jit(solution)/shard_map/ppermute | solution.py:283
  14.0 4.4 %collective-permute-start.5 = (bf16[5,16,2176]{2,1,0:T(8,128)(2,1)S(1)}, bf16[5,16,2176]{2,1,0:T(8,128)(2,1)S(1)}, u32[]{:S(2)}, u32[]{:S(2)}) collective-permute-start(bf16[5,16,2176]{2,1,0:T(8,128)(2,1)S(1)} %stack.2.refs_0_), channel_id=1, source_target_pairs={{0,1},{1,0},{2,3},{3,2},{4,5},{5,4},{6,7},{7,6},{8,9},{9,8},{10,11... | collective-permute-start | bytes 1044488 | tf_op jit(solution)/shard_map/ppermute | solution.py:283
  18.3 1.5 %collective-permute-start.6 = (bf16[3,16,2176]{2,1,0:T(8,128)(2,1)S(1)}, bf16[3,16,2176]{2,1,0:T(8,128)(2,1)S(1)}, u32[]{:S(2)}, u32[]{:S(2)}) collective-permute-start(bf16[3,16,2176]{2,1,0:T(8,128)(2,1)S(1)} %relay.1), channel_id=1, source_target_pairs={{0,1},{1,0},{2,3},{3,2},{4,5},{5,4},{6,7},{7,6},{8,9},{9,8},{10,11... | collective-permute-start | bytes 626696 | tf_op jit(solution)/shard_map/ppermute | solution.py:283
  21.3 16.4 %copy-start = (bf16[16,2048]{1,0:T(8,128)(2,1)S(1)}, bf16[16,2048]{1,0:T(8,128)(2,1)}, u32[]{:S(2)}) copy-start(bf16[16,2048]{1,0:T(8,128)(2,1)} %residual_ref.1) | copy-start | bytes 196612
  21.3 2.2 %collective-permute-start.7 = (bf16[4,16,2048]{2,1,0:T(8,128)(2,1)S(1)}, bf16[4,16,2048]{2,1,0:T(8,128)(2,1)S(1)}, u32[]{:S(2)}, u32[]{:S(2)}) collective-permute-start(bf16[4,16,2048]{2,1,0:T(8,128)(2,1)S(1)} %get-tuple-element.19), channel_id=1, source_target_pairs={{0,1},{1,0},{2,3},{3,2},{4,5},{5,4},{6,7},{7,6},{8,9},{9,8},{10,11... | collective-permute-start | bytes 786440 | tf_op jit(solution)/shard_map/ppermute | solution.py:283
  23.1 10.2 %collective-permute-start.12 = (bf16[4,16,2048]{2,1,0:T(8,128)(2,1)S(1)}, bf16[4,16,2048]{2,1,0:T(8,128)(2,1)S(1)}, u32[]{:S(2)}, u32[]{:S(2)}) collective-permute-start(bf16[4,16,2048]{2,1,0:T(8,128)(2,1)S(1)} %get-tuple-element.25), channel_id=1, source_target_pairs={{0,1},{1,0},{2,3},{3,2},{4,5},{5,4},{6,7},{7,6},{8,9},{9,8},{10,11... | collective-permute-start | bytes 786440 | tf_op jit(solution)/shard_map/ppermute | solution.py:283
  23.6 4.7 %collective-permute-start.8 = (bf16[16,2048]{1,0:T(8,128)(2,1)S(1)}, bf16[16,2048]{1,0:T(8,128)(2,1)S(1)}, u32[]{:S(2)}, u32[]{:S(2)}) collective-permute-start(bf16[16,2048]{1,0:T(8,128)(2,1)S(1)} %get-tuple-element.21), channel_id=1, source_target_pairs={{0,2},{1,3},{2,0},{3,1},{4,6},{5,7},{6,4},{7,5},{8,10},{9,11},{10,... | collective-permute-start | bytes 196616 | tf_op jit(solution)/shard_map/ppermute | solution.py:283
  25.1 6.7 %collective-permute-start.10 = (bf16[16,2048]{1,0:T(8,128)(2,1)S(1)}, bf16[16,2048]{1,0:T(8,128)(2,1)S(1)}, u32[]{:S(2)}, u32[]{:S(2)}) collective-permute-start(bf16[16,2048]{1,0:T(8,128)(2,1)S(1)} %get-tuple-element.23), channel_id=1, source_target_pairs={{0,2},{1,3},{2,0},{3,1},{4,6},{5,7},{6,4},{7,5},{8,10},{9,11},{10,... | collective-permute-start | bytes 196616 | tf_op jit(solution)/shard_map/ppermute | solution.py:283
  28.3 8.6 %collective-permute-start.9 = (bf16[16,2048]{1,0:T(8,128)(2,1)S(1)}, bf16[16,2048]{1,0:T(8,128)(2,1)S(1)}, u32[]{:S(2)}, u32[]{:S(2)}) collective-permute-start(bf16[16,2048]{1,0:T(8,128)(2,1)S(1)} %side_sum.2.refs_0_), channel_id=1, source_target_pairs={{0,12},{1,13},{2,14},{3,15},{4,8},{5,9},{6,10},{7,11},{8,4},{9,5},... | collective-permute-start | bytes 196616 | tf_op jit(solution)/shard_map/ppermute | solution.py:283
  31.8 5.9 %collective-permute-start.11 = (bf16[16,2048]{1,0:T(8,128)(2,1)S(1)}, bf16[16,2048]{1,0:T(8,128)(2,1)S(1)}, u32[]{:S(2)}, u32[]{:S(2)}) collective-permute-start(bf16[16,2048]{1,0:T(8,128)(2,1)S(1)} %side_sum.3.refs_0_), channel_id=1, source_target_pairs={{0,8},{1,9},{2,10},{3,11},{4,12},{5,13},{6,14},{7,15},{8,0},{9,1},... | collective-permute-start | bytes 196616 | tf_op jit(solution)/shard_map/ppermute | solution.py:283
  33.4 5.8 %collective-permute-start.13 = (bf16[16,2048]{1,0:T(8,128)(2,1)S(1)}, bf16[16,2048]{1,0:T(8,128)(2,1)S(1)}, u32[]{:S(2)}, u32[]{:S(2)}) collective-permute-start(bf16[16,2048]{1,0:T(8,128)(2,1)S(1)} %get-tuple-element.27), channel_id=1, source_target_pairs={{0,6},{1,7},{2,4},{3,5},{4,2},{5,3},{6,0},{7,1},{8,14},{9,15},{10,... | collective-permute-start | bytes 196616 | tf_op jit(solution)/shard_map/ppermute | solution.py:283
  34.3 5.3 %collective-permute-start.14 = (bf16[16,2048]{1,0:T(8,128)(2,1)S(1)}, bf16[16,2048]{1,0:T(8,128)(2,1)S(1)}, u32[]{:S(2)}, u32[]{:S(2)}) collective-permute-start(bf16[16,2048]{1,0:T(8,128)(2,1)S(1)} %get-tuple-element.28), channel_id=1, source_target_pairs={{0,4},{1,5},{2,6},{3,7},{4,0},{5,1},{6,2},{7,3},{8,12},{9,13},{10,... | collective-permute-start | bytes 196616 | tf_op jit(solution)/shard_map/ppermute | solution.py:283
  36.1 4.3 %collective-permute-start.15 = (bf16[16,2048]{1,0:T(8,128)(2,1)S(1)}, bf16[16,2048]{1,0:T(8,128)(2,1)S(1)}, u32[]{:S(2)}, u32[]{:S(2)}) collective-permute-start(bf16[16,2048]{1,0:T(8,128)(2,1)S(1)} %get-tuple-element.29), channel_id=1, source_target_pairs={{0,2},{1,3},{2,0},{3,1},{4,6},{5,7},{6,4},{7,5},{8,10},{9,11},{10,... | collective-permute-start | bytes 196616 | tf_op jit(solution)/shard_map/ppermute | solution.py:283

commit v10 on v8

--- a/solution.py
+++ b/solution.py
@@ -221,13 +221,8 @@
     refs[-1][...] = in_ref[...]
 
 
-def ffn_kernel(takes, *refs):
-    in_ref, down_ref = refs[4:6]
-    near_ref, far_ref = refs[-2:]
+def expert(packed, in_ref, down_ref):
     width = down_ref.shape[1]
-    packed = jnp.concatenate(
-        [refs[i][b] for i, start, stop in takes for b in range(start, stop)], axis=0
-    )
     rows = packed[:, :width]
     terms = packed[:, width:].astype(jnp.float32)
     lane = lax.broadcasted_iota(jnp.int32, terms.shape, 1)
@@ -237,9 +232,24 @@
     up = jnp.dot(rows, in_ref[width:], preferred_element_type=jnp.float32)
     hidden = (gate / (1.0 + jnp.exp(-gate)) * up).astype(jnp.bfloat16)
     out = jnp.dot(hidden, down_ref[...], preferred_element_type=jnp.float32)
-    out = (out * weight).astype(jnp.bfloat16).reshape((2,) + near_ref.shape)
-    near_ref[...] = out[0]
-    far_ref[...] = out[1]
+    return (out * weight).astype(jnp.bfloat16)
+
+
+def ffn_kernel(count, takes, *refs):
+    in_ref, down_ref = refs[count : count + 2]
+    packed = jnp.concatenate([refs[i][b] for i, b in takes], axis=0)
+    out = expert(packed, in_ref, down_ref)
+    row_count = out.shape[0] // len(takes)
+    near_ref, far_ref = refs[-2:]
+    half = near_ref.shape[0]
+    near_ref[...] = out[: half * row_count].reshape(near_ref.shape)
+    far_ref[...] = out[half * row_count :].reshape(far_ref.shape)
+
+
+def rest_kernel(blocks_ref, before_ref, in_ref, down_ref, out_ref):
+    packed = jnp.concatenate([blocks_ref[0], blocks_ref[1]], axis=0)
+    out_ref[:2] = before_ref[...]
+    out_ref[2:] = expert(packed, in_ref, down_ref).reshape(before_ref.shape)
 
 
 def pair_kernel(own_ref, other_ref, *refs):
@@ -305,25 +315,28 @@
     held = hold((expert_in, expert_down), (along,))
     along_side_far = swap(relay(along_side, held[:1]), core)
 
-    def ffn(near_takes, side_takes, after=()):
-        takes = [(i, *t) for i in (0, 2) for t in near_takes]
-        takes[len(near_takes) : len(near_takes)] = [(1, *t) for t in side_takes]
-        takes += [(3, *t) for t in side_takes]
-        return in_vmem(
-            functools.partial(ffn_kernel, takes),
-            [vmem((4,) + one, jnp.bfloat16)] * 2,
-            "ffn",
-            (near, along_side, near_far, along_side_far, *held),
-            after,
-            mebibytes=16,
-            cost_estimate=cost(8 * row_count * 2 * sum(h.size for h in held), 2 * held[0].size),
-        )
-
-    early_outs = ffn([(0, 2)], [(0, 2)])
+    def ffn(kernel, operands, rows, out_shape, after=()):
+        flops = 2 * rows * sum(h.size for h in held)
+        work = cost(flops, 2 * held[0].size)
+        return in_vmem(kernel, out_shape, "ffn", (*operands, *held), after, 16, work)
+
+    takes = [(i, b) for i in range(3) for b in range(2)]
+    early_near, early_part = ffn(
+        functools.partial(ffn_kernel, 3, takes),
+        (near, along_side, near_far),
+        6 * row_count,
+        [vmem((n,) + one, jnp.bfloat16) for n in (4, 2)],
+    )
+    early_far = ffn(
+        rest_kernel,
+        (along_side_far, early_part),
+        2 * row_count,
+        vmem((4,) + one, jnp.bfloat16),
+    )
     send = vmem(one, jnp.bfloat16)
     keep_and_send = [vmem(one, jnp.float32)] * 2 + [send] * 2
     second_keep, third_keep, second_send, third_send = in_vmem(
-        pair_kernel, keep_and_send, "pair_sum", (early_outs[0], swap(early_outs[1], core))
+        pair_kernel, keep_and_send, "pair_sum", (early_near, swap(early_far, core))
     )
     third_sum = in_vmem(add_kernel, send, "side_sum", (third_keep, swap(third_send, side)))
     second_sum = in_vmem(
@@ -335,7 +348,15 @@
         "partial_sum",
         (residual, swap(third_sum, 3 * line), swap(second_sum, 2 * line)),
     )
-    late_outs = ffn([(3, 5), (2, 3)], [(2, 3)], early_outs[:1])
+    takes = [(i, b) for i in (0, 2) for b in (3, 4, 2)]
+    takes[3:3] = [(1, 2)]
+    late_outs = ffn(
+        functools.partial(ffn_kernel, 4, takes + [(3, 2)]),
+        (near, along_side, near_far, along_side_far),
+        8 * row_count,
+        [vmem((4,) + one, jnp.bfloat16)] * 2,
+        (early_far,),
+    )
     own, across_sum, first_sum, diagonal_sum = in_vmem(
         pair_kernel,
         [vmem(one, jnp.float32), send, send, send],

time: 39.6 us -> 47.4 us (1.20)
  waiting for transfers between devices: 5.22 us -> 17.8 us
  starting transfers between devices: 21.5 us -> 14.8 us
  Pallas kernels: 11.9 us -> 13.9 us
    ppermute x16, waiting for transfers between devices: 5.22 us -> 17.8 us  [swap(): return lax.ppermute(value, 'ep', [(i, i ^ bits) for i in range(devices)])]
    ppermute x16, starting transfers between devices: 21.5 us -> 14.8 us  [swap(): return lax.ppermute(value, 'ep', [(i, i ^ bits) for i in range(devices)])]
    pallas_call x11 -> x12, Pallas kernels: 3.93 us -> 5.88 us  [in_vmem(): pl.pallas_call(kernel, out_shape=out_shape, in_specs=[HERE] * len(arrays)...]
  transfers between devices with their start and end apart: 16 -> 16, of which waited for: 6 -> 8; matrix products, arithmetic and copies ran while one was open for 0% -> 0% of each run, Pallas kernels for 22% -> 22%
where the time goes in v10:
time: 47.4 us; the launch traced here: 47.2 us
  waiting for transfers between devices  17.8 us (38%)
  starting transfers between devices  14.8 us (31%)
  Pallas kernels  13.9 us (29%)
  between operations  0.78 us (2%)
    ppermute x16, waiting for transfers between devices, swap(): return lax.ppermute(value, 'ep', [(i, i ^ bits) for i in range(devices)])  17.8 us
    ppermute x16, starting transfers between devices, swap(): return lax.ppermute(value, 'ep', [(i, i ^ bits) for i in range(devices)])  14.8 us
    pallas_call x12, Pallas kernels, in_vmem(): pl.pallas_call(kernel, out_shape=out_shape, in_specs=[HERE] * len(arrays)...  5.88 us
    pallas_call x2, Pallas kernels, from_hbm(): pl.pallas_call(kernel, out_shape=out_shape, in_specs=[pl.BlockSpec(memory...  4.25 us
    pallas_call x1, Pallas kernels, hold(): pl.pallas_call(functools.partial(hold_kernel, len(flat), pieces), out_sha...  3.75 us
  transfers between devices with their start and end apart: 16, of which 8 were waited for; matrix products, arithmetic and copies ran while one was open for 0% of the time, Pallas kernels for 22%

profile of v10, /device:TPU:0, one launch (start us, length us, event | category | flops | bytes accessed | tf_op | source)
XLA Modules:
  0.0 47.2 jit_solution(13001890353474865599)
XLA Ops:
  0.6 1.0 %prepare.1.refs_6_.refs_3_ = bf16[16,2176]{1,0:T(8,128)(2,1)S(1)} custom-call(bf16[16,2048]{1,0:T(8,128)(2,1)} %residual_ref.1, f32[1,2048]{1,0:T(1,128)} %bitcast.13, s32[8,16]{1,0:T(8,128)} %bitcast.14, f32[8,16]{1,0:T(8,128)} %bitcast.15), custom_call_target="tpu_custom_call" | custom-call | tf_op jit(solution)/shard_map/prepare/pallas_call | solution.py:77
  1.7 3.0 %collective-permute-start.3 = (bf16[16,2176]{1,0:T(8,128)(2,1)S(1)}, bf16[16,2176]{1,0:T(8,128)(2,1)S(1)}, u32[]{:S(2)}, u32[]{:S(2)}) collective-permute-start(bf16[16,2176]{1,0:T(8,128)(2,1)S(1)} %prepare.1.refs_6_.refs_3_), channel_id=1, source_target_pairs={{0,2},{1,3},{2,0},{3,1},{4,6},{5,7},{6,4},{7,5},{8,10},{9,11},{10,... | collective-permute-start | bytes 208904 | tf_op jit(solution)/shard_map/ppermute | solution.py:293
  4.7 1.6 %collective-permute-start.2 = (bf16[16,2176]{1,0:T(8,128)(2,1)S(1)}, bf16[16,2176]{1,0:T(8,128)(2,1)S(1)}, u32[]{:S(2)}, u32[]{:S(2)}) collective-permute-start(bf16[16,2176]{1,0:T(8,128)(2,1)S(1)} %prepare.1.refs_6_.refs_3_), channel_id=1, source_target_pairs={{0,4},{1,5},{2,6},{3,7},{4,0},{5,1},{6,2},{7,3},{8,12},{9,13},{10,... | collective-permute-start | bytes 208904 | tf_op jit(solution)/shard_map/ppermute | solution.py:293
  6.3 2.5 %collective-permute-start.1 = (bf16[16,2176]{1,0:T(8,128)(2,1)S(1)}, bf16[16,2176]{1,0:T(8,128)(2,1)S(1)}, u32[]{:S(2)}, u32[]{:S(2)}) collective-permute-start(bf16[16,2176]{1,0:T(8,128)(2,1)S(1)} %prepare.1.refs_6_.refs_3_), channel_id=1, source_target_pairs={{0,12},{1,13},{2,14},{3,15},{4,8},{5,9},{6,10},{7,11},{8,4},{9,5},... | collective-permute-start | bytes 208904 | tf_op jit(solution)/shard_map/ppermute | solution.py:293
  8.7 0.1 collective-permute-start
  8.8 0.0 collective-permute-done.3.refs_4_
  8.8 0.1 collective-permute-done.2.refs_2_
  9.0 4.0 %collective-permute-done.1.refs_1_ = bf16[16,2176]{1,0:T(8,128)(2,1)S(1)} collective-permute-done((bf16[16,2176]{1,0:T(8,128)(2,1)S(1)}, bf16[16,2176]{1,0:T(8,128)(2,1)S(1)}, u32[]{:S(2)}, u32[]{:S(2)}) %collective-permute-start.1) | collective-permute-done | bytes 69664 | tf_op jit(solution)/shard_map/ppermute | solution.py:293
  13.0 2.2 %collective-permute-done.refs_0_ = bf16[16,2176]{1,0:T(8,128)(2,1)S(1)} collective-permute-done((bf16[16,2176]{1,0:T(8,128)(2,1)S(1)}, bf16[16,2176]{1,0:T(8,128)(2,1)S(1)}, u32[]{:S(2)}, u32[]{:S(2)}) %collective-permute-start) | collective-permute-done | bytes 69664 | tf_op jit(solution)/shard_map/ppermute | solution.py:293
  15.3 0.1 collective-permute-start.5
  15.4 3.2 %attend.1.refs_3_ = bf16[4,32,128]{2,1,0:T(8,128)(2,1)} custom-call(s32[4]{0:T(128)} %refs_0_.3, bf16[4,32,128]{2,1,0:T(8,128)(2,1)} %refs_1_.1, bf16[4,256,128]{2,1,0:T(8,128)(2,1)} %bitcast.11, bf16[4,256,128]{2,1,0:T(8,128)(2,1)} %bitcast.12, bf16[8,128]{1,0:T(8,128)(2,1)} %bitcast.16, bf16[8,128]{1,0:T(8,128)(2,1)} %bitcast.17, ...), custom_call_target="tpu_custom_call" | custom-call | bytes 4194304 | tf_op jit(solution)/shard_map/attend/pallas_call | solution.py:77
  18.6 0.6 %collective-permute-start.4 = (bf16[3,16,2176]{2,1,0:T(8,128)(2,1)S(1)}, bf16[3,16,2176]{2,1,0:T(8,128)(2,1)S(1)}, u32[]{:S(2)}, u32[]{:S(2)}) collective-permute-start(bf16[3,16,2176]{2,1,0:T(8,128)(2,1)S(1)} %stack.3.refs_2_), channel_id=1, source_target_pairs={{0,2},{1,3},{2,0},{3,1},{4,6},{5,7},{6,4},{7,5},{8,10},{9,11},{10,... | collective-permute-start | bytes 626696 | tf_op jit(solution)/shard_map/ppermute | solution.py:293
  19.2 3.7 %hold.1 = (bf16[4096,768]{1,0:T(8,128)(2,1)S(1)}, bf16[768,2048]{1,0:T(8,128)(2,1)S(1)}) custom-call(bf16[4096,768]{1,0:T(8,128)(2,1)} %bitcast.9, bf16[768,2048]{1,0:T(8,128)(2,1)} %bitcast.10, bf16[3,16,2176]{2,1,0:T(8,128)(2,1)S(1)} %stack.3.refs_2_), custom_call_target="tpu_custom_call" | custom-call | bytes 9437184 | tf_op jit(solution)/shard_map/hold/pallas_call | solution.py:170
  23.0 3.3 %collective-permute-done.4.refs_1_.in_ref = bf16[3,16,2176]{2,1,0:T(8,128)(2,1)S(1)} collective-permute-done((bf16[3,16,2176]{2,1,0:T(8,128)(2,1)S(1)}, bf16[3,16,2176]{2,1,0:T(8,128)(2,1)S(1)}, u32[]{:S(2)}, u32[]{:S(2)}) %collective-permute-start.4) | collective-permute-done | bytes 208928 | tf_op jit(solution)/shard_map/ppermute | solution.py:293
  26.2 0.1 collective-permute-start.6
  26.3 0.0 collective-permute-done.5.refs_2_
  26.3 1.7 %ffn.3 = (bf16[4,16,2048]{2,1,0:T(8,128)(2,1)S(1)}, bf16[2,16,2048]{2,1,0:T(8,128)(2,1)S(1)}) custom-call(bf16[5,16,2176]{2,1,0:T(8,128)(2,1)S(1)} %stack.2.refs_0_, bf16[3,16,2176]{2,1,0:T(8,128)(2,1)S(1)} %collective-permute-done.4.refs_1_.in_ref, bf16[5,16,2176]{2,1,0:T(8,128)(2,1)S(1)} %collective-permute-done.5.refs_2_, ...), custom_call_target="tpu_custom_call" | custom-call | flops 905969664 | bytes 6291456 | tf_op jit(solution)/shard_map/ffn/pallas_call | solution.py:273
  28.0 0.0 collective-permute-done.6.blocks_ref.refs_3_
  28.1 1.7 %ffn.4.refs_6_ = bf16[4,16,2048]{2,1,0:T(8,128)(2,1)S(1)} custom-call(bf16[3,16,2176]{2,1,0:T(8,128)(2,1)S(1)} %collective-permute-done.6.blocks_ref.refs_3_, bf16[2,16,2048]{2,1,0:T(8,128)(2,1)S(1)} %get-tuple-element.19.before_ref, bf16[4096,768]{1,0:T(8,128)(2,1)S(1)} %get-tuple-element.16.refs_3_.refs_0_.in_ref.refs_4_, ...), custom_call_target="tpu_custom_call" | custom-call | flops 301989888 | bytes 6291456 | tf_op jit(solution)/shard_map/ffn/pallas_call | solution.py:273
  29.8 0.0 copy-start
  29.8 0.6 %collective-permute-start.7 = (bf16[4,16,2048]{2,1,0:T(8,128)(2,1)S(1)}, bf16[4,16,2048]{2,1,0:T(8,128)(2,1)S(1)}, u32[]{:S(2)}, u32[]{:S(2)}) collective-permute-start(bf16[4,16,2048]{2,1,0:T(8,128)(2,1)S(1)} %ffn.4.refs_6_), channel_id=1, source_target_pairs={{0,1},{1,0},{2,3},{3,2},{4,5},{5,4},{6,7},{7,6},{8,9},{9,8},{10,11... | collective-permute-start | bytes 786440 | tf_op jit(solution)/shard_map/ppermute | solution.py:293
  30.4 1.5 %ffn.5 = (bf16[4,16,2048]{2,1,0:T(8,128)(2,1)S(1)}, bf16[4,16,2048]{2,1,0:T(8,128)(2,1)S(1)}) custom-call(bf16[5,16,2176]{2,1,0:T(8,128)(2,1)S(1)} %stack.2.refs_0_, bf16[3,16,2176]{2,1,0:T(8,128)(2,1)S(1)} %collective-permute-done.4.refs_1_.in_ref, bf16[5,16,2176]{2,1,0:T(8,128)(2,1)S(1)} %collective-permute-done.5.refs_2_, ...), custom_call_target="tpu_custom_call" | custom-call | flops 1207959552 | bytes 6291456 | tf_op jit(solution)/shard_map/ffn/pallas_call | solution.py:273
  31.9 0.1 collective-permute-start.12
  32.0 0.0 collective-permute-done.7.other_ref
  32.0 0.1 pair_sum.2
  32.1 0.6 %collective-permute-start.8 = (bf16[16,2048]{1,0:T(8,128)(2,1)S(1)}, bf16[16,2048]{1,0:T(8,128)(2,1)S(1)}, u32[]{:S(2)}, u32[]{:S(2)}) collective-permute-start(bf16[16,2048]{1,0:T(8,128)(2,1)S(1)} %get-tuple-element.21.refs_0_), channel_id=1, source_target_pairs={{0,2},{1,3},{2,0},{3,1},{4,6},{5,7},{6,4},{7,5},{8,10},{9,11},{10,... | collective-permute-start | bytes 196616 | tf_op jit(solution)/shard_map/ppermute | solution.py:293
  32.7 1.5 %collective-permute-start.10 = (bf16[16,2048]{1,0:T(8,128)(2,1)S(1)}, bf16[16,2048]{1,0:T(8,128)(2,1)S(1)}, u32[]{:S(2)}, u32[]{:S(2)}) collective-permute-start(bf16[16,2048]{1,0:T(8,128)(2,1)S(1)} %get-tuple-element.23), channel_id=1, source_target_pairs={{0,2},{1,3},{2,0},{3,1},{4,6},{5,7},{6,4},{7,5},{8,10},{9,11},{10,... | collective-permute-start | bytes 196616 | tf_op jit(solution)/shard_map/ppermute | solution.py:293
  34.1 0.0 collective-permute-done.12.other_ref
  34.2 0.1 pair_sum.3
  34.2 0.1 collective-permute-start.13
  34.3 2.7 %collective-permute-done.8.other_ref = bf16[16,2048]{1,0:T(8,128)(2,1)S(1)} collective-permute-done((bf16[16,2048]{1,0:T(8,128)(2,1)S(1)}, bf16[16,2048]{1,0:T(8,128)(2,1)S(1)}, u32[]{:S(2)}, u32[]{:S(2)}) %collective-permute-start.8) | collective-permute-done | bytes 65568 | tf_op jit(solution)/shard_map/ppermute | solution.py:293
  37.0 1.7 %collective-permute-done.10.other_ref = bf16[16,2048]{1,0:T(8,128)(2,1)S(1)} collective-permute-done((bf16[16,2048]{1,0:T(8,128)(2,1)S(1)}, bf16[16,2048]{1,0:T(8,128)(2,1)S(1)}, u32[]{:S(2)}, u32[]{:S(2)}) %collective-permute-start.10) | collective-permute-done | bytes 65568 | tf_op jit(solution)/shard_map/ppermute | solution.py:293
  38.7 0.8 %collective-permute-start.11 = (bf16[16,2048]{1,0:T(8,128)(2,1)S(1)}, bf16[16,2048]{1,0:T(8,128)(2,1)S(1)}, u32[]{:S(2)}, u32[]{:S(2)}) collective-permute-start(bf16[16,2048]{1,0:T(8,128)(2,1)S(1)} %side_sum.3), channel_id=1, source_target_pairs={{0,8},{1,9},{2,10},{3,11},{4,12},{5,13},{6,14},{7,15},{8,0},{9,1},... | collective-permute-start | bytes 196616 | tf_op jit(solution)/shard_map/ppermute | solution.py:293
  39.5 1.7 %collective-permute-start.9 = (bf16[16,2048]{1,0:T(8,128)(2,1)S(1)}, bf16[16,2048]{1,0:T(8,128)(2,1)S(1)}, u32[]{:S(2)}, u32[]{:S(2)}) collective-permute-start(bf16[16,2048]{1,0:T(8,128)(2,1)S(1)} %side_sum.2.refs_0_), channel_id=1, source_target_pairs={{0,12},{1,13},{2,14},{3,15},{4,8},{5,9},{6,10},{7,11},{8,4},{9,5},... | collective-permute-start | bytes 196616 | tf_op jit(solution)/shard_map/ppermute | solution.py:293
  41.2 1.1 %collective-permute-start.14 = (bf16[16,2048]{1,0:T(8,128)(2,1)S(1)}, bf16[16,2048]{1,0:T(8,128)(2,1)S(1)}, u32[]{:S(2)}, u32[]{:S(2)}) collective-permute-start(bf16[16,2048]{1,0:T(8,128)(2,1)S(1)} %get-tuple-element.28), channel_id=1, source_target_pairs={{0,4},{1,5},{2,6},{3,7},{4,0},{5,1},{6,2},{7,3},{8,12},{9,13},{10,... | collective-permute-start | bytes 196616 | tf_op jit(solution)/shard_map/ppermute | solution.py:293
  42.3 0.5 %collective-permute-start.15 = (bf16[16,2048]{1,0:T(8,128)(2,1)S(1)}, bf16[16,2048]{1,0:T(8,128)(2,1)S(1)}, u32[]{:S(2)}, u32[]{:S(2)}) collective-permute-start(bf16[16,2048]{1,0:T(8,128)(2,1)S(1)} %get-tuple-element.29), channel_id=1, source_target_pairs={{0,2},{1,3},{2,0},{3,1},{4,6},{5,7},{6,4},{7,5},{8,10},{9,11},{10,... | collective-permute-start | bytes 196616 | tf_op jit(solution)/shard_map/ppermute | solution.py:293
  42.8 3.2 %collective-permute-done.11.refs_1_ = bf16[16,2048]{1,0:T(8,128)(2,1)S(1)} collective-permute-done((bf16[16,2048]{1,0:T(8,128)(2,1)S(1)}, bf16[16,2048]{1,0:T(8,128)(2,1)S(1)}, u32[]{:S(2)}, u32[]{:S(2)}) %collective-permute-start.11) | collective-permute-done | bytes 65568 | tf_op jit(solution)/shard_map/ppermute | solution.py:293
  46.0 0.0 collective-permute-done.9.refs_0_
  46.0 0.0 copy-done
  46.1 0.0 collective-permute-done.13.refs_1_
  46.1 0.5 %collective-permute-done.14.refs_2_ = bf16[16,2048]{1,0:T(8,128)(2,1)S(1)} collective-permute-done((bf16[16,2048]{1,0:T(8,128)(2,1)S(1)}, bf16[16,2048]{1,0:T(8,128)(2,1)S(1)}, u32[]{:S(2)}, u32[]{:S(2)}) %collective-permute-start.14) | collective-permute-done | bytes 65568 | tf_op jit(solution)/shard_map/ppermute | solution.py:293
  46.6 0.0 collective-permute-done.15.refs_3_
  46.6 0.7 %total.1 = bf16[16,2048]{1,0:T(8,128)(2,1)} custom-call(f32[16,2048]{1,0:T(8,128)S(1)} %partial_sum.1.residual_ref, f32[16,2048]{1,0:T(8,128)S(1)} %get-tuple-element.26.refs_0_, bf16[16,2048]{1,0:T(8,128)(2,1)S(1)} %collective-permute-done.13.refs_1_, bf16[16,2048]{1,0:T(8,128)(2,1)S(1)} %collective-permute-done.14.refs_2_, ...), custom_call_target="tpu_custom_call" | custom-call | tf_op jit(solution)/shard_map/total/pallas_call | solution.py:273
  (6 shorter events, 0.1 us)
Async XLA Ops:
  1.7 7.2 %collective-permute-start.3 = (bf16[16,2176]{1,0:T(8,128)(2,1)S(1)}, bf16[16,2176]{1,0:T(8,128)(2,1)S(1)}, u32[]{:S(2)}, u32[]{:S(2)}) collective-permute-start(bf16[16,2176]{1,0:T(8,128)(2,1)S(1)} %prepare.1.refs_6_.refs_3_), channel_id=1, source_target_pairs={{0,2},{1,3},{2,0},{3,1},{4,6},{5,7},{6,4},{7,5},{8,10},{9,11},{10,... | collective-permute-start | bytes 208904 | tf_op jit(solution)/shard_map/ppermute | solution.py:293
  4.7 4.3 %collective-permute-start.2 = (bf16[16,2176]{1,0:T(8,128)(2,1)S(1)}, bf16[16,2176]{1,0:T(8,128)(2,1)S(1)}, u32[]{:S(2)}, u32[]{:S(2)}) collective-permute-start(bf16[16,2176]{1,0:T(8,128)(2,1)S(1)} %prepare.1.refs_6_.refs_3_), channel_id=1, source_target_pairs={{0,4},{1,5},{2,6},{3,7},{4,0},{5,1},{6,2},{7,3},{8,12},{9,13},{10,... | collective-permute-start | bytes 208904 | tf_op jit(solution)/shard_map/ppermute | solution.py:293
  6.3 6.7 %collective-permute-start.1 = (bf16[16,2176]{1,0:T(8,128)(2,1)S(1)}, bf16[16,2176]{1,0:T(8,128)(2,1)S(1)}, u32[]{:S(2)}, u32[]{:S(2)}) collective-permute-start(bf16[16,2176]{1,0:T(8,128)(2,1)S(1)} %prepare.1.refs_6_.refs_3_), channel_id=1, source_target_pairs={{0,12},{1,13},{2,14},{3,15},{4,8},{5,9},{6,10},{7,11},{8,4},{9,5},... | collective-permute-start | bytes 208904 | tf_op jit(solution)/shard_map/ppermute | solution.py:293
  8.7 6.5 %collective-permute-start = (bf16[16,2176]{1,0:T(8,128)(2,1)S(1)}, bf16[16,2176]{1,0:T(8,128)(2,1)S(1)}, u32[]{:S(2)}, u32[]{:S(2)}) collective-permute-start(bf16[16,2176]{1,0:T(8,128)(2,1)S(1)} %prepare.1.refs_6_.refs_3_), channel_id=1, source_target_pairs={{0,8},{1,9},{2,10},{3,11},{4,12},{5,13},{6,14},{7,15},{8,0},{9,1},... | collective-permute-start | bytes 208904 | tf_op jit(solution)/shard_map/ppermute | solution.py:293
  15.3 11.1 %collective-permute-start.5 = (bf16[5,16,2176]{2,1,0:T(8,128)(2,1)S(1)}, bf16[5,16,2176]{2,1,0:T(8,128)(2,1)S(1)}, u32[]{:S(2)}, u32[]{:S(2)}) collective-permute-start(bf16[5,16,2176]{2,1,0:T(8,128)(2,1)S(1)} %stack.2.refs_0_), channel_id=1, source_target_pairs={{0,1},{1,0},{2,3},{3,2},{4,5},{5,4},{6,7},{7,6},{8,9},{9,8},{10,11... | collective-permute-start | bytes 1044488 | tf_op jit(solution)/shard_map/ppermute | solution.py:293
  18.6 7.6 %collective-permute-start.4 = (bf16[3,16,2176]{2,1,0:T(8,128)(2,1)S(1)}, bf16[3,16,2176]{2,1,0:T(8,128)(2,1)S(1)}, u32[]{:S(2)}, u32[]{:S(2)}) collective-permute-start(bf16[3,16,2176]{2,1,0:T(8,128)(2,1)S(1)} %stack.3.refs_2_), channel_id=1, source_target_pairs={{0,2},{1,3},{2,0},{3,1},{4,6},{5,7},{6,4},{7,5},{8,10},{9,11},{10,... | collective-permute-start | bytes 626696 | tf_op jit(solution)/shard_map/ppermute | solution.py:293
  26.2 1.8 %collective-permute-start.6 = (bf16[3,16,2176]{2,1,0:T(8,128)(2,1)S(1)}, bf16[3,16,2176]{2,1,0:T(8,128)(2,1)S(1)}, u32[]{:S(2)}, u32[]{:S(2)}) collective-permute-start(bf16[3,16,2176]{2,1,0:T(8,128)(2,1)S(1)} %relay.1), channel_id=1, source_target_pairs={{0,1},{1,0},{2,3},{3,2},{4,5},{5,4},{6,7},{7,6},{8,9},{9,8},{10,11... | collective-permute-start | bytes 626696 | tf_op jit(solution)/shard_map/ppermute | solution.py:293
  29.8 16.2 %copy-start = (bf16[16,2048]{1,0:T(8,128)(2,1)S(1)}, bf16[16,2048]{1,0:T(8,128)(2,1)}, u32[]{:S(2)}) copy-start(bf16[16,2048]{1,0:T(8,128)(2,1)} %residual_ref.1) | copy-start | bytes 196612
  29.8 2.2 %collective-permute-start.7 = (bf16[4,16,2048]{2,1,0:T(8,128)(2,1)S(1)}, bf16[4,16,2048]{2,1,0:T(8,128)(2,1)S(1)}, u32[]{:S(2)}, u32[]{:S(2)}) collective-permute-start(bf16[4,16,2048]{2,1,0:T(8,128)(2,1)S(1)} %ffn.4.refs_6_), channel_id=1, source_target_pairs={{0,1},{1,0},{2,3},{3,2},{4,5},{5,4},{6,7},{7,6},{8,9},{9,8},{10,11... | collective-permute-start | bytes 786440 | tf_op jit(solution)/shard_map/ppermute | solution.py:293
  31.9 2.3 %collective-permute-start.12 = (bf16[4,16,2048]{2,1,0:T(8,128)(2,1)S(1)}, bf16[4,16,2048]{2,1,0:T(8,128)(2,1)S(1)}, u32[]{:S(2)}, u32[]{:S(2)}) collective-permute-start(bf16[4,16,2048]{2,1,0:T(8,128)(2,1)S(1)} %get-tuple-element.25), channel_id=1, source_target_pairs={{0,1},{1,0},{2,3},{3,2},{4,5},{5,4},{6,7},{7,6},{8,9},{9,8},{10,11... | collective-permute-start | bytes 786440 | tf_op jit(solution)/shard_map/ppermute | solution.py:293
  32.1 5.0 %collective-permute-start.8 = (bf16[16,2048]{1,0:T(8,128)(2,1)S(1)}, bf16[16,2048]{1,0:T(8,128)(2,1)S(1)}, u32[]{:S(2)}, u32[]{:S(2)}) collective-permute-start(bf16[16,2048]{1,0:T(8,128)(2,1)S(1)} %get-tuple-element.21.refs_0_), channel_id=1, source_target_pairs={{0,2},{1,3},{2,0},{3,1},{4,6},{5,7},{6,4},{7,5},{8,10},{9,11},{10,... | collective-permute-start | bytes 196616 | tf_op jit(solution)/shard_map/ppermute | solution.py:293
  32.7 6.0 %collective-permute-start.10 = (bf16[16,2048]{1,0:T(8,128)(2,1)S(1)}, bf16[16,2048]{1,0:T(8,128)(2,1)S(1)}, u32[]{:S(2)}, u32[]{:S(2)}) collective-permute-start(bf16[16,2048]{1,0:T(8,128)(2,1)S(1)} %get-tuple-element.23), channel_id=1, source_target_pairs={{0,2},{1,3},{2,0},{3,1},{4,6},{5,7},{6,4},{7,5},{8,10},{9,11},{10,... | collective-permute-start | bytes 196616 | tf_op jit(solution)/shard_map/ppermute | solution.py:293
  34.2 11.8 %collective-permute-start.13 = (bf16[16,2048]{1,0:T(8,128)(2,1)S(1)}, bf16[16,2048]{1,0:T(8,128)(2,1)S(1)}, u32[]{:S(2)}, u32[]{:S(2)}) collective-permute-start(bf16[16,2048]{1,0:T(8,128)(2,1)S(1)} %get-tuple-element.27), channel_id=1, source_target_pairs={{0,6},{1,7},{2,4},{3,5},{4,2},{5,3},{6,0},{7,1},{8,14},{9,15},{10,... | collective-permute-start | bytes 196616 | tf_op jit(solution)/shard_map/ppermute | solution.py:293
  38.7 7.3 %collective-permute-start.11 = (bf16[16,2048]{1,0:T(8,128)(2,1)S(1)}, bf16[16,2048]{1,0:T(8,128)(2,1)S(1)}, u32[]{:S(2)}, u32[]{:S(2)}) collective-permute-start(bf16[16,2048]{1,0:T(8,128)(2,1)S(1)} %side_sum.3), channel_id=1, source_target_pairs={{0,8},{1,9},{2,10},{3,11},{4,12},{5,13},{6,14},{7,15},{8,0},{9,1},... | collective-permute-start | bytes 196616 | tf_op jit(solution)/shard_map/ppermute | solution.py:293
  39.5 6.5 %collective-permute-start.9 = (bf16[16,2048]{1,0:T(8,128)(2,1)S(1)}, bf16[16,2048]{1,0:T(8,128)(2,1)S(1)}, u32[]{:S(2)}, u32[]{:S(2)}) collective-permute-start(bf16[16,2048]{1,0:T(8,128)(2,1)S(1)} %side_sum.2.refs_0_), channel_id=1, source_target_pairs={{0,12},{1,13},{2,14},{3,15},{4,8},{5,9},{6,10},{7,11},{8,4},{9,5},... | collective-permute-start | bytes 196616 | tf_op jit(solution)/shard_map/ppermute | solution.py:293
  41.2 5.3 %collective-permute-start.14 = (bf16[16,2048]{1,0:T(8,128)(2,1)S(1)}, bf16[16,2048]{1,0:T(8,128)(2,1)S(1)}, u32[]{:S(2)}, u32[]{:S(2)}) collective-permute-start(bf16[16,2048]{1,0:T(8,128)(2,1)S(1)} %get-tuple-element.28), channel_id=1, source_target_pairs={{0,4},{1,5},{2,6},{3,7},{4,0},{5,1},{6,2},{7,3},{8,12},{9,13},{10,... | collective-permute-start | bytes 196616 | tf_op jit(solution)/shard_map/ppermute | solution.py:293
  42.3 4.3 %collective-permute-start.15 = (bf16[16,2048]{1,0:T(8,128)(2,1)S(1)}, bf16[16,2048]{1,0:T(8,128)(2,1)S(1)}, u32[]{:S(2)}, u32[]{:S(2)}) collective-permute-start(bf16[16,2048]{1,0:T(8,128)(2,1)S(1)} %get-tuple-element.29), channel_id=1, source_target_pairs={{0,2},{1,3},{2,0},{3,1},{4,6},{5,7},{6,4},{7,5},{8,10},{9,11},{10,... | collective-permute-start | bytes 196616 | tf_op jit(solution)/shard_map/ppermute | solution.py:293

commit v11 on v9

--- a/solution.py
+++ b/solution.py
@@ -248,8 +248,17 @@
         out_ref[...] = total.astype(out_ref.dtype)
 
 
-def add_kernel(own_ref, other_ref, *refs):
-    refs[-1][...] = (own_ref[...] + other_ref[...].astype(jnp.float32)).astype(refs[-1].dtype)
+def half_kernel(own_ref, other_ref, keep_ref, send_ref):
+    half = keep_ref.shape[0]
+    keep_ref[...] = own_ref[:half].astype(jnp.float32) + other_ref[:half].astype(jnp.float32)
+    send = own_ref[half:].astype(jnp.float32) + other_ref[half:].astype(jnp.float32)
+    send_ref[...] = send.astype(jnp.bfloat16)
+
+
+def side_kernel(own_ref, other_ref, *out_refs):
+    for i, out_ref in enumerate(out_refs):
+        total = own_ref[i] + other_ref[i].astype(jnp.float32)
+        out_ref[...] = total.astype(out_ref.dtype)
 
 
 def total_kernel(residual_ref, *refs):
@@ -321,13 +330,14 @@
 
     early_outs = ffn([(0, 2)], [(0, 2)])
     send = vmem(one, jnp.bfloat16)
-    keep_and_send = [vmem(one, jnp.float32)] * 2 + [send] * 2
-    second_keep, third_keep, second_send, third_send = in_vmem(
-        pair_kernel, keep_and_send, "pair_sum", (early_outs[0], swap(early_outs[1], core))
-    )
-    third_sum = in_vmem(add_kernel, send, "side_sum", (third_keep, swap(third_send, side)))
-    second_sum = in_vmem(
-        add_kernel, send, "side_sum", (second_keep, swap(second_send, side)), (third_sum,)
+    early_keep, early_send = in_vmem(
+        half_kernel,
+        [vmem((2,) + one, jnp.float32), vmem((2,) + one, jnp.bfloat16)],
+        "pair_sum",
+        (early_outs[0], swap(early_outs[1], core)),
+    )
+    second_sum, third_sum = in_vmem(
+        side_kernel, [send] * 2, "side_sum", (early_keep, swap(early_send, side))
     )
     partial_sum = in_vmem(
         total_kernel,
@@ -341,7 +351,7 @@
         [vmem(one, jnp.float32), send, send, send],
         "pair_sum",
         (late_outs[0], swap(late_outs[1], core)),
-        (second_sum,),
+        (early_send,),
     )
     moe_out = in_vmem(
         total_kernel,

time: 41.2 us -> 40.9 us (level)
  starting transfers between devices: 20.3 us -> 19.8 us
    ppermute x16 -> x15, starting transfers between devices: 20.3 us -> 19.8 us  [swap(): return lax.ppermute(value, 'ep', [(i, i ^ bits) for i in range(devices)])]
    ppermute x16 -> x15, waiting for transfers between devices: 8.05 us -> 8.23 us  [swap(): return lax.ppermute(value, 'ep', [(i, i ^ bits) for i in range(devices)])]
    pallas_call x11 -> x10, Pallas kernels: 3.93 us -> 3.93 us  [in_vmem(): pl.pallas_call(kernel, out_shape=out_shape, in_specs=[HERE] * len(arrays)...]
  transfers between devices with their start and end apart: 16 -> 15, of which waited for: 8 -> 6; matrix products, arithmetic and copies ran while one was open for 0% -> 0% of each run, Pallas kernels for 21% -> 21%
where the time goes in v11:
time: 40.9 us; the launch traced here: 40.7 us
  starting transfers between devices  19.8 us (48%)
  Pallas kernels  11.9 us (29%)
  waiting for transfers between devices  8.23 us (20%)
  between operations  0.76 us (2%)
    ppermute x15, starting transfers between devices, swap(): return lax.ppermute(value, 'ep', [(i, i ^ bits) for i in range(devices)])  19.8 us
    ppermute x15, waiting for transfers between devices, swap(): return lax.ppermute(value, 'ep', [(i, i ^ bits) for i in range(devices)])  8.23 us
    pallas_call x2, Pallas kernels, from_hbm(): pl.pallas_call(kernel, out_shape=out_shape, in_specs=[pl.BlockSpec(memory...  4.24 us
    pallas_call x10, Pallas kernels, in_vmem(): pl.pallas_call(kernel, out_shape=out_shape, in_specs=[HERE] * len(arrays)...  3.93 us
    pallas_call x1, Pallas kernels, hold(): pl.pallas_call(functools.partial(hold_kernel, len(flat), pieces), out_sha...  3.75 us
  transfers between devices with their start and end apart: 15, of which 6 were waited for; matrix products, arithmetic and copies ran while one was open for 0% of the time, Pallas kernels for 21%

profile of v11, /device:TPU:0, one launch (start us, length us, event | category | flops | bytes accessed | tf_op | source)
XLA Modules:
  0.0 40.7 jit_solution(11854276821901258206)
XLA Ops:
  0.6 1.0 %prepare.1.refs_6_.refs_3_ = bf16[16,2176]{1,0:T(8,128)(2,1)S(1)} custom-call(bf16[16,2048]{1,0:T(8,128)(2,1)} %residual_ref.1, f32[1,2048]{1,0:T(1,128)} %bitcast.13, s32[8,16]{1,0:T(8,128)} %bitcast.14, f32[8,16]{1,0:T(8,128)} %bitcast.15), custom_call_target="tpu_custom_call" | custom-call | tf_op jit(solution)/shard_map/prepare/pallas_call | solution.py:77
  1.7 4.1 %collective-permute-start = (bf16[16,2176]{1,0:T(8,128)(2,1)S(1)}, bf16[16,2176]{1,0:T(8,128)(2,1)S(1)}, u32[]{:S(2)}, u32[]{:S(2)}) collective-permute-start(bf16[16,2176]{1,0:T(8,128)(2,1)S(1)} %prepare.1.refs_6_.refs_3_), channel_id=1, source_target_pairs={{0,8},{1,9},{2,10},{3,11},{4,12},{5,13},{6,14},{7,15},{8,0},{9,1},... | collective-permute-start | bytes 208904 | tf_op jit(solution)/shard_map/ppermute | solution.py:292
  5.8 1.3 %collective-permute-start.1 = (bf16[16,2176]{1,0:T(8,128)(2,1)S(1)}, bf16[16,2176]{1,0:T(8,128)(2,1)S(1)}, u32[]{:S(2)}, u32[]{:S(2)}) collective-permute-start(bf16[16,2176]{1,0:T(8,128)(2,1)S(1)} %prepare.1.refs_6_.refs_3_), channel_id=1, source_target_pairs={{0,12},{1,13},{2,14},{3,15},{4,8},{5,9},{6,10},{7,11},{8,4},{9,5},... | collective-permute-start | bytes 208904 | tf_op jit(solution)/shard_map/ppermute | solution.py:292
  7.1 0.2 collective-permute-start.2
  7.4 1.5 %collective-permute-start.3 = (bf16[16,2176]{1,0:T(8,128)(2,1)S(1)}, bf16[16,2176]{1,0:T(8,128)(2,1)S(1)}, u32[]{:S(2)}, u32[]{:S(2)}) collective-permute-start(bf16[16,2176]{1,0:T(8,128)(2,1)S(1)} %prepare.1.refs_6_.refs_3_), channel_id=1, source_target_pairs={{0,2},{1,3},{2,0},{3,1},{4,6},{5,7},{6,4},{7,5},{8,10},{9,11},{10,... | collective-permute-start | bytes 208904 | tf_op jit(solution)/shard_map/ppermute | solution.py:292
  8.8 3.2 %attend.1.refs_3_ = bf16[4,32,128]{2,1,0:T(8,128)(2,1)} custom-call(s32[4]{0:T(128)} %refs_0_.3, bf16[4,32,128]{2,1,0:T(8,128)(2,1)} %refs_1_.1, bf16[4,256,128]{2,1,0:T(8,128)(2,1)} %bitcast.11, bf16[4,256,128]{2,1,0:T(8,128)(2,1)} %bitcast.12, bf16[8,128]{1,0:T(8,128)(2,1)} %bitcast.16, bf16[8,128]{1,0:T(8,128)(2,1)} %bitcast.17, ...), custom_call_target="tpu_custom_call" | custom-call | bytes 4194304 | tf_op jit(solution)/shard_map/attend/pallas_call | solution.py:77
  12.1 0.0 collective-permute-done.refs_0_
  12.1 0.0 collective-permute-done.1.refs_1_
  12.1 0.1 collective-permute-done.2.refs_2_
  12.2 1.7 %collective-permute-start.4 = (bf16[3,16,2176]{2,1,0:T(8,128)(2,1)S(1)}, bf16[3,16,2176]{2,1,0:T(8,128)(2,1)S(1)}, u32[]{:S(2)}, u32[]{:S(2)}) collective-permute-start(bf16[3,16,2176]{2,1,0:T(8,128)(2,1)S(1)} %stack.3.refs_2_), channel_id=1, source_target_pairs={{0,2},{1,3},{2,0},{3,1},{4,6},{5,7},{6,4},{7,5},{8,10},{9,11},{10,... | collective-permute-start | bytes 626696 | tf_op jit(solution)/shard_map/ppermute | solution.py:292
  13.9 0.0 collective-permute-done.3.refs_4_
  14.0 0.1 collective-permute-start.5
  14.0 3.8 %hold.1 = (bf16[4096,768]{1,0:T(8,128)(2,1)S(1)}, bf16[768,2048]{1,0:T(8,128)(2,1)S(1)}) custom-call(bf16[4096,768]{1,0:T(8,128)(2,1)} %bitcast.9, bf16[768,2048]{1,0:T(8,128)(2,1)} %bitcast.10, bf16[3,16,2176]{2,1,0:T(8,128)(2,1)S(1)} %stack.3.refs_2_), custom_call_target="tpu_custom_call" | custom-call | bytes 9437184 | tf_op jit(solution)/shard_map/hold/pallas_call | solution.py:170
  17.8 0.4 %collective-permute-done.4.in_ref.refs_1_ = bf16[3,16,2176]{2,1,0:T(8,128)(2,1)S(1)} collective-permute-done((bf16[3,16,2176]{2,1,0:T(8,128)(2,1)S(1)}, bf16[3,16,2176]{2,1,0:T(8,128)(2,1)S(1)}, u32[]{:S(2)}, u32[]{:S(2)}) %collective-permute-start.4) | collective-permute-done | bytes 208928 | tf_op jit(solution)/shard_map/ppermute | solution.py:292
  18.3 0.1 collective-permute-start.6
  18.4 0.0 collective-permute-done.5.refs_2_
  18.4 1.4 %collective-permute-done.6.refs_3_ = bf16[3,16,2176]{2,1,0:T(8,128)(2,1)S(1)} collective-permute-done((bf16[3,16,2176]{2,1,0:T(8,128)(2,1)S(1)}, bf16[3,16,2176]{2,1,0:T(8,128)(2,1)S(1)}, u32[]{:S(2)}, u32[]{:S(2)}) %collective-permute-start.6) | collective-permute-done | bytes 208928 | tf_op jit(solution)/shard_map/ppermute | solution.py:292
  19.8 1.5 %ffn.2 = (bf16[4,16,2048]{2,1,0:T(8,128)(2,1)S(1)}, bf16[4,16,2048]{2,1,0:T(8,128)(2,1)S(1)}) custom-call(bf16[5,16,2176]{2,1,0:T(8,128)(2,1)S(1)} %stack.2.refs_0_, bf16[3,16,2176]{2,1,0:T(8,128)(2,1)S(1)} %collective-permute-done.4.in_ref.refs_1_, bf16[5,16,2176]{2,1,0:T(8,128)(2,1)S(1)} %collective-permute-done.5.refs_2_, ...), custom_call_target="tpu_custom_call" | custom-call | flops 1207959552 | bytes 6291456 | tf_op jit(solution)/shard_map/ffn/pallas_call | solution.py:272
  21.3 0.0 copy-start
  21.3 0.2 collective-permute-start.7
  21.5 1.5 %ffn.3 = (bf16[4,16,2048]{2,1,0:T(8,128)(2,1)S(1)}, bf16[4,16,2048]{2,1,0:T(8,128)(2,1)S(1)}) custom-call(bf16[5,16,2176]{2,1,0:T(8,128)(2,1)S(1)} %stack.2.refs_0_, bf16[3,16,2176]{2,1,0:T(8,128)(2,1)S(1)} %collective-permute-done.4.in_ref.refs_1_, bf16[5,16,2176]{2,1,0:T(8,128)(2,1)S(1)} %collective-permute-done.5.refs_2_, ...), custom_call_target="tpu_custom_call" | custom-call | flops 1207959552 | bytes 6291456 | tf_op jit(solution)/shard_map/ffn/pallas_call | solution.py:272
  23.1 0.4 %collective-permute-start.11 = (bf16[4,16,2048]{2,1,0:T(8,128)(2,1)S(1)}, bf16[4,16,2048]{2,1,0:T(8,128)(2,1)S(1)}, u32[]{:S(2)}, u32[]{:S(2)}) collective-permute-start(bf16[4,16,2048]{2,1,0:T(8,128)(2,1)S(1)} %get-tuple-element.25), channel_id=1, source_target_pairs={{0,1},{1,0},{2,3},{3,2},{4,5},{5,4},{6,7},{7,6},{8,9},{9,8},{10,11... | collective-permute-start | bytes 786440 | tf_op jit(solution)/shard_map/ppermute | solution.py:292
  23.5 0.0 collective-permute-done.7.other_ref
  23.5 0.1 pair_sum.2
  23.6 1.5 %collective-permute-start.8 = (bf16[2,16,2048]{2,1,0:T(8,128)(2,1)S(1)}, bf16[2,16,2048]{2,1,0:T(8,128)(2,1)S(1)}, u32[]{:S(2)}, u32[]{:S(2)}) collective-permute-start(bf16[2,16,2048]{2,1,0:T(8,128)(2,1)S(1)} %get-tuple-element.21.refs_0_), channel_id=1, source_target_pairs={{0,2},{1,3},{2,0},{3,1},{4,6},{5,7},{6,4},{7,5},{8,10},{9,11},{10,... | collective-permute-start | bytes 393224 | tf_op jit(solution)/shard_map/ppermute | solution.py:292
  25.1 0.0 collective-permute-done.11.other_ref
  25.1 0.1 pair_sum.3
  25.2 2.6 %collective-permute-start.12 = (bf16[16,2048]{1,0:T(8,128)(2,1)S(1)}, bf16[16,2048]{1,0:T(8,128)(2,1)S(1)}, u32[]{:S(2)}, u32[]{:S(2)}) collective-permute-start(bf16[16,2048]{1,0:T(8,128)(2,1)S(1)} %get-tuple-element.27), channel_id=1, source_target_pairs={{0,6},{1,7},{2,4},{3,5},{4,2},{5,3},{6,0},{7,1},{8,14},{9,15},{10,... | collective-permute-start | bytes 196616 | tf_op jit(solution)/shard_map/ppermute | solution.py:292
  27.7 2.8 %collective-permute-done.8.other_ref = bf16[2,16,2048]{2,1,0:T(8,128)(2,1)S(1)} collective-permute-done((bf16[2,16,2048]{2,1,0:T(8,128)(2,1)S(1)}, bf16[2,16,2048]{2,1,0:T(8,128)(2,1)S(1)}, u32[]{:S(2)}, u32[]{:S(2)}) %collective-permute-start.8) | collective-permute-done | bytes 131104 | tf_op jit(solution)/shard_map/ppermute | solution.py:292
  30.6 3.5 %collective-permute-start.9 = (bf16[16,2048]{1,0:T(8,128)(2,1)S(1)}, bf16[16,2048]{1,0:T(8,128)(2,1)S(1)}, u32[]{:S(2)}, u32[]{:S(2)}) collective-permute-start(bf16[16,2048]{1,0:T(8,128)(2,1)S(1)} %get-tuple-element.22), channel_id=1, source_target_pairs={{0,12},{1,13},{2,14},{3,15},{4,8},{5,9},{6,10},{7,11},{8,4},{9,5},... | collective-permute-start | bytes 196616 | tf_op jit(solution)/shard_map/ppermute | solution.py:292
  34.1 0.4 %collective-permute-start.10 = (bf16[16,2048]{1,0:T(8,128)(2,1)S(1)}, bf16[16,2048]{1,0:T(8,128)(2,1)S(1)}, u32[]{:S(2)}, u32[]{:S(2)}) collective-permute-start(bf16[16,2048]{1,0:T(8,128)(2,1)S(1)} %get-tuple-element.23), channel_id=1, source_target_pairs={{0,8},{1,9},{2,10},{3,11},{4,12},{5,13},{6,14},{7,15},{8,0},{9,1},... | collective-permute-start | bytes 196616 | tf_op jit(solution)/shard_map/ppermute | solution.py:292
  34.5 0.5 %collective-permute-start.13 = (bf16[16,2048]{1,0:T(8,128)(2,1)S(1)}, bf16[16,2048]{1,0:T(8,128)(2,1)S(1)}, u32[]{:S(2)}, u32[]{:S(2)}) collective-permute-start(bf16[16,2048]{1,0:T(8,128)(2,1)S(1)} %get-tuple-element.28), channel_id=1, source_target_pairs={{0,4},{1,5},{2,6},{3,7},{4,0},{5,1},{6,2},{7,3},{8,12},{9,13},{10,... | collective-permute-start | bytes 196616 | tf_op jit(solution)/shard_map/ppermute | solution.py:292
  35.1 1.5 %collective-permute-start.14 = (bf16[16,2048]{1,0:T(8,128)(2,1)S(1)}, bf16[16,2048]{1,0:T(8,128)(2,1)S(1)}, u32[]{:S(2)}, u32[]{:S(2)}) collective-permute-start(bf16[16,2048]{1,0:T(8,128)(2,1)S(1)} %get-tuple-element.29), channel_id=1, source_target_pairs={{0,2},{1,3},{2,0},{3,1},{4,6},{5,7},{6,4},{7,5},{8,10},{9,11},{10,... | collective-permute-start | bytes 196616 | tf_op jit(solution)/shard_map/ppermute | solution.py:292
  36.5 0.8 %collective-permute-done.9.refs_0_ = bf16[16,2048]{1,0:T(8,128)(2,1)S(1)} collective-permute-done((bf16[16,2048]{1,0:T(8,128)(2,1)S(1)}, bf16[16,2048]{1,0:T(8,128)(2,1)S(1)}, u32[]{:S(2)}, u32[]{:S(2)}) %collective-permute-start.9) | collective-permute-done | bytes 65568 | tf_op jit(solution)/shard_map/ppermute | solution.py:292
  37.4 2.6 %collective-permute-done.10.refs_1_ = bf16[16,2048]{1,0:T(8,128)(2,1)S(1)} collective-permute-done((bf16[16,2048]{1,0:T(8,128)(2,1)S(1)}, bf16[16,2048]{1,0:T(8,128)(2,1)S(1)}, u32[]{:S(2)}, u32[]{:S(2)}) %collective-permute-start.10) | collective-permute-done | bytes 65568 | tf_op jit(solution)/shard_map/ppermute | solution.py:292
  40.0 0.0 copy-done
  40.0 0.0 collective-permute-done.12.refs_1_
  40.0 0.0 collective-permute-done.13.refs_2_
  40.0 0.0 collective-permute-done.14.refs_3_
  40.0 0.7 %total.1 = bf16[16,2048]{1,0:T(8,128)(2,1)} custom-call(f32[16,2048]{1,0:T(8,128)S(1)} %partial_sum.1.residual_ref, f32[16,2048]{1,0:T(8,128)S(1)} %get-tuple-element.26.refs_0_, bf16[16,2048]{1,0:T(8,128)(2,1)S(1)} %collective-permute-done.12.refs_1_, bf16[16,2048]{1,0:T(8,128)(2,1)S(1)} %collective-permute-done.13.refs_2_, ...), custom_call_target="tpu_custom_call" | custom-call | tf_op jit(solution)/shard_map/total/pallas_call | solution.py:272
  (5 shorter events, 0.1 us)
Async XLA Ops:
  1.7 10.4 %collective-permute-start = (bf16[16,2176]{1,0:T(8,128)(2,1)S(1)}, bf16[16,2176]{1,0:T(8,128)(2,1)S(1)}, u32[]{:S(2)}, u32[]{:S(2)}) collective-permute-start(bf16[16,2176]{1,0:T(8,128)(2,1)S(1)} %prepare.1.refs_6_.refs_3_), channel_id=1, source_target_pairs={{0,8},{1,9},{2,10},{3,11},{4,12},{5,13},{6,14},{7,15},{8,0},{9,1},... | collective-permute-start | bytes 208904 | tf_op jit(solution)/shard_map/ppermute | solution.py:292
  5.8 6.3 %collective-permute-start.1 = (bf16[16,2176]{1,0:T(8,128)(2,1)S(1)}, bf16[16,2176]{1,0:T(8,128)(2,1)S(1)}, u32[]{:S(2)}, u32[]{:S(2)}) collective-permute-start(bf16[16,2176]{1,0:T(8,128)(2,1)S(1)} %prepare.1.refs_6_.refs_3_), channel_id=1, source_target_pairs={{0,12},{1,13},{2,14},{3,15},{4,8},{5,9},{6,10},{7,11},{8,4},{9,5},... | collective-permute-start | bytes 208904 | tf_op jit(solution)/shard_map/ppermute | solution.py:292
  7.1 5.1 %collective-permute-start.2 = (bf16[16,2176]{1,0:T(8,128)(2,1)S(1)}, bf16[16,2176]{1,0:T(8,128)(2,1)S(1)}, u32[]{:S(2)}, u32[]{:S(2)}) collective-permute-start(bf16[16,2176]{1,0:T(8,128)(2,1)S(1)} %prepare.1.refs_6_.refs_3_), channel_id=1, source_target_pairs={{0,4},{1,5},{2,6},{3,7},{4,0},{5,1},{6,2},{7,3},{8,12},{9,13},{10,... | collective-permute-start | bytes 208904 | tf_op jit(solution)/shard_map/ppermute | solution.py:292
  7.4 6.6 %collective-permute-start.3 = (bf16[16,2176]{1,0:T(8,128)(2,1)S(1)}, bf16[16,2176]{1,0:T(8,128)(2,1)S(1)}, u32[]{:S(2)}, u32[]{:S(2)}) collective-permute-start(bf16[16,2176]{1,0:T(8,128)(2,1)S(1)} %prepare.1.refs_6_.refs_3_), channel_id=1, source_target_pairs={{0,2},{1,3},{2,0},{3,1},{4,6},{5,7},{6,4},{7,5},{8,10},{9,11},{10,... | collective-permute-start | bytes 208904 | tf_op jit(solution)/shard_map/ppermute | solution.py:292
  12.2 6.0 %collective-permute-start.4 = (bf16[3,16,2176]{2,1,0:T(8,128)(2,1)S(1)}, bf16[3,16,2176]{2,1,0:T(8,128)(2,1)S(1)}, u32[]{:S(2)}, u32[]{:S(2)}) collective-permute-start(bf16[3,16,2176]{2,1,0:T(8,128)(2,1)S(1)} %stack.3.refs_2_), channel_id=1, source_target_pairs={{0,2},{1,3},{2,0},{3,1},{4,6},{5,7},{6,4},{7,5},{8,10},{9,11},{10,... | collective-permute-start | bytes 626696 | tf_op jit(solution)/shard_map/ppermute | solution.py:292
  14.0 4.4 %collective-permute-start.5 = (bf16[5,16,2176]{2,1,0:T(8,128)(2,1)S(1)}, bf16[5,16,2176]{2,1,0:T(8,128)(2,1)S(1)}, u32[]{:S(2)}, u32[]{:S(2)}) collective-permute-start(bf16[5,16,2176]{2,1,0:T(8,128)(2,1)S(1)} %stack.2.refs_0_), channel_id=1, source_target_pairs={{0,1},{1,0},{2,3},{3,2},{4,5},{5,4},{6,7},{7,6},{8,9},{9,8},{10,11... | collective-permute-start | bytes 1044488 | tf_op jit(solution)/shard_map/ppermute | solution.py:292
  18.3 1.5 %collective-permute-start.6 = (bf16[3,16,2176]{2,1,0:T(8,128)(2,1)S(1)}, bf16[3,16,2176]{2,1,0:T(8,128)(2,1)S(1)}, u32[]{:S(2)}, u32[]{:S(2)}) collective-permute-start(bf16[3,16,2176]{2,1,0:T(8,128)(2,1)S(1)} %relay.1), channel_id=1, source_target_pairs={{0,1},{1,0},{2,3},{3,2},{4,5},{5,4},{6,7},{7,6},{8,9},{9,8},{10,11... | collective-permute-start | bytes 626696 | tf_op jit(solution)/shard_map/ppermute | solution.py:292
  21.3 18.7 %copy-start = (bf16[16,2048]{1,0:T(8,128)(2,1)S(1)}, bf16[16,2048]{1,0:T(8,128)(2,1)}, u32[]{:S(2)}) copy-start(bf16[16,2048]{1,0:T(8,128)(2,1)} %residual_ref.1) | copy-start | bytes 196612
  21.3 2.2 %collective-permute-start.7 = (bf16[4,16,2048]{2,1,0:T(8,128)(2,1)S(1)}, bf16[4,16,2048]{2,1,0:T(8,128)(2,1)S(1)}, u32[]{:S(2)}, u32[]{:S(2)}) collective-permute-start(bf16[4,16,2048]{2,1,0:T(8,128)(2,1)S(1)} %get-tuple-element.19), channel_id=1, source_target_pairs={{0,1},{1,0},{2,3},{3,2},{4,5},{5,4},{6,7},{7,6},{8,9},{9,8},{10,11... | collective-permute-start | bytes 786440 | tf_op jit(solution)/shard_map/ppermute | solution.py:292
  23.1 2.1 %collective-permute-start.11 = (bf16[4,16,2048]{2,1,0:T(8,128)(2,1)S(1)}, bf16[4,16,2048]{2,1,0:T(8,128)(2,1)S(1)}, u32[]{:S(2)}, u32[]{:S(2)}) collective-permute-start(bf16[4,16,2048]{2,1,0:T(8,128)(2,1)S(1)} %get-tuple-element.25), channel_id=1, source_target_pairs={{0,1},{1,0},{2,3},{3,2},{4,5},{5,4},{6,7},{7,6},{8,9},{9,8},{10,11... | collective-permute-start | bytes 786440 | tf_op jit(solution)/shard_map/ppermute | solution.py:292
  23.6 7.0 %collective-permute-start.8 = (bf16[2,16,2048]{2,1,0:T(8,128)(2,1)S(1)}, bf16[2,16,2048]{2,1,0:T(8,128)(2,1)S(1)}, u32[]{:S(2)}, u32[]{:S(2)}) collective-permute-start(bf16[2,16,2048]{2,1,0:T(8,128)(2,1)S(1)} %get-tuple-element.21.refs_0_), channel_id=1, source_target_pairs={{0,2},{1,3},{2,0},{3,1},{4,6},{5,7},{6,4},{7,5},{8,10},{9,11},{10,... | collective-permute-start | bytes 393224 | tf_op jit(solution)/shard_map/ppermute | solution.py:292
  25.2 14.8 %collective-permute-start.12 = (bf16[16,2048]{1,0:T(8,128)(2,1)S(1)}, bf16[16,2048]{1,0:T(8,128)(2,1)S(1)}, u32[]{:S(2)}, u32[]{:S(2)}) collective-permute-start(bf16[16,2048]{1,0:T(8,128)(2,1)S(1)} %get-tuple-element.27), channel_id=1, source_target_pairs={{0,6},{1,7},{2,4},{3,5},{4,2},{5,3},{6,0},{7,1},{8,14},{9,15},{10,... | collective-permute-start | bytes 196616 | tf_op jit(solution)/shard_map/ppermute | solution.py:292
  30.6 6.8 %collective-permute-start.9 = (bf16[16,2048]{1,0:T(8,128)(2,1)S(1)}, bf16[16,2048]{1,0:T(8,128)(2,1)S(1)}, u32[]{:S(2)}, u32[]{:S(2)}) collective-permute-start(bf16[16,2048]{1,0:T(8,128)(2,1)S(1)} %get-tuple-element.22), channel_id=1, source_target_pairs={{0,12},{1,13},{2,14},{3,15},{4,8},{5,9},{6,10},{7,11},{8,4},{9,5},... | collective-permute-start | bytes 196616 | tf_op jit(solution)/shard_map/ppermute | solution.py:292
  34.1 5.9 %collective-permute-start.10 = (bf16[16,2048]{1,0:T(8,128)(2,1)S(1)}, bf16[16,2048]{1,0:T(8,128)(2,1)S(1)}, u32[]{:S(2)}, u32[]{:S(2)}) collective-permute-start(bf16[16,2048]{1,0:T(8,128)(2,1)S(1)} %get-tuple-element.23), channel_id=1, source_target_pairs={{0,8},{1,9},{2,10},{3,11},{4,12},{5,13},{6,14},{7,15},{8,0},{9,1},... | collective-permute-start | bytes 196616 | tf_op jit(solution)/shard_map/ppermute | solution.py:292
  34.5 5.5 %collective-permute-start.13 = (bf16[16,2048]{1,0:T(8,128)(2,1)S(1)}, bf16[16,2048]{1,0:T(8,128)(2,1)S(1)}, u32[]{:S(2)}, u32[]{:S(2)}) collective-permute-start(bf16[16,2048]{1,0:T(8,128)(2,1)S(1)} %get-tuple-element.28), channel_id=1, source_target_pairs={{0,4},{1,5},{2,6},{3,7},{4,0},{5,1},{6,2},{7,3},{8,12},{9,13},{10,... | collective-permute-start | bytes 196616 | tf_op jit(solution)/shard_map/ppermute | solution.py:292
  35.1 5.0 %collective-permute-start.14 = (bf16[16,2048]{1,0:T(8,128)(2,1)S(1)}, bf16[16,2048]{1,0:T(8,128)(2,1)S(1)}, u32[]{:S(2)}, u32[]{:S(2)}) collective-permute-start(bf16[16,2048]{1,0:T(8,128)(2,1)S(1)} %get-tuple-element.29), channel_id=1, source_target_pairs={{0,2},{1,3},{2,0},{3,1},{4,6},{5,7},{6,4},{7,5},{8,10},{9,11},{10,... | collective-permute-start | bytes 196616 | tf_op jit(solution)/shard_map/ppermute | solution.py:292

commit v12 on v8

--- a/solution.py
+++ b/solution.py
@@ -325,15 +325,15 @@
     second_keep, third_keep, second_send, third_send = in_vmem(
         pair_kernel, keep_and_send, "pair_sum", (early_outs[0], swap(early_outs[1], core))
     )
-    third_sum = in_vmem(add_kernel, send, "side_sum", (third_keep, swap(third_send, side)))
-    second_sum = in_vmem(
-        add_kernel, send, "side_sum", (second_keep, swap(second_send, side)), (third_sum,)
+    second_sum = in_vmem(add_kernel, send, "side_sum", (second_keep, swap(second_send, side)))
+    third_sum = in_vmem(
+        add_kernel, send, "side_sum", (third_keep, swap(third_send, side)), (second_sum,)
     )
     partial_sum = in_vmem(
         total_kernel,
         vmem(one, jnp.float32),
         "partial_sum",
-        (residual, swap(third_sum, 3 * line), swap(second_sum, 2 * line)),
+        (residual, swap(second_sum, 2 * line), swap(third_sum, 3 * line)),
     )
     late_outs = ffn([(3, 5), (2, 3)], [(2, 3)], early_outs[:1])
     own, across_sum, first_sum, diagonal_sum = in_vmem(

time: 39.6 us -> 39.7 us (level)
  starting transfers between devices: 21.5 us -> 21.9 us
  transfers between devices with their start and end apart: 16 -> 16, of which waited for: 6 -> 7; matrix products, arithmetic and copies ran while one was open for 0% -> 0% of each run, Pallas kernels for 22% -> 22%
where the time goes in v12:
time: 39.7 us; the launch traced here: 39.5 us
  starting transfers between devices  21.9 us (55%)
  Pallas kernels  11.9 us (30%)
  waiting for transfers between devices  4.96 us (12%)
  between operations  0.75 us (2%)
    ppermute x16, starting transfers between devices, swap(): return lax.ppermute(value, 'ep', [(i, i ^ bits) for i in range(devices)])  21.9 us
    ppermute x16, waiting for transfers between devices, swap(): return lax.ppermute(value, 'ep', [(i, i ^ bits) for i in range(devices)])  4.96 us
    pallas_call x2, Pallas kernels, from_hbm(): pl.pallas_call(kernel, out_shape=out_shape, in_specs=[pl.BlockSpec(memory...  4.24 us
    pallas_call x11, Pallas kernels, in_vmem(): pl.pallas_call(kernel, out_shape=out_shape, in_specs=[HERE] * len(arrays)...  3.93 us
    pallas_call x1, Pallas kernels, hold(): pl.pallas_call(functools.partial(hold_kernel, len(flat), pieces), out_sha...  3.75 us
  transfers between devices with their start and end apart: 16, of which 7 were waited for; matrix products, arithmetic and copies ran while one was open for 0% of the time, Pallas kernels for 22%

profile of v12, /device:TPU:0, one launch (start us, length us, event | category | flops | bytes accessed | tf_op | source)
XLA Modules:
  0.0 39.5 jit_solution(14559797027594411866)
XLA Ops:
  0.6 1.0 %prepare.1.refs_6_.refs_3_ = bf16[16,2176]{1,0:T(8,128)(2,1)S(1)} custom-call(bf16[16,2048]{1,0:T(8,128)(2,1)} %residual_ref.1, f32[1,2048]{1,0:T(1,128)} %bitcast.13, s32[8,16]{1,0:T(8,128)} %bitcast.14, f32[8,16]{1,0:T(8,128)} %bitcast.15), custom_call_target="tpu_custom_call" | custom-call | tf_op jit(solution)/shard_map/prepare/pallas_call | solution.py:77
  1.7 4.1 %collective-permute-start = (bf16[16,2176]{1,0:T(8,128)(2,1)S(1)}, bf16[16,2176]{1,0:T(8,128)(2,1)S(1)}, u32[]{:S(2)}, u32[]{:S(2)}) collective-permute-start(bf16[16,2176]{1,0:T(8,128)(2,1)S(1)} %prepare.1.refs_6_.refs_3_), channel_id=1, source_target_pairs={{0,8},{1,9},{2,10},{3,11},{4,12},{5,13},{6,14},{7,15},{8,0},{9,1},... | collective-permute-start | bytes 208904 | tf_op jit(solution)/shard_map/ppermute | solution.py:283
  5.8 1.3 %collective-permute-start.1 = (bf16[16,2176]{1,0:T(8,128)(2,1)S(1)}, bf16[16,2176]{1,0:T(8,128)(2,1)S(1)}, u32[]{:S(2)}, u32[]{:S(2)}) collective-permute-start(bf16[16,2176]{1,0:T(8,128)(2,1)S(1)} %prepare.1.refs_6_.refs_3_), channel_id=1, source_target_pairs={{0,12},{1,13},{2,14},{3,15},{4,8},{5,9},{6,10},{7,11},{8,4},{9,5},... | collective-permute-start | bytes 208904 | tf_op jit(solution)/shard_map/ppermute | solution.py:283
  7.1 0.2 collective-permute-start.2
  7.4 1.5 %collective-permute-start.3 = (bf16[16,2176]{1,0:T(8,128)(2,1)S(1)}, bf16[16,2176]{1,0:T(8,128)(2,1)S(1)}, u32[]{:S(2)}, u32[]{:S(2)}) collective-permute-start(bf16[16,2176]{1,0:T(8,128)(2,1)S(1)} %prepare.1.refs_6_.refs_3_), channel_id=1, source_target_pairs={{0,2},{1,3},{2,0},{3,1},{4,6},{5,7},{6,4},{7,5},{8,10},{9,11},{10,... | collective-permute-start | bytes 208904 | tf_op jit(solution)/shard_map/ppermute | solution.py:283
  8.8 3.2 %attend.1.refs_3_ = bf16[4,32,128]{2,1,0:T(8,128)(2,1)} custom-call(s32[4]{0:T(128)} %refs_0_.3, bf16[4,32,128]{2,1,0:T(8,128)(2,1)} %refs_1_.1, bf16[4,256,128]{2,1,0:T(8,128)(2,1)} %bitcast.11, bf16[4,256,128]{2,1,0:T(8,128)(2,1)} %bitcast.12, bf16[8,128]{1,0:T(8,128)(2,1)} %bitcast.16, bf16[8,128]{1,0:T(8,128)(2,1)} %bitcast.17, ...), custom_call_target="tpu_custom_call" | custom-call | bytes 4194304 | tf_op jit(solution)/shard_map/attend/pallas_call | solution.py:77
  12.1 0.0 collective-permute-done.refs_0_
  12.1 0.0 collective-permute-done.1.refs_1_
  12.1 0.1 collective-permute-done.2.refs_2_
  12.2 1.7 %collective-permute-start.4 = (bf16[3,16,2176]{2,1,0:T(8,128)(2,1)S(1)}, bf16[3,16,2176]{2,1,0:T(8,128)(2,1)S(1)}, u32[]{:S(2)}, u32[]{:S(2)}) collective-permute-start(bf16[3,16,2176]{2,1,0:T(8,128)(2,1)S(1)} %stack.3.refs_2_), channel_id=1, source_target_pairs={{0,2},{1,3},{2,0},{3,1},{4,6},{5,7},{6,4},{7,5},{8,10},{9,11},{10,... | collective-permute-start | bytes 626696 | tf_op jit(solution)/shard_map/ppermute | solution.py:283
  13.9 0.0 collective-permute-done.3.refs_4_
  14.0 0.1 collective-permute-start.5
  14.0 3.8 %hold.1 = (bf16[4096,768]{1,0:T(8,128)(2,1)S(1)}, bf16[768,2048]{1,0:T(8,128)(2,1)S(1)}) custom-call(bf16[4096,768]{1,0:T(8,128)(2,1)} %bitcast.9, bf16[768,2048]{1,0:T(8,128)(2,1)} %bitcast.10, bf16[3,16,2176]{2,1,0:T(8,128)(2,1)S(1)} %stack.3.refs_2_), custom_call_target="tpu_custom_call" | custom-call | bytes 9437184 | tf_op jit(solution)/shard_map/hold/pallas_call | solution.py:170
  17.8 0.4 %collective-permute-done.4.in_ref.refs_1_ = bf16[3,16,2176]{2,1,0:T(8,128)(2,1)S(1)} collective-permute-done((bf16[3,16,2176]{2,1,0:T(8,128)(2,1)S(1)}, bf16[3,16,2176]{2,1,0:T(8,128)(2,1)S(1)}, u32[]{:S(2)}, u32[]{:S(2)}) %collective-permute-start.4) | collective-permute-done | bytes 208928 | tf_op jit(solution)/shard_map/ppermute | solution.py:283
  18.3 0.1 collective-permute-start.6
  18.4 0.0 collective-permute-done.5.refs_2_
  18.4 1.4 %collective-permute-done.6.refs_3_ = bf16[3,16,2176]{2,1,0:T(8,128)(2,1)S(1)} collective-permute-done((bf16[3,16,2176]{2,1,0:T(8,128)(2,1)S(1)}, bf16[3,16,2176]{2,1,0:T(8,128)(2,1)S(1)}, u32[]{:S(2)}, u32[]{:S(2)}) %collective-permute-start.6) | collective-permute-done | bytes 208928 | tf_op jit(solution)/shard_map/ppermute | solution.py:283
  19.8 1.5 %ffn.2 = (bf16[4,16,2048]{2,1,0:T(8,128)(2,1)S(1)}, bf16[4,16,2048]{2,1,0:T(8,128)(2,1)S(1)}) custom-call(bf16[5,16,2176]{2,1,0:T(8,128)(2,1)S(1)} %stack.2.refs_0_, bf16[3,16,2176]{2,1,0:T(8,128)(2,1)S(1)} %collective-permute-done.4.in_ref.refs_1_, bf16[5,16,2176]{2,1,0:T(8,128)(2,1)S(1)} %collective-permute-done.5.refs_2_, ...), custom_call_target="tpu_custom_call" | custom-call | flops 1207959552 | bytes 6291456 | tf_op jit(solution)/shard_map/ffn/pallas_call | solution.py:263
  21.3 0.0 copy-start
  21.3 0.2 collective-permute-start.7
  21.5 1.5 %ffn.3 = (bf16[4,16,2048]{2,1,0:T(8,128)(2,1)S(1)}, bf16[4,16,2048]{2,1,0:T(8,128)(2,1)S(1)}) custom-call(bf16[5,16,2176]{2,1,0:T(8,128)(2,1)S(1)} %stack.2.refs_0_, bf16[3,16,2176]{2,1,0:T(8,128)(2,1)S(1)} %collective-permute-done.4.in_ref.refs_1_, bf16[5,16,2176]{2,1,0:T(8,128)(2,1)S(1)} %collective-permute-done.5.refs_2_, ...), custom_call_target="tpu_custom_call" | custom-call | flops 1207959552 | bytes 6291456 | tf_op jit(solution)/shard_map/ffn/pallas_call | solution.py:263
  23.1 0.4 %collective-permute-start.12 = (bf16[4,16,2048]{2,1,0:T(8,128)(2,1)S(1)}, bf16[4,16,2048]{2,1,0:T(8,128)(2,1)S(1)}, u32[]{:S(2)}, u32[]{:S(2)}) collective-permute-start(bf16[4,16,2048]{2,1,0:T(8,128)(2,1)S(1)} %get-tuple-element.25), channel_id=1, source_target_pairs={{0,1},{1,0},{2,3},{3,2},{4,5},{5,4},{6,7},{7,6},{8,9},{9,8},{10,11... | collective-permute-start | bytes 786440 | tf_op jit(solution)/shard_map/ppermute | solution.py:283
  23.5 0.0 collective-permute-done.7.other_ref
  23.5 0.1 pair_sum.2
  23.6 1.5 %collective-permute-start.8 = (bf16[16,2048]{1,0:T(8,128)(2,1)S(1)}, bf16[16,2048]{1,0:T(8,128)(2,1)S(1)}, u32[]{:S(2)}, u32[]{:S(2)}) collective-permute-start(bf16[16,2048]{1,0:T(8,128)(2,1)S(1)} %get-tuple-element.21), channel_id=1, source_target_pairs={{0,2},{1,3},{2,0},{3,1},{4,6},{5,7},{6,4},{7,5},{8,10},{9,11},{10,... | collective-permute-start | bytes 196616 | tf_op jit(solution)/shard_map/ppermute | solution.py:283
  25.1 0.5 %collective-permute-start.10 = (bf16[16,2048]{1,0:T(8,128)(2,1)S(1)}, bf16[16,2048]{1,0:T(8,128)(2,1)S(1)}, u32[]{:S(2)}, u32[]{:S(2)}) collective-permute-start(bf16[16,2048]{1,0:T(8,128)(2,1)S(1)} %get-tuple-element.23.refs_0_), channel_id=1, source_target_pairs={{0,2},{1,3},{2,0},{3,1},{4,6},{5,7},{6,4},{7,5},{8,10},{9,11},{10,... | collective-permute-start | bytes 196616 | tf_op jit(solution)/shard_map/ppermute | solution.py:283
  25.7 0.0 collective-permute-done.12.other_ref
  25.7 0.1 pair_sum.3
  25.7 3.0 %collective-permute-start.13 = (bf16[16,2048]{1,0:T(8,128)(2,1)S(1)}, bf16[16,2048]{1,0:T(8,128)(2,1)S(1)}, u32[]{:S(2)}, u32[]{:S(2)}) collective-permute-start(bf16[16,2048]{1,0:T(8,128)(2,1)S(1)} %get-tuple-element.27), channel_id=1, source_target_pairs={{0,6},{1,7},{2,4},{3,5},{4,2},{5,3},{6,0},{7,1},{8,14},{9,15},{10,... | collective-permute-start | bytes 196616 | tf_op jit(solution)/shard_map/ppermute | solution.py:283
  28.7 0.0 collective-permute-done.8.other_ref
  28.7 3.4 %collective-permute-start.9 = (bf16[16,2048]{1,0:T(8,128)(2,1)S(1)}, bf16[16,2048]{1,0:T(8,128)(2,1)S(1)}, u32[]{:S(2)}, u32[]{:S(2)}) collective-permute-start(bf16[16,2048]{1,0:T(8,128)(2,1)S(1)} %side_sum.2.refs_0_), channel_id=1, source_target_pairs={{0,8},{1,9},{2,10},{3,11},{4,12},{5,13},{6,14},{7,15},{8,0},{9,1},... | collective-permute-start | bytes 196616 | tf_op jit(solution)/shard_map/ppermute | solution.py:283
  32.2 0.0 collective-permute-done.10.other_ref
  32.2 1.4 %collective-permute-start.11 = (bf16[16,2048]{1,0:T(8,128)(2,1)S(1)}, bf16[16,2048]{1,0:T(8,128)(2,1)S(1)}, u32[]{:S(2)}, u32[]{:S(2)}) collective-permute-start(bf16[16,2048]{1,0:T(8,128)(2,1)S(1)} %side_sum.3), channel_id=1, source_target_pairs={{0,12},{1,13},{2,14},{3,15},{4,8},{5,9},{6,10},{7,11},{8,4},{9,5},... | collective-permute-start | bytes 196616 | tf_op jit(solution)/shard_map/ppermute | solution.py:283
  33.6 1.0 %collective-permute-start.14 = (bf16[16,2048]{1,0:T(8,128)(2,1)S(1)}, bf16[16,2048]{1,0:T(8,128)(2,1)S(1)}, u32[]{:S(2)}, u32[]{:S(2)}) collective-permute-start(bf16[16,2048]{1,0:T(8,128)(2,1)S(1)} %get-tuple-element.28), channel_id=1, source_target_pairs={{0,4},{1,5},{2,6},{3,7},{4,0},{5,1},{6,2},{7,3},{8,12},{9,13},{10,... | collective-permute-start | bytes 196616 | tf_op jit(solution)/shard_map/ppermute | solution.py:283
  34.6 1.2 %collective-permute-start.15 = (bf16[16,2048]{1,0:T(8,128)(2,1)S(1)}, bf16[16,2048]{1,0:T(8,128)(2,1)S(1)}, u32[]{:S(2)}, u32[]{:S(2)}) collective-permute-start(bf16[16,2048]{1,0:T(8,128)(2,1)S(1)} %get-tuple-element.29), channel_id=1, source_target_pairs={{0,2},{1,3},{2,0},{3,1},{4,6},{5,7},{6,4},{7,5},{8,10},{9,11},{10,... | collective-permute-start | bytes 196616 | tf_op jit(solution)/shard_map/ppermute | solution.py:283
  35.8 0.7 %collective-permute-done.9.refs_0_ = bf16[16,2048]{1,0:T(8,128)(2,1)S(1)} collective-permute-done((bf16[16,2048]{1,0:T(8,128)(2,1)S(1)}, bf16[16,2048]{1,0:T(8,128)(2,1)S(1)}, u32[]{:S(2)}, u32[]{:S(2)}) %collective-permute-start.9) | collective-permute-done | bytes 65568 | tf_op jit(solution)/shard_map/ppermute | solution.py:283
  36.5 1.9 %collective-permute-done.11.refs_1_ = bf16[16,2048]{1,0:T(8,128)(2,1)S(1)} collective-permute-done((bf16[16,2048]{1,0:T(8,128)(2,1)S(1)}, bf16[16,2048]{1,0:T(8,128)(2,1)S(1)}, u32[]{:S(2)}, u32[]{:S(2)}) %collective-permute-start.11) | collective-permute-done | bytes 65568 | tf_op jit(solution)/shard_map/ppermute | solution.py:283
  38.4 0.0 copy-done
  38.5 0.0 collective-permute-done.13.refs_1_
  38.5 0.1 collective-permute-done.14.refs_2_
  38.6 0.2 collective-permute-done.15.refs_3_
  38.8 0.7 %total.1 = bf16[16,2048]{1,0:T(8,128)(2,1)} custom-call(f32[16,2048]{1,0:T(8,128)S(1)} %partial_sum.1.residual_ref, f32[16,2048]{1,0:T(8,128)S(1)} %get-tuple-element.26.refs_0_, bf16[16,2048]{1,0:T(8,128)(2,1)S(1)} %collective-permute-done.13.refs_1_, bf16[16,2048]{1,0:T(8,128)(2,1)S(1)} %collective-permute-done.14.refs_2_, ...), custom_call_target="tpu_custom_call" | custom-call | tf_op jit(solution)/shard_map/total/pallas_call | solution.py:263
  (6 shorter events, 0.1 us)
Async XLA Ops:
  1.7 10.4 %collective-permute-start = (bf16[16,2176]{1,0:T(8,128)(2,1)S(1)}, bf16[16,2176]{1,0:T(8,128)(2,1)S(1)}, u32[]{:S(2)}, u32[]{:S(2)}) collective-permute-start(bf16[16,2176]{1,0:T(8,128)(2,1)S(1)} %prepare.1.refs_6_.refs_3_), channel_id=1, source_target_pairs={{0,8},{1,9},{2,10},{3,11},{4,12},{5,13},{6,14},{7,15},{8,0},{9,1},... | collective-permute-start | bytes 208904 | tf_op jit(solution)/shard_map/ppermute | solution.py:283
  5.8 6.3 %collective-permute-start.1 = (bf16[16,2176]{1,0:T(8,128)(2,1)S(1)}, bf16[16,2176]{1,0:T(8,128)(2,1)S(1)}, u32[]{:S(2)}, u32[]{:S(2)}) collective-permute-start(bf16[16,2176]{1,0:T(8,128)(2,1)S(1)} %prepare.1.refs_6_.refs_3_), channel_id=1, source_target_pairs={{0,12},{1,13},{2,14},{3,15},{4,8},{5,9},{6,10},{7,11},{8,4},{9,5},... | collective-permute-start | bytes 208904 | tf_op jit(solution)/shard_map/ppermute | solution.py:283
  7.1 5.1 %collective-permute-start.2 = (bf16[16,2176]{1,0:T(8,128)(2,1)S(1)}, bf16[16,2176]{1,0:T(8,128)(2,1)S(1)}, u32[]{:S(2)}, u32[]{:S(2)}) collective-permute-start(bf16[16,2176]{1,0:T(8,128)(2,1)S(1)} %prepare.1.refs_6_.refs_3_), channel_id=1, source_target_pairs={{0,4},{1,5},{2,6},{3,7},{4,0},{5,1},{6,2},{7,3},{8,12},{9,13},{10,... | collective-permute-start | bytes 208904 | tf_op jit(solution)/shard_map/ppermute | solution.py:283
  7.4 6.6 %collective-permute-start.3 = (bf16[16,2176]{1,0:T(8,128)(2,1)S(1)}, bf16[16,2176]{1,0:T(8,128)(2,1)S(1)}, u32[]{:S(2)}, u32[]{:S(2)}) collective-permute-start(bf16[16,2176]{1,0:T(8,128)(2,1)S(1)} %prepare.1.refs_6_.refs_3_), channel_id=1, source_target_pairs={{0,2},{1,3},{2,0},{3,1},{4,6},{5,7},{6,4},{7,5},{8,10},{9,11},{10,... | collective-permute-start | bytes 208904 | tf_op jit(solution)/shard_map/ppermute | solution.py:283
  12.2 6.0 %collective-permute-start.4 = (bf16[3,16,2176]{2,1,0:T(8,128)(2,1)S(1)}, bf16[3,16,2176]{2,1,0:T(8,128)(2,1)S(1)}, u32[]{:S(2)}, u32[]{:S(2)}) collective-permute-start(bf16[3,16,2176]{2,1,0:T(8,128)(2,1)S(1)} %stack.3.refs_2_), channel_id=1, source_target_pairs={{0,2},{1,3},{2,0},{3,1},{4,6},{5,7},{6,4},{7,5},{8,10},{9,11},{10,... | collective-permute-start | bytes 626696 | tf_op jit(solution)/shard_map/ppermute | solution.py:283
  14.0 4.4 %collective-permute-start.5 = (bf16[5,16,2176]{2,1,0:T(8,128)(2,1)S(1)}, bf16[5,16,2176]{2,1,0:T(8,128)(2,1)S(1)}, u32[]{:S(2)}, u32[]{:S(2)}) collective-permute-start(bf16[5,16,2176]{2,1,0:T(8,128)(2,1)S(1)} %stack.2.refs_0_), channel_id=1, source_target_pairs={{0,1},{1,0},{2,3},{3,2},{4,5},{5,4},{6,7},{7,6},{8,9},{9,8},{10,11... | collective-permute-start | bytes 1044488 | tf_op jit(solution)/shard_map/ppermute | solution.py:283
  18.3 1.5 %collective-permute-start.6 = (bf16[3,16,2176]{2,1,0:T(8,128)(2,1)S(1)}, bf16[3,16,2176]{2,1,0:T(8,128)(2,1)S(1)}, u32[]{:S(2)}, u32[]{:S(2)}) collective-permute-start(bf16[3,16,2176]{2,1,0:T(8,128)(2,1)S(1)} %relay.1), channel_id=1, source_target_pairs={{0,1},{1,0},{2,3},{3,2},{4,5},{5,4},{6,7},{7,6},{8,9},{9,8},{10,11... | collective-permute-start | bytes 626696 | tf_op jit(solution)/shard_map/ppermute | solution.py:283
  21.3 17.1 %copy-start = (bf16[16,2048]{1,0:T(8,128)(2,1)S(1)}, bf16[16,2048]{1,0:T(8,128)(2,1)}, u32[]{:S(2)}) copy-start(bf16[16,2048]{1,0:T(8,128)(2,1)} %residual_ref.1) | copy-start | bytes 196612
  21.3 2.2 %collective-permute-start.7 = (bf16[4,16,2048]{2,1,0:T(8,128)(2,1)S(1)}, bf16[4,16,2048]{2,1,0:T(8,128)(2,1)S(1)}, u32[]{:S(2)}, u32[]{:S(2)}) collective-permute-start(bf16[4,16,2048]{2,1,0:T(8,128)(2,1)S(1)} %get-tuple-element.19), channel_id=1, source_target_pairs={{0,1},{1,0},{2,3},{3,2},{4,5},{5,4},{6,7},{7,6},{8,9},{9,8},{10,11... | collective-permute-start | bytes 786440 | tf_op jit(solution)/shard_map/ppermute | solution.py:283
  23.1 2.6 %collective-permute-start.12 = (bf16[4,16,2048]{2,1,0:T(8,128)(2,1)S(1)}, bf16[4,16,2048]{2,1,0:T(8,128)(2,1)S(1)}, u32[]{:S(2)}, u32[]{:S(2)}) collective-permute-start(bf16[4,16,2048]{2,1,0:T(8,128)(2,1)S(1)} %get-tuple-element.25), channel_id=1, source_target_pairs={{0,1},{1,0},{2,3},{3,2},{4,5},{5,4},{6,7},{7,6},{8,9},{9,8},{10,11... | collective-permute-start | bytes 786440 | tf_op jit(solution)/shard_map/ppermute | solution.py:283
  23.6 5.2 %collective-permute-start.8 = (bf16[16,2048]{1,0:T(8,128)(2,1)S(1)}, bf16[16,2048]{1,0:T(8,128)(2,1)S(1)}, u32[]{:S(2)}, u32[]{:S(2)}) collective-permute-start(bf16[16,2048]{1,0:T(8,128)(2,1)S(1)} %get-tuple-element.21), channel_id=1, source_target_pairs={{0,2},{1,3},{2,0},{3,1},{4,6},{5,7},{6,4},{7,5},{8,10},{9,11},{10,... | collective-permute-start | bytes 196616 | tf_op jit(solution)/shard_map/ppermute | solution.py:283
  25.1 7.1 %collective-permute-start.10 = (bf16[16,2048]{1,0:T(8,128)(2,1)S(1)}, bf16[16,2048]{1,0:T(8,128)(2,1)S(1)}, u32[]{:S(2)}, u32[]{:S(2)}) collective-permute-start(bf16[16,2048]{1,0:T(8,128)(2,1)S(1)} %get-tuple-element.23.refs_0_), channel_id=1, source_target_pairs={{0,2},{1,3},{2,0},{3,1},{4,6},{5,7},{6,4},{7,5},{8,10},{9,11},{10,... | collective-permute-start | bytes 196616 | tf_op jit(solution)/shard_map/ppermute | solution.py:283
  25.7 12.7 %collective-permute-start.13 = (bf16[16,2048]{1,0:T(8,128)(2,1)S(1)}, bf16[16,2048]{1,0:T(8,128)(2,1)S(1)}, u32[]{:S(2)}, u32[]{:S(2)}) collective-permute-start(bf16[16,2048]{1,0:T(8,128)(2,1)S(1)} %get-tuple-element.27), channel_id=1, source_target_pairs={{0,6},{1,7},{2,4},{3,5},{4,2},{5,3},{6,0},{7,1},{8,14},{9,15},{10,... | collective-permute-start | bytes 196616 | tf_op jit(solution)/shard_map/ppermute | solution.py:283
  28.7 7.8 %collective-permute-start.9 = (bf16[16,2048]{1,0:T(8,128)(2,1)S(1)}, bf16[16,2048]{1,0:T(8,128)(2,1)S(1)}, u32[]{:S(2)}, u32[]{:S(2)}) collective-permute-start(bf16[16,2048]{1,0:T(8,128)(2,1)S(1)} %side_sum.2.refs_0_), channel_id=1, source_target_pairs={{0,8},{1,9},{2,10},{3,11},{4,12},{5,13},{6,14},{7,15},{8,0},{9,1},... | collective-permute-start | bytes 196616 | tf_op jit(solution)/shard_map/ppermute | solution.py:283
  32.2 6.2 %collective-permute-start.11 = (bf16[16,2048]{1,0:T(8,128)(2,1)S(1)}, bf16[16,2048]{1,0:T(8,128)(2,1)S(1)}, u32[]{:S(2)}, u32[]{:S(2)}) collective-permute-start(bf16[16,2048]{1,0:T(8,128)(2,1)S(1)} %side_sum.3), channel_id=1, source_target_pairs={{0,12},{1,13},{2,14},{3,15},{4,8},{5,9},{6,10},{7,11},{8,4},{9,5},... | collective-permute-start | bytes 196616 | tf_op jit(solution)/shard_map/ppermute | solution.py:283
  33.6 5.0 %collective-permute-start.14 = (bf16[16,2048]{1,0:T(8,128)(2,1)S(1)}, bf16[16,2048]{1,0:T(8,128)(2,1)S(1)}, u32[]{:S(2)}, u32[]{:S(2)}) collective-permute-start(bf16[16,2048]{1,0:T(8,128)(2,1)S(1)} %get-tuple-element.28), channel_id=1, source_target_pairs={{0,4},{1,5},{2,6},{3,7},{4,0},{5,1},{6,2},{7,3},{8,12},{9,13},{10,... | collective-permute-start | bytes 196616 | tf_op jit(solution)/shard_map/ppermute | solution.py:283
  34.6 4.3 %collective-permute-start.15 = (bf16[16,2048]{1,0:T(8,128)(2,1)S(1)}, bf16[16,2048]{1,0:T(8,128)(2,1)S(1)}, u32[]{:S(2)}, u32[]{:S(2)}) collective-permute-start(bf16[16,2048]{1,0:T(8,128)(2,1)S(1)} %get-tuple-element.29), channel_id=1, source_target_pairs={{0,2},{1,3},{2,0},{3,1},{4,6},{5,7},{6,4},{7,5},{8,10},{9,11},{10,... | collective-permute-start | bytes 196616 | tf_op jit(solution)/shard_map/ppermute | solution.py:283
